TPU v7x, 32 devices: a whole 2x2x4 slice. The times are simulated.
32 devices in a mesh: gy: 4 (over z), gx: 4 (over y, x), gz: 2 (over core).
Axes of the slice: x: 2, y: 2, z: 4, core: 2. Of those that a mesh axis runs over, the one named last changes fastest.
Arguments:
- velocity: float32 [3, 8, 768, 256], P(None, 'gx', 'gy', 'gz'), may hold values from -36 to 36
- tendency: float32 [3, 8, 768, 256], P(None, 'gx', 'gy', 'gz'), may hold values from -6 to 6
Outputs:
- new_velocity: float32 [3, 8, 768, 256], P(None, 'gx', 'gy', 'gz')
- eddy_viscosity: float32 [8, 768, 256], P('gx', 'gy', 'gz')
All inputs are finite; a program needn't handle non-finite values.
Results may differ from a plain program's by a relative error of at most 0.0003.
Values sent between devices are 32-bit elements; how exact they have to be, the bound alone decides.
No kernel may reach another device: no remote copies, remote signals or barrier semaphores. Data moves between devices by JAX's collectives and lax.ppermute only.
A program may use at most 128 MiB of HBM per device.

v0:
```python
import jax
import jax.numpy as jnp
from jax import lax
from jax.sharding import PartitionSpec as P


def passed_along(value, axis, steps):
    count = lax.axis_size(axis)
    initial, last = (max(0, -steps), min(count, count - steps))
    return lax.ppermute(value, axis, [(source, source + steps) for source in range(initial, last)])


def extended_2(cells, sides, width, closed):
    for axis, dim in sides:
        count = lax.axis_size(axis)
        ends = count if closed else count - 1
        head = lax.slice_in_dim(cells, 0, width, axis=dim)
        tail = lax.slice_in_dim(cells, cells.shape[dim] - width, cells.shape[dim], axis=dim)
        cells = jnp.concatenate(
            [
                lax.ppermute(tail, axis, [(i, (i + 1) % count) for i in range(ends)]),
                cells,
                lax.ppermute(head, axis, [((i + 1) % count, i) for i in range(ends)]),
            ],
            axis=dim,
        )
    return cells


def contract(left_tensor, right_tensor):
    diagonal_part = (
        left_tensor[0] * right_tensor[0]
        + left_tensor[1] * right_tensor[1]
        + left_tensor[2] * right_tensor[2]
    )
    return diagonal_part + 2.0 * (
        left_tensor[3] * right_tensor[3]
        + left_tensor[4] * right_tensor[4]
        + left_tensor[5] * right_tensor[5]
    )


def products(vectors):
    return jnp.stack(
        [
            vectors[0] * vectors[0],
            vectors[1] * vectors[1],
            vectors[2] * vectors[2],
            vectors[0] * vectors[1],
            vectors[0] * vectors[2],
            vectors[1] * vectors[2],
        ]
    )


def derivatives(extended):
    grad_x = (extended[:, 2:, 1:-1, 1:-1] - extended[:, :-2, 1:-1, 1:-1]) * 0.5
    grad_y = (extended[:, 1:-1, 2:, 1:-1] - extended[:, 1:-1, :-2, 1:-1]) * 0.5
    grad_z = (extended[:, 1:-1, 1:-1, 2:] - extended[:, 1:-1, 1:-1, :-2]) * 0.5
    strain = jnp.stack(
        [
            grad_x[0],
            grad_y[1],
            grad_z[2],
            0.5 * (grad_y[0] + grad_x[1]),
            0.5 * (grad_z[0] + grad_x[2]),
            0.5 * (grad_z[1] + grad_y[2]),
        ]
    )
    return (strain, jnp.sqrt(2.0 * contract(strain, strain)))


def build_fields(vectors, strain, magnitude):
    return jnp.concatenate([vectors, products(vectors), strain, magnitude[None] * strain], axis=0)


def test_filter(fields):
    along_x = (fields[:, :-2] + 2.0 * fields[:, 1:-1] + fields[:, 2:]) * 0.25
    return (along_x[..., :-2] + 2.0 * along_x[..., 1:-1] + along_x[..., 2:]) * 0.25


def germano(filtered):
    mean_vel = filtered[0:3]
    mean_prod = filtered[3:9]
    mean_strain = filtered[9:15]
    mean_scaled = filtered[15:21]
    leonard = mean_prod - products(mean_vel)
    filtered_mag = jnp.sqrt(2.0 * contract(mean_strain, mean_strain))
    model_term = 2.0 * (mean_scaled - 4.0 * filtered_mag[None] * mean_strain)
    return (contract(leonard, model_term), contract(model_term, model_term))


def diffusion(visc_ext, vel_ext, tendency):
    upward = 1500.0 * (visc_ext[:, 1:-1] + visc_ext[:, 2:])
    downward = 1500.0 * (visc_ext[:, :-2] + visc_ext[:, 1:-1])
    centre = vel_ext[:, :, 1:-1]
    source = (
        centre
        + tendency
        + 0.5 * (upward * (vel_ext[:, :, 2:] - centre) - downward * (centre - vel_ext[:, :, :-2]))
    )
    lower_band = jnp.broadcast_to(-0.5 * downward, centre.shape)
    middle = jnp.broadcast_to(1.0 + 0.5 * (upward + downward), centre.shape)
    higher = jnp.broadcast_to(-0.5 * upward, centre.shape)
    return (lower_band, middle, higher, source)


def local_sweep(lower_band, middle, higher, source):
    inner_rows = source.shape[2] - 1
    zero_plane = jnp.zeros_like(source[:, :, 0])
    ratio_prev = zero_plane
    carried = jnp.zeros((3,) + zero_plane.shape, jnp.float32)
    ratios = []
    values = []
    for index_row in range(inner_rows):
        pivot_val = middle[:, :, index_row] - lower_band[:, :, index_row] * ratio_prev
        left_term = lower_band[:, :, 0] if index_row == 0 else zero_plane
        right_term = higher[:, :, inner_rows - 1] if index_row == inner_rows - 1 else zero_plane
        column = jnp.stack([source[:, :, index_row], left_term, right_term])
        carried = (column - lower_band[:, :, index_row] * carried) / pivot_val
        ratio_prev = higher[:, :, index_row] / pivot_val
        ratios.append(ratio_prev)
        values.append(carried)
    result = values[inner_rows - 1]
    outputs = [result]
    for index_row in range(inner_rows - 2, -1, -1):
        result = values[index_row] - ratios[index_row] * result
        outputs.append(result)
    return jnp.stack(outputs[::-1], axis=3)


def wall_solve(lower_band, middle, higher, source):
    inner_rows = source.shape[2] - 1
    partial_sol = local_sweep(lower_band, middle, higher, source)
    near_last = partial_sol[:, :, :, inner_rows - 1]
    next_first = passed_along(partial_sol[:, :, :, 0], "gy", -1)
    last_low = lower_band[:, :, inner_rows]
    last_mid = middle[:, :, inner_rows]
    last_high = higher[:, :, inner_rows]
    last_src = source[:, :, inner_rows]
    coef_left = -last_low * near_last[1]
    coef_mid = last_mid - last_low * near_last[2] - last_high * next_first[1]
    coef_right = -last_high * next_first[2]
    coef_src = last_src - last_low * near_last[0] - last_high * next_first[0]
    zero_col = jnp.zeros_like(coef_mid)
    reduced = lax.all_gather(
        jnp.stack([coef_left, coef_mid, coef_right, coef_src])[None], "gy", axis=0, tiled=True
    )
    dev_count = reduced.shape[0]
    ratio_prev = zero_col
    carried = zero_col
    ratios = []
    values = []
    for index_dev in range(dev_count):
        pivot_val = reduced[index_dev, 1] - reduced[index_dev, 0] * ratio_prev
        carried = (reduced[index_dev, 3] - reduced[index_dev, 0] * carried) / pivot_val
        ratio_prev = reduced[index_dev, 2] / pivot_val
        ratios.append(ratio_prev)
        values.append(carried)
    result = values[dev_count - 1]
    outputs = [result]
    for index_dev in range(dev_count - 2, -1, -1):
        result = values[index_dev] - ratios[index_dev] * result
        outputs.append(result)
    padded_sol = jnp.concatenate([zero_col[None], jnp.stack(outputs[::-1])], axis=0)
    position = lax.axis_index("gy")
    left_value = lax.dynamic_index_in_dim(padded_sol, position, 0, keepdims=False)
    right_value = lax.dynamic_index_in_dim(padded_sol, position + 1, 0, keepdims=False)
    interior = (
        partial_sol[0]
        - partial_sol[1] * left_value[:, :, None]
        - partial_sol[2] * right_value[:, :, None]
    )
    return jnp.concatenate([interior, right_value[:, :, None]], axis=2)


def body(velocity, tendency):
    cycle_ext = extended_2(velocity, (("gx", 1), ("gz", 3)), 1, True)
    padded_vel = extended_2(cycle_ext, (("gy", 2),), 1, False)
    strain, magnitude = derivatives(padded_vel)
    fields = build_fields(velocity, strain, magnitude)
    extended = extended_2(fields, (("gx", 1), ("gz", 3)), 1, True)
    vel_ext = padded_vel[:, 1:-1, :, 1:-1]
    leo_model, model_model = germano(test_filter(extended))
    plane_lm, plane_mm = lax.psum(
        (jnp.sum(leo_model, axis=(0, 2)), jnp.sum(model_model, axis=(0, 2))), ("gx", "gz")
    )
    cell_count = velocity.shape[1] * lax.axis_size("gx") * velocity.shape[3] * lax.axis_size("gz")
    coefficient = jnp.maximum(plane_lm / cell_count / (plane_mm / cell_count + 1e-06), 0.0)
    eddy_visc = coefficient[None, :, None] * magnitude
    visc_ext = extended_2(1.0 + eddy_visc, (("gy", 1),), 1, False)
    lower_band, middle, higher, source = diffusion(visc_ext, vel_ext, tendency)
    solution = wall_solve(lower_band, middle, higher, source)
    return (solution, eddy_visc)


def solution(mesh):
    return jax.shard_map(
        body,
        mesh=mesh,
        in_specs=(P(None, "gx", "gy", "gz"), P(None, "gx", "gy", "gz")),
        out_specs=(P(None, "gx", "gy", "gz"), P("gx", "gy", "gz")),
        check_vma=False,
    )
```

profile of v0, /device:TPU:0, one launch (start us, length us, event | category | flops | bytes accessed | tf_op | source)
XLA Modules:
  0.0 248.3 jit_solution(3802975341727107026)
XLA Ops:
  1.8 3.0 %collective-permute-start.1 = (f32[3,1,192,128]{3,2,1,0:T(8,128)S(1)}, f32[3,1,192,128]{3,2,1,0:T(8,128)S(1)}, u32[]{:S(2)}, u32[]{:S(2)}) collective-permute-start(f32[3,1,192,128]{3,2,1,0:T(8,128)S(1)} %get-tuple-element.824), channel_id=1, source_target_pairs={{0,2},{2,4},{4,6},{6,0},{1,3},{3,5},{5,7},{7,1},{8,10},{10,12},{12... | collective-permute-start | bytes 884744 | tf_op jit(solution)/shard_map/ppermute | solution.py:21
  5.8 7.8 %collective-permute-done.1 = f32[3,1,192,128]{3,2,1,0:T(8,128)S(1)} collective-permute-done((f32[3,1,192,128]{3,2,1,0:T(8,128)S(1)}, f32[3,1,192,128]{3,2,1,0:T(8,128)S(1)}, u32[]{:S(2)}, u32[]{:S(2)}) %collective-permute-start.1) | collective-permute-done | bytes 294944 | tf_op jit(solution)/shard_map/ppermute | solution.py:21
  13.6 5.7 %collective-permute-done = f32[3,1,192,128]{3,2,1,0:T(8,128)S(1)} collective-permute-done((f32[3,1,192,128]{3,2,1,0:T(8,128)S(1)}, f32[3,1,192,128]{3,2,1,0:T(8,128)S(1)}, u32[]{:S(2)}, u32[]{:S(2)}) %collective-permute-start) | collective-permute-done | bytes 294944 | tf_op jit(solution)/shard_map/ppermute | solution.py:23
  21.8 1.7 copy.1021
  30.5 2.2 copy.1024
  35.0 4.5 %collective-permute-start.5 = (f32[3,4,1,130]{3,2,1,0:T(1,128)S(1)}, f32[3,4,1,130]{3,2,1,0:T(1,128)S(1)}, u32[]{:S(2)}, u32[]{:S(2)}) collective-permute-start(f32[3,4,1,130]{3,2,1,0:T(1,128)S(1)} %get-tuple-element.612), channel_id=1, source_target_pairs={{0,8},{8,16},{16,24},{1,9},{9,17},{17,25},{2,10},{10,18},{18,26},{... | collective-permute-start | bytes 18728 | tf_op jit(solution)/shard_map/ppermute | solution.py:21
  41.0 1.8 subtract_multiply_fusion
  43.7 1.5 collective-permute-start.6
  46.7 45.8 %collective-permute-done.6 = f32[21,1,192,128]{3,2,1,0:T(8,128)S(1)} collective-permute-done((f32[21,1,192,128]{3,2,1,0:T(8,128)S(1)}, f32[21,1,192,128]{3,2,1,0:T(8,128)S(1)}, u32[]{:S(2)}, u32[]{:S(2)}) %collective-permute-start.6) | collective-permute-done | bytes 2064416 | tf_op jit(solution)/shard_map/ppermute | solution.py:21
  92.5 41.6 %collective-permute-done.7 = f32[21,1,192,128]{3,2,1,0:T(8,128)S(1)} collective-permute-done((f32[21,1,192,128]{3,2,1,0:T(8,128)S(1)}, f32[21,1,192,128]{3,2,1,0:T(8,128)S(1)}, u32[]{:S(2)}, u32[]{:S(2)}) %collective-permute-start.7) | collective-permute-done | bytes 2064416 | tf_op jit(solution)/shard_map/ppermute | solution.py:23
  136.5 7.4 %fusion.821 = (f32[21,4,192,1]{3,2,1,0:T(8,128)}, f32[21,4,192,1]{3,2,1,0:T(8,128)}) fusion(f32[21,4,192,128]{3,2,1,0:T(8,128)S(1)} %pad_maximum_fusion.1), kind=kLoop, calls=%fused_computation.1513 | loop fusion | bytes 258048 | tf_op jit(solution)/shard_map/slice | solution.py:18
  143.9 5.7 %copy.1027 = f32[21,4,192,1]{2,1,3,0:T(4,128)S(1)} copy(f32[21,4,192,1]{3,2,1,0:T(8,128)} %get-tuple-element.602) | data formatting | bytes 129024 | tf_op jit(solution)/shard_map/slice | solution.py:18
  149.7 5.7 %copy.1028 = f32[21,4,192,1]{2,1,3,0:T(4,128)S(1)} copy(f32[21,4,192,1]{3,2,1,0:T(8,128)} %get-tuple-element.603) | data formatting | bytes 129024 | tf_op jit(solution)/shard_map/slice | solution.py:17
  155.9 4.7 %copy.1029 = f32[21,4,192,1]{3,2,1,0:T(8,128)} copy(f32[21,4,192,1]{2,1,3,0:T(4,128)S(1)} %collective-permute-done.8) | data formatting | bytes 129024 | tf_op jit(solution)/shard_map/ppermute | solution.py:21
  160.7 4.8 %copy.1030 = f32[21,4,192,1]{3,2,1,0:T(8,128)} copy(f32[21,4,192,1]{2,1,3,0:T(4,128)S(1)} %collective-permute-done.9) | data formatting | bytes 129024 | tf_op jit(solution)/shard_map/ppermute | solution.py:23
  165.4 13.2 %pad_maximum_fusion = f32[21,4,192,130]{3,2,1,0:T(8,128)S(1)} fusion(f32[21,4,192,1]{3,2,1,0:T(8,128)} %copy.1030, f32[21,1,192,128]{3,2,1,0:T(8,128)} %copy-done.5, f32[21,2,192,128]{3,2,1,0:T(8,128)} %copy-done.1, f32[21,1,192,128]{3,2,1,0:T(8,128)} %copy-done.4, f32[21,4,192,1]{3,2,1,0:T(8,128)} %copy.1029), kind=kLoop, calls=%fused_computation | loop fusion | flops 8386560 | bytes 16773120 | tf_op jit(solution)/shard_map/concatenate | solution.py:19
  178.6 4.2 %fusion = f32[21,2,192,130]{3,2,1,0:T(8,128)} fusion(f32[21,4,192,130]{3,2,1,0:T(8,128)S(1)} %pad_maximum_fusion), kind=kLoop, calls=%fused_computation.2 | loop fusion | flops 4193280 | bytes 16773120 | tf_op jit(solution)/shard_map/mul | solution.py:78
  182.9 9.4 %fusion.2 = f32[21,2,192,128]{3,2,1,0:T(8,128)S(1)} fusion(f32[21,2,192,130]{3,2,1,0:T(8,128)} %fusion), kind=kLoop, calls=%fused_computation.7 | loop fusion | flops 4128768 | bytes 16515072 | tf_op jit(solution)/shard_map/mul | solution.py:79
  193.2 14.0 %all-reduce.189 = (f32[192]{0:T(256)S(1)}, f32[192]{0:T(256)S(1)}) all-reduce(f32[192]{0:T(256)S(1)} %get-tuple-element.11, f32[192]{0:T(256)S(1)} %get-tuple-element.10), channel_id=1, replica_groups=mesh['gy'=4,'gx'=4,'gz'=2] {'gx','gz'}, use_global_device_ids=true, to_apply=%region_3.0 | all-reduce | flops 384 | bytes 3072 | tf_op jit(solution)/shard_map/psum | solution.py:185
  208.1 3.4 %collective-permute-start.11 = (f32[2,1,128]{2,1,0:T(1,128)S(1)}, f32[2,1,128]{2,1,0:T(1,128)S(1)}, u32[]{:S(2)}, u32[]{:S(2)}) collective-permute-start(f32[2,1,128]{2,1,0:T(1,128)S(1)} %slice.4872), channel_id=1, source_target_pairs={{0,8},{8,16},{16,24},{1,9},{9,17},{17,25},{2,10},{10,18},{18,26},{... | collective-permute-start | bytes 3080 | tf_op jit(solution)/shard_map/ppermute | solution.py:21
  211.7 1.5 collective-permute-start.10
  213.5 3.6 %collective-permute-done.10 = f32[2,1,128]{2,0,1:T(2,128)S(1)} collective-permute-done((f32[2,1,128]{2,0,1:T(2,128)S(1)}, f32[2,1,128]{2,0,1:T(2,128)S(1)}, u32[]{:S(2)}, u32[]{:S(2)}) %collective-permute-start.10) | collective-permute-done | bytes 1056 | tf_op jit(solution)/shard_map/ppermute | solution.py:23
  229.1 4.2 %collective-permute-done.12 = f32[3,3,2,128]{3,2,1,0:T(2,128)S(1)} collective-permute-done((f32[3,3,2,128]{3,2,1,0:T(2,128)S(1)}, f32[3,3,2,128]{3,2,1,0:T(2,128)S(1)}, u32[]{:S(2)}, u32[]{:S(2)}) %collective-permute-start.12) | collective-permute-done | bytes 9248 | tf_op jit(solution)/shard_map/ppermute | solution.py:10
  233.4 13.3 %all-gather = f32[16,3,2,128]{3,2,1,0:T(2,128)S(1)} all-gather(f32[4,3,2,128]{3,2,1,0:T(2,128)S(1)} %pad_maximum_fusion.18), channel_id=2, replica_groups=mesh['gy'=4,'gx'=4,'gz'=2] {'gy'}, dimensions={0}, use_global_device_ids=true | all-gather | bytes 61440 | tf_op jit(solution)/shard_map/all_gather | solution.py:146
  (314 shorter events, 35.4 us)
Async XLA Ops:
  0.6 18.7 %copy-start.2 = (f32[3,2,192,128]{3,2,1,0:T(8,128)S(1)}, f32[3,2,192,128]{3,2,1,0:T(8,128)}, u32[]{:S(2)}) copy-start(f32[3,2,192,128]{3,2,1,0:T(8,128)} %param.2) | copy-start | bytes 1769476
  1.8 11.8 %collective-permute-start.1 = (f32[3,1,192,128]{3,2,1,0:T(8,128)S(1)}, f32[3,1,192,128]{3,2,1,0:T(8,128)S(1)}, u32[]{:S(2)}, u32[]{:S(2)}) collective-permute-start(f32[3,1,192,128]{3,2,1,0:T(8,128)S(1)} %get-tuple-element.824), channel_id=1, source_target_pairs={{0,2},{2,4},{4,6},{6,0},{1,3},{3,5},{5,7},{7,1},{8,10},{10,12},{12... | collective-permute-start | bytes 884744 | tf_op jit(solution)/shard_map/ppermute | solution.py:21
  4.8 14.5 %collective-permute-start = (f32[3,1,192,128]{3,2,1,0:T(8,128)S(1)}, f32[3,1,192,128]{3,2,1,0:T(8,128)S(1)}, u32[]{:S(2)}, u32[]{:S(2)}) collective-permute-start(f32[3,1,192,128]{3,2,1,0:T(8,128)S(1)} %get-tuple-element.823), channel_id=1, source_target_pairs={{2,0},{4,2},{6,4},{0,6},{3,1},{5,3},{7,5},{1,7},{10,8},{12,10},{14... | collective-permute-start | bytes 884744 | tf_op jit(solution)/shard_map/ppermute | solution.py:23
  23.5 5.8 %collective-permute-start.2 = (f32[3,4,192,1]{2,1,3,0:T(4,128)S(1)}, f32[3,4,192,1]{2,1,3,0:T(4,128)}, u32[]{:S(2)}, u32[]{:S(2)}) collective-permute-start(f32[3,4,192,1]{2,1,3,0:T(4,128)S(1)} %copy.1021), channel_id=1, source_target_pairs={{0,1},{1,0},{2,3},{3,2},{4,5},{5,4},{6,7},{7,6},{8,9},{9,8},{10,11... | collective-permute-start | bytes 27656 | tf_op jit(solution)/shard_map/ppermute | solution.py:21
  24.6 5.8 %collective-permute-start.3 = (f32[3,4,192,1]{2,1,3,0:T(4,128)}, f32[3,4,192,1]{2,1,3,0:T(4,128)}, u32[]{:S(2)}, u32[]{:S(2)}) collective-permute-start(f32[3,4,192,1]{2,1,3,0:T(4,128)} %copy.1022), channel_id=1, source_target_pairs={{1,0},{0,1},{3,2},{2,3},{5,4},{4,5},{7,6},{6,7},{9,8},{8,9},{11,10... | collective-permute-start | bytes 27656 | tf_op jit(solution)/shard_map/ppermute | solution.py:23
  32.7 8.3 %copy-start.3 = (f32[3,4,192,1]{3,2,1,0:T(8,128)S(1)}, f32[3,4,192,1]{3,2,1,0:T(8,128)}, u32[]{:S(2)}) copy-start(f32[3,4,192,1]{3,2,1,0:T(8,128)} %copy.1024) | copy-start | bytes 27652
  33.7 6.6 %collective-permute-start.4 = (f32[3,4,1,130]{3,2,1,0:T(1,128)S(1)}, f32[3,4,1,130]{3,2,1,0:T(1,128)S(1)}, u32[]{:S(2)}, u32[]{:S(2)}) collective-permute-start(f32[3,4,1,130]{3,2,1,0:T(1,128)S(1)} %get-tuple-element.611), channel_id=1, source_target_pairs={{8,0},{16,8},{24,16},{9,1},{17,9},{25,17},{10,2},{18,10},{26,18},{... | collective-permute-start | bytes 18728 | tf_op jit(solution)/shard_map/ppermute | solution.py:23
  35.0 5.9 %collective-permute-start.5 = (f32[3,4,1,130]{3,2,1,0:T(1,128)S(1)}, f32[3,4,1,130]{3,2,1,0:T(1,128)S(1)}, u32[]{:S(2)}, u32[]{:S(2)}) collective-permute-start(f32[3,4,1,130]{3,2,1,0:T(1,128)S(1)} %get-tuple-element.612), channel_id=1, source_target_pairs={{0,8},{8,16},{16,24},{1,9},{9,17},{17,25},{2,10},{10,18},{18,26},{... | collective-permute-start | bytes 18728 | tf_op jit(solution)/shard_map/ppermute | solution.py:21
  40.3 2.5 %copy-start = (f32[21,2,192,128]{3,2,1,0:T(8,128)S(1)}, f32[21,2,192,128]{3,2,1,0:T(8,128)}, u32[]{:S(2)}) copy-start(f32[21,2,192,128]{3,2,1,0:T(8,128)} %get-tuple-element.819) | copy-start | bytes 12386308
  43.3 90.9 %copy-start.1 = (f32[21,2,192,128]{3,2,1,0:T(8,128)}, f32[21,2,192,128]{3,2,1,0:T(8,128)S(1)}, u32[]{:S(2)}) copy-start(f32[21,2,192,128]{3,2,1,0:T(8,128)S(1)} %multiply_dynamic-update-slice_fusion) | copy-start | bytes 12386308
  43.7 48.8 %collective-permute-start.6 = (f32[21,1,192,128]{3,2,1,0:T(8,128)S(1)}, f32[21,1,192,128]{3,2,1,0:T(8,128)S(1)}, u32[]{:S(2)}, u32[]{:S(2)}) collective-permute-start(f32[21,1,192,128]{3,2,1,0:T(8,128)S(1)} %get-tuple-element.608), channel_id=1, source_target_pairs={{0,2},{2,4},{4,6},{6,0},{1,3},{3,5},{5,7},{7,1},{8,10},{10,12},{12... | collective-permute-start | bytes 6193160 | tf_op jit(solution)/shard_map/ppermute | solution.py:21
  45.3 88.9 %collective-permute-start.7 = (f32[21,1,192,128]{3,2,1,0:T(8,128)S(1)}, f32[21,1,192,128]{3,2,1,0:T(8,128)S(1)}, u32[]{:S(2)}, u32[]{:S(2)}) collective-permute-start(f32[21,1,192,128]{3,2,1,0:T(8,128)S(1)} %get-tuple-element.609), channel_id=1, source_target_pairs={{2,0},{4,2},{6,4},{0,6},{3,1},{5,3},{7,5},{1,7},{10,8},{12,10},{14... | collective-permute-start | bytes 6193160 | tf_op jit(solution)/shard_map/ppermute | solution.py:23
  92.5 41.6 %copy-start.4 = (f32[21,1,192,128]{3,2,1,0:T(8,128)}, f32[21,1,192,128]{3,2,1,0:T(8,128)S(1)}, u32[]{:S(2)}) copy-start(f32[21,1,192,128]{3,2,1,0:T(8,128)S(1)} %collective-permute-done.6) | copy-start | bytes 6193156
  134.2 1.4 copy-start.5
  149.6 6.3 %collective-permute-start.8 = (f32[21,4,192,1]{2,1,3,0:T(4,128)S(1)}, f32[21,4,192,1]{2,1,3,0:T(4,128)S(1)}, u32[]{:S(2)}, u32[]{:S(2)}) collective-permute-start(f32[21,4,192,1]{2,1,3,0:T(4,128)S(1)} %copy.1027), channel_id=1, source_target_pairs={{0,1},{1,0},{2,3},{3,2},{4,5},{5,4},{6,7},{7,6},{8,9},{9,8},{10,11... | collective-permute-start | bytes 193544 | tf_op jit(solution)/shard_map/ppermute | solution.py:21
  155.4 5.3 %collective-permute-start.9 = (f32[21,4,192,1]{2,1,3,0:T(4,128)S(1)}, f32[21,4,192,1]{2,1,3,0:T(4,128)S(1)}, u32[]{:S(2)}, u32[]{:S(2)}) collective-permute-start(f32[21,4,192,1]{2,1,3,0:T(4,128)S(1)} %copy.1028), channel_id=1, source_target_pairs={{1,0},{0,1},{3,2},{2,3},{5,4},{4,5},{7,6},{6,7},{9,8},{8,9},{11,10... | collective-permute-start | bytes 193544 | tf_op jit(solution)/shard_map/ppermute | solution.py:23
  208.1 9.5 %copy-start.6 = (f32[3,2,192,128]{3,2,1,0:T(8,128)S(1)}, f32[3,2,192,128]{3,2,1,0:T(8,128)}, u32[]{:S(2)}) copy-start(f32[3,2,192,128]{3,2,1,0:T(8,128)} %get-tuple-element.600) | copy-start | bytes 1769476
  208.1 9.5 %copy-start.7 = (f32[3,2,192,128]{3,2,1,0:T(8,128)S(1)}, f32[3,2,192,128]{3,2,1,0:T(8,128)}, u32[]{:S(2)}) copy-start(f32[3,2,192,128]{3,2,1,0:T(8,128)} %get-tuple-element.601) | copy-start | bytes 1769476
  208.1 9.5 %copy-start.8 = (f32[3,2,192,128]{3,2,1,0:T(8,128)S(1)}, f32[3,2,192,128]{3,2,1,0:T(8,128)}, u32[]{:S(2)}) copy-start(f32[3,2,192,128]{3,2,1,0:T(8,128)} %param.3) | copy-start | bytes 1769476
  208.1 5.1 %collective-permute-start.11 = (f32[2,1,128]{2,1,0:T(1,128)S(1)}, f32[2,1,128]{2,1,0:T(1,128)S(1)}, u32[]{:S(2)}, u32[]{:S(2)}) collective-permute-start(f32[2,1,128]{2,1,0:T(1,128)S(1)} %slice.4872), channel_id=1, source_target_pairs={{0,8},{8,16},{16,24},{1,9},{9,17},{17,25},{2,10},{10,18},{18,26},{... | collective-permute-start | bytes 3080 | tf_op jit(solution)/shard_map/ppermute | solution.py:21
  211.7 5.5 %collective-permute-start.10 = (f32[2,1,128]{2,0,1:T(2,128)S(1)}, f32[2,1,128]{2,0,1:T(2,128)S(1)}, u32[]{:S(2)}, u32[]{:S(2)}) collective-permute-start(f32[2,1,128]{2,0,1:T(2,128)S(1)} %slice.4871), channel_id=1, source_target_pairs={{8,0},{16,8},{24,16},{9,1},{17,9},{25,17},{10,2},{18,10},{26,18},{... | collective-permute-start | bytes 3080 | tf_op jit(solution)/shard_map/ppermute | solution.py:23
  227.8 5.6 %collective-permute-start.12 = (f32[3,3,2,128]{3,2,1,0:T(2,128)S(1)}, f32[3,3,2,128]{3,2,1,0:T(2,128)S(1)}, u32[]{:S(2)}, u32[]{:S(2)}) collective-permute-start(f32[3,3,2,128]{3,2,1,0:T(2,128)S(1)} %get-tuple-element.15), channel_id=1, source_target_pairs={{8,0},{16,8},{24,16},{9,1},{17,9},{25,17},{10,2},{18,10},{26,18},{... | collective-permute-start | bytes 27656 | tf_op jit(solution)/shard_map/ppermute | solution.py:10
where the time goes:
time: 249 us; the launch traced here: 248 us
  waiting for transfers between devices  109 us (44%)
  other arithmetic  47 us (19%)
  local copies, waits for them, and re-layouts  42.4 us (17%)
  blocking collectives  27.3 us (11%)
  starting transfers between devices  20.2 us (8%)
    ppermute x6, waiting for transfers between devices, extended_2(): lax.ppermute(tail, axis, [(i, (i + 1) % count) for i in range(ends)])  54.3 us
    ppermute x6, waiting for transfers between devices, extended_2(): lax.ppermute(head, axis, [((i + 1) % count, i) for i in range(ends)])  50.9 us
    slice x5, local copies, waits for them, and re-layouts, extended_2(): lax.slice_in_dim(cells, cells.shape[dim] - width, cells.shape[dim], axis=...  15.3 us
    concatenate x2, other arithmetic, extended_2(): jnp.concatenate([lax.ppermute(tail, axis, [(i, (i + 1) % count) for i in...  14.2 us
    psum x1, blocking collectives, body(): lax.psum((jnp.sum(leo_model, axis=(0, 2)), jnp.sum(model_model, axis=(0,...  14 us
    all_gather x1, blocking collectives, wall_solve(): lax.all_gather(jnp.stack([coef_left, coef_mid, coef_right, coef_src])[Non...  13.3 us
    ppermute x6, starting transfers between devices, extended_2(): lax.ppermute(tail, axis, [(i, (i + 1) % count) for i in range(ends)])  12.6 us
    mul x1, other arithmetic, test_filter(): (along_x[..., :-2] + 2.0 * along_x[..., 1:-1] + along_x[..., 2:]) * 0.25  9.37 us
  transfers between devices with their start and end apart: 13, of which 7 were waited for; matrix products, arithmetic and copies ran while one was open for 7% of the time, Pallas kernels for 0%

commit v1 on v0

v1 whole, which is shorter than its diff:
```python
import functools

import jax
import jax.numpy as jnp
from jax import lax
from jax.experimental import pallas as pl
from jax.experimental.pallas import tpu as pltpu
from jax.sharding import PartitionSpec as P

LANES = 128
SEGMENTS = 8
VMEM_BYTES = 24 * 2**20


def strain_parts(centre, below, above):
    nx, nz = centre[0].shape
    grad_x = [pltpu.roll(f, nx - 1, 0) - pltpu.roll(f, 1, 0) for f in centre]
    grad_z = [pltpu.roll(f, nz - 1, 1) - pltpu.roll(f, 1, 1) for f in centre]
    grad_y = [up - down for up, down in zip(above, below)]
    return (
        grad_x[0],
        grad_y[1],
        grad_z[2],
        grad_y[0] + grad_x[1],
        grad_z[0] + grad_x[2],
        grad_z[1] + grad_y[2],
    )


def strain_size(parts):
    diagonal = parts[0] * parts[0] + parts[1] * parts[1] + parts[2] * parts[2]
    mixed = parts[3] * parts[3] + parts[4] * parts[4] + parts[5] * parts[5]
    return jnp.sqrt(0.5 * diagonal + 0.25 * mixed)


def smooth(field):
    field = field + pltpu.roll(field, 1, 0)
    field = field + pltpu.roll(field, 1, 0)
    field = field + pltpu.roll(field, 1, 1)
    return field + pltpu.roll(field, 1, 1)


def products(v):
    return (v[0] * v[0], v[1] * v[1], v[2] * v[2], v[0] * v[1], v[0] * v[2], v[1] * v[2])


def germano_kernel(nz_parts, recv, below, above, out, planes, vel, filt, mag, lm, mm):
    count, _, width, rows, _ = recv.shape
    nx = (count // nz_parts) * width
    nz = nz_parts * LANES
    for k in range(count):
        x0, zb = (k // nz_parts) * width, k % nz_parts
        lanes = slice(zb * LANES, (zb + 1) * LANES)
        for c in range(3):
            for x in range(width):
                planes[c, zb, (x0 + x) * rows : (x0 + x + 1) * rows, :] = recv[k, c, x]
            vel[c, 0, x0 : x0 + width, lanes] = below[k, c]
            vel[c, rows + 1, x0 : x0 + width, lanes] = above[k, c]
    for c in range(3):
        for y in range(rows):
            for zb in range(nz_parts):
                lanes = slice(zb * LANES, (zb + 1) * LANES)
                vel[c, y + 1, :, lanes] = planes[c, zb, pl.ds(y, nx, stride=rows), :]
    for c in range(3):
        for y in range(rows + 2):
            filt[c, y] = smooth(vel[c, y])

    for y in range(rows):
        centre = [vel[c, y + 1] for c in range(3)]
        strain = strain_parts(centre, [vel[c, y] for c in range(3)], [vel[c, y + 2] for c in range(3)])
        size = strain_size(strain)
        for zb in range(nz_parts):
            mag[zb, y * nx : (y + 1) * nx, :] = size[:, zb * LANES : (zb + 1) * LANES]
        mean = [filt[c, y + 1] for c in range(3)]
        mean_strain = strain_parts(mean, [filt[c, y] for c in range(3)], [filt[c, y + 2] for c in range(3)])
        mean_size = 0.25 * strain_size(mean_strain)
        model = [smooth(size * s) - mean_size * f for s, f in zip(strain, mean_strain)]
        scaled = [0.0625 * f for f in mean]
        pairs = (
            (mean[0], scaled[0]),
            (mean[1], scaled[1]),
            (mean[2], scaled[2]),
            (mean[0], scaled[1]),
            (mean[0], scaled[2]),
            (mean[1], scaled[2]),
        )
        leonard = [smooth(p) - f * g for p, (f, g) in zip(products(centre), pairs)]
        left = leonard[0] * model[0]
        for i in range(1, 6):
            left = left + leonard[i] * model[i]
        right = (model[0] * model[0] + model[1] * model[1] + model[2] * model[2]) + 0.5 * (
            model[3] * model[3] + model[4] * model[4] + model[5] * model[5]
        )
        for total, ref in ((left, lm), (right, mm)):
            part = total[:, :LANES]
            for zb in range(1, nz_parts):
                part = part + total[:, zb * LANES : (zb + 1) * LANES]
            ref[y * nx : (y + 1) * nx, :] = part

    def plane_sum(ref):
        part = ref[pl.ds(0, rows, stride=nx), :]
        for x in range(1, nx):
            part = part + ref[pl.ds(x, rows, stride=nx), :]
        return jnp.sum(part, axis=1, keepdims=True) * (1.0 / (256.0 * nx * nz))

    coefficient = jnp.maximum(plane_sum(lm) / (plane_sum(mm) + 1e-06), 0.0)
    for k in range(count):
        x0, zb = (k // nz_parts) * width, k % nz_parts
        for x in range(width):
            out[k, x] = coefficient * mag[zb, pl.ds(x0 + x, rows, stride=nx), :]


def sweep_kernel(back, velocity, tendency, eddy, reduced, factors, tree):
    count, width, rows, _ = back.shape
    length = count * rows // SEGMENTS
    for k in range(count):
        for x in range(width):
            eddy[x, k * rows : (k + 1) * rows, :] = back[k, x]

    def row(ref, index, j):
        return ref[(*index, pl.ds(j, SEGMENTS, stride=length), slice(None))]

    for x in range(width):
        visc = 1.0 + row(eddy, (x,), 0)
        visc_first = visc
        q = jnp.ones_like(visc)
        m = jnp.ones_like(visc)
        corner = jnp.zeros_like(visc)
        first = [jnp.zeros_like(visc)] * 3
        value = None
        for j in range(length):
            if j < length - 1:
                visc_next = 1.0 + row(eddy, (x,), j + 1)
                link = 750.0 * (visc + visc_next)
                inverse = 1.0 / (q + link)
            else:
                visc_next = None
                link = None
                inverse = 1.0 / q
            left = m * inverse
            corner = corner + m * left
            source = [
                2.0 * row(velocity, (c, x), j) + row(tendency, (c, x), j) for c in range(3)
            ]
            if j > 0:
                source = [s + link_before * v for s, v in zip(source, value)]
            value = [s * inverse for s in source]
            first = [f + m * v for f, v in zip(first, value)]
            for c in range(3):
                factors[x, j, c] = value[c]
            factors[x, j, 3] = left
            if j < length - 1:
                ratio = link * inverse
                factors[x, j, 4] = ratio
                q = 1.0 + link * (q * inverse)
                m = m * ratio
                link_before = link
                visc = visc_next
            else:
                factors[x, j, 4] = inverse
        last = value
        across = left
        end = inverse
        links = 750.0 * (visc + pltpu.roll(visc_first, SEGMENTS - 1, 0))
        level, step = 0, 1
        while step < SEGMENTS:
            def other(v):
                return pltpu.roll(v, SEGMENTS - step, 0)

            link = links if step == 1 else pltpu.roll(links, SEGMENTS - (step - 1), 0)
            across_b = other(across)
            stiff = link / (1.0 + link * (end + other(corner)))
            flux = [stiff * (g - other(f)) for g, f in zip(last, first)]
            from_left = stiff * across
            from_right = stiff * across_b
            for c in range(3):
                tree[x, level, c] = flux[c]
            tree[x, level, 3] = from_left
            tree[x, level, 4] = from_right
            first = [f - across * t for f, t in zip(first, flux)]
            last = [other(g) + across_b * t for g, t in zip(last, flux)]
            corner = corner - across * from_left
            end = other(end) - across_b * from_right
            across = from_left * across_b
            level, step = level + 1, step * 2
        rows_out = [*first, *last, corner, across, end, visc_first]
        for i, v in enumerate(rows_out):
            reduced[i * width + x : i * width + x + 1, :] = v[0:1, :]
        i = len(rows_out)
        reduced[i * width + x : i * width + x + 1, :] = visc[SEGMENTS - 1 :, :]


def finish_kernel(devices, position, factors, tree, velocity, *rest):
    reduced, (out, gathered, fluxes) = rest[:devices], rest[devices:]
    width, length = factors.shape[:2]
    here = position[0]
    for shift in range(devices):
        gathered[lax.rem(here - shift + devices, devices)] = reduced[shift][...]

    def part(device, i):
        return gathered[device, i * width : (i + 1) * width, :]

    ratios, values = [], []
    for i in range(devices + 1):
        if i == 0:
            link = 750.0 * part(0, 9)
            total = part(0, 6)
            source = [-part(0, c) for c in range(3)]
        elif i == devices:
            link = 750.0 * part(i - 1, 10)
            total = part(i - 1, 8)
            source = [part(i - 1, 3 + c) for c in range(3)]
        else:
            link = 750.0 * (part(i - 1, 10) + part(i, 9))
            total = part(i - 1, 8) + part(i, 6)
            source = [part(i - 1, 3 + c) - part(i, c) for c in range(3)]
        pivot = 1.0 + link * total
        if i > 0:
            before = part(i - 1, 7)
            pivot = pivot - link * before * ratios[-1]
            source = [s + before * v for s, v in zip(source, values[-1])]
        scale = link / pivot
        values.append([scale * s for s in source])
        if i < devices:
            ratios.append(scale * part(i, 7))
    flux = values[devices]
    for i in range(devices, -1, -1):
        if i < devices:
            flux = [v + ratios[i] * f for v, f in zip(values[i], flux)]
        for c in range(3):
            fluxes[i, c * width : (c + 1) * width, :] = flux[c]

    sublane = lax.broadcasted_iota(jnp.int32, (SEGMENTS, LANES), 0)
    levels = tree.shape[1]
    for x in range(width):
        for c in range(3):
            r = c * width + x
            left = jnp.broadcast_to(fluxes[here, r : r + 1, :], (SEGMENTS, LANES))
            right = -jnp.broadcast_to(fluxes[here + 1, r : r + 1, :], (SEGMENTS, LANES))
            for level in range(levels - 1, -1, -1):
                step = 2**level
                through = tree[x, level, c] + tree[x, level, 3] * left - tree[x, level, 4] * right
                second = lax.rem(sublane, 2 * step) == step
                left = jnp.where(second, pltpu.roll(through, step, 0), left)
                right = jnp.where(second, pltpu.roll(right, step, 0), -through)
            value = right
            for j in range(length - 1, -1, -1):
                value = (factors[x, j, c] + factors[x, j, 3] * left) + factors[x, j, 4] * value
                rows = pl.ds(j, SEGMENTS, stride=length)
                out[c, x, rows, :] = value - velocity[c, x, rows, :]


def in_vmem(count):
    return [pl.BlockSpec(memory_space=pltpu.VMEM)] * count


def params():
    return pltpu.CompilerParams(vmem_limit_bytes=VMEM_BYTES)


def body(velocity, tendency):
    _, width, cells, lanes = velocity.shape
    nz_parts = lax.axis_size("gz")
    count = lax.axis_size("gx") * nz_parts
    walls = lax.axis_size("gy")
    rows = cells // count
    nx = lax.axis_size("gx") * width
    nz = nz_parts * lanes
    f32 = jnp.float32

    chunks = velocity.reshape(3, width, count, rows, lanes).transpose(2, 0, 1, 3, 4)
    recv = lax.all_to_all(chunks, ("gx", "gz"), split_axis=0, concat_axis=0, tiled=True)
    total = walls * count
    everyone = ("gy", "gx", "gz")
    below = lax.ppermute(recv[:, :, :, rows - 1], everyone, [(i, i + 1) for i in range(total - 1)])
    above = lax.ppermute(recv[:, :, :, 0], everyone, [(i + 1, i) for i in range(total - 1)])
    eddy_chunks = pl.pallas_call(
        functools.partial(germano_kernel, nz_parts),
        out_shape=jax.ShapeDtypeStruct((count, width, rows, lanes), f32),
        in_specs=in_vmem(3),
        out_specs=pl.BlockSpec(memory_space=pltpu.VMEM),
        scratch_shapes=[
            pltpu.VMEM((3, nz_parts, nx * rows, lanes), f32),
            pltpu.VMEM((3, rows + 2, nx, nz), f32),
            pltpu.VMEM((3, rows + 2, nx, nz), f32),
            pltpu.VMEM((nz_parts, rows * nx, lanes), f32),
            pltpu.VMEM((rows * nx, lanes), f32),
            pltpu.VMEM((rows * nx, lanes), f32),
        ],
        compiler_params=params(),
        name="germano",
    )(recv, below, above)
    back = lax.all_to_all(eddy_chunks, ("gx", "gz"), split_axis=0, concat_axis=0, tiled=True)

    length = cells // SEGMENTS
    levels = SEGMENTS.bit_length() - 1
    packed = -(-11 * width // 8) * 8
    eddy, reduced, factors, tree = pl.pallas_call(
        sweep_kernel,
        out_shape=(
            jax.ShapeDtypeStruct((width, cells, lanes), f32),
            jax.ShapeDtypeStruct((packed, lanes), f32),
            jax.ShapeDtypeStruct((width, length, 5, SEGMENTS, lanes), f32),
            jax.ShapeDtypeStruct((width, levels, 5, SEGMENTS, lanes), f32),
        ),
        in_specs=in_vmem(3),
        out_specs=tuple(in_vmem(4)),
        compiler_params=params(),
        name="sweep",
    )(back, velocity, tendency)

    others = [
        lax.ppermute(reduced, "gy", [(i, (i + shift) % walls) for i in range(walls)])
        for shift in range(1, walls)
    ]
    position = lax.axis_index("gy").astype(jnp.int32).reshape(1)
    new_velocity = pl.pallas_call(
        functools.partial(finish_kernel, walls),
        out_shape=jax.ShapeDtypeStruct(velocity.shape, f32),
        in_specs=[pl.BlockSpec(memory_space=pltpu.SMEM)] + in_vmem(3 + walls),
        out_specs=pl.BlockSpec(memory_space=pltpu.VMEM),
        scratch_shapes=[
            pltpu.VMEM((walls, packed, lanes), f32),
            pltpu.VMEM((walls + 1, -(-3 * width // 8) * 8, lanes), f32),
        ],
        compiler_params=params(),
        name="finish",
    )(position, factors, tree, velocity, reduced, *others)
    return (new_velocity, eddy)


def solution(mesh):
    return jax.shard_map(
        body,
        mesh=mesh,
        in_specs=(P(None, "gx", "gy", "gz"), P(None, "gx", "gy", "gz")),
        out_specs=(P(None, "gx", "gy", "gz"), P("gx", "gy", "gz")),
        check_vma=False,
    )
```

time: 249 us -> 71.8 us (0.29)
  waiting for transfers between devices: 109 us -> 5.23 us
  other arithmetic: 47 us -> 0 us
  local copies, waits for them, and re-layouts: 42.4 us -> 1.59 us
  Pallas kernels: 0 us -> 27.3 us
  starting transfers between devices: 20.2 us -> 9.61 us
    ppermute x13 -> x5, waiting for transfers between devices: 109 us -> 5.23 us  [the longest x3 4.48 us: body(): lax.ppermute(reduced, 'gy', [(i, (i + shift) % walls) for i in range(wall...]
    pallas_call x0 -> x3, Pallas kernels: none -> 27.3 us  [the longest x1 25.5 us: body(): pl.pallas_call(functools.partial(germano_kernel, nz_parts), out_shape=jax...]
    all_to_all x0 -> x2, blocking collectives: none -> 27.1 us  [the longest x1 15.4 us: body(): lax.all_to_all(chunks, ('gx', 'gz'), split_axis=0, concat_axis=0, tiled=T...]
    slice x32 -> x0, local copies, waits for them, and re-layouts: 25.3 us -> none  [the longest x5 15.3 us: extended_2(): lax.slice_in_dim(cells, cells.shape[dim] - width, cells.shape[dim], axis=...]
    mul x7 -> x0, other arithmetic: 16 us -> none  [the longest x1 9.37 us: test_filter(): (along_x[..., :-2] + 2.0 * along_x[..., 1:-1] + along_x[..., 2:]) * 0.25]
    concatenate x4 -> x0, other arithmetic: 14.5 us -> none  [the longest x2 14.2 us: extended_2(): jnp.concatenate([lax.ppermute(tail, axis, [(i, (i + 1) % count) for i in...]
    psum x1 -> x0, blocking collectives: 14 us -> none  [body(): lax.psum((jnp.sum(leo_model, axis=(0, 2)), jnp.sum(model_model, axis=(0,...]
    all_gather x1 -> x0, blocking collectives: 13.3 us -> none  [wall_solve(): lax.all_gather(jnp.stack([coef_left, coef_mid, coef_right, coef_src])[Non...]
  transfers between devices with their start and end apart: 13 -> 5, of which waited for: 7 -> 4; matrix products, arithmetic and copies ran while one was open for 7% -> 0% of each run, Pallas kernels for 0% -> 0%
where the time goes in v1:
time: 71.8 us; the launch traced here: 71.5 us
  Pallas kernels  27.3 us (38%)
  blocking collectives  27.1 us (38%)
  starting transfers between devices  9.61 us (13%)
  waiting for transfers between devices  5.23 us (7%)
  local copies, waits for them, and re-layouts  1.59 us (2%)
    pallas_call x1, Pallas kernels, body(): pl.pallas_call(functools.partial(germano_kernel, nz_parts), out_shape=jax...  25.5 us
    all_to_all x1, blocking collectives, body(): lax.all_to_all(chunks, ('gx', 'gz'), split_axis=0, concat_axis=0, tiled=T...  15.4 us
    all_to_all x1, blocking collectives, body(): lax.all_to_all(eddy_chunks, ('gx', 'gz'), split_axis=0, concat_axis=0, ti...  11.7 us
    ppermute x3, starting transfers between devices, body(): lax.ppermute(reduced, 'gy', [(i, (i + shift) % walls) for i in range(wall...  5.28 us
    ppermute x3, waiting for transfers between devices, body(): lax.ppermute(reduced, 'gy', [(i, (i + shift) % walls) for i in range(wall...  4.48 us
    ppermute x1, starting transfers between devices, body(): lax.ppermute(recv[:, :, :, rows - 1], everyone, [(i, i + 1) for i in rang...  3.03 us
    transpose x1, local copies, waits for them, and re-layouts, body(): velocity.reshape(3, width, count, rows, lanes).transpose(2, 0, 1, 3, 4)  1.52 us
  transfers between devices with their start and end apart: 5, of which 4 were waited for; matrix products, arithmetic and copies ran while one was open for 0% of the time, Pallas kernels for 0%

profile of v1, /device:TPU:0, one launch (start us, length us, event | category | flops | bytes accessed | tf_op | source)
XLA Modules:
  0.0 71.5 jit_solution(5503207027983893383)
XLA Ops:
  0.6 1.5 %copy.7 = f32[8,3,2,24,128]{4,2,1,3,0:T(2,128)S(1)} copy(f32[8,3,2,24,128]{4,3,0,2,1:T(8,128)} %bitcast.12) | data formatting | bytes 1179648 | tf_op jit(solution)/shard_map/transpose | solution.py:271
  2.2 15.4 %all_to_all.10 = f32[8,3,2,24,128]{4,2,1,3,0:T(2,128)S(1)} all-to-all(f32[8,3,2,24,128]{4,2,1,3,0:T(2,128)S(1)} %copy.7), channel_id=1, replica_groups=mesh['gy'=4,'gx'=4,'gz'=2] {'gx','gz'}, dimensions={0} | all-to-all | bytes 1179648 | tf_op jit(solution)/shard_map/all_to_all | solution.py:272
  17.6 1.3 %collective-permute-start.1 = (f32[8,3,2,128]{3,2,1,0:T(2,128)S(1)}, f32[8,3,2,128]{3,2,1,0:T(2,128)S(1)}, u32[]{:S(2)}, u32[]{:S(2)}) collective-permute-start(f32[8,3,2,128]{3,2,1,0:T(2,128)S(1)} %get-tuple-element.10), channel_id=1, source_target_pairs={{1,0},{2,1},{3,2},{4,3},{5,4},{6,5},{7,6},{8,7},{9,8},{10,9},{11,1... | collective-permute-start | bytes 73736 | tf_op jit(solution)/shard_map/ppermute | solution.py:276
  18.9 3.0 %collective-permute-start = (f32[8,3,2,128]{3,2,1,0:T(2,128)S(1)}, f32[8,3,2,128]{3,2,1,0:T(2,128)S(1)}, u32[]{:S(2)}, u32[]{:S(2)}) collective-permute-start(f32[8,3,2,128]{3,2,1,0:T(2,128)S(1)} %get-tuple-element.11), channel_id=1, source_target_pairs={{0,1},{1,2},{2,3},{3,4},{4,5},{5,6},{6,7},{7,8},{8,9},{9,10},{10,1... | collective-permute-start | bytes 73736 | tf_op jit(solution)/shard_map/ppermute | solution.py:275
  22.0 0.0 copy-start
  22.0 0.0 copy-start.1
  22.0 0.0 collective-permute-done.1.above
  22.0 0.7 %collective-permute-done.below = f32[8,3,2,128]{3,2,1,0:T(2,128)S(1)} collective-permute-done((f32[8,3,2,128]{3,2,1,0:T(2,128)S(1)}, f32[8,3,2,128]{3,2,1,0:T(2,128)S(1)}, u32[]{:S(2)}, u32[]{:S(2)}) %collective-permute-start) | collective-permute-done | bytes 24608 | tf_op jit(solution)/shard_map/ppermute | solution.py:275
  22.8 25.5 %germano.1 = f32[8,2,24,128]{3,2,1,0:T(8,128)S(1)} custom-call(f32[8,3,2,24,128]{4,3,2,1,0:T(8,128)S(1)} %copy.10.recv, f32[8,3,2,128]{3,2,1,0:T(2,128)S(1)} %collective-permute-done.below, f32[8,3,2,128]{3,2,1,0:T(2,128)S(1)} %collective-permute-done.1.above), custom_call_target="tpu_custom_call" | custom-call | tf_op jit(solution)/shard_map/germano/pallas_call | solution.py:277
  48.2 11.7 %all_to_all.11.back = f32[8,2,24,128]{3,2,1,0:T(8,128)S(1)} all-to-all(f32[8,2,24,128]{3,2,1,0:T(8,128)S(1)} %germano.1), channel_id=1, replica_groups=mesh['gy'=4,'gx'=4,'gz'=2] {'gx','gz'}, dimensions={0} | all-to-all | bytes 393216 | tf_op jit(solution)/shard_map/all_to_all | solution.py:293
  59.9 0.0 copy-done
  59.9 0.0 copy-done.1
  59.9 0.7 sweep.1
  60.6 4.3 %collective-permute-start.4 = (f32[24,128]{1,0:T(8,128)S(1)}, f32[24,128]{1,0:T(8,128)S(1)}, u32[]{:S(2)}, u32[]{:S(2)}) collective-permute-start(f32[24,128]{1,0:T(8,128)S(1)} %get-tuple-element.8.rest_0_), channel_id=1, source_target_pairs={{0,24},{8,0},{16,8},{24,16},{1,25},{9,1},{17,9},{25,17},{2,26},{10... | collective-permute-start | bytes 36872 | tf_op jit(solution)/shard_map/ppermute | solution.py:313
  64.9 0.0 collective-permute-start.3
  64.9 1.0 %collective-permute-start.2 = (f32[24,128]{1,0:T(8,128)S(1)}, f32[24,128]{1,0:T(8,128)S(1)}, u32[]{:S(2)}, u32[]{:S(2)}) collective-permute-start(f32[24,128]{1,0:T(8,128)S(1)} %get-tuple-element.8.rest_0_), channel_id=1, source_target_pairs={{0,8},{8,16},{16,24},{24,0},{1,9},{9,17},{17,25},{25,1},{2,10},{10... | collective-permute-start | bytes 36872 | tf_op jit(solution)/shard_map/ppermute | solution.py:313
  65.9 0.4 collective-permute-done.4.rest_3_
  66.3 3.2 %collective-permute-done.3.rest_2_ = f32[24,128]{1,0:T(8,128)S(1)} collective-permute-done((f32[24,128]{1,0:T(8,128)S(1)}, f32[24,128]{1,0:T(8,128)S(1)}, u32[]{:S(2)}, u32[]{:S(2)}) %collective-permute-start.3) | collective-permute-done | bytes 12320 | tf_op jit(solution)/shard_map/ppermute | solution.py:313
  69.5 0.9 %collective-permute-done.2.rest_1_ = f32[24,128]{1,0:T(8,128)S(1)} collective-permute-done((f32[24,128]{1,0:T(8,128)S(1)}, f32[24,128]{1,0:T(8,128)S(1)}, u32[]{:S(2)}, u32[]{:S(2)}) %collective-permute-start.2) | collective-permute-done | bytes 12320 | tf_op jit(solution)/shard_map/ppermute | solution.py:313
  70.4 1.1 %finish.1 = f32[3,2,192,128]{3,2,1,0:T(8,128)} custom-call(s32[1]{0:T(128)} %bitcast.position, f32[2,24,5,8,128]{4,3,2,1,0:T(8,128)S(1)} %get-tuple-element.6.factors, f32[2,3,5,8,128]{4,3,2,1,0:T(8,128)S(1)} %get-tuple-element.7.tree, f32[3,2,192,128]{3,2,1,0:T(8,128)S(1)} %copy-done, f32[24,128]{1,0:T(8,128)S(1)} %get-tuple-element.8.rest_0_, ...), custom_call_target="tpu_custom_call" | custom-call | tf_op jit(solution)/shard_map/finish/pallas_call | solution.py:317
  (2 shorter events, 0.1 us)
Async XLA Ops:
  17.6 4.4 %collective-permute-start.1 = (f32[8,3,2,128]{3,2,1,0:T(2,128)S(1)}, f32[8,3,2,128]{3,2,1,0:T(2,128)S(1)}, u32[]{:S(2)}, u32[]{:S(2)}) collective-permute-start(f32[8,3,2,128]{3,2,1,0:T(2,128)S(1)} %get-tuple-element.10), channel_id=1, source_target_pairs={{1,0},{2,1},{3,2},{4,3},{5,4},{6,5},{7,6},{8,7},{9,8},{10,9},{11,1... | collective-permute-start | bytes 73736 | tf_op jit(solution)/shard_map/ppermute | solution.py:276
  18.9 3.9 %collective-permute-start = (f32[8,3,2,128]{3,2,1,0:T(2,128)S(1)}, f32[8,3,2,128]{3,2,1,0:T(2,128)S(1)}, u32[]{:S(2)}, u32[]{:S(2)}) collective-permute-start(f32[8,3,2,128]{3,2,1,0:T(2,128)S(1)} %get-tuple-element.11), channel_id=1, source_target_pairs={{0,1},{1,2},{2,3},{3,4},{4,5},{5,6},{6,7},{7,8},{8,9},{9,10},{10,1... | collective-permute-start | bytes 73736 | tf_op jit(solution)/shard_map/ppermute | solution.py:275
  22.0 37.9 %copy-start = (f32[3,2,192,128]{3,2,1,0:T(8,128)S(1)}, f32[3,2,192,128]{3,2,1,0:T(8,128)}, u32[]{:S(2)}) copy-start(f32[3,2,192,128]{3,2,1,0:T(8,128)} %velocity.3) | copy-start | bytes 1769476
  22.0 37.9 %copy-start.1 = (f32[3,2,192,128]{3,2,1,0:T(8,128)S(1)}, f32[3,2,192,128]{3,2,1,0:T(8,128)}, u32[]{:S(2)}) copy-start(f32[3,2,192,128]{3,2,1,0:T(8,128)} %tendency.1) | copy-start | bytes 1769476
  60.6 5.7 %collective-permute-start.4 = (f32[24,128]{1,0:T(8,128)S(1)}, f32[24,128]{1,0:T(8,128)S(1)}, u32[]{:S(2)}, u32[]{:S(2)}) collective-permute-start(f32[24,128]{1,0:T(8,128)S(1)} %get-tuple-element.8.rest_0_), channel_id=1, source_target_pairs={{0,24},{8,0},{16,8},{24,16},{1,25},{9,1},{17,9},{25,17},{2,26},{10... | collective-permute-start | bytes 36872 | tf_op jit(solution)/shard_map/ppermute | solution.py:313
  64.9 4.6 %collective-permute-start.3 = (f32[24,128]{1,0:T(8,128)S(1)}, f32[24,128]{1,0:T(8,128)S(1)}, u32[]{:S(2)}, u32[]{:S(2)}) collective-permute-start(f32[24,128]{1,0:T(8,128)S(1)} %get-tuple-element.8.rest_0_), channel_id=1, source_target_pairs={{0,16},{8,24},{16,0},{24,8},{1,17},{9,25},{17,1},{25,9},{2,18},{10... | collective-permute-start | bytes 36872 | tf_op jit(solution)/shard_map/ppermute | solution.py:313
  64.9 5.5 %collective-permute-start.2 = (f32[24,128]{1,0:T(8,128)S(1)}, f32[24,128]{1,0:T(8,128)S(1)}, u32[]{:S(2)}, u32[]{:S(2)}) collective-permute-start(f32[24,128]{1,0:T(8,128)S(1)} %get-tuple-element.8.rest_0_), channel_id=1, source_target_pairs={{0,8},{8,16},{16,24},{24,0},{1,9},{9,17},{17,25},{25,1},{2,10},{10... | collective-permute-start | bytes 36872 | tf_op jit(solution)/shard_map/ppermute | solution.py:313

commit v2 on v1

--- a/solution.py
+++ b/solution.py
@@ -12,11 +12,7 @@
 VMEM_BYTES = 24 * 2**20
 
 
-def strain_parts(centre, below, above):
-    nx, nz = centre[0].shape
-    grad_x = [pltpu.roll(f, nx - 1, 0) - pltpu.roll(f, 1, 0) for f in centre]
-    grad_z = [pltpu.roll(f, nz - 1, 1) - pltpu.roll(f, 1, 1) for f in centre]
-    grad_y = [up - down for up, down in zip(above, below)]
+def strain_parts(grad_x, grad_y, grad_z):
     return (
         grad_x[0],
         grad_y[1],
@@ -33,81 +29,133 @@
     return jnp.sqrt(0.5 * diagonal + 0.25 * mixed)
 
 
-def smooth(field):
-    field = field + pltpu.roll(field, 1, 0)
-    field = field + pltpu.roll(field, 1, 0)
-    field = field + pltpu.roll(field, 1, 1)
-    return field + pltpu.roll(field, 1, 1)
+def beside(blocks):
+    count = len(blocks)
+    lanes = blocks[0].shape[1]
+    down = [pltpu.roll(f, 1, 1) for f in blocks]
+    up = [pltpu.roll(f, lanes - 1, 1) for f in blocks]
+    if count > 1:
+        lane = lax.broadcasted_iota(jnp.int32, blocks[0].shape, 1)
+        first, last = lane == 0, lane == lanes - 1
+        down, up = (
+            [jnp.where(first, down[i - 1], down[i]) for i in range(count)],
+            [jnp.where(last, up[(i + 1) % count], up[i]) for i in range(count)],
+        )
+    return down, up
+
+
+def slope_z(blocks):
+    down, up = beside(blocks)
+    return [u - d for u, d in zip(up, down)]
+
+
+def smooth_z(blocks):
+    down, up = beside(blocks)
+    return [(u + d) + 2.0 * f for f, u, d in zip(blocks, up, down)]
 
 
 def products(v):
     return (v[0] * v[0], v[1] * v[1], v[2] * v[2], v[0] * v[1], v[0] * v[2], v[1] * v[2])
 
 
-def germano_kernel(nz_parts, recv, below, above, out, planes, vel, filt, mag, lm, mm):
-    count, _, width, rows, _ = recv.shape
+def germano_kernel(nz_parts, recv, below, above, out, vel, filt, ends, mag, part):
+    count, _, width, rows, lanes = recv.shape
     nx = (count // nz_parts) * width
-    nz = nz_parts * LANES
+    nz = nz_parts * lanes
+    blocks = range(nz_parts)
+    lead = 8
+    inner = slice(lead, lead + rows)
+    lower = slice(lead - 1, lead - 1 + rows)
+    upper = slice(lead + 1, lead + 1 + rows)
     for k in range(count):
         x0, zb = (k // nz_parts) * width, k % nz_parts
-        lanes = slice(zb * LANES, (zb + 1) * LANES)
         for c in range(3):
             for x in range(width):
-                planes[c, zb, (x0 + x) * rows : (x0 + x + 1) * rows, :] = recv[k, c, x]
-            vel[c, 0, x0 : x0 + width, lanes] = below[k, c]
-            vel[c, rows + 1, x0 : x0 + width, lanes] = above[k, c]
+                vel[c, x0 + x, zb, inner, :] = recv[k, c, x]
+                for i, (ref, at) in enumerate(((below, lead - 1), (above, lead + rows))):
+                    edge = ref[k, c, x : x + 1, :]
+                    vel[c, x0 + x, zb, at : at + 1, :] = edge
+                    ends[c, x0 + x, zb, i : i + 1, :] = edge
+
+    for x in range(nx):
+        left, right = (x - 1) % nx, (x + 1) % nx
+        centre = [[vel[c, x, zb, inner, :] for zb in blocks] for c in range(3)]
+        grad_x = [[vel[c, right, zb, inner, :] - vel[c, left, zb, inner, :] for zb in blocks] for c in range(3)]
+        grad_y = [[vel[c, x, zb, upper, :] - vel[c, x, zb, lower, :] for zb in blocks] for c in range(3)]
+        grad_z = []
+        for c in range(3):
+            down, up = beside(centre[c])
+            grad_z.append([u - d for u, d in zip(up, down)])
+            for zb in blocks:
+                part[c, x, zb] = (up[zb] + down[zb]) + 2.0 * centre[c][zb]
+        strain = [
+            strain_parts(*([g[c][zb] for c in range(3)] for g in (grad_x, grad_y, grad_z)))
+            for zb in blocks
+        ]
+        size = [strain_size(s) for s in strain]
+        for zb in blocks:
+            mag[x, zb] = size[zb]
+        pairs = [products([centre[c][zb] for c in range(3)]) for zb in blocks]
+        for i in range(6):
+            for base, fields in (
+                (3, [pairs[zb][i] for zb in blocks]),
+                (9, [size[zb] * strain[zb][i] for zb in blocks]),
+            ):
+                for zb, f in enumerate(smooth_z(fields)):
+                    part[base + i, x, zb] = f
+
+    def smooth_x(read, x):
+        return (read((x - 1) % nx) + read((x + 1) % nx)) + 2.0 * read(x)
+
     for c in range(3):
-        for y in range(rows):
-            for zb in range(nz_parts):
-                lanes = slice(zb * LANES, (zb + 1) * LANES)
-                vel[c, y + 1, :, lanes] = planes[c, zb, pl.ds(y, nx, stride=rows), :]
-    for c in range(3):
-        for y in range(rows + 2):
-            filt[c, y] = smooth(vel[c, y])
-
-    for y in range(rows):
-        centre = [vel[c, y + 1] for c in range(3)]
-        strain = strain_parts(centre, [vel[c, y] for c in range(3)], [vel[c, y + 2] for c in range(3)])
-        size = strain_size(strain)
-        for zb in range(nz_parts):
-            mag[zb, y * nx : (y + 1) * nx, :] = size[:, zb * LANES : (zb + 1) * LANES]
-        mean = [filt[c, y + 1] for c in range(3)]
-        mean_strain = strain_parts(mean, [filt[c, y] for c in range(3)], [filt[c, y + 2] for c in range(3)])
-        mean_size = 0.25 * strain_size(mean_strain)
-        model = [smooth(size * s) - mean_size * f for s, f in zip(strain, mean_strain)]
-        scaled = [0.0625 * f for f in mean]
-        pairs = (
-            (mean[0], scaled[0]),
-            (mean[1], scaled[1]),
-            (mean[2], scaled[2]),
-            (mean[0], scaled[1]),
-            (mean[0], scaled[2]),
-            (mean[1], scaled[2]),
-        )
-        leonard = [smooth(p) - f * g for p, (f, g) in zip(products(centre), pairs)]
-        left = leonard[0] * model[0]
-        for i in range(1, 6):
-            left = left + leonard[i] * model[i]
-        right = (model[0] * model[0] + model[1] * model[1] + model[2] * model[2]) + 0.5 * (
-            model[3] * model[3] + model[4] * model[4] + model[5] * model[5]
-        )
-        for total, ref in ((left, lm), (right, mm)):
-            part = total[:, :LANES]
-            for zb in range(1, nz_parts):
-                part = part + total[:, zb * LANES : (zb + 1) * LANES]
-            ref[y * nx : (y + 1) * nx, :] = part
-
-    def plane_sum(ref):
-        part = ref[pl.ds(0, rows, stride=nx), :]
-        for x in range(1, nx):
-            part = part + ref[pl.ds(x, rows, stride=nx), :]
-        return jnp.sum(part, axis=1, keepdims=True) * (1.0 / (256.0 * nx * nz))
-
-    coefficient = jnp.maximum(plane_sum(lm) / (plane_sum(mm) + 1e-06), 0.0)
+        rims = []
+        for x in range(nx):
+            rims.append(smooth_z([ends[c, x, zb] for zb in blocks]))
+        for x in range(nx):
+            for zb in blocks:
+                rim = smooth_x(lambda at: rims[at][zb], x)
+                filt[c, x, zb, lead - 1 : lead, :] = rim[0:1, :]
+                filt[c, x, zb, lead + rows : lead + rows + 1, :] = rim[1:2, :]
+                filt[c, x, zb, inner, :] = smooth_x(lambda at: part[c, at, zb], x)
+
+    sum_lm = sum_mm = None
+    for x in range(nx):
+        left, right = (x - 1) % nx, (x + 1) % nx
+        mean = [[filt[c, x, zb, inner, :] for zb in blocks] for c in range(3)]
+        grad_x = [[filt[c, right, zb, inner, :] - filt[c, left, zb, inner, :] for zb in blocks] for c in range(3)]
+        grad_y = [[filt[c, x, zb, upper, :] - filt[c, x, zb, lower, :] for zb in blocks] for c in range(3)]
+        grad_z = [slope_z(mean[c]) for c in range(3)]
+        for zb in blocks:
+            strain = strain_parts(*([g[c][zb] for c in range(3)] for g in (grad_x, grad_y, grad_z)))
+            size = 0.25 * strain_size(strain)
+            v = [mean[c][zb] for c in range(3)]
+            scaled = [0.0625 * f for f in v]
+            pairs = (
+                v[0] * scaled[0],
+                v[1] * scaled[1],
+                v[2] * scaled[2],
+                v[0] * scaled[1],
+                v[0] * scaled[2],
+                v[1] * scaled[2],
+            )
+            lm = mm = None
+            for i in range(6):
+                leonard = smooth_x(lambda at: part[3 + i, at, zb], x) - pairs[i]
+                model = smooth_x(lambda at: part[9 + i, at, zb], x) - size * strain[i]
+                square = model * model if i < 3 else (0.5 * model) * model
+                lm = leonard * model if lm is None else lm + leonard * model
+                mm = square if mm is None else mm + square
+            sum_lm = lm if sum_lm is None else sum_lm + lm
+            sum_mm = mm if sum_mm is None else sum_mm + mm
+
+    def plane_mean(total):
+        return jnp.sum(total, axis=1, keepdims=True) * (1.0 / (256.0 * nx * nz))
+
+    coefficient = jnp.maximum(plane_mean(sum_lm) / (plane_mean(sum_mm) + 1e-06), 0.0)
     for k in range(count):
         x0, zb = (k // nz_parts) * width, k % nz_parts
         for x in range(width):
-            out[k, x] = coefficient * mag[zb, pl.ds(x0 + x, rows, stride=nx), :]
+            out[k, x] = coefficient * mag[x0 + x, zb]
 
 
 def sweep_kernel(back, velocity, tendency, eddy, reduced, factors, tree):
@@ -265,7 +313,7 @@
     walls = lax.axis_size("gy")
     rows = cells // count
     nx = lax.axis_size("gx") * width
-    nz = nz_parts * lanes
+    padded = 16 + -(-rows // 8) * 8
     f32 = jnp.float32
 
     chunks = velocity.reshape(3, width, count, rows, lanes).transpose(2, 0, 1, 3, 4)
@@ -280,12 +328,11 @@
         in_specs=in_vmem(3),
         out_specs=pl.BlockSpec(memory_space=pltpu.VMEM),
         scratch_shapes=[
-            pltpu.VMEM((3, nz_parts, nx * rows, lanes), f32),
-            pltpu.VMEM((3, rows + 2, nx, nz), f32),
-            pltpu.VMEM((3, rows + 2, nx, nz), f32),
-            pltpu.VMEM((nz_parts, rows * nx, lanes), f32),
-            pltpu.VMEM((rows * nx, lanes), f32),
-            pltpu.VMEM((rows * nx, lanes), f32),
+            pltpu.VMEM((3, nx, nz_parts, padded, lanes), f32),
+            pltpu.VMEM((3, nx, nz_parts, padded, lanes), f32),
+            pltpu.VMEM((3, nx, nz_parts, 8, lanes), f32),
+            pltpu.VMEM((nx, nz_parts, rows, lanes), f32),
+            pltpu.VMEM((15, nx, nz_parts, rows, lanes), f32),
         ],
         compiler_params=params(),
         name="germano",

time: 71.8 us -> 49.3 us (0.69)
  Pallas kernels: 27.3 us -> 4.86 us
    pallas_call x1, Pallas kernels: 25.5 us -> 3.04 us  [body(): pl.pallas_call(functools.partial(germano_kernel, nz_parts), out_shape=jax...]
where the time goes in v2:
time: 49.3 us; the launch traced here: 49.1 us
  blocking collectives  27.1 us (55%)
  starting transfers between devices  9.61 us (19%)
  waiting for transfers between devices  5.23 us (11%)
  Pallas kernels  4.86 us (10%)
  local copies, waits for them, and re-layouts  1.59 us (3%)
  between operations  0.7 us (1%)
    all_to_all x1, blocking collectives, body(): lax.all_to_all(chunks, ('gx', 'gz'), split_axis=0, concat_axis=0, tiled=T...  15.4 us
    all_to_all x1, blocking collectives, body(): lax.all_to_all(eddy_chunks, ('gx', 'gz'), split_axis=0, concat_axis=0, ti...  11.7 us
    ppermute x3, starting transfers between devices, body(): lax.ppermute(reduced, 'gy', [(i, (i + shift) % walls) for i in range(wall...  5.28 us
    ppermute x3, waiting for transfers between devices, body(): lax.ppermute(reduced, 'gy', [(i, (i + shift) % walls) for i in range(wall...  4.48 us
    pallas_call x1, Pallas kernels, body(): pl.pallas_call(functools.partial(germano_kernel, nz_parts), out_shape=jax...  3.04 us
    ppermute x1, starting transfers between devices, body(): lax.ppermute(recv[:, :, :, rows - 1], everyone, [(i, i + 1) for i in rang...  3.03 us
    transpose x1, local copies, waits for them, and re-layouts, body(): velocity.reshape(3, width, count, rows, lanes).transpose(2, 0, 1, 3, 4)  1.52 us
    ppermute x1, starting transfers between devices, body(): lax.ppermute(recv[:, :, :, 0], everyone, [(i + 1, i) for i in range(total...  1.29 us
  transfers between devices with their start and end apart: 5, of which 4 were waited for; matrix products, arithmetic and copies ran while one was open for 0% of the time, Pallas kernels for 0%

profile of v2, /device:TPU:0, one launch (start us, length us, event | category | flops | bytes accessed | tf_op | source)
XLA Modules:
  0.0 49.1 jit_solution(3330360009366555000)
XLA Ops:
  0.6 1.5 %copy.7 = f32[8,3,2,24,128]{4,2,1,3,0:T(2,128)S(1)} copy(f32[8,3,2,24,128]{4,3,0,2,1:T(8,128)} %bitcast.12) | data formatting | bytes 1179648 | tf_op jit(solution)/shard_map/transpose | solution.py:319
  2.2 15.4 %all_to_all.10 = f32[8,3,2,24,128]{4,2,1,3,0:T(2,128)S(1)} all-to-all(f32[8,3,2,24,128]{4,2,1,3,0:T(2,128)S(1)} %copy.7), channel_id=1, replica_groups=mesh['gy'=4,'gx'=4,'gz'=2] {'gx','gz'}, dimensions={0} | all-to-all | bytes 1179648 | tf_op jit(solution)/shard_map/all_to_all | solution.py:320
  17.6 1.3 %collective-permute-start.1 = (f32[8,3,2,128]{3,2,1,0:T(2,128)S(1)}, f32[8,3,2,128]{3,2,1,0:T(2,128)S(1)}, u32[]{:S(2)}, u32[]{:S(2)}) collective-permute-start(f32[8,3,2,128]{3,2,1,0:T(2,128)S(1)} %get-tuple-element.10), channel_id=1, source_target_pairs={{1,0},{2,1},{3,2},{4,3},{5,4},{6,5},{7,6},{8,7},{9,8},{10,9},{11,1... | collective-permute-start | bytes 73736 | tf_op jit(solution)/shard_map/ppermute | solution.py:324
  18.9 3.0 %collective-permute-start = (f32[8,3,2,128]{3,2,1,0:T(2,128)S(1)}, f32[8,3,2,128]{3,2,1,0:T(2,128)S(1)}, u32[]{:S(2)}, u32[]{:S(2)}) collective-permute-start(f32[8,3,2,128]{3,2,1,0:T(2,128)S(1)} %get-tuple-element.11), channel_id=1, source_target_pairs={{0,1},{1,2},{2,3},{3,4},{4,5},{5,6},{6,7},{7,8},{8,9},{9,10},{10,1... | collective-permute-start | bytes 73736 | tf_op jit(solution)/shard_map/ppermute | solution.py:323
  22.0 0.0 copy-start
  22.0 0.0 copy-start.1
  22.0 0.0 collective-permute-done.1.above
  22.0 0.7 %collective-permute-done.below = f32[8,3,2,128]{3,2,1,0:T(2,128)S(1)} collective-permute-done((f32[8,3,2,128]{3,2,1,0:T(2,128)S(1)}, f32[8,3,2,128]{3,2,1,0:T(2,128)S(1)}, u32[]{:S(2)}, u32[]{:S(2)}) %collective-permute-start) | collective-permute-done | bytes 24608 | tf_op jit(solution)/shard_map/ppermute | solution.py:323
  22.8 3.0 %germano.1 = f32[8,2,24,128]{3,2,1,0:T(8,128)S(1)} custom-call(f32[8,3,2,24,128]{4,3,2,1,0:T(8,128)S(1)} %copy.10.recv, f32[8,3,2,128]{3,2,1,0:T(2,128)S(1)} %collective-permute-done.below, f32[8,3,2,128]{3,2,1,0:T(2,128)S(1)} %collective-permute-done.1.above), custom_call_target="tpu_custom_call" | custom-call | tf_op jit(solution)/shard_map/germano/pallas_call | solution.py:325
  25.8 11.7 %all_to_all.11.back = f32[8,2,24,128]{3,2,1,0:T(8,128)S(1)} all-to-all(f32[8,2,24,128]{3,2,1,0:T(8,128)S(1)} %germano.1), channel_id=1, replica_groups=mesh['gy'=4,'gx'=4,'gz'=2] {'gx','gz'}, dimensions={0} | all-to-all | bytes 393216 | tf_op jit(solution)/shard_map/all_to_all | solution.py:340
  37.5 0.0 copy-done
  37.5 0.0 copy-done.1
  37.5 0.7 %sweep.1 = (f32[2,192,128]{2,1,0:T(8,128)}, f32[24,128]{1,0:T(8,128)S(1)}, f32[2,24,5,8,128]{4,3,2,1,0:T(8,128)S(1)}, f32[2,3,5,8,128]{4,3,2,1,0:T(8,128)S(1)}) custom-call(f32[8,2,24,128]{3,2,1,0:T(8,128)S(1)} %all_to_all.11.back, f32[3,2,192,128]{3,2,1,0:T(8,128)S(1)} %copy-done, f32[3,2,192,128]{3,2,1,0:T(8,128)S(1)} %copy-done.1), custom_call_target="tpu_custom_call" | custom-call | tf_op jit(solution)/shard_map/sweep/pallas_call | solution.py:345
  38.2 4.3 %collective-permute-start.4 = (f32[24,128]{1,0:T(8,128)S(1)}, f32[24,128]{1,0:T(8,128)S(1)}, u32[]{:S(2)}, u32[]{:S(2)}) collective-permute-start(f32[24,128]{1,0:T(8,128)S(1)} %get-tuple-element.8.rest_0_), channel_id=1, source_target_pairs={{0,24},{8,0},{16,8},{24,16},{1,25},{9,1},{17,9},{25,17},{2,26},{10... | collective-permute-start | bytes 36872 | tf_op jit(solution)/shard_map/ppermute | solution.py:360
  42.5 0.0 collective-permute-start.3
  42.5 1.0 %collective-permute-start.2 = (f32[24,128]{1,0:T(8,128)S(1)}, f32[24,128]{1,0:T(8,128)S(1)}, u32[]{:S(2)}, u32[]{:S(2)}) collective-permute-start(f32[24,128]{1,0:T(8,128)S(1)} %get-tuple-element.8.rest_0_), channel_id=1, source_target_pairs={{0,8},{8,16},{16,24},{24,0},{1,9},{9,17},{17,25},{25,1},{2,10},{10... | collective-permute-start | bytes 36872 | tf_op jit(solution)/shard_map/ppermute | solution.py:360
  43.5 0.4 collective-permute-done.4.rest_3_
  43.9 3.2 %collective-permute-done.3.rest_2_ = f32[24,128]{1,0:T(8,128)S(1)} collective-permute-done((f32[24,128]{1,0:T(8,128)S(1)}, f32[24,128]{1,0:T(8,128)S(1)}, u32[]{:S(2)}, u32[]{:S(2)}) %collective-permute-start.3) | collective-permute-done | bytes 12320 | tf_op jit(solution)/shard_map/ppermute | solution.py:360
  47.1 0.9 %collective-permute-done.2.rest_1_ = f32[24,128]{1,0:T(8,128)S(1)} collective-permute-done((f32[24,128]{1,0:T(8,128)S(1)}, f32[24,128]{1,0:T(8,128)S(1)}, u32[]{:S(2)}, u32[]{:S(2)}) %collective-permute-start.2) | collective-permute-done | bytes 12320 | tf_op jit(solution)/shard_map/ppermute | solution.py:360
  48.0 1.1 %finish.1 = f32[3,2,192,128]{3,2,1,0:T(8,128)} custom-call(s32[1]{0:T(128)} %bitcast.position, f32[2,24,5,8,128]{4,3,2,1,0:T(8,128)S(1)} %get-tuple-element.6.factors, f32[2,3,5,8,128]{4,3,2,1,0:T(8,128)S(1)} %get-tuple-element.7.tree, f32[3,2,192,128]{3,2,1,0:T(8,128)S(1)} %copy-done, f32[24,128]{1,0:T(8,128)S(1)} %get-tuple-element.8.rest_0_, ...), custom_call_target="tpu_custom_call" | custom-call | tf_op jit(solution)/shard_map/finish/pallas_call | solution.py:364
  (2 shorter events, 0.1 us)
Async XLA Ops:
  17.6 4.4 %collective-permute-start.1 = (f32[8,3,2,128]{3,2,1,0:T(2,128)S(1)}, f32[8,3,2,128]{3,2,1,0:T(2,128)S(1)}, u32[]{:S(2)}, u32[]{:S(2)}) collective-permute-start(f32[8,3,2,128]{3,2,1,0:T(2,128)S(1)} %get-tuple-element.10), channel_id=1, source_target_pairs={{1,0},{2,1},{3,2},{4,3},{5,4},{6,5},{7,6},{8,7},{9,8},{10,9},{11,1... | collective-permute-start | bytes 73736 | tf_op jit(solution)/shard_map/ppermute | solution.py:324
  18.9 3.9 %collective-permute-start = (f32[8,3,2,128]{3,2,1,0:T(2,128)S(1)}, f32[8,3,2,128]{3,2,1,0:T(2,128)S(1)}, u32[]{:S(2)}, u32[]{:S(2)}) collective-permute-start(f32[8,3,2,128]{3,2,1,0:T(2,128)S(1)} %get-tuple-element.11), channel_id=1, source_target_pairs={{0,1},{1,2},{2,3},{3,4},{4,5},{5,6},{6,7},{7,8},{8,9},{9,10},{10,1... | collective-permute-start | bytes 73736 | tf_op jit(solution)/shard_map/ppermute | solution.py:323
  22.0 15.5 %copy-start = (f32[3,2,192,128]{3,2,1,0:T(8,128)S(1)}, f32[3,2,192,128]{3,2,1,0:T(8,128)}, u32[]{:S(2)}) copy-start(f32[3,2,192,128]{3,2,1,0:T(8,128)} %velocity.3) | copy-start | bytes 1769476
  22.0 15.5 %copy-start.1 = (f32[3,2,192,128]{3,2,1,0:T(8,128)S(1)}, f32[3,2,192,128]{3,2,1,0:T(8,128)}, u32[]{:S(2)}) copy-start(f32[3,2,192,128]{3,2,1,0:T(8,128)} %tendency.1) | copy-start | bytes 1769476
  38.2 5.7 %collective-permute-start.4 = (f32[24,128]{1,0:T(8,128)S(1)}, f32[24,128]{1,0:T(8,128)S(1)}, u32[]{:S(2)}, u32[]{:S(2)}) collective-permute-start(f32[24,128]{1,0:T(8,128)S(1)} %get-tuple-element.8.rest_0_), channel_id=1, source_target_pairs={{0,24},{8,0},{16,8},{24,16},{1,25},{9,1},{17,9},{25,17},{2,26},{10... | collective-permute-start | bytes 36872 | tf_op jit(solution)/shard_map/ppermute | solution.py:360
  42.5 4.6 %collective-permute-start.3 = (f32[24,128]{1,0:T(8,128)S(1)}, f32[24,128]{1,0:T(8,128)S(1)}, u32[]{:S(2)}, u32[]{:S(2)}) collective-permute-start(f32[24,128]{1,0:T(8,128)S(1)} %get-tuple-element.8.rest_0_), channel_id=1, source_target_pairs={{0,16},{8,24},{16,0},{24,8},{1,17},{9,25},{17,1},{25,9},{2,18},{10... | collective-permute-start | bytes 36872 | tf_op jit(solution)/shard_map/ppermute | solution.py:360
  42.5 5.5 %collective-permute-start.2 = (f32[24,128]{1,0:T(8,128)S(1)}, f32[24,128]{1,0:T(8,128)S(1)}, u32[]{:S(2)}, u32[]{:S(2)}) collective-permute-start(f32[24,128]{1,0:T(8,128)S(1)} %get-tuple-element.8.rest_0_), channel_id=1, source_target_pairs={{0,8},{8,16},{16,24},{24,0},{1,9},{9,17},{17,25},{25,1},{2,10},{10... | collective-permute-start | bytes 36872 | tf_op jit(solution)/shard_map/ppermute | solution.py:360

commit v3 on v2

--- a/solution.py
+++ b/solution.py
@@ -58,8 +58,34 @@
     return (v[0] * v[0], v[1] * v[1], v[2] * v[2], v[0] * v[1], v[0] * v[2], v[1] * v[2])
 
 
-def germano_kernel(nz_parts, recv, below, above, out, vel, filt, ends, mag, part):
-    count, _, width, rows, lanes = recv.shape
+def row_order(count):
+    return [0, count - 1, *range(1, count - 1)]
+
+
+def pack_kernel(rows, velocity, out):
+    _, width, cells, _ = velocity.shape
+    count, depth, lanes = out.shape
+    planes = 3 * width
+    for rank, place in enumerate(row_order(count)):
+        first = place * rows
+        before = max(first - 1, 0)
+        after = min(first + rows, cells - 1)
+        for i in range(planes):
+            c, x = divmod(i, width)
+            out[rank, i * rows : (i + 1) * rows, :] = velocity[c, x, first : first + rows, :]
+            at = planes * rows + i
+            out[rank, at : at + 1, :] = velocity[c, x, before : before + 1, :]
+            at += planes
+            out[rank, at : at + 1, :] = velocity[c, x, after : after + 1, :]
+        filled = planes * (rows + 2)
+        if filled < depth:
+            out[rank, filled:, :] = jnp.zeros((depth - filled, lanes), jnp.float32)
+
+
+def germano_kernel(nz_parts, width, rows, rank, recv, swapped, out, vel, filt, ends, mag, part):
+    count, _, lanes = recv.shape
+    planes = 3 * width
+    outer = (rank[0] == 0, rank[0] == 1)
     nx = (count // nz_parts) * width
     nz = nz_parts * lanes
     blocks = range(nz_parts)
@@ -71,11 +97,14 @@
         x0, zb = (k // nz_parts) * width, k % nz_parts
         for c in range(3):
             for x in range(width):
-                vel[c, x0 + x, zb, inner, :] = recv[k, c, x]
-                for i, (ref, at) in enumerate(((below, lead - 1), (above, lead + rows))):
-                    edge = ref[k, c, x : x + 1, :]
+                i = c * width + x
+                vel[c, x0 + x, zb, inner, :] = recv[k, i * rows : (i + 1) * rows, :]
+                for side, at in ((0, lead - 1), (1, lead + rows)):
+                    own = planes * rows + side * planes + i
+                    far = (1 - side) * planes + i
+                    edge = jnp.where(outer[side], swapped[k, far : far + 1, :], recv[k, own : own + 1, :])
                     vel[c, x0 + x, zb, at : at + 1, :] = edge
-                    ends[c, x0 + x, zb, i : i + 1, :] = edge
+                    ends[c, x0 + x, zb, side : side + 1, :] = edge
 
     for x in range(nx):
         left, right = (x - 1) % nx, (x + 1) % nx
@@ -161,9 +190,9 @@
 def sweep_kernel(back, velocity, tendency, eddy, reduced, factors, tree):
     count, width, rows, _ = back.shape
     length = count * rows // SEGMENTS
-    for k in range(count):
+    for k, place in enumerate(row_order(count)):
         for x in range(width):
-            eddy[x, k * rows : (k + 1) * rows, :] = back[k, x]
+            eddy[x, place * rows : (place + 1) * rows, :] = back[k, x]
 
     def row(ref, index, j):
         return ref[(*index, pl.ds(j, SEGMENTS, stride=length), slice(None))]
@@ -316,16 +345,27 @@
     padded = 16 + -(-rows // 8) * 8
     f32 = jnp.float32
 
-    chunks = velocity.reshape(3, width, count, rows, lanes).transpose(2, 0, 1, 3, 4)
+    filled = 3 * width * (rows + 2)
+    depth = -(-filled // 8) * 8
+    chunks = pl.pallas_call(
+        functools.partial(pack_kernel, rows),
+        out_shape=jax.ShapeDtypeStruct((count, depth, lanes), f32),
+        in_specs=in_vmem(1),
+        out_specs=pl.BlockSpec(memory_space=pltpu.VMEM),
+        compiler_params=params(),
+        name="pack",
+    )(velocity)
     recv = lax.all_to_all(chunks, ("gx", "gz"), split_axis=0, concat_axis=0, tiled=True)
-    total = walls * count
-    everyone = ("gy", "gx", "gz")
-    below = lax.ppermute(recv[:, :, :, rows - 1], everyone, [(i, i + 1) for i in range(total - 1)])
-    above = lax.ppermute(recv[:, :, :, 0], everyone, [(i + 1, i) for i in range(total - 1)])
+    pairs = []
+    for wall in range(walls - 1):
+        upper, lower = wall * count + 1, (wall + 1) * count
+        pairs += [(upper, lower), (lower, upper)]
+    swapped = lax.ppermute(recv[:, 3 * width * rows :], ("gy", "gx", "gz"), pairs)
+    rank = lax.axis_index(("gx", "gz")).astype(jnp.int32).reshape(1)
     eddy_chunks = pl.pallas_call(
-        functools.partial(germano_kernel, nz_parts),
+        functools.partial(germano_kernel, nz_parts, width, rows),
         out_shape=jax.ShapeDtypeStruct((count, width, rows, lanes), f32),
-        in_specs=in_vmem(3),
+        in_specs=[pl.BlockSpec(memory_space=pltpu.SMEM)] + in_vmem(2),
         out_specs=pl.BlockSpec(memory_space=pltpu.VMEM),
         scratch_shapes=[
             pltpu.VMEM((3, nx, nz_parts, padded, lanes), f32),
@@ -336,7 +376,7 @@
         ],
         compiler_params=params(),
         name="germano",
-    )(recv, below, above)
+    )(rank, recv, swapped)
     back = lax.all_to_all(eddy_chunks, ("gx", "gz"), split_axis=0, concat_axis=0, tiled=True)
 
     length = cells // SEGMENTS

time: 49.3 us -> 46.3 us (0.939)
  starting transfers between devices: 9.61 us -> 6.64 us
  blocking collectives: 27.1 us -> 28.3 us
  waiting for transfers between devices: 5.23 us -> 4.48 us
  local copies, waits for them, and re-layouts: 1.59 us -> 1.08 us
    ppermute x2 -> x1, starting transfers between devices: 4.32 us -> 0.65 us  [body(): lax.ppermute(recv[:, 3 * width * rows:], ('gy', 'gx', 'gz'), pairs)]
    transpose x1 -> x0, local copies, waits for them, and re-layouts: 1.52 us -> none  [body(): velocity.reshape(3, width, count, rows, lanes).transpose(2, 0, 1, 3, 4)]
    unnamed x4 -> x6, local copies, waits for them, and re-layouts: 0.01 us -> 1.07 us
    ppermute x2 -> x1, waiting for transfers between devices: 0.75 us -> 0.01 us  [body(): lax.ppermute(recv[:, 3 * width * rows:], ('gy', 'gx', 'gz'), pairs)]
    all_to_all x1, blocking collectives: 15.4 us -> 16.1 us  [body(): lax.all_to_all(chunks, ('gx', 'gz'), split_axis=0, concat_axis=0, tiled=T...]
    ppermute x3, starting transfers between devices: 5.28 us -> 5.98 us  [body(): lax.ppermute(reduced, 'gy', [(i, (i + shift) % walls) for i in range(wall...]
    pallas_call x1 -> x2, Pallas kernels: 3.04 us -> 3.11 us  [the longest x1 3.04 us: body(): pl.pallas_call(functools.partial(germano_kernel, nz_parts, width, rows),...]
  transfers between devices with their start and end apart: 5 -> 4, of which waited for: 4 -> 3; matrix products, arithmetic and copies ran while one was open for 0% -> 0% of each run, Pallas kernels for 0% -> 0%
where the time goes in v3:
time: 46.3 us; the launch traced here: 46.1 us
  blocking collectives  28.3 us (61%)
  starting transfers between devices  6.64 us (14%)
  Pallas kernels  4.93 us (11%)
  waiting for transfers between devices  4.48 us (10%)
  local copies, waits for them, and re-layouts  1.08 us (2%)
  between operations  0.69 us (1%)
    all_to_all x1, blocking collectives, body(): lax.all_to_all(chunks, ('gx', 'gz'), split_axis=0, concat_axis=0, tiled=T...  16.1 us
    all_to_all x1, blocking collectives, body(): lax.all_to_all(eddy_chunks, ('gx', 'gz'), split_axis=0, concat_axis=0, ti...  12.1 us
    ppermute x3, starting transfers between devices, body(): lax.ppermute(reduced, 'gy', [(i, (i + shift) % walls) for i in range(wall...  5.98 us
    ppermute x3, waiting for transfers between devices, body(): lax.ppermute(reduced, 'gy', [(i, (i + shift) % walls) for i in range(wall...  4.48 us
    pallas_call x1, Pallas kernels, body(): pl.pallas_call(functools.partial(germano_kernel, nz_parts, width, rows),...  3.04 us
    pallas_call x1, Pallas kernels, body(): pl.pallas_call(functools.partial(finish_kernel, walls), out_shape=jax.Sha...  1.11 us
    unnamed x6, local copies, waits for them, and re-layouts  1.07 us
  transfers between devices with their start and end apart: 4, of which 3 were waited for; matrix products, arithmetic and copies ran while one was open for 0% of the time, Pallas kernels for 0%

profile of v3, /device:TPU:0, one launch (start us, length us, event | category | flops | bytes accessed | tf_op | source)
XLA Modules:
  0.0 46.1 jit_solution(14422222280504851396)
XLA Ops:
  0.6 0.0 copy-start
  0.6 1.1 %copy-done = f32[3,2,192,128]{3,2,1,0:T(8,128)S(1)} copy-done((f32[3,2,192,128]{3,2,1,0:T(8,128)S(1)}, f32[3,2,192,128]{3,2,1,0:T(8,128)}, u32[]{:S(2)}) %copy-start) | copy-done | bytes 589848
  1.7 0.1 pack.1
  1.8 16.1 %all_to_all.10.recv = f32[8,160,128]{2,1,0:T(8,128)S(1)} all-to-all(f32[8,160,128]{2,1,0:T(8,128)S(1)} %pack.1), channel_id=1, replica_groups=mesh['gy'=4,'gx'=4,'gz'=2] {'gx','gz'}, dimensions={0} | all-to-all | bytes 1310720 | tf_op jit(solution)/shard_map/all_to_all | solution.py:358
  17.9 0.7 %collective-permute-start = (f32[8,16,128]{2,1,0:T(8,128)S(1)}, f32[8,16,128]{2,1,0:T(8,128)S(1)}, u32[]{:S(2)}, u32[]{:S(2)}) collective-permute-start(f32[8,16,128]{2,1,0:T(8,128)S(1)} %slice.4), channel_id=1, source_target_pairs={{1,8},{8,1},{9,16},{16,9},{17,24},{24,17}} | collective-permute-start | bytes 196616 | tf_op jit(solution)/shard_map/ppermute | solution.py:363
  18.6 0.0 collective-permute-done.swapped
  18.6 0.0 copy-start.1
  18.6 0.0 copy-start.2
  18.6 3.0 %germano.1 = f32[8,2,24,128]{3,2,1,0:T(8,128)S(1)} custom-call(s32[1]{0:T(128)} %bitcast.1.rank, f32[8,160,128]{2,1,0:T(8,128)S(1)} %all_to_all.10.recv, f32[8,16,128]{2,1,0:T(8,128)S(1)} %collective-permute-done.swapped), custom_call_target="tpu_custom_call" | custom-call | tf_op jit(solution)/shard_map/germano/pallas_call | solution.py:365
  21.6 12.1 %all_to_all.11.back = f32[8,2,24,128]{3,2,1,0:T(8,128)S(1)} all-to-all(f32[8,2,24,128]{3,2,1,0:T(8,128)S(1)} %germano.1), channel_id=1, replica_groups=mesh['gy'=4,'gx'=4,'gz'=2] {'gx','gz'}, dimensions={0} | all-to-all | bytes 393216 | tf_op jit(solution)/shard_map/all_to_all | solution.py:380
  33.8 0.0 copy-done.1
  33.8 0.0 copy-done.2
  33.8 0.7 %sweep.1 = (f32[2,192,128]{2,1,0:T(8,128)}, f32[24,128]{1,0:T(8,128)S(1)}, f32[2,24,5,8,128]{4,3,2,1,0:T(8,128)S(1)}, f32[2,3,5,8,128]{4,3,2,1,0:T(8,128)S(1)}) custom-call(f32[8,2,24,128]{3,2,1,0:T(8,128)S(1)} %all_to_all.11.back, f32[3,2,192,128]{3,2,1,0:T(8,128)S(1)} %copy-done.1, f32[3,2,192,128]{3,2,1,0:T(8,128)S(1)} %copy-done.2), custom_call_target="tpu_custom_call" | custom-call | tf_op jit(solution)/shard_map/sweep/pallas_call | solution.py:385
  34.5 5.0 %collective-permute-start.3 = (f32[24,128]{1,0:T(8,128)S(1)}, f32[24,128]{1,0:T(8,128)S(1)}, u32[]{:S(2)}, u32[]{:S(2)}) collective-permute-start(f32[24,128]{1,0:T(8,128)S(1)} %get-tuple-element.8.rest_0_), channel_id=1, source_target_pairs={{0,24},{8,0},{16,8},{24,16},{1,25},{9,1},{17,9},{25,17},{2,26},{10... | collective-permute-start | bytes 36872 | tf_op jit(solution)/shard_map/ppermute | solution.py:400
  39.5 0.0 collective-permute-start.2
  39.5 1.0 %collective-permute-start.1 = (f32[24,128]{1,0:T(8,128)S(1)}, f32[24,128]{1,0:T(8,128)S(1)}, u32[]{:S(2)}, u32[]{:S(2)}) collective-permute-start(f32[24,128]{1,0:T(8,128)S(1)} %get-tuple-element.8.rest_0_), channel_id=1, source_target_pairs={{0,8},{8,16},{16,24},{24,0},{1,9},{9,17},{17,25},{25,1},{2,10},{10... | collective-permute-start | bytes 36872 | tf_op jit(solution)/shard_map/ppermute | solution.py:400
  40.5 0.4 collective-permute-done.3.rest_3_
  40.9 3.2 %collective-permute-done.2.rest_2_ = f32[24,128]{1,0:T(8,128)S(1)} collective-permute-done((f32[24,128]{1,0:T(8,128)S(1)}, f32[24,128]{1,0:T(8,128)S(1)}, u32[]{:S(2)}, u32[]{:S(2)}) %collective-permute-start.2) | collective-permute-done | bytes 12320 | tf_op jit(solution)/shard_map/ppermute | solution.py:400
  44.1 0.9 %collective-permute-done.1.rest_1_ = f32[24,128]{1,0:T(8,128)S(1)} collective-permute-done((f32[24,128]{1,0:T(8,128)S(1)}, f32[24,128]{1,0:T(8,128)S(1)}, u32[]{:S(2)}, u32[]{:S(2)}) %collective-permute-start.1) | collective-permute-done | bytes 12320 | tf_op jit(solution)/shard_map/ppermute | solution.py:400
  45.0 1.1 %finish.1 = f32[3,2,192,128]{3,2,1,0:T(8,128)} custom-call(s32[1]{0:T(128)} %bitcast.position, f32[2,24,5,8,128]{4,3,2,1,0:T(8,128)S(1)} %get-tuple-element.6.factors, f32[2,3,5,8,128]{4,3,2,1,0:T(8,128)S(1)} %get-tuple-element.7.tree, f32[3,2,192,128]{3,2,1,0:T(8,128)S(1)} %copy-done.1, f32[24,128]{1,0:T(8,128)S(1)} %get-tuple-element.8.rest_0_, ...), custom_call_target="tpu_custom_call" | custom-call | tf_op jit(solution)/shard_map/finish/pallas_call | solution.py:404
  (1 shorter events, 0.0 us)
Async XLA Ops:
  0.6 1.1 %copy-start = (f32[3,2,192,128]{3,2,1,0:T(8,128)S(1)}, f32[3,2,192,128]{3,2,1,0:T(8,128)}, u32[]{:S(2)}) copy-start(f32[3,2,192,128]{3,2,1,0:T(8,128)} %velocity.5) | copy-start | bytes 1769476
  17.9 0.7 %collective-permute-start = (f32[8,16,128]{2,1,0:T(8,128)S(1)}, f32[8,16,128]{2,1,0:T(8,128)S(1)}, u32[]{:S(2)}, u32[]{:S(2)}) collective-permute-start(f32[8,16,128]{2,1,0:T(8,128)S(1)} %slice.4), channel_id=1, source_target_pairs={{1,8},{8,1},{9,16},{16,9},{17,24},{24,17}} | collective-permute-start | bytes 196616 | tf_op jit(solution)/shard_map/ppermute | solution.py:363
  18.6 15.2 %copy-start.1 = (f32[3,2,192,128]{3,2,1,0:T(8,128)S(1)}, f32[3,2,192,128]{3,2,1,0:T(8,128)}, u32[]{:S(2)}) copy-start(f32[3,2,192,128]{3,2,1,0:T(8,128)} %velocity.5) | copy-start | bytes 1769476
  18.6 15.2 %copy-start.2 = (f32[3,2,192,128]{3,2,1,0:T(8,128)S(1)}, f32[3,2,192,128]{3,2,1,0:T(8,128)}, u32[]{:S(2)}) copy-start(f32[3,2,192,128]{3,2,1,0:T(8,128)} %tendency.1) | copy-start | bytes 1769476
  34.5 6.4 %collective-permute-start.3 = (f32[24,128]{1,0:T(8,128)S(1)}, f32[24,128]{1,0:T(8,128)S(1)}, u32[]{:S(2)}, u32[]{:S(2)}) collective-permute-start(f32[24,128]{1,0:T(8,128)S(1)} %get-tuple-element.8.rest_0_), channel_id=1, source_target_pairs={{0,24},{8,0},{16,8},{24,16},{1,25},{9,1},{17,9},{25,17},{2,26},{10... | collective-permute-start | bytes 36872 | tf_op jit(solution)/shard_map/ppermute | solution.py:400
  39.5 4.6 %collective-permute-start.2 = (f32[24,128]{1,0:T(8,128)S(1)}, f32[24,128]{1,0:T(8,128)S(1)}, u32[]{:S(2)}, u32[]{:S(2)}) collective-permute-start(f32[24,128]{1,0:T(8,128)S(1)} %get-tuple-element.8.rest_0_), channel_id=1, source_target_pairs={{0,16},{8,24},{16,0},{24,8},{1,17},{9,25},{17,1},{25,9},{2,18},{10... | collective-permute-start | bytes 36872 | tf_op jit(solution)/shard_map/ppermute | solution.py:400
  39.5 5.5 %collective-permute-start.1 = (f32[24,128]{1,0:T(8,128)S(1)}, f32[24,128]{1,0:T(8,128)S(1)}, u32[]{:S(2)}, u32[]{:S(2)}) collective-permute-start(f32[24,128]{1,0:T(8,128)S(1)} %get-tuple-element.8.rest_0_), channel_id=1, source_target_pairs={{0,8},{8,16},{16,24},{24,0},{1,9},{9,17},{17,25},{25,1},{2,10},{10... | collective-permute-start | bytes 36872 | tf_op jit(solution)/shard_map/ppermute | solution.py:400

commit v4 on v3

--- a/solution.py
+++ b/solution.py
@@ -261,18 +261,16 @@
             across = from_left * across_b
             level, step = level + 1, step * 2
         rows_out = [*first, *last, corner, across, end, visc_first]
+        rows_out = [v[0:1, :] for v in rows_out] + [visc[SEGMENTS - 1 :, :]]
         for i, v in enumerate(rows_out):
-            reduced[i * width + x : i * width + x + 1, :] = v[0:1, :]
-        i = len(rows_out)
-        reduced[i * width + x : i * width + x + 1, :] = visc[SEGMENTS - 1 :, :]
-
-
-def finish_kernel(devices, position, factors, tree, velocity, *rest):
-    reduced, (out, gathered, fluxes) = rest[:devices], rest[devices:]
+            for device in range(reduced.shape[0]):
+                reduced[device, i * width + x : i * width + x + 1, :] = v
+
+
+def finish_kernel(position, factors, tree, velocity, gathered, out, fluxes):
+    devices = gathered.shape[0]
     width, length = factors.shape[:2]
     here = position[0]
-    for shift in range(devices):
-        gathered[lax.rem(here - shift + devices, devices)] = reduced[shift][...]
 
     def part(device, i):
         return gathered[device, i * width : (i + 1) * width, :]
@@ -386,7 +384,7 @@
         sweep_kernel,
         out_shape=(
             jax.ShapeDtypeStruct((width, cells, lanes), f32),
-            jax.ShapeDtypeStruct((packed, lanes), f32),
+            jax.ShapeDtypeStruct((walls, packed, lanes), f32),
             jax.ShapeDtypeStruct((width, length, 5, SEGMENTS, lanes), f32),
             jax.ShapeDtypeStruct((width, levels, 5, SEGMENTS, lanes), f32),
         ),
@@ -396,23 +394,19 @@
         name="sweep",
     )(back, velocity, tendency)
 
-    others = [
-        lax.ppermute(reduced, "gy", [(i, (i + shift) % walls) for i in range(walls)])
-        for shift in range(1, walls)
-    ]
+    gathered = lax.all_to_all(reduced, "gy", split_axis=0, concat_axis=0, tiled=True)
     position = lax.axis_index("gy").astype(jnp.int32).reshape(1)
     new_velocity = pl.pallas_call(
-        functools.partial(finish_kernel, walls),
+        finish_kernel,
         out_shape=jax.ShapeDtypeStruct(velocity.shape, f32),
-        in_specs=[pl.BlockSpec(memory_space=pltpu.SMEM)] + in_vmem(3 + walls),
+        in_specs=[pl.BlockSpec(memory_space=pltpu.SMEM)] + in_vmem(4),
         out_specs=pl.BlockSpec(memory_space=pltpu.VMEM),
         scratch_shapes=[
-            pltpu.VMEM((walls, packed, lanes), f32),
             pltpu.VMEM((walls + 1, -(-3 * width // 8) * 8, lanes), f32),
         ],
         compiler_params=params(),
         name="finish",
-    )(position, factors, tree, velocity, reduced, *others)
+    )(position, factors, tree, velocity, gathered)
     return (new_velocity, eddy)
 
 

time: 46.3 us -> 48.3 us (1.043)
  waiting for transfers between devices: 4.48 us -> 5.7 us
    all_to_all x0 -> x1, starting transfers between devices: none -> 6.24 us  [body(): lax.all_to_all(reduced, 'gy', split_axis=0, concat_axis=0, tiled=True)]
    ppermute x3 -> x0, starting transfers between devices: 5.98 us -> none  [body(): lax.ppermute(reduced, 'gy', [(i, (i + shift) % walls) for i in range(wall...]
    all_to_all x0 -> x1, waiting for transfers between devices: none -> 5.7 us  [body(): lax.all_to_all(reduced, 'gy', split_axis=0, concat_axis=0, tiled=True)]
    ppermute x3 -> x0, waiting for transfers between devices: 4.48 us -> none  [body(): lax.ppermute(reduced, 'gy', [(i, (i + shift) % walls) for i in range(wall...]
  transfers between devices with their start and end apart: 4 -> 2, of which waited for: 3 -> 1; matrix products, arithmetic and copies ran while one was open for 0% -> 0% of each run, Pallas kernels for 0% -> 0%
where the time goes in v4:
time: 48.3 us; the launch traced here: 47.9 us
  blocking collectives  28.3 us (59%)
  starting transfers between devices  6.89 us (14%)
  waiting for transfers between devices  5.7 us (12%)
  Pallas kernels  5.32 us (11%)
  local copies, waits for them, and re-layouts  1.08 us (2%)
  between operations  0.69 us (1%)
    all_to_all x1, blocking collectives, body(): lax.all_to_all(chunks, ('gx', 'gz'), split_axis=0, concat_axis=0, tiled=T...  16.1 us
    all_to_all x1, blocking collectives, body(): lax.all_to_all(eddy_chunks, ('gx', 'gz'), split_axis=0, concat_axis=0, ti...  12.1 us
    all_to_all x1, starting transfers between devices, body(): lax.all_to_all(reduced, 'gy', split_axis=0, concat_axis=0, tiled=True)  6.24 us
    all_to_all x1, waiting for transfers between devices, body(): lax.all_to_all(reduced, 'gy', split_axis=0, concat_axis=0, tiled=True)  5.7 us
    pallas_call x1, Pallas kernels, body(): pl.pallas_call(functools.partial(germano_kernel, nz_parts, width, rows),...  3.04 us
    pallas_call x1, Pallas kernels, body(): pl.pallas_call(sweep_kernel, out_shape=(jax.ShapeDtypeStruct((width, cell...  1.11 us
    pallas_call x1, Pallas kernels, body(): pl.pallas_call(finish_kernel, out_shape=jax.ShapeDtypeStruct(velocity.sha...  1.1 us
    unnamed x6, local copies, waits for them, and re-layouts  1.07 us
  transfers between devices with their start and end apart: 2, of which 1 were waited for; matrix products, arithmetic and copies ran while one was open for 0% of the time, Pallas kernels for 0%

profile of v4, /device:TPU:0, one launch (start us, length us, event | category | flops | bytes accessed | tf_op | source)
XLA Modules:
  0.0 47.9 jit_solution(9403619443526306861)
XLA Ops:
  0.6 0.0 copy-start
  0.6 1.1 %copy-done = f32[3,2,192,128]{3,2,1,0:T(8,128)S(1)} copy-done((f32[3,2,192,128]{3,2,1,0:T(8,128)S(1)}, f32[3,2,192,128]{3,2,1,0:T(8,128)}, u32[]{:S(2)}) %copy-start) | copy-done | bytes 589848
  1.7 0.1 pack.1
  1.8 16.1 %all_to_all.15.recv = f32[8,160,128]{2,1,0:T(8,128)S(1)} all-to-all(f32[8,160,128]{2,1,0:T(8,128)S(1)} %pack.1), channel_id=1, replica_groups=mesh['gy'=4,'gx'=4,'gz'=2] {'gx','gz'}, dimensions={0} | all-to-all | bytes 1310720 | tf_op jit(solution)/shard_map/all_to_all | solution.py:356
  17.9 0.7 %collective-permute-start = (f32[8,16,128]{2,1,0:T(8,128)S(1)}, f32[8,16,128]{2,1,0:T(8,128)S(1)}, u32[]{:S(2)}, u32[]{:S(2)}) collective-permute-start(f32[8,16,128]{2,1,0:T(8,128)S(1)} %slice.4), channel_id=1, source_target_pairs={{1,8},{8,1},{9,16},{16,9},{17,24},{24,17}} | collective-permute-start | bytes 196616 | tf_op jit(solution)/shard_map/ppermute | solution.py:361
  18.6 0.0 collective-permute-done.swapped
  18.6 0.0 copy-start.1
  18.6 0.0 copy-start.2
  18.6 3.0 %germano.1 = f32[8,2,24,128]{3,2,1,0:T(8,128)S(1)} custom-call(s32[1]{0:T(128)} %bitcast.1.rank, f32[8,160,128]{2,1,0:T(8,128)S(1)} %all_to_all.15.recv, f32[8,16,128]{2,1,0:T(8,128)S(1)} %collective-permute-done.swapped), custom_call_target="tpu_custom_call" | custom-call | tf_op jit(solution)/shard_map/germano/pallas_call | solution.py:363
  21.6 12.1 %all_to_all.16.back = f32[8,2,24,128]{3,2,1,0:T(8,128)S(1)} all-to-all(f32[8,2,24,128]{3,2,1,0:T(8,128)S(1)} %germano.1), channel_id=1, replica_groups=mesh['gy'=4,'gx'=4,'gz'=2] {'gx','gz'}, dimensions={0} | all-to-all | bytes 393216 | tf_op jit(solution)/shard_map/all_to_all | solution.py:378
  33.8 0.0 copy-done.1
  33.8 0.0 copy-done.2
  33.8 1.1 %sweep.1 = (f32[2,192,128]{2,1,0:T(8,128)}, f32[4,24,128]{2,1,0:T(8,128)}, f32[2,24,5,8,128]{4,3,2,1,0:T(8,128)S(1)}, f32[2,3,5,8,128]{4,3,2,1,0:T(8,128)S(1)}) custom-call(f32[8,2,24,128]{3,2,1,0:T(8,128)S(1)} %all_to_all.16.back, f32[3,2,192,128]{3,2,1,0:T(8,128)S(1)} %copy-done.1, f32[3,2,192,128]{3,2,1,0:T(8,128)S(1)} %copy-done.2), custom_call_target="tpu_custom_call" | custom-call | tf_op jit(solution)/shard_map/sweep/pallas_call | solution.py:383
  34.9 6.2 %all-to-all-start.2 = ((f32[4,24,128]{2,1,0:T(8,128)}), f32[4,24,128]{2,1,0:T(8,128)S(1)}, u32[]{:S(2)}, u32[]{:S(2)}) async-start(f32[4,24,128]{2,1,0:T(8,128)} %get-tuple-element.8), calls=%async_computation.2 | async-start | bytes 98304 | tf_op jit(solution)/shard_map/all_to_all | solution.py:397
  41.1 5.7 %all-to-all-done.2.gathered = f32[4,24,128]{2,1,0:T(8,128)S(1)} async-done(((f32[4,24,128]{2,1,0:T(8,128)}), f32[4,24,128]{2,1,0:T(8,128)S(1)}, u32[]{:S(2)}, u32[]{:S(2)}) %all-to-all-start.2) | async-done | bytes 49184 | tf_op jit(solution)/shard_map/all_to_all | solution.py:397
  46.8 1.1 %finish.1 = f32[3,2,192,128]{3,2,1,0:T(8,128)} custom-call(s32[1]{0:T(128)} %bitcast.position, f32[2,24,5,8,128]{4,3,2,1,0:T(8,128)S(1)} %get-tuple-element.6.factors, f32[2,3,5,8,128]{4,3,2,1,0:T(8,128)S(1)} %get-tuple-element.7.tree, f32[3,2,192,128]{3,2,1,0:T(8,128)S(1)} %copy-done.1, f32[4,24,128]{2,1,0:T(8,128)S(1)} %all-to-all-done.2.gathered), custom_call_target="tpu_custom_call" | custom-call | tf_op jit(solution)/shard_map/finish/pallas_call | solution.py:399
  (1 shorter events, 0.0 us)
Async XLA Ops:
  0.6 1.1 %copy-start = (f32[3,2,192,128]{3,2,1,0:T(8,128)S(1)}, f32[3,2,192,128]{3,2,1,0:T(8,128)}, u32[]{:S(2)}) copy-start(f32[3,2,192,128]{3,2,1,0:T(8,128)} %velocity.5) | copy-start | bytes 1769476
  17.9 0.7 %collective-permute-start = (f32[8,16,128]{2,1,0:T(8,128)S(1)}, f32[8,16,128]{2,1,0:T(8,128)S(1)}, u32[]{:S(2)}, u32[]{:S(2)}) collective-permute-start(f32[8,16,128]{2,1,0:T(8,128)S(1)} %slice.4), channel_id=1, source_target_pairs={{1,8},{8,1},{9,16},{16,9},{17,24},{24,17}} | collective-permute-start | bytes 196616 | tf_op jit(solution)/shard_map/ppermute | solution.py:361
  18.6 15.2 %copy-start.1 = (f32[3,2,192,128]{3,2,1,0:T(8,128)S(1)}, f32[3,2,192,128]{3,2,1,0:T(8,128)}, u32[]{:S(2)}) copy-start(f32[3,2,192,128]{3,2,1,0:T(8,128)} %velocity.5) | copy-start | bytes 1769476
  18.6 15.2 %copy-start.2 = (f32[3,2,192,128]{3,2,1,0:T(8,128)S(1)}, f32[3,2,192,128]{3,2,1,0:T(8,128)}, u32[]{:S(2)}) copy-start(f32[3,2,192,128]{3,2,1,0:T(8,128)} %tendency.1) | copy-start | bytes 1769476
  34.9 11.9 %all-to-all-start.2 = ((f32[4,24,128]{2,1,0:T(8,128)}), f32[4,24,128]{2,1,0:T(8,128)S(1)}, u32[]{:S(2)}, u32[]{:S(2)}) async-start(f32[4,24,128]{2,1,0:T(8,128)} %get-tuple-element.8), calls=%async_computation.2 | async-start | bytes 98304 | tf_op jit(solution)/shard_map/all_to_all | solution.py:397

commit v5 on v3

--- a/solution.py
+++ b/solution.py
@@ -58,34 +58,63 @@
     return (v[0] * v[0], v[1] * v[1], v[2] * v[2], v[0] * v[1], v[0] * v[2], v[1] * v[2])
 
 
-def row_order(count):
-    return [0, count - 1, *range(1, count - 1)]
-
-
-def pack_kernel(rows, velocity, out):
+def place_of(rank, parity, count):
+    if rank >= 2:
+        return rank - 1
+    return 0 if rank == parity else count - 1
+
+
+def by_parity(parity, count, fill):
+    for rank in range(2, count):
+        fill(rank, place_of(rank, 0, count))
+    for turn in range(2):
+
+        @pl.when(parity[0] == turn)
+        def _():
+            for rank in range(2):
+                fill(rank, place_of(rank, turn, count))
+
+
+def aligned(n):
+    return -(-n // 8) * 8
+
+
+def pack_kernel(rows, parity, velocity, out):
     _, width, cells, _ = velocity.shape
     count, depth, lanes = out.shape
     planes = 3 * width
-    for rank, place in enumerate(row_order(count)):
+    slots = planes * rows
+
+    def fill(rank, place):
         first = place * rows
-        before = max(first - 1, 0)
-        after = min(first + rows, cells - 1)
+        beside = [first - 1, first + rows]
+        if place == 0:
+            beside = [first, first + rows]
+        if place == count - 1:
+            beside = [first + rows - 1, first - 1]
         for i in range(planes):
             c, x = divmod(i, width)
             out[rank, i * rows : (i + 1) * rows, :] = velocity[c, x, first : first + rows, :]
-            at = planes * rows + i
-            out[rank, at : at + 1, :] = velocity[c, x, before : before + 1, :]
-            at += planes
-            out[rank, at : at + 1, :] = velocity[c, x, after : after + 1, :]
-        filled = planes * (rows + 2)
-        if filled < depth:
-            out[rank, filled:, :] = jnp.zeros((depth - filled, lanes), jnp.float32)
-
-
-def germano_kernel(nz_parts, width, rows, rank, recv, swapped, out, vel, filt, ends, mag, part):
+            for slot, row in enumerate(beside):
+                at = slots + slot * aligned(planes) + i
+                out[rank, at : at + 1, :] = velocity[c, x, row : row + 1, :]
+
+    by_parity(parity, count, fill)
+    blank = aligned(planes) - planes
+    for rank in range(count):
+        for slot in range(2):
+            at = slots + slot * aligned(planes) + planes
+            out[rank, at : at + blank, :] = jnp.zeros((blank, lanes), jnp.float32)
+        at = slots + 2 * aligned(planes)
+        if at < depth:
+            out[rank, at:, :] = jnp.zeros((depth - at, lanes), jnp.float32)
+
+
+def germano_kernel(nz_parts, width, rows, rank, parity, recv, swapped, out, vel, filt, ends, mag, part):
     count, _, lanes = recv.shape
     planes = 3 * width
-    outer = (rank[0] == 0, rank[0] == 1)
+    bottom = rank[0] == parity[0]
+    top = rank[0] == 1 - parity[0]
     nx = (count // nz_parts) * width
     nz = nz_parts * lanes
     blocks = range(nz_parts)
@@ -99,10 +128,14 @@
             for x in range(width):
                 i = c * width + x
                 vel[c, x0 + x, zb, inner, :] = recv[k, i * rows : (i + 1) * rows, :]
-                for side, at in ((0, lead - 1), (1, lead + rows)):
-                    own = planes * rows + side * planes + i
-                    far = (1 - side) * planes + i
-                    edge = jnp.where(outer[side], swapped[k, far : far + 1, :], recv[k, own : own + 1, :])
+                slots = planes * rows + i
+                near = recv[k, slots : slots + 1, :]
+                slots += aligned(planes)
+                other = recv[k, slots : slots + 1, :]
+                far = swapped[k, i : i + 1, :]
+                below = jnp.where(bottom, far, jnp.where(top, other, near))
+                above = jnp.where(top, far, other)
+                for side, (edge, at) in enumerate(((below, lead - 1), (above, lead + rows))):
                     vel[c, x0 + x, zb, at : at + 1, :] = edge
                     ends[c, x0 + x, zb, side : side + 1, :] = edge
 
@@ -187,12 +220,15 @@
             out[k, x] = coefficient * mag[x0 + x, zb]
 
 
-def sweep_kernel(back, velocity, tendency, eddy, reduced, factors, tree):
+def sweep_kernel(parity, back, velocity, tendency, eddy, reduced, factors, tree):
     count, width, rows, _ = back.shape
     length = count * rows // SEGMENTS
-    for k, place in enumerate(row_order(count)):
+
+    def fill(rank, place):
         for x in range(width):
-            eddy[x, place * rows : (place + 1) * rows, :] = back[k, x]
+            eddy[x, place * rows : (place + 1) * rows, :] = back[rank, x]
+
+    by_parity(parity, count, fill)
 
     def row(ref, index, j):
         return ref[(*index, pl.ds(j, SEGMENTS, stride=length), slice(None))]
@@ -331,6 +367,10 @@
     return [pl.BlockSpec(memory_space=pltpu.VMEM)] * count
 
 
+def in_smem(count):
+    return [pl.BlockSpec(memory_space=pltpu.SMEM)] * count
+
+
 def params():
     return pltpu.CompilerParams(vmem_limit_bytes=VMEM_BYTES)
 
@@ -342,30 +382,33 @@
     walls = lax.axis_size("gy")
     rows = cells // count
     nx = lax.axis_size("gx") * width
-    padded = 16 + -(-rows // 8) * 8
+    padded = 16 + aligned(rows)
     f32 = jnp.float32
 
-    filled = 3 * width * (rows + 2)
-    depth = -(-filled // 8) * 8
+    planes = 3 * width
+    depth = aligned(planes * rows + 2 * aligned(planes))
+    position = lax.axis_index("gy").astype(jnp.int32).reshape(1)
+    parity = lax.rem(position, 2)
     chunks = pl.pallas_call(
         functools.partial(pack_kernel, rows),
         out_shape=jax.ShapeDtypeStruct((count, depth, lanes), f32),
-        in_specs=in_vmem(1),
+        in_specs=in_smem(1) + in_vmem(1),
         out_specs=pl.BlockSpec(memory_space=pltpu.VMEM),
         compiler_params=params(),
         name="pack",
-    )(velocity)
+    )(parity, velocity)
     recv = lax.all_to_all(chunks, ("gx", "gz"), split_axis=0, concat_axis=0, tiled=True)
     pairs = []
     for wall in range(walls - 1):
-        upper, lower = wall * count + 1, (wall + 1) * count
-        pairs += [(upper, lower), (lower, upper)]
-    swapped = lax.ppermute(recv[:, 3 * width * rows :], ("gy", "gx", "gz"), pairs)
+        outer = wall * count + (1 - wall % 2)
+        pairs += [(outer, outer + count), (outer + count, outer)]
+    slot = lax.slice_in_dim(recv, planes * rows, planes * rows + aligned(planes), axis=1)
+    swapped = lax.ppermute(slot, ("gy", "gx", "gz"), pairs)
     rank = lax.axis_index(("gx", "gz")).astype(jnp.int32).reshape(1)
     eddy_chunks = pl.pallas_call(
         functools.partial(germano_kernel, nz_parts, width, rows),
         out_shape=jax.ShapeDtypeStruct((count, width, rows, lanes), f32),
-        in_specs=[pl.BlockSpec(memory_space=pltpu.SMEM)] + in_vmem(2),
+        in_specs=in_smem(2) + in_vmem(2),
         out_specs=pl.BlockSpec(memory_space=pltpu.VMEM),
         scratch_shapes=[
             pltpu.VMEM((3, nx, nz_parts, padded, lanes), f32),
@@ -376,12 +419,12 @@
         ],
         compiler_params=params(),
         name="germano",
-    )(rank, recv, swapped)
+    )(rank, parity, recv, swapped)
     back = lax.all_to_all(eddy_chunks, ("gx", "gz"), split_axis=0, concat_axis=0, tiled=True)
 
     length = cells // SEGMENTS
     levels = SEGMENTS.bit_length() - 1
-    packed = -(-11 * width // 8) * 8
+    packed = aligned(11 * width)
     eddy, reduced, factors, tree = pl.pallas_call(
         sweep_kernel,
         out_shape=(
@@ -390,25 +433,24 @@
             jax.ShapeDtypeStruct((width, length, 5, SEGMENTS, lanes), f32),
             jax.ShapeDtypeStruct((width, levels, 5, SEGMENTS, lanes), f32),
         ),
-        in_specs=in_vmem(3),
+        in_specs=in_smem(1) + in_vmem(3),
         out_specs=tuple(in_vmem(4)),
         compiler_params=params(),
         name="sweep",
-    )(back, velocity, tendency)
+    )(parity, back, velocity, tendency)
 
     others = [
         lax.ppermute(reduced, "gy", [(i, (i + shift) % walls) for i in range(walls)])
         for shift in range(1, walls)
     ]
-    position = lax.axis_index("gy").astype(jnp.int32).reshape(1)
     new_velocity = pl.pallas_call(
         functools.partial(finish_kernel, walls),
         out_shape=jax.ShapeDtypeStruct(velocity.shape, f32),
-        in_specs=[pl.BlockSpec(memory_space=pltpu.SMEM)] + in_vmem(3 + walls),
+        in_specs=in_smem(1) + in_vmem(3 + walls),
         out_specs=pl.BlockSpec(memory_space=pltpu.VMEM),
         scratch_shapes=[
             pltpu.VMEM((walls, packed, lanes), f32),
-            pltpu.VMEM((walls + 1, -(-3 * width // 8) * 8, lanes), f32),
+            pltpu.VMEM((walls + 1, aligned(3 * width), lanes), f32),
         ],
         compiler_params=params(),
         name="finish",

time: 46.3 us -> 46 us (level)
  starting transfers between devices: 6.64 us -> 8.11 us
  blocking collectives: 28.3 us -> 27 us
  waiting for transfers between devices: 4.48 us -> 3.91 us
    ppermute x3, starting transfers between devices: 5.98 us -> 7.45 us  [body(): lax.ppermute(reduced, 'gy', [(i, (i + shift) % walls) for i in range(wall...]
    all_to_all x1, blocking collectives: 12.1 us -> 10.9 us  [body(): lax.all_to_all(eddy_chunks, ('gx', 'gz'), split_axis=0, concat_axis=0, ti...]
    ppermute x3, waiting for transfers between devices: 4.48 us -> 3.91 us  [body(): lax.ppermute(reduced, 'gy', [(i, (i + shift) % walls) for i in range(wall...]
  transfers between devices with their start and end apart: 4 -> 4, of which waited for: 3 -> 2; matrix products, arithmetic and copies ran while one was open for 0% -> 0% of each run, Pallas kernels for 0% -> 0%
where the time goes in v5:
time: 46 us; the launch traced here: 45.8 us
  blocking collectives  27 us (59%)
  starting transfers between devices  8.11 us (18%)
  Pallas kernels  4.95 us (11%)
  waiting for transfers between devices  3.91 us (8%)
  local copies, waits for them, and re-layouts  1.08 us (2%)
  between operations  0.7 us (2%)
    all_to_all x1, blocking collectives, body(): lax.all_to_all(chunks, ('gx', 'gz'), split_axis=0, concat_axis=0, tiled=T...  16.1 us
    all_to_all x1, blocking collectives, body(): lax.all_to_all(eddy_chunks, ('gx', 'gz'), split_axis=0, concat_axis=0, ti...  10.9 us
    ppermute x3, starting transfers between devices, body(): lax.ppermute(reduced, 'gy', [(i, (i + shift) % walls) for i in range(wall...  7.45 us
    ppermute x3, waiting for transfers between devices, body(): lax.ppermute(reduced, 'gy', [(i, (i + shift) % walls) for i in range(wall...  3.91 us
    pallas_call x1, Pallas kernels, body(): pl.pallas_call(functools.partial(germano_kernel, nz_parts, width, rows),...  3.05 us
    pallas_call x1, Pallas kernels, body(): pl.pallas_call(functools.partial(finish_kernel, walls), out_shape=jax.Sha...  1.13 us
    unnamed x6, local copies, waits for them, and re-layouts  1.07 us
  transfers between devices with their start and end apart: 4, of which 2 were waited for; matrix products, arithmetic and copies ran while one was open for 0% of the time, Pallas kernels for 0%

profile of v5, /device:TPU:0, one launch (start us, length us, event | category | flops | bytes accessed | tf_op | source)
XLA Modules:
  0.0 45.8 jit_solution(3330235805160670667)
XLA Ops:
  0.6 0.0 copy-start
  0.6 1.1 %copy-done = f32[3,2,192,128]{3,2,1,0:T(8,128)S(1)} copy-done((f32[3,2,192,128]{3,2,1,0:T(8,128)S(1)}, f32[3,2,192,128]{3,2,1,0:T(8,128)}, u32[]{:S(2)}) %copy-start) | copy-done | bytes 589848
  1.7 0.1 pack.1
  1.8 16.1 %all_to_all.10.recv = f32[8,160,128]{2,1,0:T(8,128)S(1)} all-to-all(f32[8,160,128]{2,1,0:T(8,128)S(1)} %pack.1), channel_id=1, replica_groups=mesh['gy'=4,'gx'=4,'gz'=2] {'gx','gz'}, dimensions={0} | all-to-all | bytes 1310720 | tf_op jit(solution)/shard_map/all_to_all | solution.py:400
  17.9 0.7 %collective-permute-start = (f32[8,8,128]{2,1,0:T(8,128)S(1)}, f32[8,8,128]{2,1,0:T(8,128)S(1)}, u32[]{:S(2)}, u32[]{:S(2)}) collective-permute-start(f32[8,8,128]{2,1,0:T(8,128)S(1)} %slice.4), channel_id=1, source_target_pairs={{1,9},{9,1},{8,16},{16,8},{17,25},{25,17}} | collective-permute-start | bytes 98312 | tf_op jit(solution)/shard_map/ppermute | solution.py:406
  18.6 0.0 collective-permute-done.swapped
  18.6 0.0 copy-start.1
  18.6 0.0 copy-start.2
  18.6 3.0 %germano.1 = f32[8,2,24,128]{3,2,1,0:T(8,128)S(1)} custom-call(s32[1]{0:T(128)} %bitcast.1.rank, s32[1]{0:T(128)S(6)} %rem.18.parity, f32[8,160,128]{2,1,0:T(8,128)S(1)} %all_to_all.10.recv, f32[8,8,128]{2,1,0:T(8,128)S(1)} %collective-permute-done.swapped), custom_call_target="tpu_custom_call" | custom-call | tf_op jit(solution)/shard_map/germano/pallas_call | solution.py:408
  21.7 10.9 %all_to_all.11.back = f32[8,2,24,128]{3,2,1,0:T(8,128)S(1)} all-to-all(f32[8,2,24,128]{3,2,1,0:T(8,128)S(1)} %germano.1), channel_id=1, replica_groups=mesh['gy'=4,'gx'=4,'gz'=2] {'gx','gz'}, dimensions={0} | all-to-all | bytes 393216 | tf_op jit(solution)/shard_map/all_to_all | solution.py:423
  32.6 0.0 copy-done.1
  32.6 0.0 copy-done.2
  32.6 0.7 %sweep.1 = (f32[2,192,128]{2,1,0:T(8,128)}, f32[24,128]{1,0:T(8,128)S(1)}, f32[2,24,5,8,128]{4,3,2,1,0:T(8,128)S(1)}, f32[2,3,5,8,128]{4,3,2,1,0:T(8,128)S(1)}) custom-call(s32[1]{0:T(128)S(6)} %rem.18.parity, f32[8,2,24,128]{3,2,1,0:T(8,128)S(1)} %all_to_all.11.back, f32[3,2,192,128]{3,2,1,0:T(8,128)S(1)} %copy-done.1, f32[3,2,192,128]{3,2,1,0:T(8,128)S(1)} %copy-done.2), custom_call_target="tpu_custom_call" | custom-call | tf_op jit(solution)/shard_map/sweep/pallas_call | solution.py:428
  33.3 3.6 %collective-permute-start.3 = (f32[24,128]{1,0:T(8,128)S(1)}, f32[24,128]{1,0:T(8,128)S(1)}, u32[]{:S(2)}, u32[]{:S(2)}) collective-permute-start(f32[24,128]{1,0:T(8,128)S(1)} %get-tuple-element.8.rest_0_), channel_id=1, source_target_pairs={{0,24},{8,0},{16,8},{24,16},{1,25},{9,1},{17,9},{25,17},{2,26},{10... | collective-permute-start | bytes 36872 | tf_op jit(solution)/shard_map/ppermute | solution.py:443
  36.9 2.3 %collective-permute-start.2 = (f32[24,128]{1,0:T(8,128)S(1)}, f32[24,128]{1,0:T(8,128)S(1)}, u32[]{:S(2)}, u32[]{:S(2)}) collective-permute-start(f32[24,128]{1,0:T(8,128)S(1)} %get-tuple-element.8.rest_0_), channel_id=1, source_target_pairs={{0,16},{8,24},{16,0},{24,8},{1,17},{9,25},{17,1},{25,9},{2,18},{10... | collective-permute-start | bytes 36872 | tf_op jit(solution)/shard_map/ppermute | solution.py:443
  39.1 1.6 %collective-permute-start.1 = (f32[24,128]{1,0:T(8,128)S(1)}, f32[24,128]{1,0:T(8,128)S(1)}, u32[]{:S(2)}, u32[]{:S(2)}) collective-permute-start(f32[24,128]{1,0:T(8,128)S(1)} %get-tuple-element.8.rest_0_), channel_id=1, source_target_pairs={{0,8},{8,16},{16,24},{24,0},{1,9},{9,17},{17,25},{25,1},{2,10},{10... | collective-permute-start | bytes 36872 | tf_op jit(solution)/shard_map/ppermute | solution.py:443
  40.7 0.0 collective-permute-done.3.rest_3_
  40.7 0.7 %collective-permute-done.2.rest_2_ = f32[24,128]{1,0:T(8,128)S(1)} collective-permute-done((f32[24,128]{1,0:T(8,128)S(1)}, f32[24,128]{1,0:T(8,128)S(1)}, u32[]{:S(2)}, u32[]{:S(2)}) %collective-permute-start.2) | collective-permute-done | bytes 12320 | tf_op jit(solution)/shard_map/ppermute | solution.py:443
  41.5 3.2 %collective-permute-done.1.rest_1_ = f32[24,128]{1,0:T(8,128)S(1)} collective-permute-done((f32[24,128]{1,0:T(8,128)S(1)}, f32[24,128]{1,0:T(8,128)S(1)}, u32[]{:S(2)}, u32[]{:S(2)}) %collective-permute-start.1) | collective-permute-done | bytes 12320 | tf_op jit(solution)/shard_map/ppermute | solution.py:443
  44.6 1.1 %finish.1 = f32[3,2,192,128]{3,2,1,0:T(8,128)} custom-call(s32[1]{0:T(128)} %bitcast.position, f32[2,24,5,8,128]{4,3,2,1,0:T(8,128)S(1)} %get-tuple-element.6.factors, f32[2,3,5,8,128]{4,3,2,1,0:T(8,128)S(1)} %get-tuple-element.7.tree, f32[3,2,192,128]{3,2,1,0:T(8,128)S(1)} %copy-done.1, f32[24,128]{1,0:T(8,128)S(1)} %get-tuple-element.8.rest_0_, ...), custom_call_target="tpu_custom_call" | custom-call | tf_op jit(solution)/shard_map/finish/pallas_call | solution.py:446
  (1 shorter events, 0.0 us)
Async XLA Ops:
  0.6 1.1 %copy-start = (f32[3,2,192,128]{3,2,1,0:T(8,128)S(1)}, f32[3,2,192,128]{3,2,1,0:T(8,128)}, u32[]{:S(2)}) copy-start(f32[3,2,192,128]{3,2,1,0:T(8,128)} %velocity.5) | copy-start | bytes 1769476
  17.9 0.7 %collective-permute-start = (f32[8,8,128]{2,1,0:T(8,128)S(1)}, f32[8,8,128]{2,1,0:T(8,128)S(1)}, u32[]{:S(2)}, u32[]{:S(2)}) collective-permute-start(f32[8,8,128]{2,1,0:T(8,128)S(1)} %slice.4), channel_id=1, source_target_pairs={{1,9},{9,1},{8,16},{16,8},{17,25},{25,17}} | collective-permute-start | bytes 98312 | tf_op jit(solution)/shard_map/ppermute | solution.py:406
  18.6 14.0 %copy-start.1 = (f32[3,2,192,128]{3,2,1,0:T(8,128)S(1)}, f32[3,2,192,128]{3,2,1,0:T(8,128)}, u32[]{:S(2)}) copy-start(f32[3,2,192,128]{3,2,1,0:T(8,128)} %velocity.5) | copy-start | bytes 1769476
  18.6 14.0 %copy-start.2 = (f32[3,2,192,128]{3,2,1,0:T(8,128)S(1)}, f32[3,2,192,128]{3,2,1,0:T(8,128)}, u32[]{:S(2)}) copy-start(f32[3,2,192,128]{3,2,1,0:T(8,128)} %tendency.1) | copy-start | bytes 1769476
  33.3 7.5 %collective-permute-start.3 = (f32[24,128]{1,0:T(8,128)S(1)}, f32[24,128]{1,0:T(8,128)S(1)}, u32[]{:S(2)}, u32[]{:S(2)}) collective-permute-start(f32[24,128]{1,0:T(8,128)S(1)} %get-tuple-element.8.rest_0_), channel_id=1, source_target_pairs={{0,24},{8,0},{16,8},{24,16},{1,25},{9,1},{17,9},{25,17},{2,26},{10... | collective-permute-start | bytes 36872 | tf_op jit(solution)/shard_map/ppermute | solution.py:443
  36.9 4.6 %collective-permute-start.2 = (f32[24,128]{1,0:T(8,128)S(1)}, f32[24,128]{1,0:T(8,128)S(1)}, u32[]{:S(2)}, u32[]{:S(2)}) collective-permute-start(f32[24,128]{1,0:T(8,128)S(1)} %get-tuple-element.8.rest_0_), channel_id=1, source_target_pairs={{0,16},{8,24},{16,0},{24,8},{1,17},{9,25},{17,1},{25,9},{2,18},{10... | collective-permute-start | bytes 36872 | tf_op jit(solution)/shard_map/ppermute | solution.py:443
  39.1 5.5 %collective-permute-start.1 = (f32[24,128]{1,0:T(8,128)S(1)}, f32[24,128]{1,0:T(8,128)S(1)}, u32[]{:S(2)}, u32[]{:S(2)}) collective-permute-start(f32[24,128]{1,0:T(8,128)S(1)} %get-tuple-element.8.rest_0_), channel_id=1, source_target_pairs={{0,8},{8,16},{16,24},{24,0},{1,9},{9,17},{17,25},{25,1},{2,10},{10... | collective-permute-start | bytes 36872 | tf_op jit(solution)/shard_map/ppermute | solution.py:443

commit v6 on v5

--- a/solution.py
+++ b/solution.py
@@ -58,21 +58,30 @@
     return (v[0] * v[0], v[1] * v[1], v[2] * v[2], v[0] * v[1], v[0] * v[2], v[1] * v[2])
 
 
-def place_of(rank, parity, count):
-    if rank >= 2:
-        return rank - 1
-    return 0 if rank == parity else count - 1
+def outer_ranks(count):
+    return (count - 1, count - 3)
+
+
+def places(parity, count):
+    outer = outer_ranks(count)
+    inner = iter(range(1, count - 1))
+    return [
+        (0 if outer[parity] == rank else count - 1) if rank in outer else next(inner)
+        for rank in range(count)
+    ]
 
 
 def by_parity(parity, count, fill):
-    for rank in range(2, count):
-        fill(rank, place_of(rank, 0, count))
+    outer = outer_ranks(count)
+    for rank, place in enumerate(places(0, count)):
+        if rank not in outer:
+            fill(rank, place)
     for turn in range(2):
 
         @pl.when(parity[0] == turn)
         def _():
-            for rank in range(2):
-                fill(rank, place_of(rank, turn, count))
+            for rank in outer:
+                fill(rank, places(turn, count)[rank])
 
 
 def aligned(n):
@@ -113,8 +122,10 @@
 def germano_kernel(nz_parts, width, rows, rank, parity, recv, swapped, out, vel, filt, ends, mag, part):
     count, _, lanes = recv.shape
     planes = 3 * width
-    bottom = rank[0] == parity[0]
-    top = rank[0] == 1 - parity[0]
+    outer = outer_ranks(count)
+    even = parity[0] == 0
+    bottom = rank[0] == jnp.where(even, outer[0], outer[1])
+    top = rank[0] == jnp.where(even, outer[1], outer[0])
     nx = (count // nz_parts) * width
     nz = nz_parts * lanes
     blocks = range(nz_parts)
@@ -400,7 +411,7 @@
     recv = lax.all_to_all(chunks, ("gx", "gz"), split_axis=0, concat_axis=0, tiled=True)
     pairs = []
     for wall in range(walls - 1):
-        outer = wall * count + (1 - wall % 2)
+        outer = wall * count + outer_ranks(count)[1 - wall % 2]
         pairs += [(outer, outer + count), (outer + count, outer)]
     slot = lax.slice_in_dim(recv, planes * rows, planes * rows + aligned(planes), axis=1)
     swapped = lax.ppermute(slot, ("gy", "gx", "gz"), pairs)

time: 46 us -> 43.9 us (0.954)
  starting transfers between devices: 8.11 us -> 5.43 us
    ppermute x3, starting transfers between devices: 7.45 us -> 4.77 us  [body(): lax.ppermute(reduced, 'gy', [(i, (i + shift) % walls) for i in range(wall...]
  transfers between devices with their start and end apart: 4 -> 4, of which waited for: 2 -> 3; matrix products, arithmetic and copies ran while one was open for 0% -> 0% of each run, Pallas kernels for 0% -> 0%
where the time goes in v6:
time: 43.9 us; the launch traced here: 43.7 us
  blocking collectives  27.2 us (62%)
  starting transfers between devices  5.43 us (12%)
  Pallas kernels  4.95 us (11%)
  waiting for transfers between devices  4.32 us (10%)
  local copies, waits for them, and re-layouts  1.08 us (2%)
  between operations  0.7 us (2%)
    all_to_all x1, blocking collectives, body(): lax.all_to_all(chunks, ('gx', 'gz'), split_axis=0, concat_axis=0, tiled=T...  16.1 us
    all_to_all x1, blocking collectives, body(): lax.all_to_all(eddy_chunks, ('gx', 'gz'), split_axis=0, concat_axis=0, ti...  11.1 us
    ppermute x3, starting transfers between devices, body(): lax.ppermute(reduced, 'gy', [(i, (i + shift) % walls) for i in range(wall...  4.77 us
    ppermute x3, waiting for transfers between devices, body(): lax.ppermute(reduced, 'gy', [(i, (i + shift) % walls) for i in range(wall...  4.32 us
    pallas_call x1, Pallas kernels, body(): pl.pallas_call(functools.partial(germano_kernel, nz_parts, width, rows),...  3.04 us
    pallas_call x1, Pallas kernels, body(): pl.pallas_call(functools.partial(finish_kernel, walls), out_shape=jax.Sha...  1.13 us
    unnamed x6, local copies, waits for them, and re-layouts  1.07 us
  transfers between devices with their start and end apart: 4, of which 3 were waited for; matrix products, arithmetic and copies ran while one was open for 0% of the time, Pallas kernels for 0%

profile of v6, /device:TPU:0, one launch (start us, length us, event | category | flops | bytes accessed | tf_op | source)
XLA Modules:
  0.0 43.7 jit_solution(4022072002460263052)
XLA Ops:
  0.6 0.0 copy-start
  0.6 1.1 %copy-done = f32[3,2,192,128]{3,2,1,0:T(8,128)S(1)} copy-done((f32[3,2,192,128]{3,2,1,0:T(8,128)S(1)}, f32[3,2,192,128]{3,2,1,0:T(8,128)}, u32[]{:S(2)}) %copy-start) | copy-done | bytes 589848
  1.7 0.1 pack.1
  1.8 16.1 %all_to_all.10.recv = f32[8,160,128]{2,1,0:T(8,128)S(1)} all-to-all(f32[8,160,128]{2,1,0:T(8,128)S(1)} %pack.1), channel_id=1, replica_groups=mesh['gy'=4,'gx'=4,'gz'=2] {'gx','gz'}, dimensions={0} | all-to-all | bytes 1310720 | tf_op jit(solution)/shard_map/all_to_all | solution.py:411
  17.9 0.7 %collective-permute-start = (f32[8,8,128]{2,1,0:T(8,128)S(1)}, f32[8,8,128]{2,1,0:T(8,128)S(1)}, u32[]{:S(2)}, u32[]{:S(2)}) collective-permute-start(f32[8,8,128]{2,1,0:T(8,128)S(1)} %slice.4), channel_id=1, source_target_pairs={{5,13},{13,5},{15,23},{23,15},{21,29},{29,21}} | collective-permute-start | bytes 98312 | tf_op jit(solution)/shard_map/ppermute | solution.py:417
  18.6 0.0 collective-permute-done.swapped
  18.6 0.0 copy-start.1
  18.6 0.0 copy-start.2
  18.6 3.0 %germano.1 = f32[8,2,24,128]{3,2,1,0:T(8,128)S(1)} custom-call(s32[1]{0:T(128)} %bitcast.1.rank, s32[1]{0:T(128)S(6)} %rem.18.parity, f32[8,160,128]{2,1,0:T(8,128)S(1)} %all_to_all.10.recv, f32[8,8,128]{2,1,0:T(8,128)S(1)} %collective-permute-done.swapped), custom_call_target="tpu_custom_call" | custom-call | tf_op jit(solution)/shard_map/germano/pallas_call | solution.py:419
  21.7 11.1 %all_to_all.11.back = f32[8,2,24,128]{3,2,1,0:T(8,128)S(1)} all-to-all(f32[8,2,24,128]{3,2,1,0:T(8,128)S(1)} %germano.1), channel_id=1, replica_groups=mesh['gy'=4,'gx'=4,'gz'=2] {'gx','gz'}, dimensions={0} | all-to-all | bytes 393216 | tf_op jit(solution)/shard_map/all_to_all | solution.py:434
  32.7 0.0 copy-done.1
  32.7 0.0 copy-done.2
  32.7 0.7 %sweep.1 = (f32[2,192,128]{2,1,0:T(8,128)}, f32[24,128]{1,0:T(8,128)S(1)}, f32[2,24,5,8,128]{4,3,2,1,0:T(8,128)S(1)}, f32[2,3,5,8,128]{4,3,2,1,0:T(8,128)S(1)}) custom-call(s32[1]{0:T(128)S(6)} %rem.18.parity, f32[8,2,24,128]{3,2,1,0:T(8,128)S(1)} %all_to_all.11.back, f32[3,2,192,128]{3,2,1,0:T(8,128)S(1)} %copy-done.1, f32[3,2,192,128]{3,2,1,0:T(8,128)S(1)} %copy-done.2), custom_call_target="tpu_custom_call" | custom-call | tf_op jit(solution)/shard_map/sweep/pallas_call | solution.py:439
  33.4 3.6 %collective-permute-start.3 = (f32[24,128]{1,0:T(8,128)S(1)}, f32[24,128]{1,0:T(8,128)S(1)}, u32[]{:S(2)}, u32[]{:S(2)}) collective-permute-start(f32[24,128]{1,0:T(8,128)S(1)} %get-tuple-element.8.rest_0_), channel_id=1, source_target_pairs={{0,24},{8,0},{16,8},{24,16},{1,25},{9,1},{17,9},{25,17},{2,26},{10... | collective-permute-start | bytes 36872 | tf_op jit(solution)/shard_map/ppermute | solution.py:454
  37.0 0.0 collective-permute-start.2
  37.0 1.2 %collective-permute-start.1 = (f32[24,128]{1,0:T(8,128)S(1)}, f32[24,128]{1,0:T(8,128)S(1)}, u32[]{:S(2)}, u32[]{:S(2)}) collective-permute-start(f32[24,128]{1,0:T(8,128)S(1)} %get-tuple-element.8.rest_0_), channel_id=1, source_target_pairs={{0,8},{8,16},{16,24},{24,0},{1,9},{9,17},{17,25},{25,1},{2,10},{10... | collective-permute-start | bytes 36872 | tf_op jit(solution)/shard_map/ppermute | solution.py:454
  38.2 0.2 collective-permute-done.3.rest_3_
  38.4 3.2 %collective-permute-done.2.rest_2_ = f32[24,128]{1,0:T(8,128)S(1)} collective-permute-done((f32[24,128]{1,0:T(8,128)S(1)}, f32[24,128]{1,0:T(8,128)S(1)}, u32[]{:S(2)}, u32[]{:S(2)}) %collective-permute-start.2) | collective-permute-done | bytes 12320 | tf_op jit(solution)/shard_map/ppermute | solution.py:454
  41.6 0.9 %collective-permute-done.1.rest_1_ = f32[24,128]{1,0:T(8,128)S(1)} collective-permute-done((f32[24,128]{1,0:T(8,128)S(1)}, f32[24,128]{1,0:T(8,128)S(1)}, u32[]{:S(2)}, u32[]{:S(2)}) %collective-permute-start.1) | collective-permute-done | bytes 12320 | tf_op jit(solution)/shard_map/ppermute | solution.py:454
  42.5 1.1 %finish.1 = f32[3,2,192,128]{3,2,1,0:T(8,128)} custom-call(s32[1]{0:T(128)} %bitcast.position, f32[2,24,5,8,128]{4,3,2,1,0:T(8,128)S(1)} %get-tuple-element.6.factors, f32[2,3,5,8,128]{4,3,2,1,0:T(8,128)S(1)} %get-tuple-element.7.tree, f32[3,2,192,128]{3,2,1,0:T(8,128)S(1)} %copy-done.1, f32[24,128]{1,0:T(8,128)S(1)} %get-tuple-element.8.rest_0_, ...), custom_call_target="tpu_custom_call" | custom-call | tf_op jit(solution)/shard_map/finish/pallas_call | solution.py:457
  (1 shorter events, 0.0 us)
Async XLA Ops:
  0.6 1.1 %copy-start = (f32[3,2,192,128]{3,2,1,0:T(8,128)S(1)}, f32[3,2,192,128]{3,2,1,0:T(8,128)}, u32[]{:S(2)}) copy-start(f32[3,2,192,128]{3,2,1,0:T(8,128)} %velocity.5) | copy-start | bytes 1769476
  17.9 0.7 %collective-permute-start = (f32[8,8,128]{2,1,0:T(8,128)S(1)}, f32[8,8,128]{2,1,0:T(8,128)S(1)}, u32[]{:S(2)}, u32[]{:S(2)}) collective-permute-start(f32[8,8,128]{2,1,0:T(8,128)S(1)} %slice.4), channel_id=1, source_target_pairs={{5,13},{13,5},{15,23},{23,15},{21,29},{29,21}} | collective-permute-start | bytes 98312 | tf_op jit(solution)/shard_map/ppermute | solution.py:417
  18.6 14.1 %copy-start.1 = (f32[3,2,192,128]{3,2,1,0:T(8,128)S(1)}, f32[3,2,192,128]{3,2,1,0:T(8,128)}, u32[]{:S(2)}) copy-start(f32[3,2,192,128]{3,2,1,0:T(8,128)} %velocity.5) | copy-start | bytes 1769476
  18.6 14.1 %copy-start.2 = (f32[3,2,192,128]{3,2,1,0:T(8,128)S(1)}, f32[3,2,192,128]{3,2,1,0:T(8,128)}, u32[]{:S(2)}) copy-start(f32[3,2,192,128]{3,2,1,0:T(8,128)} %tendency.1) | copy-start | bytes 1769476
  33.4 5.0 %collective-permute-start.3 = (f32[24,128]{1,0:T(8,128)S(1)}, f32[24,128]{1,0:T(8,128)S(1)}, u32[]{:S(2)}, u32[]{:S(2)}) collective-permute-start(f32[24,128]{1,0:T(8,128)S(1)} %get-tuple-element.8.rest_0_), channel_id=1, source_target_pairs={{0,24},{8,0},{16,8},{24,16},{1,25},{9,1},{17,9},{25,17},{2,26},{10... | collective-permute-start | bytes 36872 | tf_op jit(solution)/shard_map/ppermute | solution.py:454
  37.0 4.6 %collective-permute-start.2 = (f32[24,128]{1,0:T(8,128)S(1)}, f32[24,128]{1,0:T(8,128)S(1)}, u32[]{:S(2)}, u32[]{:S(2)}) collective-permute-start(f32[24,128]{1,0:T(8,128)S(1)} %get-tuple-element.8.rest_0_), channel_id=1, source_target_pairs={{0,16},{8,24},{16,0},{24,8},{1,17},{9,25},{17,1},{25,9},{2,18},{10... | collective-permute-start | bytes 36872 | tf_op jit(solution)/shard_map/ppermute | solution.py:454
  37.0 5.5 %collective-permute-start.1 = (f32[24,128]{1,0:T(8,128)S(1)}, f32[24,128]{1,0:T(8,128)S(1)}, u32[]{:S(2)}, u32[]{:S(2)}) collective-permute-start(f32[24,128]{1,0:T(8,128)S(1)} %get-tuple-element.8.rest_0_), channel_id=1, source_target_pairs={{0,8},{8,16},{16,24},{24,0},{1,9},{9,17},{17,25},{25,1},{2,10},{10... | collective-permute-start | bytes 36872 | tf_op jit(solution)/shard_map/ppermute | solution.py:454

commit v7 on v6

--- a/solution.py
+++ b/solution.py
@@ -119,13 +119,104 @@
             out[rank, at:, :] = jnp.zeros((depth - at, lanes), jnp.float32)
 
 
-def germano_kernel(nz_parts, width, rows, rank, parity, recv, swapped, out, vel, filt, ends, mag, part):
-    count, _, lanes = recv.shape
-    planes = 3 * width
+def outer_sides(rank, parity, count):
     outer = outer_ranks(count)
     even = parity[0] == 0
     bottom = rank[0] == jnp.where(even, outer[0], outer[1])
     top = rank[0] == jnp.where(even, outer[1], outer[0])
+    return bottom, top
+
+
+def edge_kernel(nz_parts, width, rows, rank, parity, recv, swapped, given, out, vel):
+    count, _, lanes = recv.shape
+    planes = 3 * width
+    nx = (count // nz_parts) * width
+    nz = nz_parts * lanes
+    bottom, top = outer_sides(rank, parity, count)
+
+    def rows_of(k, i):
+        first = i * rows
+        own = [recv[k, first + j : first + j + 1, :] for j in (0, 1, rows - 2, rows - 1)]
+        far = swapped[k, i : i + 1, :]
+        return (
+            jnp.where(bottom, far, own[2]),
+            jnp.where(bottom, own[0], own[3]),
+            jnp.where(bottom, own[1], far),
+        )
+
+    def roll_x(f, shift):
+        return pltpu.roll(f, shift % nx, 0)
+
+    def roll_z(f, shift):
+        return pltpu.roll(f, shift % nz, 1)
+
+    def smooth_x(f):
+        return (roll_x(f, 1) + roll_x(f, -1)) + 2.0 * f
+
+    def smooth(f):
+        f = smooth_x(f)
+        return (roll_z(f, 1) + roll_z(f, -1)) + 2.0 * f
+
+    def slopes(below, centre, above):
+        return strain_parts(
+            [roll_x(f, -1) - roll_x(f, 1) for f in centre],
+            [a - b for a, b in zip(above, below)],
+            [roll_z(f, -1) - roll_z(f, 1) for f in centre],
+        )
+
+    @pl.when(jnp.logical_or(bottom, top))
+    def _():
+        for k in range(count):
+            x0, zb = (k // nz_parts) * width, k % nz_parts
+            for i in range(planes):
+                c, x = divmod(i, width)
+                for j, row in enumerate(rows_of(k, i)):
+                    vel[j, c, x0 + x : x0 + x + 1, zb * lanes : (zb + 1) * lanes] = row
+        u = [[vel[j, c] for c in range(3)] for j in range(3)]
+        v = [[smooth(f) for f in row] for row in u]
+        strain = slopes(*u)
+        size = strain_size(strain)
+        mean_strain = slopes(*v)
+        mean_size = 0.25 * strain_size(mean_strain)
+        scaled = [0.0625 * f for f in v[1]]
+        pairs = [v[1][i] * scaled[j] for i, j in ((0, 0), (1, 1), (2, 2), (0, 1), (0, 2), (1, 2))]
+        leonard = [smooth(p) - q for p, q in zip(products(u[1]), pairs)]
+        model = [smooth(size * s) - mean_size * f for s, f in zip(strain, mean_strain)]
+        lm, mm = contracted(leonard, model)
+        coefficient = coefficient_of(
+            *(jnp.sum(f, axis=(0, 1), keepdims=True) for f in (lm, mm)), nx * nz
+        )
+        eddy = coefficient * size
+
+        def put(at):
+            for k in range(count):
+                x0, zb = (k // nz_parts) * width, k % nz_parts
+                for x in range(width):
+                    out[k, x, at : at + 1, :] = eddy[x0 + x : x0 + x + 1, zb * lanes : (zb + 1) * lanes]
+
+        pl.when(bottom)(lambda: put(0))
+        pl.when(top)(lambda: put(rows - 1))
+
+
+def contracted(leonard, model):
+    lm = mm = None
+    for i in range(6):
+        square = model[i] * model[i] if i < 3 else (0.5 * model[i]) * model[i]
+        product = leonard[i] * model[i]
+        lm = product if lm is None else lm + product
+        mm = square if mm is None else mm + square
+    return lm, mm
+
+
+def coefficient_of(plane_lm, plane_mm, cells):
+    scale = 1.0 / (256.0 * cells)
+    return jnp.maximum(plane_lm * scale / (plane_mm * scale + 1e-06), 0.0)
+
+
+def germano_kernel(nz_parts, width, rows, rank, parity, recv, out, vel, filt, ends, mag, part):
+    count, _, lanes = recv.shape
+    planes = 3 * width
+    _, top = outer_sides(rank, parity, count)
     nx = (count // nz_parts) * width
     nz = nz_parts * lanes
     blocks = range(nz_parts)
@@ -143,10 +234,8 @@
                 near = recv[k, slots : slots + 1, :]
                 slots += aligned(planes)
                 other = recv[k, slots : slots + 1, :]
-                far = swapped[k, i : i + 1, :]
-                below = jnp.where(bottom, far, jnp.where(top, other, near))
-                above = jnp.where(top, far, other)
-                for side, (edge, at) in enumerate(((below, lead - 1), (above, lead + rows))):
+                below = jnp.where(top, other, near)
+                for side, (edge, at) in enumerate(((below, lead - 1), (other, lead + rows))):
                     vel[c, x0 + x, zb, at : at + 1, :] = edge
                     ends[c, x0 + x, zb, side : side + 1, :] = edge
 
@@ -211,20 +300,15 @@
                 v[0] * scaled[2],
                 v[1] * scaled[2],
             )
-            lm = mm = None
-            for i in range(6):
-                leonard = smooth_x(lambda at: part[3 + i, at, zb], x) - pairs[i]
-                model = smooth_x(lambda at: part[9 + i, at, zb], x) - size * strain[i]
-                square = model * model if i < 3 else (0.5 * model) * model
-                lm = leonard * model if lm is None else lm + leonard * model
-                mm = square if mm is None else mm + square
+            leonard = [smooth_x(lambda at: part[3 + i, at, zb], x) - pairs[i] for i in range(6)]
+            model = [smooth_x(lambda at: part[9 + i, at, zb], x) - size * strain[i] for i in range(6)]
+            lm, mm = contracted(leonard, model)
             sum_lm = lm if sum_lm is None else sum_lm + lm
             sum_mm = mm if sum_mm is None else sum_mm + mm
 
-    def plane_mean(total):
-        return jnp.sum(total, axis=1, keepdims=True) * (1.0 / (256.0 * nx * nz))
-
-    coefficient = jnp.maximum(plane_mean(sum_lm) / (plane_mean(sum_mm) + 1e-06), 0.0)
+    coefficient = coefficient_of(
+        *(jnp.sum(total, axis=1, keepdims=True) for total in (sum_lm, sum_mm)), nx * nz
+    )
     for k in range(count):
         x0, zb = (k // nz_parts) * width, k % nz_parts
         for x in range(width):
@@ -416,10 +500,12 @@
     slot = lax.slice_in_dim(recv, planes * rows, planes * rows + aligned(planes), axis=1)
     swapped = lax.ppermute(slot, ("gy", "gx", "gz"), pairs)
     rank = lax.axis_index(("gx", "gz")).astype(jnp.int32).reshape(1)
-    eddy_chunks = pl.pallas_call(
+    chunk_shape = jax.ShapeDtypeStruct((count, width, rows, lanes), f32)
+    cells_here = nx * nz_parts * rows * lanes
+    provisional = pl.pallas_call(
         functools.partial(germano_kernel, nz_parts, width, rows),
-        out_shape=jax.ShapeDtypeStruct((count, width, rows, lanes), f32),
-        in_specs=in_smem(2) + in_vmem(2),
+        out_shape=chunk_shape,
+        in_specs=in_smem(2) + in_vmem(1),
         out_specs=pl.BlockSpec(memory_space=pltpu.VMEM),
         scratch_shapes=[
             pltpu.VMEM((3, nx, nz_parts, padded, lanes), f32),
@@ -429,8 +515,21 @@
             pltpu.VMEM((15, nx, nz_parts, rows, lanes), f32),
         ],
         compiler_params=params(),
+        cost_estimate=pl.CostEstimate(
+            flops=300 * cells_here, bytes_accessed=16 * cells_here, transcendentals=2 * cells_here
+        ),
         name="germano",
-    )(rank, parity, recv, swapped)
+    )(rank, parity, recv)
+    eddy_chunks = pl.pallas_call(
+        functools.partial(edge_kernel, nz_parts, width, rows),
+        out_shape=chunk_shape,
+        in_specs=in_smem(2) + in_vmem(3),
+        out_specs=pl.BlockSpec(memory_space=pltpu.VMEM),
+        scratch_shapes=[pltpu.VMEM((3, 3, nx, nz_parts * lanes), f32)],
+        input_output_aliases={4: 0},
+        compiler_params=params(),
+        name="edge",
+    )(rank, parity, recv, swapped, provisional)
     back = lax.all_to_all(eddy_chunks, ("gx", "gz"), split_axis=0, concat_axis=0, tiled=True)
 
     length = cells // SEGMENTS

time: 43.9 us -> 42.5 us (0.968)
  blocking collectives: 27.2 us -> 26.1 us
    all_to_all x1, blocking collectives: 11.1 us -> 10 us  [body(): lax.all_to_all(eddy_chunks, ('gx', 'gz'), split_axis=0, concat_axis=0, ti...]
  transfers between devices with their start and end apart: 4 -> 4, of which waited for: 3 -> 2; matrix products, arithmetic and copies ran while one was open for 0% -> 0% of each run, Pallas kernels for 0% -> 7%
where the time goes in v7:
time: 42.5 us; the launch traced here: 42.2 us
  blocking collectives  26.1 us (61%)
  starting transfers between devices  5.27 us (12%)
  Pallas kernels  4.95 us (12%)
  waiting for transfers between devices  4.08 us (10%)
  local copies, waits for them, and re-layouts  1.08 us (3%)
  between operations  0.71 us (2%)
    all_to_all x1, blocking collectives, body(): lax.all_to_all(chunks, ('gx', 'gz'), split_axis=0, concat_axis=0, tiled=T...  16.1 us
    all_to_all x1, blocking collectives, body(): lax.all_to_all(eddy_chunks, ('gx', 'gz'), split_axis=0, concat_axis=0, ti...  10 us
    ppermute x3, starting transfers between devices, body(): lax.ppermute(reduced, 'gy', [(i, (i + shift) % walls) for i in range(wall...  4.61 us
    ppermute x3, waiting for transfers between devices, body(): lax.ppermute(reduced, 'gy', [(i, (i + shift) % walls) for i in range(wall...  4.08 us
    pallas_call x1, Pallas kernels, body(): pl.pallas_call(functools.partial(germano_kernel, nz_parts, width, rows),...  3.04 us
    pallas_call x1, Pallas kernels, body(): pl.pallas_call(functools.partial(finish_kernel, walls), out_shape=jax.Sha...  1.13 us
    unnamed x6, local copies, waits for them, and re-layouts  1.07 us
  transfers between devices with their start and end apart: 4, of which 2 were waited for; matrix products, arithmetic and copies ran while one was open for 0% of the time, Pallas kernels for 7%

profile of v7, /device:TPU:0, one launch (start us, length us, event | category | flops | bytes accessed | tf_op | source)
XLA Modules:
  0.0 42.2 jit_solution(15785693929337736354)
XLA Ops:
  0.6 0.0 copy-start
  0.6 1.1 %copy-done = f32[3,2,192,128]{3,2,1,0:T(8,128)S(1)} copy-done((f32[3,2,192,128]{3,2,1,0:T(8,128)S(1)}, f32[3,2,192,128]{3,2,1,0:T(8,128)}, u32[]{:S(2)}) %copy-start) | copy-done | bytes 589848
  1.7 0.1 pack.1
  1.8 16.1 %all_to_all.10.recv = f32[8,160,128]{2,1,0:T(8,128)S(1)} all-to-all(f32[8,160,128]{2,1,0:T(8,128)S(1)} %pack.1), channel_id=1, replica_groups=mesh['gy'=4,'gx'=4,'gz'=2] {'gx','gz'}, dimensions={0} | all-to-all | bytes 1310720 | tf_op jit(solution)/shard_map/all_to_all | solution.py:495
  17.9 0.7 %collective-permute-start = (f32[8,8,128]{2,1,0:T(8,128)S(1)}, f32[8,8,128]{2,1,0:T(8,128)S(1)}, u32[]{:S(2)}, u32[]{:S(2)}) collective-permute-start(f32[8,8,128]{2,1,0:T(8,128)S(1)} %slice.4), channel_id=1, source_target_pairs={{5,13},{13,5},{15,23},{23,15},{21,29},{29,21}} | collective-permute-start | bytes 98312 | tf_op jit(solution)/shard_map/ppermute | solution.py:501
  18.6 3.0 %germano.1.given = f32[8,2,24,128]{3,2,1,0:T(8,128)S(1)} custom-call(s32[1]{0:T(128)} %bitcast.1.rank, s32[1]{0:T(128)S(6)} %rem.18.parity, f32[8,160,128]{2,1,0:T(8,128)S(1)} %all_to_all.10.recv), custom_call_target="tpu_custom_call" | custom-call | flops 14745600 | bytes 786432 | tf_op jit(solution)/shard_map/germano/pallas_call | solution.py:505
  21.6 0.0 copy-start.1
  21.6 0.0 copy-start.2
  21.6 0.0 collective-permute-done.swapped
  21.7 10.0 %all_to_all.11.back = f32[8,2,24,128]{3,2,1,0:T(8,128)S(1)} all-to-all(f32[8,2,24,128]{3,2,1,0:T(8,128)S(1)} %edge.1), channel_id=1, replica_groups=mesh['gy'=4,'gx'=4,'gz'=2] {'gx','gz'}, dimensions={0} | all-to-all | bytes 393216 | tf_op jit(solution)/shard_map/all_to_all | solution.py:533
  31.7 0.0 copy-done.1
  31.7 0.0 copy-done.2
  31.7 0.7 %sweep.1 = (f32[2,192,128]{2,1,0:T(8,128)}, f32[24,128]{1,0:T(8,128)S(1)}, f32[2,24,5,8,128]{4,3,2,1,0:T(8,128)S(1)}, f32[2,3,5,8,128]{4,3,2,1,0:T(8,128)S(1)}) custom-call(s32[1]{0:T(128)S(6)} %rem.18.parity, f32[8,2,24,128]{3,2,1,0:T(8,128)S(1)} %all_to_all.11.back, f32[3,2,192,128]{3,2,1,0:T(8,128)S(1)} %copy-done.1, f32[3,2,192,128]{3,2,1,0:T(8,128)S(1)} %copy-done.2), custom_call_target="tpu_custom_call" | custom-call | tf_op jit(solution)/shard_map/sweep/pallas_call | solution.py:538
  32.4 2.5 %collective-permute-start.3 = (f32[24,128]{1,0:T(8,128)S(1)}, f32[24,128]{1,0:T(8,128)S(1)}, u32[]{:S(2)}, u32[]{:S(2)}) collective-permute-start(f32[24,128]{1,0:T(8,128)S(1)} %get-tuple-element.8.rest_0_), channel_id=1, source_target_pairs={{0,24},{8,0},{16,8},{24,16},{1,25},{9,1},{17,9},{25,17},{2,26},{10... | collective-permute-start | bytes 36872 | tf_op jit(solution)/shard_map/ppermute | solution.py:553
  34.9 0.7 %collective-permute-start.2 = (f32[24,128]{1,0:T(8,128)S(1)}, f32[24,128]{1,0:T(8,128)S(1)}, u32[]{:S(2)}, u32[]{:S(2)}) collective-permute-start(f32[24,128]{1,0:T(8,128)S(1)} %get-tuple-element.8.rest_0_), channel_id=1, source_target_pairs={{0,16},{8,24},{16,0},{24,8},{1,17},{9,25},{17,1},{25,9},{2,18},{10... | collective-permute-start | bytes 36872 | tf_op jit(solution)/shard_map/ppermute | solution.py:553
  35.6 1.4 %collective-permute-start.1 = (f32[24,128]{1,0:T(8,128)S(1)}, f32[24,128]{1,0:T(8,128)S(1)}, u32[]{:S(2)}, u32[]{:S(2)}) collective-permute-start(f32[24,128]{1,0:T(8,128)S(1)} %get-tuple-element.8.rest_0_), channel_id=1, source_target_pairs={{0,8},{8,16},{16,24},{24,0},{1,9},{9,17},{17,25},{25,1},{2,10},{10... | collective-permute-start | bytes 36872 | tf_op jit(solution)/shard_map/ppermute | solution.py:553
  37.0 0.0 collective-permute-done.3.rest_3_
  37.0 2.5 %collective-permute-done.2.rest_2_ = f32[24,128]{1,0:T(8,128)S(1)} collective-permute-done((f32[24,128]{1,0:T(8,128)S(1)}, f32[24,128]{1,0:T(8,128)S(1)}, u32[]{:S(2)}, u32[]{:S(2)}) %collective-permute-start.2) | collective-permute-done | bytes 12320 | tf_op jit(solution)/shard_map/ppermute | solution.py:553
  39.5 1.6 %collective-permute-done.1.rest_1_ = f32[24,128]{1,0:T(8,128)S(1)} collective-permute-done((f32[24,128]{1,0:T(8,128)S(1)}, f32[24,128]{1,0:T(8,128)S(1)}, u32[]{:S(2)}, u32[]{:S(2)}) %collective-permute-start.1) | collective-permute-done | bytes 12320 | tf_op jit(solution)/shard_map/ppermute | solution.py:553
  41.1 1.1 %finish.1 = f32[3,2,192,128]{3,2,1,0:T(8,128)} custom-call(s32[1]{0:T(128)} %bitcast.position, f32[2,24,5,8,128]{4,3,2,1,0:T(8,128)S(1)} %get-tuple-element.6.factors, f32[2,3,5,8,128]{4,3,2,1,0:T(8,128)S(1)} %get-tuple-element.7.tree, f32[3,2,192,128]{3,2,1,0:T(8,128)S(1)} %copy-done.1, f32[24,128]{1,0:T(8,128)S(1)} %get-tuple-element.8.rest_0_, ...), custom_call_target="tpu_custom_call" | custom-call | tf_op jit(solution)/shard_map/finish/pallas_call | solution.py:556
  (2 shorter events, 0.0 us)
Async XLA Ops:
  0.6 1.1 %copy-start = (f32[3,2,192,128]{3,2,1,0:T(8,128)S(1)}, f32[3,2,192,128]{3,2,1,0:T(8,128)}, u32[]{:S(2)}) copy-start(f32[3,2,192,128]{3,2,1,0:T(8,128)} %velocity.5) | copy-start | bytes 1769476
  17.9 3.7 %collective-permute-start = (f32[8,8,128]{2,1,0:T(8,128)S(1)}, f32[8,8,128]{2,1,0:T(8,128)S(1)}, u32[]{:S(2)}, u32[]{:S(2)}) collective-permute-start(f32[8,8,128]{2,1,0:T(8,128)S(1)} %slice.4), channel_id=1, source_target_pairs={{5,13},{13,5},{15,23},{23,15},{21,29},{29,21}} | collective-permute-start | bytes 98312 | tf_op jit(solution)/shard_map/ppermute | solution.py:501
  21.6 10.1 %copy-start.1 = (f32[3,2,192,128]{3,2,1,0:T(8,128)S(1)}, f32[3,2,192,128]{3,2,1,0:T(8,128)}, u32[]{:S(2)}) copy-start(f32[3,2,192,128]{3,2,1,0:T(8,128)} %velocity.5) | copy-start | bytes 1769476
  21.6 10.1 %copy-start.2 = (f32[3,2,192,128]{3,2,1,0:T(8,128)S(1)}, f32[3,2,192,128]{3,2,1,0:T(8,128)}, u32[]{:S(2)}) copy-start(f32[3,2,192,128]{3,2,1,0:T(8,128)} %tendency.1) | copy-start | bytes 1769476
  32.4 4.6 %collective-permute-start.3 = (f32[24,128]{1,0:T(8,128)S(1)}, f32[24,128]{1,0:T(8,128)S(1)}, u32[]{:S(2)}, u32[]{:S(2)}) collective-permute-start(f32[24,128]{1,0:T(8,128)S(1)} %get-tuple-element.8.rest_0_), channel_id=1, source_target_pairs={{0,24},{8,0},{16,8},{24,16},{1,25},{9,1},{17,9},{25,17},{2,26},{10... | collective-permute-start | bytes 36872 | tf_op jit(solution)/shard_map/ppermute | solution.py:553
  34.9 4.6 %collective-permute-start.2 = (f32[24,128]{1,0:T(8,128)S(1)}, f32[24,128]{1,0:T(8,128)S(1)}, u32[]{:S(2)}, u32[]{:S(2)}) collective-permute-start(f32[24,128]{1,0:T(8,128)S(1)} %get-tuple-element.8.rest_0_), channel_id=1, source_target_pairs={{0,16},{8,24},{16,0},{24,8},{1,17},{9,25},{17,1},{25,9},{2,18},{10... | collective-permute-start | bytes 36872 | tf_op jit(solution)/shard_map/ppermute | solution.py:553
  35.6 5.5 %collective-permute-start.1 = (f32[24,128]{1,0:T(8,128)S(1)}, f32[24,128]{1,0:T(8,128)S(1)}, u32[]{:S(2)}, u32[]{:S(2)}) collective-permute-start(f32[24,128]{1,0:T(8,128)S(1)} %get-tuple-element.8.rest_0_), channel_id=1, source_target_pairs={{0,8},{8,16},{16,24},{24,0},{1,9},{9,17},{17,25},{25,1},{2,10},{10... | collective-permute-start | bytes 36872 | tf_op jit(solution)/shard_map/ppermute | solution.py:553

commit v8 on v7

--- a/solution.py
+++ b/solution.py
@@ -398,12 +398,18 @@
         reduced[i * width + x : i * width + x + 1, :] = visc[SEGMENTS - 1 :, :]
 
 
+def partner(i, step, count):
+    if count & (count - 1) == 0:
+        return i ^ step
+    return (i - step + count) % count
+
+
 def finish_kernel(devices, position, factors, tree, velocity, *rest):
     reduced, (out, gathered, fluxes) = rest[:devices], rest[devices:]
     width, length = factors.shape[:2]
     here = position[0]
-    for shift in range(devices):
-        gathered[lax.rem(here - shift + devices, devices)] = reduced[shift][...]
+    for step in range(devices):
+        gathered[partner(here, step, devices)] = reduced[step][...]
 
     def part(device, i):
         return gathered[device, i * width : (i + 1) * width, :]
@@ -550,8 +556,8 @@
     )(parity, back, velocity, tendency)
 
     others = [
-        lax.ppermute(reduced, "gy", [(i, (i + shift) % walls) for i in range(walls)])
-        for shift in range(1, walls)
+        lax.ppermute(reduced, "gy", [(partner(i, step, walls), i) for i in range(walls)])
+        for step in range(1, walls)
     ]
     new_velocity = pl.pallas_call(
         functools.partial(finish_kernel, walls),

time: 42.5 us -> 40.9 us (0.962)
  waiting for transfers between devices: 4.08 us -> 2.7 us
    ppermute x3, waiting for transfers between devices: 4.08 us -> 2.7 us  [body(): lax.ppermute(reduced, 'gy', [(partner(i, step, walls), i) for i in range(...]
where the time goes in v8:
time: 40.9 us; the launch traced here: 40.6 us
  blocking collectives  26.1 us (64%)
  starting transfers between devices  5.04 us (12%)
  Pallas kernels  4.95 us (12%)
  waiting for transfers between devices  2.7 us (7%)
  local copies, waits for them, and re-layouts  1.08 us (3%)
  between operations  0.71 us (2%)
    all_to_all x1, blocking collectives, body(): lax.all_to_all(chunks, ('gx', 'gz'), split_axis=0, concat_axis=0, tiled=T...  16.1 us
    all_to_all x1, blocking collectives, body(): lax.all_to_all(eddy_chunks, ('gx', 'gz'), split_axis=0, concat_axis=0, ti...  10 us
    ppermute x3, starting transfers between devices, body(): lax.ppermute(reduced, 'gy', [(partner(i, step, walls), i) for i in range(...  4.39 us
    pallas_call x1, Pallas kernels, body(): pl.pallas_call(functools.partial(germano_kernel, nz_parts, width, rows),...  3.04 us
    ppermute x3, waiting for transfers between devices, body(): lax.ppermute(reduced, 'gy', [(partner(i, step, walls), i) for i in range(...  2.7 us
    pallas_call x1, Pallas kernels, body(): pl.pallas_call(functools.partial(finish_kernel, walls), out_shape=jax.Sha...  1.13 us
    unnamed x6, local copies, waits for them, and re-layouts  1.07 us
  transfers between devices with their start and end apart: 4, of which 2 were waited for; matrix products, arithmetic and copies ran while one was open for 0% of the time, Pallas kernels for 7%

profile of v8, /device:TPU:0, one launch (start us, length us, event | category | flops | bytes accessed | tf_op | source)
XLA Modules:
  0.0 40.6 jit_solution(2585025628828732328)
XLA Ops:
  0.6 0.0 copy-start
  0.6 1.1 %copy-done = f32[3,2,192,128]{3,2,1,0:T(8,128)S(1)} copy-done((f32[3,2,192,128]{3,2,1,0:T(8,128)S(1)}, f32[3,2,192,128]{3,2,1,0:T(8,128)}, u32[]{:S(2)}) %copy-start) | copy-done | bytes 589848
  1.7 0.1 pack.1
  1.8 16.1 %all_to_all.10.recv = f32[8,160,128]{2,1,0:T(8,128)S(1)} all-to-all(f32[8,160,128]{2,1,0:T(8,128)S(1)} %pack.1), channel_id=1, replica_groups=mesh['gy'=4,'gx'=4,'gz'=2] {'gx','gz'}, dimensions={0} | all-to-all | bytes 1310720 | tf_op jit(solution)/shard_map/all_to_all | solution.py:501
  17.9 0.7 %collective-permute-start = (f32[8,8,128]{2,1,0:T(8,128)S(1)}, f32[8,8,128]{2,1,0:T(8,128)S(1)}, u32[]{:S(2)}, u32[]{:S(2)}) collective-permute-start(f32[8,8,128]{2,1,0:T(8,128)S(1)} %slice.4), channel_id=1, source_target_pairs={{5,13},{13,5},{15,23},{23,15},{21,29},{29,21}} | collective-permute-start | bytes 98312 | tf_op jit(solution)/shard_map/ppermute | solution.py:507
  18.6 3.0 %germano.1.given = f32[8,2,24,128]{3,2,1,0:T(8,128)S(1)} custom-call(s32[1]{0:T(128)} %bitcast.1.rank, s32[1]{0:T(128)S(6)} %rem.18.parity, f32[8,160,128]{2,1,0:T(8,128)S(1)} %all_to_all.10.recv), custom_call_target="tpu_custom_call" | custom-call | flops 14745600 | bytes 786432 | tf_op jit(solution)/shard_map/germano/pallas_call | solution.py:511
  21.6 0.0 copy-start.1
  21.6 0.0 copy-start.2
  21.6 0.0 collective-permute-done.swapped
  21.7 10.0 %all_to_all.11.back = f32[8,2,24,128]{3,2,1,0:T(8,128)S(1)} all-to-all(f32[8,2,24,128]{3,2,1,0:T(8,128)S(1)} %edge.1), channel_id=1, replica_groups=mesh['gy'=4,'gx'=4,'gz'=2] {'gx','gz'}, dimensions={0} | all-to-all | bytes 393216 | tf_op jit(solution)/shard_map/all_to_all | solution.py:539
  31.7 0.0 copy-done.1
  31.7 0.0 copy-done.2
  31.7 0.7 %sweep.1 = (f32[2,192,128]{2,1,0:T(8,128)}, f32[24,128]{1,0:T(8,128)S(1)}, f32[2,24,5,8,128]{4,3,2,1,0:T(8,128)S(1)}, f32[2,3,5,8,128]{4,3,2,1,0:T(8,128)S(1)}) custom-call(s32[1]{0:T(128)S(6)} %rem.18.parity, f32[8,2,24,128]{3,2,1,0:T(8,128)S(1)} %all_to_all.11.back, f32[3,2,192,128]{3,2,1,0:T(8,128)S(1)} %copy-done.1, f32[3,2,192,128]{3,2,1,0:T(8,128)S(1)} %copy-done.2), custom_call_target="tpu_custom_call" | custom-call | tf_op jit(solution)/shard_map/sweep/pallas_call | solution.py:544
  32.4 2.5 %collective-permute-start.3 = (f32[24,128]{1,0:T(8,128)S(1)}, f32[24,128]{1,0:T(8,128)S(1)}, u32[]{:S(2)}, u32[]{:S(2)}) collective-permute-start(f32[24,128]{1,0:T(8,128)S(1)} %get-tuple-element.8.rest_0_), channel_id=1, source_target_pairs={{24,0},{16,8},{8,16},{0,24},{25,1},{17,9},{9,17},{1,25},{26,2},{18... | collective-permute-start | bytes 36872 | tf_op jit(solution)/shard_map/ppermute | solution.py:559
  34.9 0.7 %collective-permute-start.2 = (f32[24,128]{1,0:T(8,128)S(1)}, f32[24,128]{1,0:T(8,128)S(1)}, u32[]{:S(2)}, u32[]{:S(2)}) collective-permute-start(f32[24,128]{1,0:T(8,128)S(1)} %get-tuple-element.8.rest_0_), channel_id=1, source_target_pairs={{16,0},{24,8},{0,16},{8,24},{17,1},{25,9},{1,17},{9,25},{18,2},{26... | collective-permute-start | bytes 36872 | tf_op jit(solution)/shard_map/ppermute | solution.py:559
  35.6 1.2 %collective-permute-start.1 = (f32[24,128]{1,0:T(8,128)S(1)}, f32[24,128]{1,0:T(8,128)S(1)}, u32[]{:S(2)}, u32[]{:S(2)}) collective-permute-start(f32[24,128]{1,0:T(8,128)S(1)} %get-tuple-element.8.rest_0_), channel_id=1, source_target_pairs={{8,0},{0,8},{24,16},{16,24},{9,1},{1,9},{25,17},{17,25},{10,2},{2,... | collective-permute-start | bytes 36872 | tf_op jit(solution)/shard_map/ppermute | solution.py:559
  36.8 1.2 %collective-permute-done.3.rest_3_ = f32[24,128]{1,0:T(8,128)S(1)} collective-permute-done((f32[24,128]{1,0:T(8,128)S(1)}, f32[24,128]{1,0:T(8,128)S(1)}, u32[]{:S(2)}, u32[]{:S(2)}) %collective-permute-start.3) | collective-permute-done | bytes 12320 | tf_op jit(solution)/shard_map/ppermute | solution.py:559
  38.0 1.5 %collective-permute-done.2.rest_2_ = f32[24,128]{1,0:T(8,128)S(1)} collective-permute-done((f32[24,128]{1,0:T(8,128)S(1)}, f32[24,128]{1,0:T(8,128)S(1)}, u32[]{:S(2)}, u32[]{:S(2)}) %collective-permute-start.2) | collective-permute-done | bytes 12320 | tf_op jit(solution)/shard_map/ppermute | solution.py:559
  39.5 0.0 collective-permute-done.1.rest_1_
  39.5 1.1 %finish.1 = f32[3,2,192,128]{3,2,1,0:T(8,128)} custom-call(s32[1]{0:T(128)} %bitcast.position, f32[2,24,5,8,128]{4,3,2,1,0:T(8,128)S(1)} %get-tuple-element.6.factors, f32[2,3,5,8,128]{4,3,2,1,0:T(8,128)S(1)} %get-tuple-element.7.tree, f32[3,2,192,128]{3,2,1,0:T(8,128)S(1)} %copy-done.1, f32[24,128]{1,0:T(8,128)S(1)} %get-tuple-element.8.rest_0_, ...), custom_call_target="tpu_custom_call" | custom-call | tf_op jit(solution)/shard_map/finish/pallas_call | solution.py:562
  (2 shorter events, 0.0 us)
Async XLA Ops:
  0.6 1.1 %copy-start = (f32[3,2,192,128]{3,2,1,0:T(8,128)S(1)}, f32[3,2,192,128]{3,2,1,0:T(8,128)}, u32[]{:S(2)}) copy-start(f32[3,2,192,128]{3,2,1,0:T(8,128)} %velocity.5) | copy-start | bytes 1769476
  17.9 3.7 %collective-permute-start = (f32[8,8,128]{2,1,0:T(8,128)S(1)}, f32[8,8,128]{2,1,0:T(8,128)S(1)}, u32[]{:S(2)}, u32[]{:S(2)}) collective-permute-start(f32[8,8,128]{2,1,0:T(8,128)S(1)} %slice.4), channel_id=1, source_target_pairs={{5,13},{13,5},{15,23},{23,15},{21,29},{29,21}} | collective-permute-start | bytes 98312 | tf_op jit(solution)/shard_map/ppermute | solution.py:507
  21.6 10.1 %copy-start.1 = (f32[3,2,192,128]{3,2,1,0:T(8,128)S(1)}, f32[3,2,192,128]{3,2,1,0:T(8,128)}, u32[]{:S(2)}) copy-start(f32[3,2,192,128]{3,2,1,0:T(8,128)} %velocity.5) | copy-start | bytes 1769476
  21.6 10.1 %copy-start.2 = (f32[3,2,192,128]{3,2,1,0:T(8,128)S(1)}, f32[3,2,192,128]{3,2,1,0:T(8,128)}, u32[]{:S(2)}) copy-start(f32[3,2,192,128]{3,2,1,0:T(8,128)} %tendency.1) | copy-start | bytes 1769476
  32.4 5.6 %collective-permute-start.3 = (f32[24,128]{1,0:T(8,128)S(1)}, f32[24,128]{1,0:T(8,128)S(1)}, u32[]{:S(2)}, u32[]{:S(2)}) collective-permute-start(f32[24,128]{1,0:T(8,128)S(1)} %get-tuple-element.8.rest_0_), channel_id=1, source_target_pairs={{24,0},{16,8},{8,16},{0,24},{25,1},{17,9},{9,17},{1,25},{26,2},{18... | collective-permute-start | bytes 36872 | tf_op jit(solution)/shard_map/ppermute | solution.py:559
  34.9 4.6 %collective-permute-start.2 = (f32[24,128]{1,0:T(8,128)S(1)}, f32[24,128]{1,0:T(8,128)S(1)}, u32[]{:S(2)}, u32[]{:S(2)}) collective-permute-start(f32[24,128]{1,0:T(8,128)S(1)} %get-tuple-element.8.rest_0_), channel_id=1, source_target_pairs={{16,0},{24,8},{0,16},{8,24},{17,1},{25,9},{1,17},{9,25},{18,2},{26... | collective-permute-start | bytes 36872 | tf_op jit(solution)/shard_map/ppermute | solution.py:559
  35.6 3.9 %collective-permute-start.1 = (f32[24,128]{1,0:T(8,128)S(1)}, f32[24,128]{1,0:T(8,128)S(1)}, u32[]{:S(2)}, u32[]{:S(2)}) collective-permute-start(f32[24,128]{1,0:T(8,128)S(1)} %get-tuple-element.8.rest_0_), channel_id=1, source_target_pairs={{8,0},{0,8},{24,16},{16,24},{9,1},{1,9},{25,17},{17,25},{10,2},{2,... | collective-permute-start | bytes 36872 | tf_op jit(solution)/shard_map/ppermute | solution.py:559

commit v9 on v8

--- a/solution.py
+++ b/solution.py
@@ -127,17 +127,20 @@
     return bottom, top
 
 
-def edge_kernel(nz_parts, width, rows, rank, parity, recv, swapped, given, out, vel):
+def edge_kernel(nz_parts, width, rows, walls, rank, position, recv, swapped, given, out, vel):
     count, _, lanes = recv.shape
     planes = 3 * width
     nx = (count // nz_parts) * width
     nz = nz_parts * lanes
-    bottom, top = outer_sides(rank, parity, count)
+    bottom, top = outer_sides(rank, [lax.rem(position[0], 2)], count)
+    at_wall = jnp.logical_or(
+        jnp.logical_and(bottom, position[0] == 0), jnp.logical_and(top, position[0] == walls - 1)
+    )
 
     def rows_of(k, i):
         first = i * rows
         own = [recv[k, first + j : first + j + 1, :] for j in (0, 1, rows - 2, rows - 1)]
-        far = swapped[k, i : i + 1, :]
+        far = jnp.where(at_wall, 0.0, swapped[k, i : i + 1, :])
         return (
             jnp.where(bottom, far, own[2]),
             jnp.where(bottom, own[0], own[3]),
@@ -500,9 +503,11 @@
     )(parity, velocity)
     recv = lax.all_to_all(chunks, ("gx", "gz"), split_axis=0, concat_axis=0, tiled=True)
     pairs = []
-    for wall in range(walls - 1):
-        outer = wall * count + outer_ranks(count)[1 - wall % 2]
-        pairs += [(outer, outer + count), (outer + count, outer)]
+    for r in range(count):
+        shift = 1 if r == outer_ranks(count)[0] else 0
+        for wall in range(walls):
+            beside = (wall + 1) % walls if (wall - shift) % 2 == 0 else (wall - 1) % walls
+            pairs.append((wall * count + r, beside * count + r))
     slot = lax.slice_in_dim(recv, planes * rows, planes * rows + aligned(planes), axis=1)
     swapped = lax.ppermute(slot, ("gy", "gx", "gz"), pairs)
     rank = lax.axis_index(("gx", "gz")).astype(jnp.int32).reshape(1)
@@ -527,7 +532,7 @@
         name="germano",
     )(rank, parity, recv)
     eddy_chunks = pl.pallas_call(
-        functools.partial(edge_kernel, nz_parts, width, rows),
+        functools.partial(edge_kernel, nz_parts, width, rows, walls),
         out_shape=chunk_shape,
         in_specs=in_smem(2) + in_vmem(3),
         out_specs=pl.BlockSpec(memory_space=pltpu.VMEM),
@@ -535,7 +540,7 @@
         input_output_aliases={4: 0},
         compiler_params=params(),
         name="edge",
-    )(rank, parity, recv, swapped, provisional)
+    )(rank, position, recv, swapped, provisional)
     back = lax.all_to_all(eddy_chunks, ("gx", "gz"), split_axis=0, concat_axis=0, tiled=True)
 
     length = cells // SEGMENTS

time: 40.9 us -> 40.7 us (level)
  starting transfers between devices: 5.04 us -> 5.96 us
  blocking collectives: 26.1 us -> 25.5 us
    ppermute x1, starting transfers between devices: 0.65 us -> 1.57 us  [body(): swapped = lax.ppermute(slot, ('gy', 'gx', 'gz'), pairs)]
    all_to_all x1, blocking collectives: 10 us -> 9.4 us  [body(): lax.all_to_all(eddy_chunks, ('gx', 'gz'), split_axis=0, concat_axis=0, ti...]
where the time goes in v9:
time: 40.7 us; the launch traced here: 40.5 us
  blocking collectives  25.5 us (63%)
  starting transfers between devices  5.96 us (15%)
  Pallas kernels  4.95 us (12%)
  waiting for transfers between devices  2.3 us (6%)
  local copies, waits for them, and re-layouts  1.08 us (3%)
  between operations  0.7 us (2%)
    all_to_all x1, blocking collectives, body(): lax.all_to_all(chunks, ('gx', 'gz'), split_axis=0, concat_axis=0, tiled=T...  16.1 us
    all_to_all x1, blocking collectives, body(): lax.all_to_all(eddy_chunks, ('gx', 'gz'), split_axis=0, concat_axis=0, ti...  9.4 us
    ppermute x3, starting transfers between devices, body(): lax.ppermute(reduced, 'gy', [(partner(i, step, walls), i) for i in range(...  4.39 us
    pallas_call x1, Pallas kernels, body(): pl.pallas_call(functools.partial(germano_kernel, nz_parts, width, rows),...  3.03 us
    ppermute x3, waiting for transfers between devices, body(): lax.ppermute(reduced, 'gy', [(partner(i, step, walls), i) for i in range(...  2.3 us
    ppermute x1, starting transfers between devices, body(): swapped = lax.ppermute(slot, ('gy', 'gx', 'gz'), pairs)  1.57 us
    pallas_call x1, Pallas kernels, body(): pl.pallas_call(functools.partial(finish_kernel, walls), out_shape=jax.Sha...  1.13 us
    unnamed x6, local copies, waits for them, and re-layouts  1.07 us
  transfers between devices with their start and end apart: 4, of which 2 were waited for; matrix products, arithmetic and copies ran while one was open for 0% of the time, Pallas kernels for 7%

profile of v9, /device:TPU:0, one launch (start us, length us, event | category | flops | bytes accessed | tf_op | source)
XLA Modules:
  0.0 40.5 jit_solution(2650387502413355174)
XLA Ops:
  0.6 0.0 copy-start
  0.6 1.1 %copy-done = f32[3,2,192,128]{3,2,1,0:T(8,128)S(1)} copy-done((f32[3,2,192,128]{3,2,1,0:T(8,128)S(1)}, f32[3,2,192,128]{3,2,1,0:T(8,128)}, u32[]{:S(2)}) %copy-start) | copy-done | bytes 589848
  1.7 0.1 pack.1
  1.8 16.1 %all_to_all.10.recv = f32[8,160,128]{2,1,0:T(8,128)S(1)} all-to-all(f32[8,160,128]{2,1,0:T(8,128)S(1)} %pack.1), channel_id=1, replica_groups=mesh['gy'=4,'gx'=4,'gz'=2] {'gx','gz'}, dimensions={0} | all-to-all | bytes 1310720 | tf_op jit(solution)/shard_map/all_to_all | solution.py:504
  17.9 1.6 %collective-permute-start = (f32[8,8,128]{2,1,0:T(8,128)S(1)}, f32[8,8,128]{2,1,0:T(8,128)S(1)}, u32[]{:S(2)}, u32[]{:S(2)}) collective-permute-start(f32[8,8,128]{2,1,0:T(8,128)S(1)} %slice.4), channel_id=1, source_target_pairs={{0,8},{8,0},{16,24},{24,16},{1,9},{9,1},{17,25},{25,17},{2,10},{10... | collective-permute-start | bytes 98312 | tf_op jit(solution)/shard_map/ppermute | solution.py:512
  19.5 3.0 %germano.1.given = f32[8,2,24,128]{3,2,1,0:T(8,128)S(1)} custom-call(s32[1]{0:T(128)} %bitcast.1.rank, s32[1]{0:T(128)S(6)} %rem.18.parity, f32[8,160,128]{2,1,0:T(8,128)S(1)} %all_to_all.10.recv), custom_call_target="tpu_custom_call" | custom-call | flops 14745600 | bytes 786432 | tf_op jit(solution)/shard_map/germano/pallas_call | solution.py:516
  22.5 0.0 copy-start.1
  22.5 0.0 copy-start.2
  22.5 0.0 collective-permute-done.swapped
  22.6 9.4 %all_to_all.11.back = f32[8,2,24,128]{3,2,1,0:T(8,128)S(1)} all-to-all(f32[8,2,24,128]{3,2,1,0:T(8,128)S(1)} %edge.1), channel_id=1, replica_groups=mesh['gy'=4,'gx'=4,'gz'=2] {'gx','gz'}, dimensions={0} | all-to-all | bytes 393216 | tf_op jit(solution)/shard_map/all_to_all | solution.py:544
  32.0 0.0 copy-done.1
  32.0 0.0 copy-done.2
  32.0 0.7 %sweep.1 = (f32[2,192,128]{2,1,0:T(8,128)}, f32[24,128]{1,0:T(8,128)S(1)}, f32[2,24,5,8,128]{4,3,2,1,0:T(8,128)S(1)}, f32[2,3,5,8,128]{4,3,2,1,0:T(8,128)S(1)}) custom-call(s32[1]{0:T(128)S(6)} %rem.18.parity, f32[8,2,24,128]{3,2,1,0:T(8,128)S(1)} %all_to_all.11.back, f32[3,2,192,128]{3,2,1,0:T(8,128)S(1)} %copy-done.1, f32[3,2,192,128]{3,2,1,0:T(8,128)S(1)} %copy-done.2), custom_call_target="tpu_custom_call" | custom-call | tf_op jit(solution)/shard_map/sweep/pallas_call | solution.py:549
  32.7 2.1 %collective-permute-start.3 = (f32[24,128]{1,0:T(8,128)S(1)}, f32[24,128]{1,0:T(8,128)S(1)}, u32[]{:S(2)}, u32[]{:S(2)}) collective-permute-start(f32[24,128]{1,0:T(8,128)S(1)} %get-tuple-element.8.rest_0_), channel_id=1, source_target_pairs={{24,0},{16,8},{8,16},{0,24},{25,1},{17,9},{9,17},{1,25},{26,2},{18... | collective-permute-start | bytes 36872 | tf_op jit(solution)/shard_map/ppermute | solution.py:564
  34.8 0.0 collective-permute-start.2
  34.8 2.3 %collective-permute-start.1 = (f32[24,128]{1,0:T(8,128)S(1)}, f32[24,128]{1,0:T(8,128)S(1)}, u32[]{:S(2)}, u32[]{:S(2)}) collective-permute-start(f32[24,128]{1,0:T(8,128)S(1)} %get-tuple-element.8.rest_0_), channel_id=1, source_target_pairs={{8,0},{0,8},{24,16},{16,24},{9,1},{1,9},{25,17},{17,25},{10,2},{2,... | collective-permute-start | bytes 36872 | tf_op jit(solution)/shard_map/ppermute | solution.py:564
  37.1 1.1 %collective-permute-done.3.rest_3_ = f32[24,128]{1,0:T(8,128)S(1)} collective-permute-done((f32[24,128]{1,0:T(8,128)S(1)}, f32[24,128]{1,0:T(8,128)S(1)}, u32[]{:S(2)}, u32[]{:S(2)}) %collective-permute-start.3) | collective-permute-done | bytes 12320 | tf_op jit(solution)/shard_map/ppermute | solution.py:564
  38.2 1.2 %collective-permute-done.2.rest_2_ = f32[24,128]{1,0:T(8,128)S(1)} collective-permute-done((f32[24,128]{1,0:T(8,128)S(1)}, f32[24,128]{1,0:T(8,128)S(1)}, u32[]{:S(2)}, u32[]{:S(2)}) %collective-permute-start.2) | collective-permute-done | bytes 12320 | tf_op jit(solution)/shard_map/ppermute | solution.py:564
  39.4 0.0 collective-permute-done.1.rest_1_
  39.4 1.1 %finish.1 = f32[3,2,192,128]{3,2,1,0:T(8,128)} custom-call(s32[1]{0:T(128)} %bitcast.position, f32[2,24,5,8,128]{4,3,2,1,0:T(8,128)S(1)} %get-tuple-element.6.factors, f32[2,3,5,8,128]{4,3,2,1,0:T(8,128)S(1)} %get-tuple-element.7.tree, f32[3,2,192,128]{3,2,1,0:T(8,128)S(1)} %copy-done.1, f32[24,128]{1,0:T(8,128)S(1)} %get-tuple-element.8.rest_0_, ...), custom_call_target="tpu_custom_call" | custom-call | tf_op jit(solution)/shard_map/finish/pallas_call | solution.py:567
  (2 shorter events, 0.0 us)
Async XLA Ops:
  0.6 1.1 %copy-start = (f32[3,2,192,128]{3,2,1,0:T(8,128)S(1)}, f32[3,2,192,128]{3,2,1,0:T(8,128)}, u32[]{:S(2)}) copy-start(f32[3,2,192,128]{3,2,1,0:T(8,128)} %velocity.5) | copy-start | bytes 1769476
  17.9 4.6 %collective-permute-start = (f32[8,8,128]{2,1,0:T(8,128)S(1)}, f32[8,8,128]{2,1,0:T(8,128)S(1)}, u32[]{:S(2)}, u32[]{:S(2)}) collective-permute-start(f32[8,8,128]{2,1,0:T(8,128)S(1)} %slice.4), channel_id=1, source_target_pairs={{0,8},{8,0},{16,24},{24,16},{1,9},{9,1},{17,25},{25,17},{2,10},{10... | collective-permute-start | bytes 98312 | tf_op jit(solution)/shard_map/ppermute | solution.py:512
  22.5 9.5 %copy-start.1 = (f32[3,2,192,128]{3,2,1,0:T(8,128)S(1)}, f32[3,2,192,128]{3,2,1,0:T(8,128)}, u32[]{:S(2)}) copy-start(f32[3,2,192,128]{3,2,1,0:T(8,128)} %velocity.5) | copy-start | bytes 1769476
  22.5 9.4 %copy-start.2 = (f32[3,2,192,128]{3,2,1,0:T(8,128)S(1)}, f32[3,2,192,128]{3,2,1,0:T(8,128)}, u32[]{:S(2)}) copy-start(f32[3,2,192,128]{3,2,1,0:T(8,128)} %tendency.1) | copy-start | bytes 1769476
  32.7 5.5 %collective-permute-start.3 = (f32[24,128]{1,0:T(8,128)S(1)}, f32[24,128]{1,0:T(8,128)S(1)}, u32[]{:S(2)}, u32[]{:S(2)}) collective-permute-start(f32[24,128]{1,0:T(8,128)S(1)} %get-tuple-element.8.rest_0_), channel_id=1, source_target_pairs={{24,0},{16,8},{8,16},{0,24},{25,1},{17,9},{9,17},{1,25},{26,2},{18... | collective-permute-start | bytes 36872 | tf_op jit(solution)/shard_map/ppermute | solution.py:564
  34.8 4.6 %collective-permute-start.2 = (f32[24,128]{1,0:T(8,128)S(1)}, f32[24,128]{1,0:T(8,128)S(1)}, u32[]{:S(2)}, u32[]{:S(2)}) collective-permute-start(f32[24,128]{1,0:T(8,128)S(1)} %get-tuple-element.8.rest_0_), channel_id=1, source_target_pairs={{16,0},{24,8},{0,16},{8,24},{17,1},{25,9},{1,17},{9,25},{18,2},{26... | collective-permute-start | bytes 36872 | tf_op jit(solution)/shard_map/ppermute | solution.py:564
  34.8 4.6 %collective-permute-start.1 = (f32[24,128]{1,0:T(8,128)S(1)}, f32[24,128]{1,0:T(8,128)S(1)}, u32[]{:S(2)}, u32[]{:S(2)}) collective-permute-start(f32[24,128]{1,0:T(8,128)S(1)} %get-tuple-element.8.rest_0_), channel_id=1, source_target_pairs={{8,0},{0,8},{24,16},{16,24},{9,1},{1,9},{25,17},{17,25},{10,2},{2,... | collective-permute-start | bytes 36872 | tf_op jit(solution)/shard_map/ppermute | solution.py:564

commit v10 on v9

--- a/solution.py
+++ b/solution.py
@@ -504,9 +504,12 @@
     recv = lax.all_to_all(chunks, ("gx", "gz"), split_axis=0, concat_axis=0, tiled=True)
     pairs = []
     for r in range(count):
-        shift = 1 if r == outer_ranks(count)[0] else 0
         for wall in range(walls):
-            beside = (wall + 1) % walls if (wall - shift) % 2 == 0 else (wall - 1) % walls
+            beside = wall
+            if r in outer_ranks(count):
+                up = (wall - outer_ranks(count)[::-1].index(r)) % 2 == 0
+                beside = wall + 1 if up else wall - 1
+            beside = beside if 0 <= beside < walls else wall
             pairs.append((wall * count + r, beside * count + r))
     slot = lax.slice_in_dim(recv, planes * rows, planes * rows + aligned(planes), axis=1)
     swapped = lax.ppermute(slot, ("gy", "gx", "gz"), pairs)

time: 40.7 us -> 40.9 us (level)
  starting transfers between devices: 5.96 us -> 5.04 us
  blocking collectives: 25.5 us -> 26.1 us
    ppermute x1, starting transfers between devices: 1.57 us -> 0.65 us  [body(): swapped = lax.ppermute(slot, ('gy', 'gx', 'gz'), pairs)]
    all_to_all x1, blocking collectives: 9.4 us -> 10 us  [body(): lax.all_to_all(eddy_chunks, ('gx', 'gz'), split_axis=0, concat_axis=0, ti...]
where the time goes in v10:
time: 40.9 us; the launch traced here: 40.6 us
  blocking collectives  26.1 us (64%)
  starting transfers between devices  5.04 us (12%)
  Pallas kernels  4.95 us (12%)
  waiting for transfers between devices  2.7 us (7%)
  local copies, waits for them, and re-layouts  1.08 us (3%)
  between operations  0.71 us (2%)
    all_to_all x1, blocking collectives, body(): lax.all_to_all(chunks, ('gx', 'gz'), split_axis=0, concat_axis=0, tiled=T...  16.1 us
    all_to_all x1, blocking collectives, body(): lax.all_to_all(eddy_chunks, ('gx', 'gz'), split_axis=0, concat_axis=0, ti...  10 us
    ppermute x3, starting transfers between devices, body(): lax.ppermute(reduced, 'gy', [(partner(i, step, walls), i) for i in range(...  4.39 us
    pallas_call x1, Pallas kernels, body(): pl.pallas_call(functools.partial(germano_kernel, nz_parts, width, rows),...  3.04 us
    ppermute x3, waiting for transfers between devices, body(): lax.ppermute(reduced, 'gy', [(partner(i, step, walls), i) for i in range(...  2.7 us
    pallas_call x1, Pallas kernels, body(): pl.pallas_call(functools.partial(finish_kernel, walls), out_shape=jax.Sha...  1.13 us
    unnamed x6, local copies, waits for them, and re-layouts  1.07 us
  transfers between devices with their start and end apart: 4, of which 2 were waited for; matrix products, arithmetic and copies ran while one was open for 0% of the time, Pallas kernels for 7%

profile of v10, /device:TPU:0, one launch (start us, length us, event | category | flops | bytes accessed | tf_op | source)
XLA Modules:
  0.0 40.6 jit_solution(5998505357986487407)
XLA Ops:
  0.6 0.0 copy-start
  0.6 1.1 %copy-done = f32[3,2,192,128]{3,2,1,0:T(8,128)S(1)} copy-done((f32[3,2,192,128]{3,2,1,0:T(8,128)S(1)}, f32[3,2,192,128]{3,2,1,0:T(8,128)}, u32[]{:S(2)}) %copy-start) | copy-done | bytes 589848
  1.7 0.1 pack.1
  1.8 16.1 %all_to_all.10.recv = f32[8,160,128]{2,1,0:T(8,128)S(1)} all-to-all(f32[8,160,128]{2,1,0:T(8,128)S(1)} %pack.1), channel_id=1, replica_groups=mesh['gy'=4,'gx'=4,'gz'=2] {'gx','gz'}, dimensions={0} | all-to-all | bytes 1310720 | tf_op jit(solution)/shard_map/all_to_all | solution.py:504
  17.9 0.7 %collective-permute-start = (f32[8,8,128]{2,1,0:T(8,128)S(1)}, f32[8,8,128]{2,1,0:T(8,128)S(1)}, u32[]{:S(2)}, u32[]{:S(2)}) collective-permute-start(f32[8,8,128]{2,1,0:T(8,128)S(1)} %slice.4), channel_id=1, source_target_pairs={{0,0},{8,8},{16,16},{24,24},{1,1},{9,9},{17,17},{25,25},{2,2},{10,... | collective-permute-start | bytes 98312 | tf_op jit(solution)/shard_map/ppermute | solution.py:515
  18.6 3.0 %germano.1.given = f32[8,2,24,128]{3,2,1,0:T(8,128)S(1)} custom-call(s32[1]{0:T(128)} %bitcast.1.rank, s32[1]{0:T(128)S(6)} %rem.18.parity, f32[8,160,128]{2,1,0:T(8,128)S(1)} %all_to_all.10.recv), custom_call_target="tpu_custom_call" | custom-call | flops 14745600 | bytes 786432 | tf_op jit(solution)/shard_map/germano/pallas_call | solution.py:519
  21.6 0.0 copy-start.1
  21.6 0.0 copy-start.2
  21.6 0.0 collective-permute-done.swapped
  21.7 10.0 %all_to_all.11.back = f32[8,2,24,128]{3,2,1,0:T(8,128)S(1)} all-to-all(f32[8,2,24,128]{3,2,1,0:T(8,128)S(1)} %edge.1), channel_id=1, replica_groups=mesh['gy'=4,'gx'=4,'gz'=2] {'gx','gz'}, dimensions={0} | all-to-all | bytes 393216 | tf_op jit(solution)/shard_map/all_to_all | solution.py:547
  31.7 0.0 copy-done.1
  31.7 0.0 copy-done.2
  31.7 0.7 %sweep.1 = (f32[2,192,128]{2,1,0:T(8,128)}, f32[24,128]{1,0:T(8,128)S(1)}, f32[2,24,5,8,128]{4,3,2,1,0:T(8,128)S(1)}, f32[2,3,5,8,128]{4,3,2,1,0:T(8,128)S(1)}) custom-call(s32[1]{0:T(128)S(6)} %rem.18.parity, f32[8,2,24,128]{3,2,1,0:T(8,128)S(1)} %all_to_all.11.back, f32[3,2,192,128]{3,2,1,0:T(8,128)S(1)} %copy-done.1, f32[3,2,192,128]{3,2,1,0:T(8,128)S(1)} %copy-done.2), custom_call_target="tpu_custom_call" | custom-call | tf_op jit(solution)/shard_map/sweep/pallas_call | solution.py:552
  32.4 2.5 %collective-permute-start.3 = (f32[24,128]{1,0:T(8,128)S(1)}, f32[24,128]{1,0:T(8,128)S(1)}, u32[]{:S(2)}, u32[]{:S(2)}) collective-permute-start(f32[24,128]{1,0:T(8,128)S(1)} %get-tuple-element.8.rest_0_), channel_id=1, source_target_pairs={{24,0},{16,8},{8,16},{0,24},{25,1},{17,9},{9,17},{1,25},{26,2},{18... | collective-permute-start | bytes 36872 | tf_op jit(solution)/shard_map/ppermute | solution.py:567
  34.9 0.7 %collective-permute-start.2 = (f32[24,128]{1,0:T(8,128)S(1)}, f32[24,128]{1,0:T(8,128)S(1)}, u32[]{:S(2)}, u32[]{:S(2)}) collective-permute-start(f32[24,128]{1,0:T(8,128)S(1)} %get-tuple-element.8.rest_0_), channel_id=1, source_target_pairs={{16,0},{24,8},{0,16},{8,24},{17,1},{25,9},{1,17},{9,25},{18,2},{26... | collective-permute-start | bytes 36872 | tf_op jit(solution)/shard_map/ppermute | solution.py:567
  35.6 1.2 %collective-permute-start.1 = (f32[24,128]{1,0:T(8,128)S(1)}, f32[24,128]{1,0:T(8,128)S(1)}, u32[]{:S(2)}, u32[]{:S(2)}) collective-permute-start(f32[24,128]{1,0:T(8,128)S(1)} %get-tuple-element.8.rest_0_), channel_id=1, source_target_pairs={{8,0},{0,8},{24,16},{16,24},{9,1},{1,9},{25,17},{17,25},{10,2},{2,... | collective-permute-start | bytes 36872 | tf_op jit(solution)/shard_map/ppermute | solution.py:567
  36.8 1.2 %collective-permute-done.3.rest_3_ = f32[24,128]{1,0:T(8,128)S(1)} collective-permute-done((f32[24,128]{1,0:T(8,128)S(1)}, f32[24,128]{1,0:T(8,128)S(1)}, u32[]{:S(2)}, u32[]{:S(2)}) %collective-permute-start.3) | collective-permute-done | bytes 12320 | tf_op jit(solution)/shard_map/ppermute | solution.py:567
  38.0 1.5 %collective-permute-done.2.rest_2_ = f32[24,128]{1,0:T(8,128)S(1)} collective-permute-done((f32[24,128]{1,0:T(8,128)S(1)}, f32[24,128]{1,0:T(8,128)S(1)}, u32[]{:S(2)}, u32[]{:S(2)}) %collective-permute-start.2) | collective-permute-done | bytes 12320 | tf_op jit(solution)/shard_map/ppermute | solution.py:567
  39.5 0.0 collective-permute-done.1.rest_1_
  39.5 1.1 %finish.1 = f32[3,2,192,128]{3,2,1,0:T(8,128)} custom-call(s32[1]{0:T(128)} %bitcast.position, f32[2,24,5,8,128]{4,3,2,1,0:T(8,128)S(1)} %get-tuple-element.6.factors, f32[2,3,5,8,128]{4,3,2,1,0:T(8,128)S(1)} %get-tuple-element.7.tree, f32[3,2,192,128]{3,2,1,0:T(8,128)S(1)} %copy-done.1, f32[24,128]{1,0:T(8,128)S(1)} %get-tuple-element.8.rest_0_, ...), custom_call_target="tpu_custom_call" | custom-call | tf_op jit(solution)/shard_map/finish/pallas_call | solution.py:570
  (2 shorter events, 0.0 us)
Async XLA Ops:
  0.6 1.1 %copy-start = (f32[3,2,192,128]{3,2,1,0:T(8,128)S(1)}, f32[3,2,192,128]{3,2,1,0:T(8,128)}, u32[]{:S(2)}) copy-start(f32[3,2,192,128]{3,2,1,0:T(8,128)} %velocity.5) | copy-start | bytes 1769476
  17.9 3.7 %collective-permute-start = (f32[8,8,128]{2,1,0:T(8,128)S(1)}, f32[8,8,128]{2,1,0:T(8,128)S(1)}, u32[]{:S(2)}, u32[]{:S(2)}) collective-permute-start(f32[8,8,128]{2,1,0:T(8,128)S(1)} %slice.4), channel_id=1, source_target_pairs={{0,0},{8,8},{16,16},{24,24},{1,1},{9,9},{17,17},{25,25},{2,2},{10,... | collective-permute-start | bytes 98312 | tf_op jit(solution)/shard_map/ppermute | solution.py:515
  21.6 10.1 %copy-start.1 = (f32[3,2,192,128]{3,2,1,0:T(8,128)S(1)}, f32[3,2,192,128]{3,2,1,0:T(8,128)}, u32[]{:S(2)}) copy-start(f32[3,2,192,128]{3,2,1,0:T(8,128)} %velocity.5) | copy-start | bytes 1769476
  21.6 10.1 %copy-start.2 = (f32[3,2,192,128]{3,2,1,0:T(8,128)S(1)}, f32[3,2,192,128]{3,2,1,0:T(8,128)}, u32[]{:S(2)}) copy-start(f32[3,2,192,128]{3,2,1,0:T(8,128)} %tendency.1) | copy-start | bytes 1769476
  32.4 5.6 %collective-permute-start.3 = (f32[24,128]{1,0:T(8,128)S(1)}, f32[24,128]{1,0:T(8,128)S(1)}, u32[]{:S(2)}, u32[]{:S(2)}) collective-permute-start(f32[24,128]{1,0:T(8,128)S(1)} %get-tuple-element.8.rest_0_), channel_id=1, source_target_pairs={{24,0},{16,8},{8,16},{0,24},{25,1},{17,9},{9,17},{1,25},{26,2},{18... | collective-permute-start | bytes 36872 | tf_op jit(solution)/shard_map/ppermute | solution.py:567
  34.9 4.6 %collective-permute-start.2 = (f32[24,128]{1,0:T(8,128)S(1)}, f32[24,128]{1,0:T(8,128)S(1)}, u32[]{:S(2)}, u32[]{:S(2)}) collective-permute-start(f32[24,128]{1,0:T(8,128)S(1)} %get-tuple-element.8.rest_0_), channel_id=1, source_target_pairs={{16,0},{24,8},{0,16},{8,24},{17,1},{25,9},{1,17},{9,25},{18,2},{26... | collective-permute-start | bytes 36872 | tf_op jit(solution)/shard_map/ppermute | solution.py:567
  35.6 3.9 %collective-permute-start.1 = (f32[24,128]{1,0:T(8,128)S(1)}, f32[24,128]{1,0:T(8,128)S(1)}, u32[]{:S(2)}, u32[]{:S(2)}) collective-permute-start(f32[24,128]{1,0:T(8,128)S(1)} %get-tuple-element.8.rest_0_), channel_id=1, source_target_pairs={{8,0},{0,8},{24,16},{16,24},{9,1},{1,9},{25,17},{17,25},{10,2},{2,... | collective-permute-start | bytes 36872 | tf_op jit(solution)/shard_map/ppermute | solution.py:567

commit v11 on v9

--- a/solution.py
+++ b/solution.py
@@ -68,6 +68,41 @@
     return [
         (0 if outer[parity] == rank else count - 1) if rank in outer else next(inner)
         for rank in range(count)
+    ]
+
+
+def swap_pairs(walls, count):
+    odd, even = outer_ranks(count)
+    spare = count - 5
+    partners = {}
+
+    def join(a, b):
+        partners[a], partners[b] = b, a
+
+    def join_walls(rank, first):
+        for wall in range(first, walls - 1, 2):
+            join((wall, rank), (wall + 1, rank))
+
+    join_walls(even, 0)
+    join_walls(odd, 1)
+    join_walls(spare, 1)
+    join((0, odd), (0, spare))
+    if walls % 2 == 0:
+        join((walls - 1, odd), (walls - 1, spare))
+    others = [r for r in range(count) if r not in (odd, even, spare)]
+    for core in range(2):
+        ranks = [r for r in others if r % 2 == core]
+        half = len(ranks) // 2
+        for wall in range(walls):
+            for a, b in zip(ranks[:half], ranks[half : 2 * half]):
+                join((wall, a), (wall, b))
+        for rank in ranks[2 * half :]:
+            join_walls(rank, 0)
+    return [
+        (wall * count + rank, to[0] * count + to[1])
+        for wall in range(walls)
+        for rank in range(count)
+        for to in [partners.get((wall, rank), (wall, rank))]
     ]
 
 
@@ -502,14 +537,8 @@
         name="pack",
     )(parity, velocity)
     recv = lax.all_to_all(chunks, ("gx", "gz"), split_axis=0, concat_axis=0, tiled=True)
-    pairs = []
-    for r in range(count):
-        shift = 1 if r == outer_ranks(count)[0] else 0
-        for wall in range(walls):
-            beside = (wall + 1) % walls if (wall - shift) % 2 == 0 else (wall - 1) % walls
-            pairs.append((wall * count + r, beside * count + r))
     slot = lax.slice_in_dim(recv, planes * rows, planes * rows + aligned(planes), axis=1)
-    swapped = lax.ppermute(slot, ("gy", "gx", "gz"), pairs)
+    swapped = lax.ppermute(slot, ("gy", "gx", "gz"), swap_pairs(walls, count))
     rank = lax.axis_index(("gx", "gz")).astype(jnp.int32).reshape(1)
     chunk_shape = jax.ShapeDtypeStruct((count, width, rows, lanes), f32)
     cells_here = nx * nz_parts * rows * lanes

time: 40.7 us -> 40.8 us (level)
  waiting for transfers between devices: 2.3 us -> 4.09 us
  starting transfers between devices: 5.96 us -> 4.95 us
  blocking collectives: 25.5 us -> 24.9 us
    ppermute x3, waiting for transfers between devices: 2.3 us -> 3.8 us  [body(): lax.ppermute(reduced, 'gy', [(partner(i, step, walls), i) for i in range(...]
    ppermute x1, starting transfers between devices: 1.57 us -> 0.56 us  [body(): swapped = lax.ppermute(slot, ('gy', 'gx', 'gz'), swap_pairs(walls, count))]
    all_to_all x1, blocking collectives: 9.4 us -> 8.75 us  [body(): lax.all_to_all(eddy_chunks, ('gx', 'gz'), split_axis=0, concat_axis=0, ti...]
  transfers between devices with their start and end apart: 4 -> 4, of which waited for: 2 -> 3; matrix products, arithmetic and copies ran while one was open for 0% -> 0% of each run, Pallas kernels for 7% -> 7%
where the time goes in v11:
time: 40.8 us; the launch traced here: 40.6 us
  blocking collectives  24.9 us (61%)
  starting transfers between devices  4.95 us (12%)
  Pallas kernels  4.93 us (12%)
  waiting for transfers between devices  4.09 us (10%)
  local copies, waits for them, and re-layouts  1.08 us (3%)
  between operations  0.68 us (2%)
    all_to_all x1, blocking collectives, body(): lax.all_to_all(chunks, ('gx', 'gz'), split_axis=0, concat_axis=0, tiled=T...  16.1 us
    all_to_all x1, blocking collectives, body(): lax.all_to_all(eddy_chunks, ('gx', 'gz'), split_axis=0, concat_axis=0, ti...  8.75 us
    ppermute x3, starting transfers between devices, body(): lax.ppermute(reduced, 'gy', [(partner(i, step, walls), i) for i in range(...  4.39 us
    ppermute x3, waiting for transfers between devices, body(): lax.ppermute(reduced, 'gy', [(partner(i, step, walls), i) for i in range(...  3.8 us
    pallas_call x1, Pallas kernels, body(): pl.pallas_call(functools.partial(germano_kernel, nz_parts, width, rows),...  3.03 us
    pallas_call x1, Pallas kernels, body(): pl.pallas_call(functools.partial(finish_kernel, walls), out_shape=jax.Sha...  1.13 us
    unnamed x6, local copies, waits for them, and re-layouts  1.07 us
  transfers between devices with their start and end apart: 4, of which 3 were waited for; matrix products, arithmetic and copies ran while one was open for 0% of the time, Pallas kernels for 7%

profile of v11, /device:TPU:0, one launch (start us, length us, event | category | flops | bytes accessed | tf_op | source)
XLA Modules:
  0.0 40.6 jit_solution(5000121306483790788)
XLA Ops:
  0.6 0.0 copy-start
  0.6 1.1 %copy-done = f32[3,2,192,128]{3,2,1,0:T(8,128)S(1)} copy-done((f32[3,2,192,128]{3,2,1,0:T(8,128)S(1)}, f32[3,2,192,128]{3,2,1,0:T(8,128)}, u32[]{:S(2)}) %copy-start) | copy-done | bytes 589848
  1.7 0.1 pack.1
  1.8 16.1 %all_to_all.10.recv = f32[8,160,128]{2,1,0:T(8,128)S(1)} all-to-all(f32[8,160,128]{2,1,0:T(8,128)S(1)} %pack.1), channel_id=1, replica_groups=mesh['gy'=4,'gx'=4,'gz'=2] {'gx','gz'}, dimensions={0} | all-to-all | bytes 1310720 | tf_op jit(solution)/shard_map/all_to_all | solution.py:539
  17.9 0.6 %collective-permute-start = (f32[8,8,128]{2,1,0:T(8,128)S(1)}, f32[8,8,128]{2,1,0:T(8,128)S(1)}, u32[]{:S(2)}, u32[]{:S(2)}) collective-permute-start(f32[8,8,128]{2,1,0:T(8,128)S(1)} %slice.4), channel_id=1, source_target_pairs={{0,4},{1,9},{2,6},{3,7},{4,0},{5,13},{6,2},{7,3},{8,12},{9,1},{10,... | collective-permute-start | bytes 98312 | tf_op jit(solution)/shard_map/ppermute | solution.py:541
  18.5 3.0 %germano.1.given = f32[8,2,24,128]{3,2,1,0:T(8,128)S(1)} custom-call(s32[1]{0:T(128)} %bitcast.1.rank, s32[1]{0:T(128)S(6)} %rem.18.parity, f32[8,160,128]{2,1,0:T(8,128)S(1)} %all_to_all.10.recv), custom_call_target="tpu_custom_call" | custom-call | flops 14745600 | bytes 786432 | tf_op jit(solution)/shard_map/germano/pallas_call | solution.py:545
  21.5 0.0 copy-start.1
  21.5 0.0 copy-start.2
  21.5 0.3 collective-permute-done.swapped
  21.8 8.8 %all_to_all.11.back = f32[8,2,24,128]{3,2,1,0:T(8,128)S(1)} all-to-all(f32[8,2,24,128]{3,2,1,0:T(8,128)S(1)} %edge.1), channel_id=1, replica_groups=mesh['gy'=4,'gx'=4,'gz'=2] {'gx','gz'}, dimensions={0} | all-to-all | bytes 393216 | tf_op jit(solution)/shard_map/all_to_all | solution.py:573
  30.6 0.0 copy-done.1
  30.6 0.0 copy-done.2
  30.6 0.7 %sweep.1 = (f32[2,192,128]{2,1,0:T(8,128)}, f32[24,128]{1,0:T(8,128)S(1)}, f32[2,24,5,8,128]{4,3,2,1,0:T(8,128)S(1)}, f32[2,3,5,8,128]{4,3,2,1,0:T(8,128)S(1)}) custom-call(s32[1]{0:T(128)S(6)} %rem.18.parity, f32[8,2,24,128]{3,2,1,0:T(8,128)S(1)} %all_to_all.11.back, f32[3,2,192,128]{3,2,1,0:T(8,128)S(1)} %copy-done.1, f32[3,2,192,128]{3,2,1,0:T(8,128)S(1)} %copy-done.2), custom_call_target="tpu_custom_call" | custom-call | tf_op jit(solution)/shard_map/sweep/pallas_call | solution.py:578
  31.3 3.6 %collective-permute-start.3 = (f32[24,128]{1,0:T(8,128)S(1)}, f32[24,128]{1,0:T(8,128)S(1)}, u32[]{:S(2)}, u32[]{:S(2)}) collective-permute-start(f32[24,128]{1,0:T(8,128)S(1)} %get-tuple-element.8.rest_0_), channel_id=1, source_target_pairs={{24,0},{16,8},{8,16},{0,24},{25,1},{17,9},{9,17},{1,25},{26,2},{18... | collective-permute-start | bytes 36872 | tf_op jit(solution)/shard_map/ppermute | solution.py:593
  34.9 0.0 collective-permute-start.2
  34.9 0.8 %collective-permute-start.1 = (f32[24,128]{1,0:T(8,128)S(1)}, f32[24,128]{1,0:T(8,128)S(1)}, u32[]{:S(2)}, u32[]{:S(2)}) collective-permute-start(f32[24,128]{1,0:T(8,128)S(1)} %get-tuple-element.8.rest_0_), channel_id=1, source_target_pairs={{8,0},{0,8},{24,16},{16,24},{9,1},{1,9},{25,17},{17,25},{10,2},{2,... | collective-permute-start | bytes 36872 | tf_op jit(solution)/shard_map/ppermute | solution.py:593
  35.7 1.3 %collective-permute-done.3.rest_3_ = f32[24,128]{1,0:T(8,128)S(1)} collective-permute-done((f32[24,128]{1,0:T(8,128)S(1)}, f32[24,128]{1,0:T(8,128)S(1)}, u32[]{:S(2)}, u32[]{:S(2)}) %collective-permute-start.3) | collective-permute-done | bytes 12320 | tf_op jit(solution)/shard_map/ppermute | solution.py:593
  37.0 2.5 %collective-permute-done.2.rest_2_ = f32[24,128]{1,0:T(8,128)S(1)} collective-permute-done((f32[24,128]{1,0:T(8,128)S(1)}, f32[24,128]{1,0:T(8,128)S(1)}, u32[]{:S(2)}, u32[]{:S(2)}) %collective-permute-start.2) | collective-permute-done | bytes 12320 | tf_op jit(solution)/shard_map/ppermute | solution.py:593
  39.5 0.0 collective-permute-done.1.rest_1_
  39.5 1.1 %finish.1 = f32[3,2,192,128]{3,2,1,0:T(8,128)} custom-call(s32[1]{0:T(128)} %bitcast.position, f32[2,24,5,8,128]{4,3,2,1,0:T(8,128)S(1)} %get-tuple-element.6.factors, f32[2,3,5,8,128]{4,3,2,1,0:T(8,128)S(1)} %get-tuple-element.7.tree, f32[3,2,192,128]{3,2,1,0:T(8,128)S(1)} %copy-done.1, f32[24,128]{1,0:T(8,128)S(1)} %get-tuple-element.8.rest_0_, ...), custom_call_target="tpu_custom_call" | custom-call | tf_op jit(solution)/shard_map/finish/pallas_call | solution.py:596
  (2 shorter events, 0.0 us)
Async XLA Ops:
  0.6 1.1 %copy-start = (f32[3,2,192,128]{3,2,1,0:T(8,128)S(1)}, f32[3,2,192,128]{3,2,1,0:T(8,128)}, u32[]{:S(2)}) copy-start(f32[3,2,192,128]{3,2,1,0:T(8,128)} %velocity.5) | copy-start | bytes 1769476
  17.9 3.9 %collective-permute-start = (f32[8,8,128]{2,1,0:T(8,128)S(1)}, f32[8,8,128]{2,1,0:T(8,128)S(1)}, u32[]{:S(2)}, u32[]{:S(2)}) collective-permute-start(f32[8,8,128]{2,1,0:T(8,128)S(1)} %slice.4), channel_id=1, source_target_pairs={{0,4},{1,9},{2,6},{3,7},{4,0},{5,13},{6,2},{7,3},{8,12},{9,1},{10,... | collective-permute-start | bytes 98312 | tf_op jit(solution)/shard_map/ppermute | solution.py:541
  21.5 9.1 %copy-start.1 = (f32[3,2,192,128]{3,2,1,0:T(8,128)S(1)}, f32[3,2,192,128]{3,2,1,0:T(8,128)}, u32[]{:S(2)}) copy-start(f32[3,2,192,128]{3,2,1,0:T(8,128)} %velocity.5) | copy-start | bytes 1769476
  21.5 9.1 %copy-start.2 = (f32[3,2,192,128]{3,2,1,0:T(8,128)S(1)}, f32[3,2,192,128]{3,2,1,0:T(8,128)}, u32[]{:S(2)}) copy-start(f32[3,2,192,128]{3,2,1,0:T(8,128)} %tendency.1) | copy-start | bytes 1769476
  31.3 5.7 %collective-permute-start.3 = (f32[24,128]{1,0:T(8,128)S(1)}, f32[24,128]{1,0:T(8,128)S(1)}, u32[]{:S(2)}, u32[]{:S(2)}) collective-permute-start(f32[24,128]{1,0:T(8,128)S(1)} %get-tuple-element.8.rest_0_), channel_id=1, source_target_pairs={{24,0},{16,8},{8,16},{0,24},{25,1},{17,9},{9,17},{1,25},{26,2},{18... | collective-permute-start | bytes 36872 | tf_op jit(solution)/shard_map/ppermute | solution.py:593
  34.9 4.6 %collective-permute-start.2 = (f32[24,128]{1,0:T(8,128)S(1)}, f32[24,128]{1,0:T(8,128)S(1)}, u32[]{:S(2)}, u32[]{:S(2)}) collective-permute-start(f32[24,128]{1,0:T(8,128)S(1)} %get-tuple-element.8.rest_0_), channel_id=1, source_target_pairs={{16,0},{24,8},{0,16},{8,24},{17,1},{25,9},{1,17},{9,25},{18,2},{26... | collective-permute-start | bytes 36872 | tf_op jit(solution)/shard_map/ppermute | solution.py:593
  34.9 4.6 %collective-permute-start.1 = (f32[24,128]{1,0:T(8,128)S(1)}, f32[24,128]{1,0:T(8,128)S(1)}, u32[]{:S(2)}, u32[]{:S(2)}) collective-permute-start(f32[24,128]{1,0:T(8,128)S(1)} %get-tuple-element.8.rest_0_), channel_id=1, source_target_pairs={{8,0},{0,8},{24,16},{16,24},{9,1},{1,9},{25,17},{17,25},{10,2},{2,... | collective-permute-start | bytes 36872 | tf_op jit(solution)/shard_map/ppermute | solution.py:593

commit v12 on v11

--- a/solution.py
+++ b/solution.py
@@ -353,7 +353,7 @@
             out[k, x] = coefficient * mag[x0 + x, zb]
 
 
-def sweep_kernel(parity, back, velocity, tendency, eddy, reduced, factors, tree):
+def sweep_kernel(parity, back, velocity, tendency, eddy_out, reduced, factors, tree, eddy, sent):
     count, width, rows, _ = back.shape
     length = count * rows // SEGMENTS
 
@@ -362,6 +362,8 @@
             eddy[x, place * rows : (place + 1) * rows, :] = back[rank, x]
 
     by_parity(parity, count, fill)
+    write = pltpu.make_async_copy(eddy, eddy_out, sent)
+    write.start()
 
     def row(ref, index, j):
         return ref[(*index, pl.ds(j, SEGMENTS, stride=length), slice(None))]
@@ -434,6 +436,7 @@
             reduced[i * width + x : i * width + x + 1, :] = v[0:1, :]
         i = len(rows_out)
         reduced[i * width + x : i * width + x + 1, :] = visc[SEGMENTS - 1 :, :]
+    write.wait()
 
 
 def partner(i, step, count):
@@ -443,7 +446,7 @@
 
 
 def finish_kernel(devices, position, factors, tree, velocity, *rest):
-    reduced, (out, gathered, fluxes) = rest[:devices], rest[devices:]
+    reduced, (result, gathered, fluxes, out, sent) = rest[:devices], rest[devices:]
     width, length = factors.shape[:2]
     here = position[0]
     for step in range(devices):
@@ -484,8 +487,9 @@
 
     sublane = lax.broadcasted_iota(jnp.int32, (SEGMENTS, LANES), 0)
     levels = tree.shape[1]
-    for x in range(width):
-        for c in range(3):
+    writes = []
+    for c in range(3):
+        for x in range(width):
             r = c * width + x
             left = jnp.broadcast_to(fluxes[here, r : r + 1, :], (SEGMENTS, LANES))
             right = -jnp.broadcast_to(fluxes[here + 1, r : r + 1, :], (SEGMENTS, LANES))
@@ -500,10 +504,18 @@
                 value = (factors[x, j, c] + factors[x, j, 3] * left) + factors[x, j, 4] * value
                 rows = pl.ds(j, SEGMENTS, stride=length)
                 out[c, x, rows, :] = value - velocity[c, x, rows, :]
+            writes.append(pltpu.make_async_copy(out.at[c, x], result.at[c, x], sent.at[r]))
+            writes[-1].start()
+    for write in writes:
+        write.wait()
 
 
 def in_vmem(count):
     return [pl.BlockSpec(memory_space=pltpu.VMEM)] * count
+
+
+def in_hbm(count):
+    return [pl.BlockSpec(memory_space=pltpu.HBM)] * count
 
 
 def in_smem(count):
@@ -584,7 +596,8 @@
             jax.ShapeDtypeStruct((width, levels, 5, SEGMENTS, lanes), f32),
         ),
         in_specs=in_smem(1) + in_vmem(3),
-        out_specs=tuple(in_vmem(4)),
+        out_specs=tuple(in_hbm(1) + in_vmem(3)),
+        scratch_shapes=[pltpu.VMEM((width, cells, lanes), f32), pltpu.SemaphoreType.DMA],
         compiler_params=params(),
         name="sweep",
     )(parity, back, velocity, tendency)
@@ -597,10 +610,12 @@
         functools.partial(finish_kernel, walls),
         out_shape=jax.ShapeDtypeStruct(velocity.shape, f32),
         in_specs=in_smem(1) + in_vmem(3 + walls),
-        out_specs=pl.BlockSpec(memory_space=pltpu.VMEM),
+        out_specs=in_hbm(1)[0],
         scratch_shapes=[
             pltpu.VMEM((walls, packed, lanes), f32),
             pltpu.VMEM((walls + 1, aligned(3 * width), lanes), f32),
+            pltpu.VMEM(velocity.shape, f32),
+            pltpu.SemaphoreType.DMA((planes,)),
         ],
         compiler_params=params(),
         name="finish",

time: 40.8 us -> 40.9 us (level)
  no operation moved by 1% of the time
where the time goes in v12:
time: 40.9 us; the launch traced here: 40.6 us
  blocking collectives  24.9 us (61%)
  starting transfers between devices  5.01 us (12%)
  Pallas kernels  4.86 us (12%)
  waiting for transfers between devices  4.09 us (10%)
  local copies, waits for them, and re-layouts  1.08 us (3%)
  between operations  0.69 us (2%)
    all_to_all x1, blocking collectives, body(): lax.all_to_all(chunks, ('gx', 'gz'), split_axis=0, concat_axis=0, tiled=T...  16.1 us
    all_to_all x1, blocking collectives, body(): lax.all_to_all(eddy_chunks, ('gx', 'gz'), split_axis=0, concat_axis=0, ti...  8.75 us
    ppermute x3, starting transfers between devices, body(): lax.ppermute(reduced, 'gy', [(partner(i, step, walls), i) for i in range(...  4.45 us
    ppermute x3, waiting for transfers between devices, body(): lax.ppermute(reduced, 'gy', [(partner(i, step, walls), i) for i in range(...  3.8 us
    pallas_call x1, Pallas kernels, body(): pl.pallas_call(functools.partial(germano_kernel, nz_parts, width, rows),...  3.03 us
    unnamed x6, local copies, waits for them, and re-layouts  1.07 us
    pallas_call x1, Pallas kernels, body(): pl.pallas_call(functools.partial(finish_kernel, walls), out_shape=jax.Sha...  1.05 us
  transfers between devices with their start and end apart: 4, of which 3 were waited for; matrix products, arithmetic and copies ran while one was open for 0% of the time, Pallas kernels for 7%

profile of v12, /device:TPU:0, one launch (start us, length us, event | category | flops | bytes accessed | tf_op | source)
XLA Modules:
  0.0 40.6 jit_solution(8879844944392720878)
XLA Ops:
  0.6 0.0 copy-start
  0.6 1.1 %copy-done = f32[3,2,192,128]{3,2,1,0:T(8,128)S(1)} copy-done((f32[3,2,192,128]{3,2,1,0:T(8,128)S(1)}, f32[3,2,192,128]{3,2,1,0:T(8,128)}, u32[]{:S(2)}) %copy-start) | copy-done | bytes 589848
  1.7 0.1 pack.1
  1.8 16.1 %all_to_all.10.recv = f32[8,160,128]{2,1,0:T(8,128)S(1)} all-to-all(f32[8,160,128]{2,1,0:T(8,128)S(1)} %pack.1), channel_id=1, replica_groups=mesh['gy'=4,'gx'=4,'gz'=2] {'gx','gz'}, dimensions={0} | all-to-all | bytes 1310720 | tf_op jit(solution)/shard_map/all_to_all | solution.py:551
  17.9 0.6 %collective-permute-start = (f32[8,8,128]{2,1,0:T(8,128)S(1)}, f32[8,8,128]{2,1,0:T(8,128)S(1)}, u32[]{:S(2)}, u32[]{:S(2)}) collective-permute-start(f32[8,8,128]{2,1,0:T(8,128)S(1)} %slice.4), channel_id=1, source_target_pairs={{0,4},{1,9},{2,6},{3,7},{4,0},{5,13},{6,2},{7,3},{8,12},{9,1},{10,... | collective-permute-start | bytes 98312 | tf_op jit(solution)/shard_map/ppermute | solution.py:553
  18.5 3.0 %germano.1.given = f32[8,2,24,128]{3,2,1,0:T(8,128)S(1)} custom-call(s32[1]{0:T(128)} %bitcast.1.rank, s32[1]{0:T(128)S(6)} %rem.18.parity, f32[8,160,128]{2,1,0:T(8,128)S(1)} %all_to_all.10.recv), custom_call_target="tpu_custom_call" | custom-call | flops 14745600 | bytes 786432 | tf_op jit(solution)/shard_map/germano/pallas_call | solution.py:557
  21.5 0.0 copy-start.1
  21.5 0.0 copy-start.2
  21.5 0.3 collective-permute-done.swapped
  21.8 8.8 %all_to_all.11.back = f32[8,2,24,128]{3,2,1,0:T(8,128)S(1)} all-to-all(f32[8,2,24,128]{3,2,1,0:T(8,128)S(1)} %edge.1), channel_id=1, replica_groups=mesh['gy'=4,'gx'=4,'gz'=2] {'gx','gz'}, dimensions={0} | all-to-all | bytes 393216 | tf_op jit(solution)/shard_map/all_to_all | solution.py:585
  30.6 0.0 copy-done.1
  30.6 0.0 copy-done.2
  30.6 0.7 %sweep.1 = (f32[2,192,128]{2,1,0:T(8,128)}, f32[24,128]{1,0:T(8,128)S(1)}, f32[2,24,5,8,128]{4,3,2,1,0:T(8,128)S(1)}, f32[2,3,5,8,128]{4,3,2,1,0:T(8,128)S(1)}) custom-call(s32[1]{0:T(128)S(6)} %rem.18.parity, f32[8,2,24,128]{3,2,1,0:T(8,128)S(1)} %all_to_all.11.back, f32[3,2,192,128]{3,2,1,0:T(8,128)S(1)} %copy-done.1, f32[3,2,192,128]{3,2,1,0:T(8,128)S(1)} %copy-done.2), custom_call_target="tpu_custom_call" | custom-call | tf_op jit(solution)/shard_map/sweep/pallas_call | solution.py:590
  31.3 3.7 %collective-permute-start.3 = (f32[24,128]{1,0:T(8,128)S(1)}, f32[24,128]{1,0:T(8,128)S(1)}, u32[]{:S(2)}, u32[]{:S(2)}) collective-permute-start(f32[24,128]{1,0:T(8,128)S(1)} %get-tuple-element.8.rest_0_), channel_id=1, source_target_pairs={{24,0},{16,8},{8,16},{0,24},{25,1},{17,9},{9,17},{1,25},{26,2},{18... | collective-permute-start | bytes 36872 | tf_op jit(solution)/shard_map/ppermute | solution.py:606
  35.0 0.0 collective-permute-start.2
  35.0 0.8 %collective-permute-start.1 = (f32[24,128]{1,0:T(8,128)S(1)}, f32[24,128]{1,0:T(8,128)S(1)}, u32[]{:S(2)}, u32[]{:S(2)}) collective-permute-start(f32[24,128]{1,0:T(8,128)S(1)} %get-tuple-element.8.rest_0_), channel_id=1, source_target_pairs={{8,0},{0,8},{24,16},{16,24},{9,1},{1,9},{25,17},{17,25},{10,2},{2,... | collective-permute-start | bytes 36872 | tf_op jit(solution)/shard_map/ppermute | solution.py:606
  35.7 1.3 %collective-permute-done.3.rest_3_ = f32[24,128]{1,0:T(8,128)S(1)} collective-permute-done((f32[24,128]{1,0:T(8,128)S(1)}, f32[24,128]{1,0:T(8,128)S(1)}, u32[]{:S(2)}, u32[]{:S(2)}) %collective-permute-start.3) | collective-permute-done | bytes 12320 | tf_op jit(solution)/shard_map/ppermute | solution.py:606
  37.0 2.5 %collective-permute-done.2.rest_2_ = f32[24,128]{1,0:T(8,128)S(1)} collective-permute-done((f32[24,128]{1,0:T(8,128)S(1)}, f32[24,128]{1,0:T(8,128)S(1)}, u32[]{:S(2)}, u32[]{:S(2)}) %collective-permute-start.2) | collective-permute-done | bytes 12320 | tf_op jit(solution)/shard_map/ppermute | solution.py:606
  39.6 0.0 collective-permute-done.1.rest_1_
  39.6 1.1 %finish.1 = f32[3,2,192,128]{3,2,1,0:T(8,128)} custom-call(s32[1]{0:T(128)} %bitcast.position, f32[2,24,5,8,128]{4,3,2,1,0:T(8,128)S(1)} %get-tuple-element.6.factors, f32[2,3,5,8,128]{4,3,2,1,0:T(8,128)S(1)} %get-tuple-element.7.tree, f32[3,2,192,128]{3,2,1,0:T(8,128)S(1)} %copy-done.1, f32[24,128]{1,0:T(8,128)S(1)} %get-tuple-element.8.rest_0_, ...), custom_call_target="tpu_custom_call" | custom-call | tf_op jit(solution)/shard_map/finish/pallas_call | solution.py:609
  (2 shorter events, 0.0 us)
Async XLA Ops:
  0.6 1.1 %copy-start = (f32[3,2,192,128]{3,2,1,0:T(8,128)S(1)}, f32[3,2,192,128]{3,2,1,0:T(8,128)}, u32[]{:S(2)}) copy-start(f32[3,2,192,128]{3,2,1,0:T(8,128)} %velocity.5) | copy-start | bytes 1769476
  17.9 3.9 %collective-permute-start = (f32[8,8,128]{2,1,0:T(8,128)S(1)}, f32[8,8,128]{2,1,0:T(8,128)S(1)}, u32[]{:S(2)}, u32[]{:S(2)}) collective-permute-start(f32[8,8,128]{2,1,0:T(8,128)S(1)} %slice.4), channel_id=1, source_target_pairs={{0,4},{1,9},{2,6},{3,7},{4,0},{5,13},{6,2},{7,3},{8,12},{9,1},{10,... | collective-permute-start | bytes 98312 | tf_op jit(solution)/shard_map/ppermute | solution.py:553
  21.5 9.1 %copy-start.1 = (f32[3,2,192,128]{3,2,1,0:T(8,128)S(1)}, f32[3,2,192,128]{3,2,1,0:T(8,128)}, u32[]{:S(2)}) copy-start(f32[3,2,192,128]{3,2,1,0:T(8,128)} %velocity.5) | copy-start | bytes 1769476
  21.5 9.1 %copy-start.2 = (f32[3,2,192,128]{3,2,1,0:T(8,128)S(1)}, f32[3,2,192,128]{3,2,1,0:T(8,128)}, u32[]{:S(2)}) copy-start(f32[3,2,192,128]{3,2,1,0:T(8,128)} %tendency.1) | copy-start | bytes 1769476
  31.3 5.7 %collective-permute-start.3 = (f32[24,128]{1,0:T(8,128)S(1)}, f32[24,128]{1,0:T(8,128)S(1)}, u32[]{:S(2)}, u32[]{:S(2)}) collective-permute-start(f32[24,128]{1,0:T(8,128)S(1)} %get-tuple-element.8.rest_0_), channel_id=1, source_target_pairs={{24,0},{16,8},{8,16},{0,24},{25,1},{17,9},{9,17},{1,25},{26,2},{18... | collective-permute-start | bytes 36872 | tf_op jit(solution)/shard_map/ppermute | solution.py:606
  35.0 4.6 %collective-permute-start.2 = (f32[24,128]{1,0:T(8,128)S(1)}, f32[24,128]{1,0:T(8,128)S(1)}, u32[]{:S(2)}, u32[]{:S(2)}) collective-permute-start(f32[24,128]{1,0:T(8,128)S(1)} %get-tuple-element.8.rest_0_), channel_id=1, source_target_pairs={{16,0},{24,8},{0,16},{8,24},{17,1},{25,9},{1,17},{9,25},{18,2},{26... | collective-permute-start | bytes 36872 | tf_op jit(solution)/shard_map/ppermute | solution.py:606
  35.0 4.6 %collective-permute-start.1 = (f32[24,128]{1,0:T(8,128)S(1)}, f32[24,128]{1,0:T(8,128)S(1)}, u32[]{:S(2)}, u32[]{:S(2)}) collective-permute-start(f32[24,128]{1,0:T(8,128)S(1)} %get-tuple-element.8.rest_0_), channel_id=1, source_target_pairs={{8,0},{0,8},{24,16},{16,24},{9,1},{1,9},{25,17},{17,25},{10,2},{2,... | collective-permute-start | bytes 36872 | tf_op jit(solution)/shard_map/ppermute | solution.py:606

commit v13 on v12

--- a/solution.py
+++ b/solution.py
@@ -29,29 +29,60 @@
     return jnp.sqrt(0.5 * diagonal + 0.25 * mixed)
 
 
-def beside(blocks):
+def lane_of(shape):
+    return lax.broadcasted_iota(jnp.int32, shape, len(shape) - 1)
+
+
+def picked(f, lanes):
+    return jnp.take_along_axis(f, lanes, axis=1)
+
+
+def to_phases(blocks):
     count = len(blocks)
+    if count == 1:
+        return blocks
     lanes = blocks[0].shape[1]
-    down = [pltpu.roll(f, 1, 1) for f in blocks]
-    up = [pltpu.roll(f, lanes - 1, 1) for f in blocks]
-    if count > 1:
-        lane = lax.broadcasted_iota(jnp.int32, blocks[0].shape, 1)
-        first, last = lane == 0, lane == lanes - 1
-        down, up = (
-            [jnp.where(first, down[i - 1], down[i]) for i in range(count)],
-            [jnp.where(last, up[(i + 1) % count], up[i]) for i in range(count)],
-        )
-    return down, up
-
-
-def slope_z(blocks):
-    down, up = beside(blocks)
-    return [u - d for u, d in zip(up, down)]
-
-
-def smooth_z(blocks):
-    down, up = beside(blocks)
-    return [(u + d) + 2.0 * f for f, u, d in zip(blocks, up, down)]
+    phases = []
+    for j in range(count):
+        z = lane_of(blocks[0].shape) * count + j
+        phase = picked(blocks[0], lax.rem(z, lanes))
+        for b in range(1, count):
+            phase = jnp.where(z >= b * lanes, picked(blocks[b], lax.rem(z, lanes)), phase)
+        phases.append(phase)
+    return phases
+
+
+def to_blocks(phases):
+    count = len(phases)
+    if count == 1:
+        return phases
+    lanes = phases[0].shape[1]
+    blocks = []
+    for b in range(count):
+        z = lane_of(phases[0].shape) + b * lanes
+        block = picked(phases[0], lax.div(z, count))
+        for j in range(1, count):
+            block = jnp.where(lax.rem(z, count) == j, picked(phases[j], lax.div(z, count)), block)
+        blocks.append(block)
+    return blocks
+
+
+def after(phases):
+    return [*phases[1:], pltpu.roll(phases[0], phases[0].shape[1] - 1, 1)]
+
+
+def before(phases):
+    return [pltpu.roll(phases[-1], 1, 1), *phases[:-1]]
+
+
+def smooth_z(phases, up=None):
+    sums = [f + u for f, u in zip(phases, after(phases) if up is None else up)]
+    return [f + d for f, d in zip(sums, before(sums))]
+
+
+def smooth_pair(a, b, c, d):
+    middle = b + c
+    return (a + b) + middle, middle + (c + d)
 
 
 def products(v):
@@ -257,100 +288,114 @@
     _, top = outer_sides(rank, parity, count)
     nx = (count // nz_parts) * width
     nz = nz_parts * lanes
-    blocks = range(nz_parts)
+    phases = range(nz_parts)
     lead = 8
-    inner = slice(lead, lead + rows)
-    lower = slice(lead - 1, lead - 1 + rows)
-    upper = slice(lead + 1, lead + 1 + rows)
-    for k in range(count):
-        x0, zb = (k // nz_parts) * width, k % nz_parts
-        for c in range(3):
-            for x in range(width):
-                i = c * width + x
-                vel[c, x0 + x, zb, inner, :] = recv[k, i * rows : (i + 1) * rows, :]
+    tile = min(rows, 8)
+    tiles = [lead + t for t in range(0, rows, tile)]
+
+    for c in range(3):
+        for x in range(nx):
+            i = c * width + x % width
+            ranks = [x // width * nz_parts + zb for zb in phases]
+            for t in tiles:
+                first = i * rows + t - lead
+                blocks = [recv[k, first : first + tile, :] for k in ranks]
+                for j, f in enumerate(to_phases(blocks)):
+                    vel[c, x, j, t : t + tile, :] = f
+            for zb, k in enumerate(ranks):
                 slots = planes * rows + i
                 near = recv[k, slots : slots + 1, :]
                 slots += aligned(planes)
                 other = recv[k, slots : slots + 1, :]
-                below = jnp.where(top, other, near)
-                for side, (edge, at) in enumerate(((below, lead - 1), (other, lead + rows))):
-                    vel[c, x0 + x, zb, at : at + 1, :] = edge
-                    ends[c, x0 + x, zb, side : side + 1, :] = edge
+                ends[c, x, zb, 0:1, :] = jnp.where(top, other, near)
+                ends[c, x, zb, 1:2, :] = other
+            for j, f in enumerate(to_phases([ends[c, x, zb] for zb in phases])):
+                ends[c, x, j] = f
+                vel[c, x, j, lead - 1 : lead, :] = f[0:1, :]
+                vel[c, x, j, lead + rows : lead + rows + 1, :] = f[1:2, :]
 
     for x in range(nx):
         left, right = (x - 1) % nx, (x + 1) % nx
-        centre = [[vel[c, x, zb, inner, :] for zb in blocks] for c in range(3)]
-        grad_x = [[vel[c, right, zb, inner, :] - vel[c, left, zb, inner, :] for zb in blocks] for c in range(3)]
-        grad_y = [[vel[c, x, zb, upper, :] - vel[c, x, zb, lower, :] for zb in blocks] for c in range(3)]
-        grad_z = []
-        for c in range(3):
-            down, up = beside(centre[c])
-            grad_z.append([u - d for u, d in zip(up, down)])
-            for zb in blocks:
-                part[c, x, zb] = (up[zb] + down[zb]) + 2.0 * centre[c][zb]
-        strain = [
-            strain_parts(*([g[c][zb] for c in range(3)] for g in (grad_x, grad_y, grad_z)))
-            for zb in blocks
-        ]
-        size = [strain_size(s) for s in strain]
-        for zb in blocks:
-            mag[x, zb] = size[zb]
-        pairs = [products([centre[c][zb] for c in range(3)]) for zb in blocks]
-        for i in range(6):
-            for base, fields in (
-                (3, [pairs[zb][i] for zb in blocks]),
-                (9, [size[zb] * strain[zb][i] for zb in blocks]),
-            ):
-                for zb, f in enumerate(smooth_z(fields)):
-                    part[base + i, x, zb] = f
-
-    def smooth_x(read, x):
-        return (read((x - 1) % nx) + read((x + 1) % nx)) + 2.0 * read(x)
+        for t in tiles:
+            at = slice(t, t + tile)
+            lower, upper = slice(t - 1, t - 1 + tile), slice(t + 1, t + 1 + tile)
+            own = slice(t - lead, t - lead + tile)
+            centre = [[vel[c, x, j, at, :] for j in phases] for c in range(3)]
+            grad_x = [[vel[c, right, j, at, :] - vel[c, left, j, at, :] for j in phases] for c in range(3)]
+            grad_y = [[vel[c, x, j, upper, :] - vel[c, x, j, lower, :] for j in phases] for c in range(3)]
+            grad_z = []
+            for c in range(3):
+                up, down = after(centre[c]), before(centre[c])
+                grad_z.append([u - d for u, d in zip(up, down)])
+                for j, f in enumerate(smooth_z(centre[c], up)):
+                    part[c, x, j, own, :] = f
+            strain = [
+                strain_parts(*([g[c][j] for c in range(3)] for g in (grad_x, grad_y, grad_z)))
+                for j in phases
+            ]
+            size = [strain_size(s) for s in strain]
+            for j in phases:
+                mag[x, j, own, :] = size[j]
+            pairs = [products([centre[c][j] for c in range(3)]) for j in phases]
+            for i in range(6):
+                for base, fields in (
+                    (3, [pairs[j][i] for j in phases]),
+                    (9, [size[j] * strain[j][i] for j in phases]),
+                ):
+                    for j, f in enumerate(smooth_z(fields)):
+                        part[base + i, x, j, own, :] = f
 
     for c in range(3):
-        rims = []
+        rims = [smooth_z([ends[c, x, j] for j in phases]) for x in range(nx)]
+        for x in range(0, nx, 2):
+            around = [(x - 1) % nx, x, x + 1, (x + 2) % nx]
+            for j in phases:
+                for at, rim in zip(around[1:3], smooth_pair(*(rims[a][j] for a in around))):
+                    filt[c, at, j, lead - 1 : lead, :] = rim[0:1, :]
+                    filt[c, at, j, lead + rows : lead + rows + 1, :] = rim[1:2, :]
+                for t in tiles:
+                    own = slice(t - lead, t - lead + tile)
+                    pair = smooth_pair(*(part[c, a, j, own, :] for a in around))
+                    for at, f in zip(around[1:3], pair):
+                        filt[c, at, j, t : t + tile, :] = f
+
+    sums = [[None, None] for _ in tiles]
+    for x in range(0, nx, 2):
+        around = [(x - 1) % nx, x, x + 1, (x + 2) % nx]
+        for n, t in enumerate(tiles):
+            lower, upper = slice(t - 1, t - 1 + tile), slice(t + 1, t + 1 + tile)
+            own = slice(t - lead, t - lead + tile)
+            mean = [[[filt[c, a, j, t : t + tile, :] for j in phases] for a in around] for c in range(3)]
+            slopes_z = [
+                [[u - d for u, d in zip(after(m), before(m))] for m in mean[c][1:3]] for c in range(3)
+            ]
+            for j in phases:
+                leonard = [smooth_pair(*(part[3 + i, a, j, own, :] for a in around)) for i in range(6)]
+                scaled = [smooth_pair(*(part[9 + i, a, j, own, :] for a in around)) for i in range(6)]
+                for w in range(2):
+                    at = around[1 + w]
+                    grad_x = [mean[c][2 + w][j] - mean[c][w][j] for c in range(3)]
+                    grad_y = [filt[c, at, j, upper, :] - filt[c, at, j, lower, :] for c in range(3)]
+                    strain = strain_parts(grad_x, grad_y, [slopes_z[c][w][j] for c in range(3)])
+                    size = 0.25 * strain_size(strain)
+                    v = [mean[c][1 + w][j] for c in range(3)]
+                    q = [0.0625 * f for f in v]
+                    pairs = [v[a] * q[b] for a, b in ((0, 0), (1, 1), (2, 2), (0, 1), (0, 2), (1, 2))]
+                    totals = contracted(
+                        [leonard[i][w] - pairs[i] for i in range(6)],
+                        [scaled[i][w] - size * strain[i] for i in range(6)],
+                    )
+                    sums[n] = [f if s is None else s + f for s, f in zip(sums[n], totals)]
+
+    for n, t in enumerate(tiles):
+        own = slice(t - lead, t - lead + tile)
+        coefficient = coefficient_of(
+            *(jnp.sum(total, axis=1, keepdims=True) for total in sums[n]), nx * nz
+        )
         for x in range(nx):
-            rims.append(smooth_z([ends[c, x, zb] for zb in blocks]))
-        for x in range(nx):
-            for zb in blocks:
-                rim = smooth_x(lambda at: rims[at][zb], x)
-                filt[c, x, zb, lead - 1 : lead, :] = rim[0:1, :]
-                filt[c, x, zb, lead + rows : lead + rows + 1, :] = rim[1:2, :]
-                filt[c, x, zb, inner, :] = smooth_x(lambda at: part[c, at, zb], x)
-
-    sum_lm = sum_mm = None
-    for x in range(nx):
-        left, right = (x - 1) % nx, (x + 1) % nx
-        mean = [[filt[c, x, zb, inner, :] for zb in blocks] for c in range(3)]
-        grad_x = [[filt[c, right, zb, inner, :] - filt[c, left, zb, inner, :] for zb in blocks] for c in range(3)]
-        grad_y = [[filt[c, x, zb, upper, :] - filt[c, x, zb, lower, :] for zb in blocks] for c in range(3)]
-        grad_z = [slope_z(mean[c]) for c in range(3)]
-        for zb in blocks:
-            strain = strain_parts(*([g[c][zb] for c in range(3)] for g in (grad_x, grad_y, grad_z)))
-            size = 0.25 * strain_size(strain)
-            v = [mean[c][zb] for c in range(3)]
-            scaled = [0.0625 * f for f in v]
-            pairs = (
-                v[0] * scaled[0],
-                v[1] * scaled[1],
-                v[2] * scaled[2],
-                v[0] * scaled[1],
-                v[0] * scaled[2],
-                v[1] * scaled[2],
-            )
-            leonard = [smooth_x(lambda at: part[3 + i, at, zb], x) - pairs[i] for i in range(6)]
-            model = [smooth_x(lambda at: part[9 + i, at, zb], x) - size * strain[i] for i in range(6)]
-            lm, mm = contracted(leonard, model)
-            sum_lm = lm if sum_lm is None else sum_lm + lm
-            sum_mm = mm if sum_mm is None else sum_mm + mm
-
-    coefficient = coefficient_of(
-        *(jnp.sum(total, axis=1, keepdims=True) for total in (sum_lm, sum_mm)), nx * nz
-    )
-    for k in range(count):
-        x0, zb = (k // nz_parts) * width, k % nz_parts
-        for x in range(width):
-            out[k, x] = coefficient * mag[x0 + x, zb]
+            blocks = to_blocks([coefficient * mag[x, j, own, :] for j in phases])
+            for zb, f in enumerate(blocks):
+                out[x // width * nz_parts + zb, x % width, own, :] = f
 
 
 def sweep_kernel(parity, back, velocity, tendency, eddy_out, reduced, factors, tree, eddy, sent):

time: 40.9 us -> 45.5 us (1.11)
  Pallas kernels: 4.86 us -> 9.61 us
    pallas_call x1, Pallas kernels: 3.03 us -> 7.76 us  [body(): pl.pallas_call(functools.partial(germano_kernel, nz_parts, width, rows),...]
  transfers between devices with their start and end apart: 4 -> 4, of which waited for: 3 -> 2; matrix products, arithmetic and copies ran while one was open for 0% -> 0% of each run, Pallas kernels for 7% -> 17%
where the time goes in v13:
time: 45.5 us; the launch traced here: 45.2 us
  blocking collectives  25 us (55%)
  Pallas kernels  9.61 us (21%)
  starting transfers between devices  5.01 us (11%)
  waiting for transfers between devices  3.81 us (8%)
  local copies, waits for them, and re-layouts  1.08 us (2%)
  between operations  0.7 us (2%)
    all_to_all x1, blocking collectives, body(): lax.all_to_all(chunks, ('gx', 'gz'), split_axis=0, concat_axis=0, tiled=T...  16.1 us
    all_to_all x1, blocking collectives, body(): lax.all_to_all(eddy_chunks, ('gx', 'gz'), split_axis=0, concat_axis=0, ti...  8.9 us
    pallas_call x1, Pallas kernels, body(): pl.pallas_call(functools.partial(germano_kernel, nz_parts, width, rows),...  7.76 us
    ppermute x3, starting transfers between devices, body(): lax.ppermute(reduced, 'gy', [(partner(i, step, walls), i) for i in range(...  4.45 us
    ppermute x3, waiting for transfers between devices, body(): lax.ppermute(reduced, 'gy', [(partner(i, step, walls), i) for i in range(...  3.8 us
    unnamed x6, local copies, waits for them, and re-layouts  1.07 us
    pallas_call x1, Pallas kernels, body(): pl.pallas_call(functools.partial(finish_kernel, walls), out_shape=jax.Sha...  1.05 us
  transfers between devices with their start and end apart: 4, of which 2 were waited for; matrix products, arithmetic and copies ran while one was open for 0% of the time, Pallas kernels for 17%

profile of v13, /device:TPU:0, one launch (start us, length us, event | category | flops | bytes accessed | tf_op | source)
XLA Modules:
  0.0 45.2 jit_solution(8031197811757233441)
XLA Ops:
  0.6 0.0 copy-start
  0.6 1.1 %copy-done = f32[3,2,192,128]{3,2,1,0:T(8,128)S(1)} copy-done((f32[3,2,192,128]{3,2,1,0:T(8,128)S(1)}, f32[3,2,192,128]{3,2,1,0:T(8,128)}, u32[]{:S(2)}) %copy-start) | copy-done | bytes 589848
  1.7 0.1 pack.1
  1.8 16.1 %all_to_all.10.recv = f32[8,160,128]{2,1,0:T(8,128)S(1)} all-to-all(f32[8,160,128]{2,1,0:T(8,128)S(1)} %pack.1), channel_id=1, replica_groups=mesh['gy'=4,'gx'=4,'gz'=2] {'gx','gz'}, dimensions={0} | all-to-all | bytes 1310720 | tf_op jit(solution)/shard_map/all_to_all | solution.py:596
  17.9 0.6 %collective-permute-start = (f32[8,8,128]{2,1,0:T(8,128)S(1)}, f32[8,8,128]{2,1,0:T(8,128)S(1)}, u32[]{:S(2)}, u32[]{:S(2)}) collective-permute-start(f32[8,8,128]{2,1,0:T(8,128)S(1)} %slice.4), channel_id=1, source_target_pairs={{0,4},{1,9},{2,6},{3,7},{4,0},{5,13},{6,2},{7,3},{8,12},{9,1},{10,... | collective-permute-start | bytes 98312 | tf_op jit(solution)/shard_map/ppermute | solution.py:598
  18.5 7.8 %germano.1.given = f32[8,2,24,128]{3,2,1,0:T(8,128)S(1)} custom-call(s32[1]{0:T(128)} %bitcast.1.rank, s32[1]{0:T(128)S(6)} %rem.18.parity, f32[8,160,128]{2,1,0:T(8,128)S(1)} %all_to_all.10.recv), custom_call_target="tpu_custom_call" | custom-call | flops 14745600 | bytes 786432 | tf_op jit(solution)/shard_map/germano/pallas_call | solution.py:602
  26.2 0.0 copy-start.1
  26.2 0.0 copy-start.2
  26.3 0.0 collective-permute-done.swapped
  26.3 8.9 %all_to_all.11.back = f32[8,2,24,128]{3,2,1,0:T(8,128)S(1)} all-to-all(f32[8,2,24,128]{3,2,1,0:T(8,128)S(1)} %edge.1), channel_id=1, replica_groups=mesh['gy'=4,'gx'=4,'gz'=2] {'gx','gz'}, dimensions={0} | all-to-all | bytes 393216 | tf_op jit(solution)/shard_map/all_to_all | solution.py:630
  35.2 0.0 copy-done.1
  35.2 0.0 copy-done.2
  35.2 0.7 %sweep.1 = (f32[2,192,128]{2,1,0:T(8,128)}, f32[24,128]{1,0:T(8,128)S(1)}, f32[2,24,5,8,128]{4,3,2,1,0:T(8,128)S(1)}, f32[2,3,5,8,128]{4,3,2,1,0:T(8,128)S(1)}) custom-call(s32[1]{0:T(128)S(6)} %rem.18.parity, f32[8,2,24,128]{3,2,1,0:T(8,128)S(1)} %all_to_all.11.back, f32[3,2,192,128]{3,2,1,0:T(8,128)S(1)} %copy-done.1, f32[3,2,192,128]{3,2,1,0:T(8,128)S(1)} %copy-done.2), custom_call_target="tpu_custom_call" | custom-call | tf_op jit(solution)/shard_map/sweep/pallas_call | solution.py:635
  35.9 3.7 %collective-permute-start.3 = (f32[24,128]{1,0:T(8,128)S(1)}, f32[24,128]{1,0:T(8,128)S(1)}, u32[]{:S(2)}, u32[]{:S(2)}) collective-permute-start(f32[24,128]{1,0:T(8,128)S(1)} %get-tuple-element.8.rest_0_), channel_id=1, source_target_pairs={{24,0},{16,8},{8,16},{0,24},{25,1},{17,9},{9,17},{1,25},{26,2},{18... | collective-permute-start | bytes 36872 | tf_op jit(solution)/shard_map/ppermute | solution.py:651
  39.6 0.0 collective-permute-start.2
  39.6 0.8 %collective-permute-start.1 = (f32[24,128]{1,0:T(8,128)S(1)}, f32[24,128]{1,0:T(8,128)S(1)}, u32[]{:S(2)}, u32[]{:S(2)}) collective-permute-start(f32[24,128]{1,0:T(8,128)S(1)} %get-tuple-element.8.rest_0_), channel_id=1, source_target_pairs={{8,0},{0,8},{24,16},{16,24},{9,1},{1,9},{25,17},{17,25},{10,2},{2,... | collective-permute-start | bytes 36872 | tf_op jit(solution)/shard_map/ppermute | solution.py:651
  40.4 1.3 %collective-permute-done.3.rest_3_ = f32[24,128]{1,0:T(8,128)S(1)} collective-permute-done((f32[24,128]{1,0:T(8,128)S(1)}, f32[24,128]{1,0:T(8,128)S(1)}, u32[]{:S(2)}, u32[]{:S(2)}) %collective-permute-start.3) | collective-permute-done | bytes 12320 | tf_op jit(solution)/shard_map/ppermute | solution.py:651
  41.6 2.5 %collective-permute-done.2.rest_2_ = f32[24,128]{1,0:T(8,128)S(1)} collective-permute-done((f32[24,128]{1,0:T(8,128)S(1)}, f32[24,128]{1,0:T(8,128)S(1)}, u32[]{:S(2)}, u32[]{:S(2)}) %collective-permute-start.2) | collective-permute-done | bytes 12320 | tf_op jit(solution)/shard_map/ppermute | solution.py:651
  44.2 0.0 collective-permute-done.1.rest_1_
  44.2 1.1 %finish.1 = f32[3,2,192,128]{3,2,1,0:T(8,128)} custom-call(s32[1]{0:T(128)} %bitcast.position, f32[2,24,5,8,128]{4,3,2,1,0:T(8,128)S(1)} %get-tuple-element.6.factors, f32[2,3,5,8,128]{4,3,2,1,0:T(8,128)S(1)} %get-tuple-element.7.tree, f32[3,2,192,128]{3,2,1,0:T(8,128)S(1)} %copy-done.1, f32[24,128]{1,0:T(8,128)S(1)} %get-tuple-element.8.rest_0_, ...), custom_call_target="tpu_custom_call" | custom-call | tf_op jit(solution)/shard_map/finish/pallas_call | solution.py:654
  (2 shorter events, 0.0 us)
Async XLA Ops:
  0.6 1.1 %copy-start = (f32[3,2,192,128]{3,2,1,0:T(8,128)S(1)}, f32[3,2,192,128]{3,2,1,0:T(8,128)}, u32[]{:S(2)}) copy-start(f32[3,2,192,128]{3,2,1,0:T(8,128)} %velocity.5) | copy-start | bytes 1769476
  17.9 8.4 %collective-permute-start = (f32[8,8,128]{2,1,0:T(8,128)S(1)}, f32[8,8,128]{2,1,0:T(8,128)S(1)}, u32[]{:S(2)}, u32[]{:S(2)}) collective-permute-start(f32[8,8,128]{2,1,0:T(8,128)S(1)} %slice.4), channel_id=1, source_target_pairs={{0,4},{1,9},{2,6},{3,7},{4,0},{5,13},{6,2},{7,3},{8,12},{9,1},{10,... | collective-permute-start | bytes 98312 | tf_op jit(solution)/shard_map/ppermute | solution.py:598
  26.2 9.0 %copy-start.1 = (f32[3,2,192,128]{3,2,1,0:T(8,128)S(1)}, f32[3,2,192,128]{3,2,1,0:T(8,128)}, u32[]{:S(2)}) copy-start(f32[3,2,192,128]{3,2,1,0:T(8,128)} %velocity.5) | copy-start | bytes 1769476
  26.2 9.0 %copy-start.2 = (f32[3,2,192,128]{3,2,1,0:T(8,128)S(1)}, f32[3,2,192,128]{3,2,1,0:T(8,128)}, u32[]{:S(2)}) copy-start(f32[3,2,192,128]{3,2,1,0:T(8,128)} %tendency.1) | copy-start | bytes 1769476
  35.9 5.7 %collective-permute-start.3 = (f32[24,128]{1,0:T(8,128)S(1)}, f32[24,128]{1,0:T(8,128)S(1)}, u32[]{:S(2)}, u32[]{:S(2)}) collective-permute-start(f32[24,128]{1,0:T(8,128)S(1)} %get-tuple-element.8.rest_0_), channel_id=1, source_target_pairs={{24,0},{16,8},{8,16},{0,24},{25,1},{17,9},{9,17},{1,25},{26,2},{18... | collective-permute-start | bytes 36872 | tf_op jit(solution)/shard_map/ppermute | solution.py:651
  39.6 4.6 %collective-permute-start.2 = (f32[24,128]{1,0:T(8,128)S(1)}, f32[24,128]{1,0:T(8,128)S(1)}, u32[]{:S(2)}, u32[]{:S(2)}) collective-permute-start(f32[24,128]{1,0:T(8,128)S(1)} %get-tuple-element.8.rest_0_), channel_id=1, source_target_pairs={{16,0},{24,8},{0,16},{8,24},{17,1},{25,9},{1,17},{9,25},{18,2},{26... | collective-permute-start | bytes 36872 | tf_op jit(solution)/shard_map/ppermute | solution.py:651
  39.6 4.6 %collective-permute-start.1 = (f32[24,128]{1,0:T(8,128)S(1)}, f32[24,128]{1,0:T(8,128)S(1)}, u32[]{:S(2)}, u32[]{:S(2)}) collective-permute-start(f32[24,128]{1,0:T(8,128)S(1)} %get-tuple-element.8.rest_0_), channel_id=1, source_target_pairs={{8,0},{0,8},{24,16},{16,24},{9,1},{1,9},{25,17},{17,25},{10,2},{2,... | collective-permute-start | bytes 36872 | tf_op jit(solution)/shard_map/ppermute | solution.py:651

commit v14 on v13

--- a/solution.py
+++ b/solution.py
@@ -290,7 +290,7 @@
     nz = nz_parts * lanes
     phases = range(nz_parts)
     lead = 8
-    tile = min(rows, 8)
+    tile = rows
     tiles = [lead + t for t in range(0, rows, tile)]
 
     for c in range(3):

time: 45.5 us -> 48 us (1.055)
  Pallas kernels: 9.61 us -> 12.1 us
    pallas_call x1, Pallas kernels: 7.76 us -> 10.2 us  [body(): pl.pallas_call(functools.partial(germano_kernel, nz_parts, width, rows),...]
  transfers between devices with their start and end apart: 4 -> 4, of which waited for: 2 -> 2; matrix products, arithmetic and copies ran while one was open for 0% -> 0% of each run, Pallas kernels for 17% -> 21%
where the time goes in v14:
time: 48 us; the launch traced here: 47.7 us
  blocking collectives  25 us (52%)
  Pallas kernels  12.1 us (25%)
  starting transfers between devices  5.01 us (10%)
  waiting for transfers between devices  3.81 us (8%)
  local copies, waits for them, and re-layouts  1.08 us (2%)
  between operations  0.71 us (1%)
    all_to_all x1, blocking collectives, body(): lax.all_to_all(chunks, ('gx', 'gz'), split_axis=0, concat_axis=0, tiled=T...  16.1 us
    pallas_call x1, Pallas kernels, body(): pl.pallas_call(functools.partial(germano_kernel, nz_parts, width, rows),...  10.2 us
    all_to_all x1, blocking collectives, body(): lax.all_to_all(eddy_chunks, ('gx', 'gz'), split_axis=0, concat_axis=0, ti...  8.9 us
    ppermute x3, starting transfers between devices, body(): lax.ppermute(reduced, 'gy', [(partner(i, step, walls), i) for i in range(...  4.45 us
    ppermute x3, waiting for transfers between devices, body(): lax.ppermute(reduced, 'gy', [(partner(i, step, walls), i) for i in range(...  3.8 us
    unnamed x6, local copies, waits for them, and re-layouts  1.07 us
    pallas_call x1, Pallas kernels, body(): pl.pallas_call(functools.partial(finish_kernel, walls), out_shape=jax.Sha...  1.05 us
  transfers between devices with their start and end apart: 4, of which 2 were waited for; matrix products, arithmetic and copies ran while one was open for 0% of the time, Pallas kernels for 21%

profile of v14, /device:TPU:0, one launch (start us, length us, event | category | flops | bytes accessed | tf_op | source)
XLA Modules:
  0.0 47.7 jit_solution(8222355311934219929)
XLA Ops:
  0.6 0.0 copy-start
  0.6 1.1 %copy-done = f32[3,2,192,128]{3,2,1,0:T(8,128)S(1)} copy-done((f32[3,2,192,128]{3,2,1,0:T(8,128)S(1)}, f32[3,2,192,128]{3,2,1,0:T(8,128)}, u32[]{:S(2)}) %copy-start) | copy-done | bytes 589848
  1.7 0.1 pack.1
  1.8 16.1 %all_to_all.10.recv = f32[8,160,128]{2,1,0:T(8,128)S(1)} all-to-all(f32[8,160,128]{2,1,0:T(8,128)S(1)} %pack.1), channel_id=1, replica_groups=mesh['gy'=4,'gx'=4,'gz'=2] {'gx','gz'}, dimensions={0} | all-to-all | bytes 1310720 | tf_op jit(solution)/shard_map/all_to_all | solution.py:596
  17.9 0.6 %collective-permute-start = (f32[8,8,128]{2,1,0:T(8,128)S(1)}, f32[8,8,128]{2,1,0:T(8,128)S(1)}, u32[]{:S(2)}, u32[]{:S(2)}) collective-permute-start(f32[8,8,128]{2,1,0:T(8,128)S(1)} %slice.4), channel_id=1, source_target_pairs={{0,4},{1,9},{2,6},{3,7},{4,0},{5,13},{6,2},{7,3},{8,12},{9,1},{10,... | collective-permute-start | bytes 98312 | tf_op jit(solution)/shard_map/ppermute | solution.py:598
  18.5 10.2 %germano.1.given = f32[8,2,24,128]{3,2,1,0:T(8,128)S(1)} custom-call(s32[1]{0:T(128)} %bitcast.1.rank, s32[1]{0:T(128)S(6)} %rem.18.parity, f32[8,160,128]{2,1,0:T(8,128)S(1)} %all_to_all.10.recv), custom_call_target="tpu_custom_call" | custom-call | flops 14745600 | bytes 786432 | tf_op jit(solution)/shard_map/germano/pallas_call | solution.py:602
  28.7 0.0 copy-start.1
  28.7 0.0 copy-start.2
  28.7 0.0 collective-permute-done.swapped
  28.8 8.9 %all_to_all.11.back = f32[8,2,24,128]{3,2,1,0:T(8,128)S(1)} all-to-all(f32[8,2,24,128]{3,2,1,0:T(8,128)S(1)} %edge.1), channel_id=1, replica_groups=mesh['gy'=4,'gx'=4,'gz'=2] {'gx','gz'}, dimensions={0} | all-to-all | bytes 393216 | tf_op jit(solution)/shard_map/all_to_all | solution.py:630
  37.7 0.0 copy-done.1
  37.7 0.0 copy-done.2
  37.7 0.7 %sweep.1 = (f32[2,192,128]{2,1,0:T(8,128)}, f32[24,128]{1,0:T(8,128)S(1)}, f32[2,24,5,8,128]{4,3,2,1,0:T(8,128)S(1)}, f32[2,3,5,8,128]{4,3,2,1,0:T(8,128)S(1)}) custom-call(s32[1]{0:T(128)S(6)} %rem.18.parity, f32[8,2,24,128]{3,2,1,0:T(8,128)S(1)} %all_to_all.11.back, f32[3,2,192,128]{3,2,1,0:T(8,128)S(1)} %copy-done.1, f32[3,2,192,128]{3,2,1,0:T(8,128)S(1)} %copy-done.2), custom_call_target="tpu_custom_call" | custom-call | tf_op jit(solution)/shard_map/sweep/pallas_call | solution.py:635
  38.4 3.7 %collective-permute-start.3 = (f32[24,128]{1,0:T(8,128)S(1)}, f32[24,128]{1,0:T(8,128)S(1)}, u32[]{:S(2)}, u32[]{:S(2)}) collective-permute-start(f32[24,128]{1,0:T(8,128)S(1)} %get-tuple-element.8.rest_0_), channel_id=1, source_target_pairs={{24,0},{16,8},{8,16},{0,24},{25,1},{17,9},{9,17},{1,25},{26,2},{18... | collective-permute-start | bytes 36872 | tf_op jit(solution)/shard_map/ppermute | solution.py:651
  42.1 0.0 collective-permute-start.2
  42.1 0.8 %collective-permute-start.1 = (f32[24,128]{1,0:T(8,128)S(1)}, f32[24,128]{1,0:T(8,128)S(1)}, u32[]{:S(2)}, u32[]{:S(2)}) collective-permute-start(f32[24,128]{1,0:T(8,128)S(1)} %get-tuple-element.8.rest_0_), channel_id=1, source_target_pairs={{8,0},{0,8},{24,16},{16,24},{9,1},{1,9},{25,17},{17,25},{10,2},{2,... | collective-permute-start | bytes 36872 | tf_op jit(solution)/shard_map/ppermute | solution.py:651
  42.9 1.3 %collective-permute-done.3.rest_3_ = f32[24,128]{1,0:T(8,128)S(1)} collective-permute-done((f32[24,128]{1,0:T(8,128)S(1)}, f32[24,128]{1,0:T(8,128)S(1)}, u32[]{:S(2)}, u32[]{:S(2)}) %collective-permute-start.3) | collective-permute-done | bytes 12320 | tf_op jit(solution)/shard_map/ppermute | solution.py:651
  44.1 2.5 %collective-permute-done.2.rest_2_ = f32[24,128]{1,0:T(8,128)S(1)} collective-permute-done((f32[24,128]{1,0:T(8,128)S(1)}, f32[24,128]{1,0:T(8,128)S(1)}, u32[]{:S(2)}, u32[]{:S(2)}) %collective-permute-start.2) | collective-permute-done | bytes 12320 | tf_op jit(solution)/shard_map/ppermute | solution.py:651
  46.7 0.0 collective-permute-done.1.rest_1_
  46.7 1.1 %finish.1 = f32[3,2,192,128]{3,2,1,0:T(8,128)} custom-call(s32[1]{0:T(128)} %bitcast.position, f32[2,24,5,8,128]{4,3,2,1,0:T(8,128)S(1)} %get-tuple-element.6.factors, f32[2,3,5,8,128]{4,3,2,1,0:T(8,128)S(1)} %get-tuple-element.7.tree, f32[3,2,192,128]{3,2,1,0:T(8,128)S(1)} %copy-done.1, f32[24,128]{1,0:T(8,128)S(1)} %get-tuple-element.8.rest_0_, ...), custom_call_target="tpu_custom_call" | custom-call | tf_op jit(solution)/shard_map/finish/pallas_call | solution.py:654
  (2 shorter events, 0.0 us)
Async XLA Ops:
  0.6 1.1 %copy-start = (f32[3,2,192,128]{3,2,1,0:T(8,128)S(1)}, f32[3,2,192,128]{3,2,1,0:T(8,128)}, u32[]{:S(2)}) copy-start(f32[3,2,192,128]{3,2,1,0:T(8,128)} %velocity.5) | copy-start | bytes 1769476
  17.9 10.8 %collective-permute-start = (f32[8,8,128]{2,1,0:T(8,128)S(1)}, f32[8,8,128]{2,1,0:T(8,128)S(1)}, u32[]{:S(2)}, u32[]{:S(2)}) collective-permute-start(f32[8,8,128]{2,1,0:T(8,128)S(1)} %slice.4), channel_id=1, source_target_pairs={{0,4},{1,9},{2,6},{3,7},{4,0},{5,13},{6,2},{7,3},{8,12},{9,1},{10,... | collective-permute-start | bytes 98312 | tf_op jit(solution)/shard_map/ppermute | solution.py:598
  28.7 9.0 %copy-start.1 = (f32[3,2,192,128]{3,2,1,0:T(8,128)S(1)}, f32[3,2,192,128]{3,2,1,0:T(8,128)}, u32[]{:S(2)}) copy-start(f32[3,2,192,128]{3,2,1,0:T(8,128)} %velocity.5) | copy-start | bytes 1769476
  28.7 9.0 %copy-start.2 = (f32[3,2,192,128]{3,2,1,0:T(8,128)S(1)}, f32[3,2,192,128]{3,2,1,0:T(8,128)}, u32[]{:S(2)}) copy-start(f32[3,2,192,128]{3,2,1,0:T(8,128)} %tendency.1) | copy-start | bytes 1769476
  38.4 5.7 %collective-permute-start.3 = (f32[24,128]{1,0:T(8,128)S(1)}, f32[24,128]{1,0:T(8,128)S(1)}, u32[]{:S(2)}, u32[]{:S(2)}) collective-permute-start(f32[24,128]{1,0:T(8,128)S(1)} %get-tuple-element.8.rest_0_), channel_id=1, source_target_pairs={{24,0},{16,8},{8,16},{0,24},{25,1},{17,9},{9,17},{1,25},{26,2},{18... | collective-permute-start | bytes 36872 | tf_op jit(solution)/shard_map/ppermute | solution.py:651
  42.1 4.6 %collective-permute-start.2 = (f32[24,128]{1,0:T(8,128)S(1)}, f32[24,128]{1,0:T(8,128)S(1)}, u32[]{:S(2)}, u32[]{:S(2)}) collective-permute-start(f32[24,128]{1,0:T(8,128)S(1)} %get-tuple-element.8.rest_0_), channel_id=1, source_target_pairs={{16,0},{24,8},{0,16},{8,24},{17,1},{25,9},{1,17},{9,25},{18,2},{26... | collective-permute-start | bytes 36872 | tf_op jit(solution)/shard_map/ppermute | solution.py:651
  42.1 4.6 %collective-permute-start.1 = (f32[24,128]{1,0:T(8,128)S(1)}, f32[24,128]{1,0:T(8,128)S(1)}, u32[]{:S(2)}, u32[]{:S(2)}) collective-permute-start(f32[24,128]{1,0:T(8,128)S(1)} %get-tuple-element.8.rest_0_), channel_id=1, source_target_pairs={{8,0},{0,8},{24,16},{16,24},{9,1},{1,9},{25,17},{17,25},{10,2},{2,... | collective-permute-start | bytes 36872 | tf_op jit(solution)/shard_map/ppermute | solution.py:651

commit v15 on v12

--- a/solution.py
+++ b/solution.py
@@ -368,75 +368,114 @@
     def row(ref, index, j):
         return ref[(*index, pl.ds(j, SEGMENTS, stride=length), slice(None))]
 
-    for x in range(width):
-        visc = 1.0 + row(eddy, (x,), 0)
-        visc_first = visc
-        q = jnp.ones_like(visc)
-        m = jnp.ones_like(visc)
-        corner = jnp.zeros_like(visc)
-        first = [jnp.zeros_like(visc)] * 3
-        value = None
-        for j in range(length):
-            if j < length - 1:
-                visc_next = 1.0 + row(eddy, (x,), j + 1)
-                link = 750.0 * (visc + visc_next)
-                inverse = 1.0 / (q + link)
-            else:
-                visc_next = None
-                link = None
-                inverse = 1.0 / q
-            left = m * inverse
-            corner = corner + m * left
-            source = [
-                2.0 * row(velocity, (c, x), j) + row(tendency, (c, x), j) for c in range(3)
-            ]
-            if j > 0:
-                source = [s + link_before * v for s, v in zip(source, value)]
-            value = [s * inverse for s in source]
-            first = [f + m * v for f, v in zip(first, value)]
+    planes = range(width)
+    last_row = length - 1
+    visc = [[1.0 + row(eddy, (x,), j) for x in planes] for j in range(length)]
+    links = [[750.0 * (v + w) for v, w in zip(visc[j], visc[j + 1])] for j in range(last_row)]
+
+    over = [jnp.ones_like(v) for v in visc[0]]
+    under = [jnp.ones_like(v) for v in visc[0]]
+    inverses = []
+    for j in range(last_row):
+        inverses.append([u / (o + e * u) for o, u, e in zip(over, under, links[j])])
+        steps = [o * (1.0 / e) for o, e in zip(over, links[j])]
+        under, over = (
+            [u + t for u, t in zip(under, steps)],
+            [(o + u) + t for o, u, t in zip(over, under, steps)],
+        )
+    inverses.append([u / o for o, u in zip(over, under)])
+
+    value = first = corner = left = None
+    reach = [jnp.ones_like(v) for v in visc[0]]
+    for j in range(length):
+        inverse = inverses[j]
+        before = value
+        source = [[2.0 * row(velocity, (c, x), j) + row(tendency, (c, x), j) for x in planes] for c in range(3)]
+        value = [[f * r for f, r in zip(source[c], inverse)] for c in range(3)]
+        if j > 0:
+            carry = [e * r for e, r in zip(links[j - 1], inverse)]
+            value = [[v + k * w for v, k, w in zip(value[c], carry, before[c])] for c in range(3)]
+        left = [m * r for m, r in zip(reach, inverse)]
+        if j == 0:
+            first, corner = value, left
+        else:
+            first = [[f + m * v for f, m, v in zip(first[c], reach, value[c])] for c in range(3)]
+            corner = [a + m * v for a, m, v in zip(corner, reach, left)]
+        ratio = inverse
+        if j < last_row:
+            ratio = [e * r for e, r in zip(links[j], inverse)]
+            reach = [m * r for m, r in zip(reach, ratio)]
+        for x in planes:
             for c in range(3):
-                factors[x, j, c] = value[c]
-            factors[x, j, 3] = left
-            if j < length - 1:
-                ratio = link * inverse
-                factors[x, j, 4] = ratio
-                q = 1.0 + link * (q * inverse)
-                m = m * ratio
-                link_before = link
-                visc = visc_next
-            else:
-                factors[x, j, 4] = inverse
-        last = value
-        across = left
-        end = inverse
-        links = 750.0 * (visc + pltpu.roll(visc_first, SEGMENTS - 1, 0))
-        level, step = 0, 1
-        while step < SEGMENTS:
-            def other(v):
-                return pltpu.roll(v, SEGMENTS - step, 0)
-
-            link = links if step == 1 else pltpu.roll(links, SEGMENTS - (step - 1), 0)
-            across_b = other(across)
-            stiff = link / (1.0 + link * (end + other(corner)))
-            flux = [stiff * (g - other(f)) for g, f in zip(last, first)]
-            from_left = stiff * across
-            from_right = stiff * across_b
+                factors[x, j, c] = value[c][x]
+            factors[x, j, 3] = left[x]
+            factors[x, j, 4] = ratio[x]
+
+    def other(fields, step):
+        return [pltpu.roll(f, (SEGMENTS - step) % SEGMENTS, 0) if step else f for f in fields]
+
+    last, across, end = value, left, inverse
+    seams = [750.0 * (v + w) for v, w in zip(visc[last_row], other(visc[0], 1))]
+    level, step = 0, 1
+    while step < SEGMENTS:
+        link = other(seams, step - 1)
+        first_b = [other(f, step) for f in first]
+        last_b = [other(f, step) for f in last]
+        corner_b, end_b, across_b = other(corner, step), other(end, step), other(across, step)
+        stiff = [e / (1.0 + e * (d + a)) for e, d, a in zip(link, end, corner_b)]
+        flux = [[k * (g - f) for k, g, f in zip(stiff, last[c], first_b[c])] for c in range(3)]
+        from_left = [k * b for k, b in zip(stiff, across)]
+        from_right = [k * b for k, b in zip(stiff, across_b)]
+        for x in planes:
             for c in range(3):
-                tree[x, level, c] = flux[c]
-            tree[x, level, 3] = from_left
-            tree[x, level, 4] = from_right
-            first = [f - across * t for f, t in zip(first, flux)]
-            last = [other(g) + across_b * t for g, t in zip(last, flux)]
-            corner = corner - across * from_left
-            end = other(end) - across_b * from_right
-            across = from_left * across_b
-            level, step = level + 1, step * 2
-        rows_out = [*first, *last, corner, across, end, visc_first]
+                tree[x, level, c] = flux[c][x]
+            tree[x, level, 3] = from_left[x]
+            tree[x, level, 4] = from_right[x]
+        first = [[f - b * t for f, b, t in zip(first[c], across, flux[c])] for c in range(3)]
+        last = [[g + b * t for g, b, t in zip(last_b[c], across_b, flux[c])] for c in range(3)]
+        corner = [a - b * k for a, b, k in zip(corner, across, from_left)]
+        end = [d - b * k for d, b, k in zip(end_b, across_b, from_right)]
+        across = [k * b for k, b in zip(from_left, across_b)]
+        level, step = level + 1, step * 2
+    for x in planes:
+        rows_out = [f[x][0:1, :] for f in (*first, *last, corner, across, end, visc[0])]
+        rows_out.append(visc[last_row][x][SEGMENTS - 1 :, :])
         for i, v in enumerate(rows_out):
-            reduced[i * width + x : i * width + x + 1, :] = v[0:1, :]
-        i = len(rows_out)
-        reduced[i * width + x : i * width + x + 1, :] = visc[SEGMENTS - 1 :, :]
+            reduced[i * width + x : i * width + x + 1, :] = v
     write.wait()
+
+
+def spread_kernel(factors, tree, velocity, particular, response):
+    width, length = factors.shape[:2]
+    levels = tree.shape[1]
+    sublane = lax.broadcasted_iota(jnp.int32, (SEGMENTS, LANES), 0)
+    one, zero = (jnp.full((SEGMENTS, LANES), v, jnp.float32) for v in (1.0, 0.0))
+    sides = [(c, zero, zero) for c in range(3)] + [(None, one, zero), (None, zero, one)]
+    lefts = [[side[1]] * width for side in sides]
+    rights = [[side[2]] * width for side in sides]
+    for level in range(levels - 1, -1, -1):
+        step = 2**level
+        second = lax.rem(sublane, 2 * step) == step
+        for n, (c, _, _) in enumerate(sides):
+            for x in range(width):
+                left, right = lefts[n][x], rights[n][x]
+                through = tree[x, level, 3] * left - tree[x, level, 4] * right
+                if c is not None:
+                    through = tree[x, level, c] + through
+                lefts[n][x] = jnp.where(second, pltpu.roll(through, step, 0), left)
+                rights[n][x] = jnp.where(second, pltpu.roll(right, step, 0), -through)
+    values = rights
+    for j in range(length - 1, -1, -1):
+        rows = pl.ds(j, SEGMENTS, stride=length)
+        for n, (c, _, _) in enumerate(sides):
+            for x in range(width):
+                value = factors[x, j, 3] * lefts[n][x] + factors[x, j, 4] * values[n][x]
+                if c is not None:
+                    value = factors[x, j, c] + value
+                    particular[c, x, rows, :] = value - velocity[c, x, rows, :]
+                else:
+                    response[n - 3, x, rows, :] = value
+                values[n][x] = value
 
 
 def partner(i, step, count):
@@ -445,9 +484,9 @@
     return (i - step + count) % count
 
 
-def finish_kernel(devices, position, factors, tree, velocity, *rest):
+def finish_kernel(devices, position, particular, response, *rest):
     reduced, (result, gathered, fluxes, out, sent) = rest[:devices], rest[devices:]
-    width, length = factors.shape[:2]
+    width = particular.shape[1]
     here = position[0]
     for step in range(devices):
         gathered[partner(here, step, devices)] = reduced[step][...]
@@ -485,25 +524,12 @@
         for c in range(3):
             fluxes[i, c * width : (c + 1) * width, :] = flux[c]
 
-    sublane = lax.broadcasted_iota(jnp.int32, (SEGMENTS, LANES), 0)
-    levels = tree.shape[1]
     writes = []
     for c in range(3):
         for x in range(width):
             r = c * width + x
-            left = jnp.broadcast_to(fluxes[here, r : r + 1, :], (SEGMENTS, LANES))
-            right = -jnp.broadcast_to(fluxes[here + 1, r : r + 1, :], (SEGMENTS, LANES))
-            for level in range(levels - 1, -1, -1):
-                step = 2**level
-                through = tree[x, level, c] + tree[x, level, 3] * left - tree[x, level, 4] * right
-                second = lax.rem(sublane, 2 * step) == step
-                left = jnp.where(second, pltpu.roll(through, step, 0), left)
-                right = jnp.where(second, pltpu.roll(right, step, 0), -through)
-            value = right
-            for j in range(length - 1, -1, -1):
-                value = (factors[x, j, c] + factors[x, j, 3] * left) + factors[x, j, 4] * value
-                rows = pl.ds(j, SEGMENTS, stride=length)
-                out[c, x, rows, :] = value - velocity[c, x, rows, :]
+            left, right = fluxes[here, r : r + 1, :], fluxes[here + 1, r : r + 1, :]
+            out[c, x] = particular[c, x] + (response[0, x] * left - response[1, x] * right)
             writes.append(pltpu.make_async_copy(out.at[c, x], result.at[c, x], sent.at[r]))
             writes[-1].start()
     for write in writes:
@@ -606,10 +632,24 @@
         lax.ppermute(reduced, "gy", [(partner(i, step, walls), i) for i in range(walls)])
         for step in range(1, walls)
     ]
+    particular, response = pl.pallas_call(
+        spread_kernel,
+        out_shape=(
+            jax.ShapeDtypeStruct(velocity.shape, f32),
+            jax.ShapeDtypeStruct((2, *velocity.shape[1:]), f32),
+        ),
+        in_specs=in_vmem(3),
+        out_specs=tuple(in_vmem(2)),
+        compiler_params=params(),
+        cost_estimate=pl.CostEstimate(
+            flops=20 * velocity.size, bytes_accessed=16 * velocity.size, transcendentals=0
+        ),
+        name="spread",
+    )(factors, tree, velocity)
     new_velocity = pl.pallas_call(
         functools.partial(finish_kernel, walls),
         out_shape=jax.ShapeDtypeStruct(velocity.shape, f32),
-        in_specs=in_smem(1) + in_vmem(3 + walls),
+        in_specs=in_smem(1) + in_vmem(2 + walls),
         out_specs=in_hbm(1)[0],
         scratch_shapes=[
             pltpu.VMEM((walls, packed, lanes), f32),
@@ -619,7 +659,7 @@
         ],
         compiler_params=params(),
         name="finish",
-    )(position, factors, tree, velocity, reduced, *others)
+    )(position, particular, response, reduced, *others)
     return (new_velocity, eddy)
 
 

time: 40.9 us -> 40.7 us (level)
  transfers between devices with their start and end apart: 4 -> 4, of which waited for: 3 -> 3; matrix products, arithmetic and copies ran while one was open for 0% -> 0% of each run, Pallas kernels for 7% -> 8%
where the time goes in v15:
time: 40.7 us; the launch traced here: 40.5 us
  blocking collectives  24.9 us (61%)
  Pallas kernels  5.03 us (12%)
  starting transfers between devices  5.01 us (12%)
  waiting for transfers between devices  3.81 us (9%)
  local copies, waits for them, and re-layouts  1.08 us (3%)
  between operations  0.7 us (2%)
    all_to_all x1, blocking collectives, body(): lax.all_to_all(chunks, ('gx', 'gz'), split_axis=0, concat_axis=0, tiled=T...  16.1 us
    all_to_all x1, blocking collectives, body(): lax.all_to_all(eddy_chunks, ('gx', 'gz'), split_axis=0, concat_axis=0, ti...  8.75 us
    ppermute x3, starting transfers between devices, body(): lax.ppermute(reduced, 'gy', [(partner(i, step, walls), i) for i in range(...  4.45 us
    ppermute x3, waiting for transfers between devices, body(): lax.ppermute(reduced, 'gy', [(partner(i, step, walls), i) for i in range(...  3.52 us
    pallas_call x1, Pallas kernels, body(): pl.pallas_call(functools.partial(germano_kernel, nz_parts, width, rows),...  3.03 us
    unnamed x6, local copies, waits for them, and re-layouts  1.07 us
    pallas_call x1, Pallas kernels, body(): pl.pallas_call(functools.partial(finish_kernel, walls), out_shape=jax.Sha...  0.95 us
  transfers between devices with their start and end apart: 4, of which 3 were waited for; matrix products, arithmetic and copies ran while one was open for 0% of the time, Pallas kernels for 8%

profile of v15, /device:TPU:0, one launch (start us, length us, event | category | flops | bytes accessed | tf_op | source)
XLA Modules:
  0.0 40.5 jit_solution(3438292544493859112)
XLA Ops:
  0.6 0.0 copy-start
  0.6 1.1 %copy-done = f32[3,2,192,128]{3,2,1,0:T(8,128)S(1)} copy-done((f32[3,2,192,128]{3,2,1,0:T(8,128)S(1)}, f32[3,2,192,128]{3,2,1,0:T(8,128)}, u32[]{:S(2)}) %copy-start) | copy-done | bytes 589848
  1.7 0.1 pack.1
  1.8 16.1 %all_to_all.10.recv = f32[8,160,128]{2,1,0:T(8,128)S(1)} all-to-all(f32[8,160,128]{2,1,0:T(8,128)S(1)} %pack.1), channel_id=1, replica_groups=mesh['gy'=4,'gx'=4,'gz'=2] {'gx','gz'}, dimensions={0} | all-to-all | bytes 1310720 | tf_op jit(solution)/shard_map/all_to_all | solution.py:577
  17.9 0.6 %collective-permute-start = (f32[8,8,128]{2,1,0:T(8,128)S(1)}, f32[8,8,128]{2,1,0:T(8,128)S(1)}, u32[]{:S(2)}, u32[]{:S(2)}) collective-permute-start(f32[8,8,128]{2,1,0:T(8,128)S(1)} %slice.4), channel_id=1, source_target_pairs={{0,4},{1,9},{2,6},{3,7},{4,0},{5,13},{6,2},{7,3},{8,12},{9,1},{10,... | collective-permute-start | bytes 98312 | tf_op jit(solution)/shard_map/ppermute | solution.py:579
  18.5 3.0 %germano.1.given = f32[8,2,24,128]{3,2,1,0:T(8,128)S(1)} custom-call(s32[1]{0:T(128)} %bitcast.1.rank, s32[1]{0:T(128)S(6)} %rem.18.parity, f32[8,160,128]{2,1,0:T(8,128)S(1)} %all_to_all.10.recv), custom_call_target="tpu_custom_call" | custom-call | flops 14745600 | bytes 786432 | tf_op jit(solution)/shard_map/germano/pallas_call | solution.py:583
  21.5 0.0 copy-start.1
  21.5 0.0 copy-start.2
  21.5 0.3 collective-permute-done.swapped
  21.8 8.8 %all_to_all.11.back = f32[8,2,24,128]{3,2,1,0:T(8,128)S(1)} all-to-all(f32[8,2,24,128]{3,2,1,0:T(8,128)S(1)} %edge.1), channel_id=1, replica_groups=mesh['gy'=4,'gx'=4,'gz'=2] {'gx','gz'}, dimensions={0} | all-to-all | bytes 393216 | tf_op jit(solution)/shard_map/all_to_all | solution.py:611
  30.6 0.0 copy-done.1
  30.6 0.0 copy-done.2
  30.6 0.7 %sweep.1 = (f32[2,192,128]{2,1,0:T(8,128)}, f32[24,128]{1,0:T(8,128)S(1)}, f32[2,24,5,8,128]{4,3,2,1,0:T(8,128)S(1)}, f32[2,3,5,8,128]{4,3,2,1,0:T(8,128)S(1)}) custom-call(s32[1]{0:T(128)S(6)} %rem.18.parity, f32[8,2,24,128]{3,2,1,0:T(8,128)S(1)} %all_to_all.11.back, f32[3,2,192,128]{3,2,1,0:T(8,128)S(1)} %copy-done.1, f32[3,2,192,128]{3,2,1,0:T(8,128)S(1)} %copy-done.2), custom_call_target="tpu_custom_call" | custom-call | tf_op jit(solution)/shard_map/sweep/pallas_call | solution.py:616
  31.3 3.7 %collective-permute-start.3 = (f32[24,128]{1,0:T(8,128)S(1)}, f32[24,128]{1,0:T(8,128)S(1)}, u32[]{:S(2)}, u32[]{:S(2)}) collective-permute-start(f32[24,128]{1,0:T(8,128)S(1)} %get-tuple-element.12.rest_0_), channel_id=1, source_target_pairs={{24,0},{16,8},{8,16},{0,24},{25,1},{17,9},{9,17},{1,25},{26,2},{18... | collective-permute-start | bytes 36872 | tf_op jit(solution)/shard_map/ppermute | solution.py:632
  35.0 0.0 collective-permute-start.2
  35.0 0.8 %collective-permute-start.1 = (f32[24,128]{1,0:T(8,128)S(1)}, f32[24,128]{1,0:T(8,128)S(1)}, u32[]{:S(2)}, u32[]{:S(2)}) collective-permute-start(f32[24,128]{1,0:T(8,128)S(1)} %get-tuple-element.12.rest_0_), channel_id=1, source_target_pairs={{8,0},{0,8},{24,16},{16,24},{9,1},{1,9},{25,17},{17,25},{10,2},{2,... | collective-permute-start | bytes 36872 | tf_op jit(solution)/shard_map/ppermute | solution.py:632
  35.7 0.3 spread.1
  36.0 1.0 %collective-permute-done.3.rest_3_ = f32[24,128]{1,0:T(8,128)S(1)} collective-permute-done((f32[24,128]{1,0:T(8,128)S(1)}, f32[24,128]{1,0:T(8,128)S(1)}, u32[]{:S(2)}, u32[]{:S(2)}) %collective-permute-start.3) | collective-permute-done | bytes 12320 | tf_op jit(solution)/shard_map/ppermute | solution.py:632
  37.0 2.5 %collective-permute-done.2.rest_2_ = f32[24,128]{1,0:T(8,128)S(1)} collective-permute-done((f32[24,128]{1,0:T(8,128)S(1)}, f32[24,128]{1,0:T(8,128)S(1)}, u32[]{:S(2)}, u32[]{:S(2)}) %collective-permute-start.2) | collective-permute-done | bytes 12320 | tf_op jit(solution)/shard_map/ppermute | solution.py:632
  39.6 0.0 collective-permute-done.1.rest_1_
  39.6 1.0 %finish.1 = f32[3,2,192,128]{3,2,1,0:T(8,128)} custom-call(s32[1]{0:T(128)} %bitcast.position, f32[3,2,192,128]{3,2,1,0:T(8,128)S(1)} %get-tuple-element.10.particular, f32[2,2,192,128]{3,2,1,0:T(8,128)S(1)} %get-tuple-element.11.response, f32[24,128]{1,0:T(8,128)S(1)} %get-tuple-element.12.rest_0_, f32[24,128]{1,0:T(8,128)S(1)} %collective-permute-done.1.rest_1_, ...), custom_call_target="tpu_custom_call" | custom-call | tf_op jit(solution)/shard_map/finish/pallas_call | solution.py:649
  (2 shorter events, 0.0 us)
Async XLA Ops:
  0.6 1.1 %copy-start = (f32[3,2,192,128]{3,2,1,0:T(8,128)S(1)}, f32[3,2,192,128]{3,2,1,0:T(8,128)}, u32[]{:S(2)}) copy-start(f32[3,2,192,128]{3,2,1,0:T(8,128)} %velocity.5) | copy-start | bytes 1769476
  17.9 3.9 %collective-permute-start = (f32[8,8,128]{2,1,0:T(8,128)S(1)}, f32[8,8,128]{2,1,0:T(8,128)S(1)}, u32[]{:S(2)}, u32[]{:S(2)}) collective-permute-start(f32[8,8,128]{2,1,0:T(8,128)S(1)} %slice.4), channel_id=1, source_target_pairs={{0,4},{1,9},{2,6},{3,7},{4,0},{5,13},{6,2},{7,3},{8,12},{9,1},{10,... | collective-permute-start | bytes 98312 | tf_op jit(solution)/shard_map/ppermute | solution.py:579
  21.5 9.1 %copy-start.1 = (f32[3,2,192,128]{3,2,1,0:T(8,128)S(1)}, f32[3,2,192,128]{3,2,1,0:T(8,128)}, u32[]{:S(2)}) copy-start(f32[3,2,192,128]{3,2,1,0:T(8,128)} %velocity.5) | copy-start | bytes 1769476
  21.5 9.1 %copy-start.2 = (f32[3,2,192,128]{3,2,1,0:T(8,128)S(1)}, f32[3,2,192,128]{3,2,1,0:T(8,128)}, u32[]{:S(2)}) copy-start(f32[3,2,192,128]{3,2,1,0:T(8,128)} %tendency.1) | copy-start | bytes 1769476
  31.3 5.7 %collective-permute-start.3 = (f32[24,128]{1,0:T(8,128)S(1)}, f32[24,128]{1,0:T(8,128)S(1)}, u32[]{:S(2)}, u32[]{:S(2)}) collective-permute-start(f32[24,128]{1,0:T(8,128)S(1)} %get-tuple-element.12.rest_0_), channel_id=1, source_target_pairs={{24,0},{16,8},{8,16},{0,24},{25,1},{17,9},{9,17},{1,25},{26,2},{18... | collective-permute-start | bytes 36872 | tf_op jit(solution)/shard_map/ppermute | solution.py:632
  35.0 4.6 %collective-permute-start.2 = (f32[24,128]{1,0:T(8,128)S(1)}, f32[24,128]{1,0:T(8,128)S(1)}, u32[]{:S(2)}, u32[]{:S(2)}) collective-permute-start(f32[24,128]{1,0:T(8,128)S(1)} %get-tuple-element.12.rest_0_), channel_id=1, source_target_pairs={{16,0},{24,8},{0,16},{8,24},{17,1},{25,9},{1,17},{9,25},{18,2},{26... | collective-permute-start | bytes 36872 | tf_op jit(solution)/shard_map/ppermute | solution.py:632
  35.0 4.6 %collective-permute-start.1 = (f32[24,128]{1,0:T(8,128)S(1)}, f32[24,128]{1,0:T(8,128)S(1)}, u32[]{:S(2)}, u32[]{:S(2)}) collective-permute-start(f32[24,128]{1,0:T(8,128)S(1)} %get-tuple-element.12.rest_0_), channel_id=1, source_target_pairs={{8,0},{0,8},{24,16},{16,24},{9,1},{1,9},{25,17},{17,25},{10,2},{2,... | collective-permute-start | bytes 36872 | tf_op jit(solution)/shard_map/ppermute | solution.py:632

commit v16 on v15

--- a/solution.py
+++ b/solution.py
@@ -353,7 +353,7 @@
             out[k, x] = coefficient * mag[x0 + x, zb]
 
 
-def sweep_kernel(parity, back, velocity, tendency, eddy_out, reduced, factors, tree, eddy, sent):
+def sweep_kernel(parity, back, velocity, tendency, eddy, reduced, factors, tree):
     count, width, rows, _ = back.shape
     length = count * rows // SEGMENTS
 
@@ -362,8 +362,6 @@
             eddy[x, place * rows : (place + 1) * rows, :] = back[rank, x]
 
     by_parity(parity, count, fill)
-    write = pltpu.make_async_copy(eddy, eddy_out, sent)
-    write.start()
 
     def row(ref, index, j):
         return ref[(*index, pl.ds(j, SEGMENTS, stride=length), slice(None))]
@@ -442,10 +440,11 @@
         rows_out.append(visc[last_row][x][SEGMENTS - 1 :, :])
         for i, v in enumerate(rows_out):
             reduced[i * width + x : i * width + x + 1, :] = v
-    write.wait()
-
-
-def spread_kernel(factors, tree, velocity, particular, response):
+
+
+def spread_kernel(factors, tree, velocity, eddy, particular, response, eddy_out, sent):
+    write = pltpu.make_async_copy(eddy, eddy_out, sent)
+    write.start()
     width, length = factors.shape[:2]
     levels = tree.shape[1]
     sublane = lax.broadcasted_iota(jnp.int32, (SEGMENTS, LANES), 0)
@@ -476,6 +475,7 @@
                 else:
                     response[n - 3, x, rows, :] = value
                 values[n][x] = value
+    write.wait()
 
 
 def partner(i, step, count):
@@ -494,33 +494,28 @@
     def part(device, i):
         return gathered[device, i * width : (i + 1) * width, :]
 
-    ratios, values = [], []
+    pivots, sources = [], []
     for i in range(devices + 1):
-        if i == 0:
-            link = 750.0 * part(0, 9)
-            total = part(0, 6)
-            source = [-part(0, c) for c in range(3)]
-        elif i == devices:
-            link = 750.0 * part(i - 1, 10)
-            total = part(i - 1, 8)
-            source = [part(i - 1, 3 + c) for c in range(3)]
-        else:
-            link = 750.0 * (part(i - 1, 10) + part(i, 9))
-            total = part(i - 1, 8) + part(i, 6)
-            source = [part(i - 1, 3 + c) - part(i, c) for c in range(3)]
-        pivot = 1.0 + link * total
-        if i > 0:
-            before = part(i - 1, 7)
-            pivot = pivot - link * before * ratios[-1]
-            source = [s + before * v for s, v in zip(source, values[-1])]
-        scale = link / pivot
-        values.append([scale * s for s in source])
+        visc = [part(i - 1, 10)] if i > 0 else []
+        total = [part(i - 1, 8)] if i > 0 else []
+        source = [part(i - 1, 3 + c) for c in range(3)] if i > 0 else [0.0] * 3
         if i < devices:
-            ratios.append(scale * part(i, 7))
-    flux = values[devices]
+            visc.append(part(i, 9))
+            total.append(part(i, 6))
+            source = [s - part(i, c) for c, s in enumerate(source)]
+        pivots.append(sum(total) + 1.0 / (750.0 * sum(visc)))
+        sources.append(source)
+    across = [part(i, 7) for i in range(devices)]
+    minors = [jnp.ones_like(pivots[0]), pivots[0]]
+    for i in range(1, devices + 1):
+        minors.append(pivots[i] * minors[i] - (across[i - 1] * across[i - 1]) * minors[i - 1])
+    inverses = [minors[i] / minors[i + 1] for i in range(devices + 1)]
+    ratios = [b * r for b, r in zip(across, inverses)]
+    for i in range(1, devices + 1):
+        sources[i] = [s + ratios[i - 1] * t for s, t in zip(sources[i], sources[i - 1])]
     for i in range(devices, -1, -1):
-        if i < devices:
-            flux = [v + ratios[i] * f for v, f in zip(values[i], flux)]
+        flux_here = [inverses[i] * s for s in sources[i]]
+        flux = flux_here if i == devices else [f + ratios[i] * g for f, g in zip(flux_here, flux)]
         for c in range(3):
             fluxes[i, c * width : (c + 1) * width, :] = flux[c]
 
@@ -613,7 +608,7 @@
     length = cells // SEGMENTS
     levels = SEGMENTS.bit_length() - 1
     packed = aligned(11 * width)
-    eddy, reduced, factors, tree = pl.pallas_call(
+    eddy_here, reduced, factors, tree = pl.pallas_call(
         sweep_kernel,
         out_shape=(
             jax.ShapeDtypeStruct((width, cells, lanes), f32),
@@ -622,8 +617,7 @@
             jax.ShapeDtypeStruct((width, levels, 5, SEGMENTS, lanes), f32),
         ),
         in_specs=in_smem(1) + in_vmem(3),
-        out_specs=tuple(in_hbm(1) + in_vmem(3)),
-        scratch_shapes=[pltpu.VMEM((width, cells, lanes), f32), pltpu.SemaphoreType.DMA],
+        out_specs=tuple(in_vmem(4)),
         compiler_params=params(),
         name="sweep",
     )(parity, back, velocity, tendency)
@@ -632,20 +626,22 @@
         lax.ppermute(reduced, "gy", [(partner(i, step, walls), i) for i in range(walls)])
         for step in range(1, walls)
     ]
-    particular, response = pl.pallas_call(
+    particular, response, eddy = pl.pallas_call(
         spread_kernel,
         out_shape=(
             jax.ShapeDtypeStruct(velocity.shape, f32),
             jax.ShapeDtypeStruct((2, *velocity.shape[1:]), f32),
+            jax.ShapeDtypeStruct(eddy_here.shape, f32),
         ),
-        in_specs=in_vmem(3),
-        out_specs=tuple(in_vmem(2)),
+        in_specs=in_vmem(4),
+        out_specs=tuple(in_vmem(2) + in_hbm(1)),
+        scratch_shapes=[pltpu.SemaphoreType.DMA],
         compiler_params=params(),
         cost_estimate=pl.CostEstimate(
             flops=20 * velocity.size, bytes_accessed=16 * velocity.size, transcendentals=0
         ),
         name="spread",
-    )(factors, tree, velocity)
+    )(factors, tree, velocity, eddy_here)
     new_velocity = pl.pallas_call(
         functools.partial(finish_kernel, walls),
         out_shape=jax.ShapeDtypeStruct(velocity.shape, f32),

time: 40.7 us -> 40.4 us (level)
  waiting for transfers between devices: 3.81 us -> 3.4 us
    ppermute x3, waiting for transfers between devices: 3.52 us -> 3.11 us  [body(): lax.ppermute(reduced, 'gy', [(partner(i, step, walls), i) for i in range(...]
    pallas_call x1, Pallas kernels: 0.27 us -> 0.68 us  [body(): pl.pallas_call(spread_kernel, out_shape=(jax.ShapeDtypeStruct(velocity.sh...]
  transfers between devices with their start and end apart: 4 -> 4, of which waited for: 3 -> 3; matrix products, arithmetic and copies ran while one was open for 0% -> 0% of each run, Pallas kernels for 8% -> 9%
where the time goes in v16:
time: 40.4 us; the launch traced here: 40.2 us
  blocking collectives  24.9 us (62%)
  Pallas kernels  5.12 us (13%)
  starting transfers between devices  5.01 us (12%)
  waiting for transfers between devices  3.4 us (8%)
  local copies, waits for them, and re-layouts  1.08 us (3%)
  between operations  0.69 us (2%)
    all_to_all x1, blocking collectives, body(): lax.all_to_all(chunks, ('gx', 'gz'), split_axis=0, concat_axis=0, tiled=T...  16.1 us
    all_to_all x1, blocking collectives, body(): lax.all_to_all(eddy_chunks, ('gx', 'gz'), split_axis=0, concat_axis=0, ti...  8.75 us
    ppermute x3, starting transfers between devices, body(): lax.ppermute(reduced, 'gy', [(partner(i, step, walls), i) for i in range(...  4.45 us
    ppermute x3, waiting for transfers between devices, body(): lax.ppermute(reduced, 'gy', [(partner(i, step, walls), i) for i in range(...  3.11 us
    pallas_call x1, Pallas kernels, body(): pl.pallas_call(functools.partial(germano_kernel, nz_parts, width, rows),...  3.03 us
    unnamed x6, local copies, waits for them, and re-layouts  1.07 us
    pallas_call x1, Pallas kernels, body(): pl.pallas_call(functools.partial(finish_kernel, walls), out_shape=jax.Sha...  0.93 us
  transfers between devices with their start and end apart: 4, of which 3 were waited for; matrix products, arithmetic and copies ran while one was open for 0% of the time, Pallas kernels for 9%

profile of v16, /device:TPU:0, one launch (start us, length us, event | category | flops | bytes accessed | tf_op | source)
XLA Modules:
  0.0 40.2 jit_solution(6979937992465889021)
XLA Ops:
  0.6 0.0 copy-start
  0.6 1.1 %copy-done = f32[3,2,192,128]{3,2,1,0:T(8,128)S(1)} copy-done((f32[3,2,192,128]{3,2,1,0:T(8,128)S(1)}, f32[3,2,192,128]{3,2,1,0:T(8,128)}, u32[]{:S(2)}) %copy-start) | copy-done | bytes 589848
  1.7 0.1 pack.1
  1.8 16.1 %all_to_all.10.recv = f32[8,160,128]{2,1,0:T(8,128)S(1)} all-to-all(f32[8,160,128]{2,1,0:T(8,128)S(1)} %pack.1), channel_id=1, replica_groups=mesh['gy'=4,'gx'=4,'gz'=2] {'gx','gz'}, dimensions={0} | all-to-all | bytes 1310720 | tf_op jit(solution)/shard_map/all_to_all | solution.py:572
  17.9 0.6 %collective-permute-start = (f32[8,8,128]{2,1,0:T(8,128)S(1)}, f32[8,8,128]{2,1,0:T(8,128)S(1)}, u32[]{:S(2)}, u32[]{:S(2)}) collective-permute-start(f32[8,8,128]{2,1,0:T(8,128)S(1)} %slice.4), channel_id=1, source_target_pairs={{0,4},{1,9},{2,6},{3,7},{4,0},{5,13},{6,2},{7,3},{8,12},{9,1},{10,... | collective-permute-start | bytes 98312 | tf_op jit(solution)/shard_map/ppermute | solution.py:574
  18.5 3.0 %germano.1.given = f32[8,2,24,128]{3,2,1,0:T(8,128)S(1)} custom-call(s32[1]{0:T(128)} %bitcast.1.rank, s32[1]{0:T(128)S(6)} %rem.18.parity, f32[8,160,128]{2,1,0:T(8,128)S(1)} %all_to_all.10.recv), custom_call_target="tpu_custom_call" | custom-call | flops 14745600 | bytes 786432 | tf_op jit(solution)/shard_map/germano/pallas_call | solution.py:578
  21.5 0.0 copy-start.1
  21.5 0.0 copy-start.2
  21.5 0.3 collective-permute-done.swapped
  21.8 8.8 %all_to_all.11.back = f32[8,2,24,128]{3,2,1,0:T(8,128)S(1)} all-to-all(f32[8,2,24,128]{3,2,1,0:T(8,128)S(1)} %edge.1), channel_id=1, replica_groups=mesh['gy'=4,'gx'=4,'gz'=2] {'gx','gz'}, dimensions={0} | all-to-all | bytes 393216 | tf_op jit(solution)/shard_map/all_to_all | solution.py:606
  30.6 0.0 copy-done.1
  30.6 0.0 copy-done.2
  30.6 0.4 sweep.1
  31.0 3.7 %collective-permute-start.3 = (f32[24,128]{1,0:T(8,128)S(1)}, f32[24,128]{1,0:T(8,128)S(1)}, u32[]{:S(2)}, u32[]{:S(2)}) collective-permute-start(f32[24,128]{1,0:T(8,128)S(1)} %get-tuple-element.14.rest_0_), channel_id=1, source_target_pairs={{24,0},{16,8},{8,16},{0,24},{25,1},{17,9},{9,17},{1,25},{26,2},{18... | collective-permute-start | bytes 36872 | tf_op jit(solution)/shard_map/ppermute | solution.py:626
  34.6 0.0 collective-permute-start.2
  34.7 0.8 %collective-permute-start.1 = (f32[24,128]{1,0:T(8,128)S(1)}, f32[24,128]{1,0:T(8,128)S(1)}, u32[]{:S(2)}, u32[]{:S(2)}) collective-permute-start(f32[24,128]{1,0:T(8,128)S(1)} %get-tuple-element.14.rest_0_), channel_id=1, source_target_pairs={{8,0},{0,8},{24,16},{16,24},{9,1},{1,9},{25,17},{17,25},{10,2},{2,... | collective-permute-start | bytes 36872 | tf_op jit(solution)/shard_map/ppermute | solution.py:626
  35.4 0.7 %spread.1 = (f32[3,2,192,128]{3,2,1,0:T(8,128)S(1)}, f32[2,2,192,128]{3,2,1,0:T(8,128)S(1)}, f32[2,192,128]{2,1,0:T(8,128)}) custom-call(f32[2,24,5,8,128]{4,3,2,1,0:T(8,128)S(1)} %get-tuple-element.9.factors, f32[2,3,5,8,128]{4,3,2,1,0:T(8,128)S(1)} %get-tuple-element.10.tree, f32[3,2,192,128]{3,2,1,0:T(8,128)S(1)} %copy-done.1, ...), custom_call_target="tpu_custom_call" | custom-call | flops 2949120 | bytes 2359296 | tf_op jit(solution)/shard_map/spread/pallas_call | solution.py:629
  36.1 0.6 %collective-permute-done.3.rest_3_ = f32[24,128]{1,0:T(8,128)S(1)} collective-permute-done((f32[24,128]{1,0:T(8,128)S(1)}, f32[24,128]{1,0:T(8,128)S(1)}, u32[]{:S(2)}, u32[]{:S(2)}) %collective-permute-start.3) | collective-permute-done | bytes 12320 | tf_op jit(solution)/shard_map/ppermute | solution.py:626
  36.7 2.5 %collective-permute-done.2.rest_2_ = f32[24,128]{1,0:T(8,128)S(1)} collective-permute-done((f32[24,128]{1,0:T(8,128)S(1)}, f32[24,128]{1,0:T(8,128)S(1)}, u32[]{:S(2)}, u32[]{:S(2)}) %collective-permute-start.2) | collective-permute-done | bytes 12320 | tf_op jit(solution)/shard_map/ppermute | solution.py:626
  39.2 0.0 collective-permute-done.1.rest_1_
  39.2 0.9 %finish.1 = f32[3,2,192,128]{3,2,1,0:T(8,128)} custom-call(s32[1]{0:T(128)} %bitcast.position, f32[3,2,192,128]{3,2,1,0:T(8,128)S(1)} %get-tuple-element.12.particular, f32[2,2,192,128]{3,2,1,0:T(8,128)S(1)} %get-tuple-element.13.response, f32[24,128]{1,0:T(8,128)S(1)} %get-tuple-element.14.rest_0_, f32[24,128]{1,0:T(8,128)S(1)} %collective-permute-done.1.rest_1_, ...), custom_call_target="tpu_custom_call" | custom-call | tf_op jit(solution)/shard_map/finish/pallas_call | solution.py:645
  (2 shorter events, 0.0 us)
Async XLA Ops:
  0.6 1.1 %copy-start = (f32[3,2,192,128]{3,2,1,0:T(8,128)S(1)}, f32[3,2,192,128]{3,2,1,0:T(8,128)}, u32[]{:S(2)}) copy-start(f32[3,2,192,128]{3,2,1,0:T(8,128)} %velocity.5) | copy-start | bytes 1769476
  17.9 3.9 %collective-permute-start = (f32[8,8,128]{2,1,0:T(8,128)S(1)}, f32[8,8,128]{2,1,0:T(8,128)S(1)}, u32[]{:S(2)}, u32[]{:S(2)}) collective-permute-start(f32[8,8,128]{2,1,0:T(8,128)S(1)} %slice.4), channel_id=1, source_target_pairs={{0,4},{1,9},{2,6},{3,7},{4,0},{5,13},{6,2},{7,3},{8,12},{9,1},{10,... | collective-permute-start | bytes 98312 | tf_op jit(solution)/shard_map/ppermute | solution.py:574
  21.5 9.1 %copy-start.1 = (f32[3,2,192,128]{3,2,1,0:T(8,128)S(1)}, f32[3,2,192,128]{3,2,1,0:T(8,128)}, u32[]{:S(2)}) copy-start(f32[3,2,192,128]{3,2,1,0:T(8,128)} %velocity.5) | copy-start | bytes 1769476
  21.5 9.1 %copy-start.2 = (f32[3,2,192,128]{3,2,1,0:T(8,128)S(1)}, f32[3,2,192,128]{3,2,1,0:T(8,128)}, u32[]{:S(2)}) copy-start(f32[3,2,192,128]{3,2,1,0:T(8,128)} %tendency.1) | copy-start | bytes 1769476
  31.0 5.7 %collective-permute-start.3 = (f32[24,128]{1,0:T(8,128)S(1)}, f32[24,128]{1,0:T(8,128)S(1)}, u32[]{:S(2)}, u32[]{:S(2)}) collective-permute-start(f32[24,128]{1,0:T(8,128)S(1)} %get-tuple-element.14.rest_0_), channel_id=1, source_target_pairs={{24,0},{16,8},{8,16},{0,24},{25,1},{17,9},{9,17},{1,25},{26,2},{18... | collective-permute-start | bytes 36872 | tf_op jit(solution)/shard_map/ppermute | solution.py:626
  34.6 4.6 %collective-permute-start.2 = (f32[24,128]{1,0:T(8,128)S(1)}, f32[24,128]{1,0:T(8,128)S(1)}, u32[]{:S(2)}, u32[]{:S(2)}) collective-permute-start(f32[24,128]{1,0:T(8,128)S(1)} %get-tuple-element.14.rest_0_), channel_id=1, source_target_pairs={{16,0},{24,8},{0,16},{8,24},{17,1},{25,9},{1,17},{9,25},{18,2},{26... | collective-permute-start | bytes 36872 | tf_op jit(solution)/shard_map/ppermute | solution.py:626
  34.7 4.6 %collective-permute-start.1 = (f32[24,128]{1,0:T(8,128)S(1)}, f32[24,128]{1,0:T(8,128)S(1)}, u32[]{:S(2)}, u32[]{:S(2)}) collective-permute-start(f32[24,128]{1,0:T(8,128)S(1)} %get-tuple-element.14.rest_0_), channel_id=1, source_target_pairs={{8,0},{0,8},{24,16},{16,24},{9,1},{1,9},{25,17},{17,25},{10,2},{2,... | collective-permute-start | bytes 36872 | tf_op jit(solution)/shard_map/ppermute | solution.py:626

commit v17 on v16

--- a/solution.py
+++ b/solution.py
@@ -478,6 +478,51 @@
     write.wait()
 
 
+def sources_of(step, count):
+    ring = [0, *range(1, count, 2), *range(count - 2 + count % 2, 0, -2)]
+    return [ring[(ring.index(i) - step) % count] for i in range(count)]
+
+
+def exchange_order(count):
+    return [1, *range(count - 1, 1, -1)]
+
+
+def spread_kernel(factors, tree, velocity, eddy, particular, response, eddy_out, sent):
+    write = pltpu.make_async_copy(eddy, eddy_out, sent)
+    write.start()
+    width, length = factors.shape[:2]
+    levels = tree.shape[1]
+    sublane = lax.broadcasted_iota(jnp.int32, (SEGMENTS, LANES), 0)
+    one, zero = (jnp.full((SEGMENTS, LANES), v, jnp.float32) for v in (1.0, 0.0))
+    sides = [(c, zero, zero) for c in range(3)] + [(None, one, zero), (None, zero, one)]
+    lefts = [[side[1]] * width for side in sides]
+    rights = [[side[2]] * width for side in sides]
+    for level in range(levels - 1, -1, -1):
+        step = 2**level
+        second = lax.rem(sublane, 2 * step) == step
+        for n, (c, _, _) in enumerate(sides):
+            for x in range(width):
+                left, right = lefts[n][x], rights[n][x]
+                through = tree[x, level, 3] * left - tree[x, level, 4] * right
+                if c is not None:
+                    through = tree[x, level, c] + through
+                lefts[n][x] = jnp.where(second, pltpu.roll(through, step, 0), left)
+                rights[n][x] = jnp.where(second, pltpu.roll(right, step, 0), -through)
+    values = rights
+    for j in range(length - 1, -1, -1):
+        rows = pl.ds(j, SEGMENTS, stride=length)
+        for n, (c, _, _) in enumerate(sides):
+            for x in range(width):
+                value = factors[x, j, 3] * lefts[n][x] + factors[x, j, 4] * values[n][x]
+                if c is not None:
+                    value = factors[x, j, c] + value
+                    particular[c, x, rows, :] = value - velocity[c, x, rows, :]
+                else:
+                    response[n - 3, x, rows, :] = value
+                values[n][x] = value
+    write.wait()
+
+
 def partner(i, step, count):
     if count & (count - 1) == 0:
         return i ^ step
@@ -488,8 +533,9 @@
     reduced, (result, gathered, fluxes, out, sent) = rest[:devices], rest[devices:]
     width = particular.shape[1]
     here = position[0]
-    for step in range(devices):
-        gathered[partner(here, step, devices)] = reduced[step][...]
+    for step, ref in zip([0, *exchange_order(devices)], reduced):
+        source = sum(jnp.where(here == i, s, 0) for i, s in enumerate(sources_of(step, devices)))
+        gathered[source] = ref[...]
 
     def part(device, i):
         return gathered[device, i * width : (i + 1) * width, :]
@@ -623,8 +669,8 @@
     )(parity, back, velocity, tendency)
 
     others = [
-        lax.ppermute(reduced, "gy", [(partner(i, step, walls), i) for i in range(walls)])
-        for step in range(1, walls)
+        lax.ppermute(reduced, "gy", [(s, i) for i, s in enumerate(sources_of(step, walls))])
+        for step in exchange_order(walls)
     ]
     particular, response, eddy = pl.pallas_call(
         spread_kernel,

time: 40.4 us -> 40.4 us (level)
  starting transfers between devices: 5.01 us -> 6.25 us
  waiting for transfers between devices: 3.4 us -> 2.16 us
    ppermute x3, waiting for transfers between devices: 3.11 us -> 1.87 us  [body(): lax.ppermute(reduced, 'gy', [(s, i) for i, s in enumerate(sources_of(step...]
    ppermute x3, starting transfers between devices: 4.45 us -> 5.69 us  [body(): lax.ppermute(reduced, 'gy', [(s, i) for i, s in enumerate(sources_of(step...]
where the time goes in v17:
time: 40.4 us; the launch traced here: 40.2 us
  blocking collectives  24.9 us (62%)
  starting transfers between devices  6.25 us (15%)
  Pallas kernels  5.12 us (13%)
  waiting for transfers between devices  2.16 us (5%)
  local copies, waits for them, and re-layouts  1.08 us (3%)
  between operations  0.7 us (2%)
    all_to_all x1, blocking collectives, body(): lax.all_to_all(chunks, ('gx', 'gz'), split_axis=0, concat_axis=0, tiled=T...  16.1 us
    all_to_all x1, blocking collectives, body(): lax.all_to_all(eddy_chunks, ('gx', 'gz'), split_axis=0, concat_axis=0, ti...  8.75 us
    ppermute x3, starting transfers between devices, body(): lax.ppermute(reduced, 'gy', [(s, i) for i, s in enumerate(sources_of(step...  5.69 us
    pallas_call x1, Pallas kernels, body(): pl.pallas_call(functools.partial(germano_kernel, nz_parts, width, rows),...  3.03 us
    ppermute x3, waiting for transfers between devices, body(): lax.ppermute(reduced, 'gy', [(s, i) for i, s in enumerate(sources_of(step...  1.87 us
    unnamed x6, local copies, waits for them, and re-layouts  1.07 us
    pallas_call x1, Pallas kernels, body(): pl.pallas_call(functools.partial(finish_kernel, walls), out_shape=jax.Sha...  0.93 us
  transfers between devices with their start and end apart: 4, of which 3 were waited for; matrix products, arithmetic and copies ran while one was open for 0% of the time, Pallas kernels for 9%

profile of v17, /device:TPU:0, one launch (start us, length us, event | category | flops | bytes accessed | tf_op | source)
XLA Modules:
  0.0 40.2 jit_solution(8165270973164230557)
XLA Ops:
  0.6 0.0 copy-start
  0.6 1.1 %copy-done = f32[3,2,192,128]{3,2,1,0:T(8,128)S(1)} copy-done((f32[3,2,192,128]{3,2,1,0:T(8,128)S(1)}, f32[3,2,192,128]{3,2,1,0:T(8,128)}, u32[]{:S(2)}) %copy-start) | copy-done | bytes 589848
  1.7 0.1 pack.1
  1.8 16.1 %all_to_all.10.recv = f32[8,160,128]{2,1,0:T(8,128)S(1)} all-to-all(f32[8,160,128]{2,1,0:T(8,128)S(1)} %pack.1), channel_id=1, replica_groups=mesh['gy'=4,'gx'=4,'gz'=2] {'gx','gz'}, dimensions={0} | all-to-all | bytes 1310720 | tf_op jit(solution)/shard_map/all_to_all | solution.py:618
  17.9 0.6 %collective-permute-start = (f32[8,8,128]{2,1,0:T(8,128)S(1)}, f32[8,8,128]{2,1,0:T(8,128)S(1)}, u32[]{:S(2)}, u32[]{:S(2)}) collective-permute-start(f32[8,8,128]{2,1,0:T(8,128)S(1)} %slice.4), channel_id=1, source_target_pairs={{0,4},{1,9},{2,6},{3,7},{4,0},{5,13},{6,2},{7,3},{8,12},{9,1},{10,... | collective-permute-start | bytes 98312 | tf_op jit(solution)/shard_map/ppermute | solution.py:620
  18.5 3.0 %germano.1.given = f32[8,2,24,128]{3,2,1,0:T(8,128)S(1)} custom-call(s32[1]{0:T(128)} %bitcast.1.rank, s32[1]{0:T(128)S(6)} %rem.18.parity, f32[8,160,128]{2,1,0:T(8,128)S(1)} %all_to_all.10.recv), custom_call_target="tpu_custom_call" | custom-call | flops 14745600 | bytes 786432 | tf_op jit(solution)/shard_map/germano/pallas_call | solution.py:624
  21.5 0.0 copy-start.1
  21.5 0.0 copy-start.2
  21.5 0.3 collective-permute-done.swapped
  21.8 8.8 %all_to_all.11.back = f32[8,2,24,128]{3,2,1,0:T(8,128)S(1)} all-to-all(f32[8,2,24,128]{3,2,1,0:T(8,128)S(1)} %edge.1), channel_id=1, replica_groups=mesh['gy'=4,'gx'=4,'gz'=2] {'gx','gz'}, dimensions={0} | all-to-all | bytes 393216 | tf_op jit(solution)/shard_map/all_to_all | solution.py:652
  30.6 0.0 copy-done.1
  30.6 0.0 copy-done.2
  30.6 0.4 sweep.1
  31.0 3.7 %collective-permute-start.3 = (f32[24,128]{1,0:T(8,128)S(1)}, f32[24,128]{1,0:T(8,128)S(1)}, u32[]{:S(2)}, u32[]{:S(2)}) collective-permute-start(f32[24,128]{1,0:T(8,128)S(1)} %get-tuple-element.14.rest_0_), channel_id=1, source_target_pairs={{24,0},{16,8},{8,16},{0,24},{25,1},{17,9},{9,17},{1,25},{26,2},{18... | collective-permute-start | bytes 36872 | tf_op jit(solution)/shard_map/ppermute | solution.py:672
  34.6 0.0 collective-permute-start.2
  34.7 2.0 %collective-permute-start.1 = (f32[24,128]{1,0:T(8,128)S(1)}, f32[24,128]{1,0:T(8,128)S(1)}, u32[]{:S(2)}, u32[]{:S(2)}) collective-permute-start(f32[24,128]{1,0:T(8,128)S(1)} %get-tuple-element.14.rest_0_), channel_id=1, source_target_pairs={{16,0},{0,8},{24,16},{8,24},{17,1},{1,9},{25,17},{9,25},{18,2},{2,... | collective-permute-start | bytes 36872 | tf_op jit(solution)/shard_map/ppermute | solution.py:672
  36.7 0.7 %spread.1 = (f32[3,2,192,128]{3,2,1,0:T(8,128)S(1)}, f32[2,2,192,128]{3,2,1,0:T(8,128)S(1)}, f32[2,192,128]{2,1,0:T(8,128)}) custom-call(f32[2,24,5,8,128]{4,3,2,1,0:T(8,128)S(1)} %get-tuple-element.9.factors, f32[2,3,5,8,128]{4,3,2,1,0:T(8,128)S(1)} %get-tuple-element.10.tree, f32[3,2,192,128]{3,2,1,0:T(8,128)S(1)} %copy-done.1, ...), custom_call_target="tpu_custom_call" | custom-call | flops 2949120 | bytes 2359296 | tf_op jit(solution)/shard_map/spread/pallas_call | solution.py:675
  37.4 0.0 collective-permute-done.3.rest_3_
  37.4 1.0 %collective-permute-done.2.rest_2_ = f32[24,128]{1,0:T(8,128)S(1)} collective-permute-done((f32[24,128]{1,0:T(8,128)S(1)}, f32[24,128]{1,0:T(8,128)S(1)}, u32[]{:S(2)}, u32[]{:S(2)}) %collective-permute-start.2) | collective-permute-done | bytes 12320 | tf_op jit(solution)/shard_map/ppermute | solution.py:672
  38.3 0.9 %collective-permute-done.1.rest_1_ = f32[24,128]{1,0:T(8,128)S(1)} collective-permute-done((f32[24,128]{1,0:T(8,128)S(1)}, f32[24,128]{1,0:T(8,128)S(1)}, u32[]{:S(2)}, u32[]{:S(2)}) %collective-permute-start.1) | collective-permute-done | bytes 12320 | tf_op jit(solution)/shard_map/ppermute | solution.py:672
  39.2 0.9 %finish.1 = f32[3,2,192,128]{3,2,1,0:T(8,128)} custom-call(s32[1]{0:T(128)} %bitcast.position, f32[3,2,192,128]{3,2,1,0:T(8,128)S(1)} %get-tuple-element.12.particular, f32[2,2,192,128]{3,2,1,0:T(8,128)S(1)} %get-tuple-element.13.response, f32[24,128]{1,0:T(8,128)S(1)} %get-tuple-element.14.rest_0_, f32[24,128]{1,0:T(8,128)S(1)} %collective-permute-done.1.rest_1_, ...), custom_call_target="tpu_custom_call" | custom-call | tf_op jit(solution)/shard_map/finish/pallas_call | solution.py:691
  (2 shorter events, 0.0 us)
Async XLA Ops:
  0.6 1.1 %copy-start = (f32[3,2,192,128]{3,2,1,0:T(8,128)S(1)}, f32[3,2,192,128]{3,2,1,0:T(8,128)}, u32[]{:S(2)}) copy-start(f32[3,2,192,128]{3,2,1,0:T(8,128)} %velocity.5) | copy-start | bytes 1769476
  17.9 3.9 %collective-permute-start = (f32[8,8,128]{2,1,0:T(8,128)S(1)}, f32[8,8,128]{2,1,0:T(8,128)S(1)}, u32[]{:S(2)}, u32[]{:S(2)}) collective-permute-start(f32[8,8,128]{2,1,0:T(8,128)S(1)} %slice.4), channel_id=1, source_target_pairs={{0,4},{1,9},{2,6},{3,7},{4,0},{5,13},{6,2},{7,3},{8,12},{9,1},{10,... | collective-permute-start | bytes 98312 | tf_op jit(solution)/shard_map/ppermute | solution.py:620
  21.5 9.1 %copy-start.1 = (f32[3,2,192,128]{3,2,1,0:T(8,128)S(1)}, f32[3,2,192,128]{3,2,1,0:T(8,128)}, u32[]{:S(2)}) copy-start(f32[3,2,192,128]{3,2,1,0:T(8,128)} %velocity.5) | copy-start | bytes 1769476
  21.5 9.1 %copy-start.2 = (f32[3,2,192,128]{3,2,1,0:T(8,128)S(1)}, f32[3,2,192,128]{3,2,1,0:T(8,128)}, u32[]{:S(2)}) copy-start(f32[3,2,192,128]{3,2,1,0:T(8,128)} %tendency.1) | copy-start | bytes 1769476
  31.0 6.4 %collective-permute-start.3 = (f32[24,128]{1,0:T(8,128)S(1)}, f32[24,128]{1,0:T(8,128)S(1)}, u32[]{:S(2)}, u32[]{:S(2)}) collective-permute-start(f32[24,128]{1,0:T(8,128)S(1)} %get-tuple-element.14.rest_0_), channel_id=1, source_target_pairs={{24,0},{16,8},{8,16},{0,24},{25,1},{17,9},{9,17},{1,25},{26,2},{18... | collective-permute-start | bytes 36872 | tf_op jit(solution)/shard_map/ppermute | solution.py:672
  34.6 3.7 %collective-permute-start.2 = (f32[24,128]{1,0:T(8,128)S(1)}, f32[24,128]{1,0:T(8,128)S(1)}, u32[]{:S(2)}, u32[]{:S(2)}) collective-permute-start(f32[24,128]{1,0:T(8,128)S(1)} %get-tuple-element.14.rest_0_), channel_id=1, source_target_pairs={{8,0},{24,8},{0,16},{16,24},{9,1},{25,9},{1,17},{17,25},{10,2},{26... | collective-permute-start | bytes 36872 | tf_op jit(solution)/shard_map/ppermute | solution.py:672
  34.7 4.6 %collective-permute-start.1 = (f32[24,128]{1,0:T(8,128)S(1)}, f32[24,128]{1,0:T(8,128)S(1)}, u32[]{:S(2)}, u32[]{:S(2)}) collective-permute-start(f32[24,128]{1,0:T(8,128)S(1)} %get-tuple-element.14.rest_0_), channel_id=1, source_target_pairs={{16,0},{0,8},{24,16},{8,24},{17,1},{1,9},{25,17},{9,25},{18,2},{2,... | collective-permute-start | bytes 36872 | tf_op jit(solution)/shard_map/ppermute | solution.py:672

commit v18 on v17

--- a/solution.py
+++ b/solution.py
@@ -260,8 +260,6 @@
     blocks = range(nz_parts)
     lead = 8
     inner = slice(lead, lead + rows)
-    lower = slice(lead - 1, lead - 1 + rows)
-    upper = slice(lead + 1, lead + 1 + rows)
     for k in range(count):
         x0, zb = (k // nz_parts) * width, k % nz_parts
         for c in range(3):
@@ -277,8 +275,15 @@
                     vel[c, x0 + x, zb, at : at + 1, :] = edge
                     ends[c, x0 + x, zb, side : side + 1, :] = edge
 
-    for x in range(nx):
+    tile = min(rows, 8)
+    tiles = [slice(t, t + tile) for t in range(0, rows, tile)]
+
+    def moved(own, by):
+        return slice(lead + own.start + by, lead + own.stop + by)
+
+    for x, own in [(x, own) for x in range(nx) for own in tiles]:
         left, right = (x - 1) % nx, (x + 1) % nx
+        inner, lower, upper = (moved(own, by) for by in (0, -1, 1))
         centre = [[vel[c, x, zb, inner, :] for zb in blocks] for c in range(3)]
         grad_x = [[vel[c, right, zb, inner, :] - vel[c, left, zb, inner, :] for zb in blocks] for c in range(3)]
         grad_y = [[vel[c, x, zb, upper, :] - vel[c, x, zb, lower, :] for zb in blocks] for c in range(3)]
@@ -287,14 +292,14 @@
             down, up = beside(centre[c])
             grad_z.append([u - d for u, d in zip(up, down)])
             for zb in blocks:
-                part[c, x, zb] = (up[zb] + down[zb]) + 2.0 * centre[c][zb]
+                part[c, x, zb, own, :] = (up[zb] + down[zb]) + 2.0 * centre[c][zb]
         strain = [
             strain_parts(*([g[c][zb] for c in range(3)] for g in (grad_x, grad_y, grad_z)))
             for zb in blocks
         ]
         size = [strain_size(s) for s in strain]
         for zb in blocks:
-            mag[x, zb] = size[zb]
+            mag[x, zb, own, :] = size[zb]
         pairs = [products([centre[c][zb] for c in range(3)]) for zb in blocks]
         for i in range(6):
             for base, fields in (
@@ -302,7 +307,7 @@
                 (9, [size[zb] * strain[zb][i] for zb in blocks]),
             ):
                 for zb, f in enumerate(smooth_z(fields)):
-                    part[base + i, x, zb] = f
+                    part[base + i, x, zb, own, :] = f
 
     def smooth_x(read, x):
         return (read((x - 1) % nx) + read((x + 1) % nx)) + 2.0 * read(x)
@@ -316,11 +321,14 @@
                 rim = smooth_x(lambda at: rims[at][zb], x)
                 filt[c, x, zb, lead - 1 : lead, :] = rim[0:1, :]
                 filt[c, x, zb, lead + rows : lead + rows + 1, :] = rim[1:2, :]
-                filt[c, x, zb, inner, :] = smooth_x(lambda at: part[c, at, zb], x)
-
-    sum_lm = sum_mm = None
-    for x in range(nx):
+                for own in tiles:
+                    filt[c, x, zb, moved(own, 0), :] = smooth_x(lambda at: part[c, at, zb, own, :], x)
+
+    sums = [[None, None] for _ in tiles]
+    for x, n in [(x, n) for x in range(nx) for n in range(len(tiles))]:
+        own = tiles[n]
         left, right = (x - 1) % nx, (x + 1) % nx
+        inner, lower, upper = (moved(own, by) for by in (0, -1, 1))
         mean = [[filt[c, x, zb, inner, :] for zb in blocks] for c in range(3)]
         grad_x = [[filt[c, right, zb, inner, :] - filt[c, left, zb, inner, :] for zb in blocks] for c in range(3)]
         grad_y = [[filt[c, x, zb, upper, :] - filt[c, x, zb, lower, :] for zb in blocks] for c in range(3)]
@@ -330,27 +338,20 @@
             size = 0.25 * strain_size(strain)
             v = [mean[c][zb] for c in range(3)]
             scaled = [0.0625 * f for f in v]
-            pairs = (
-                v[0] * scaled[0],
-                v[1] * scaled[1],
-                v[2] * scaled[2],
-                v[0] * scaled[1],
-                v[0] * scaled[2],
-                v[1] * scaled[2],
-            )
-            leonard = [smooth_x(lambda at: part[3 + i, at, zb], x) - pairs[i] for i in range(6)]
-            model = [smooth_x(lambda at: part[9 + i, at, zb], x) - size * strain[i] for i in range(6)]
-            lm, mm = contracted(leonard, model)
-            sum_lm = lm if sum_lm is None else sum_lm + lm
-            sum_mm = mm if sum_mm is None else sum_mm + mm
-
-    coefficient = coefficient_of(
-        *(jnp.sum(total, axis=1, keepdims=True) for total in (sum_lm, sum_mm)), nx * nz
-    )
-    for k in range(count):
-        x0, zb = (k // nz_parts) * width, k % nz_parts
-        for x in range(width):
-            out[k, x] = coefficient * mag[x0 + x, zb]
+            pairs = [v[i] * scaled[j] for i, j in ((0, 0), (1, 1), (2, 2), (0, 1), (0, 2), (1, 2))]
+            leonard = [smooth_x(lambda at: part[3 + i, at, zb, own, :], x) - pairs[i] for i in range(6)]
+            model = [smooth_x(lambda at: part[9 + i, at, zb, own, :], x) - size * strain[i] for i in range(6)]
+            totals = contracted(leonard, model)
+            sums[n] = [f if s is None else s + f for s, f in zip(sums[n], totals)]
+
+    for own, totals in zip(tiles, sums):
+        coefficient = coefficient_of(
+            *(jnp.sum(total, axis=1, keepdims=True) for total in totals), nx * nz
+        )
+        for k in range(count):
+            x0, zb = (k // nz_parts) * width, k % nz_parts
+            for x in range(width):
+                out[k, x, own, :] = coefficient * mag[x0 + x, zb, own, :]
 
 
 def sweep_kernel(parity, back, velocity, tendency, eddy, reduced, factors, tree):
@@ -484,7 +485,7 @@
 
 
 def exchange_order(count):
-    return [1, *range(count - 1, 1, -1)]
+    return range(count - 1, 0, -1)
 
 
 def spread_kernel(factors, tree, velocity, eddy, particular, response, eddy_out, sent):

time: 40.4 us -> 40.9 us (1.012)
  Pallas kernels: 5.12 us -> 6.16 us
  waiting for transfers between devices: 2.16 us -> 1.43 us
    pallas_call x1, Pallas kernels: 3.03 us -> 4.06 us  [body(): pl.pallas_call(functools.partial(germano_kernel, nz_parts, width, rows),...]
    ppermute x3, waiting for transfers between devices: 1.87 us -> 1.42 us  [body(): lax.ppermute(reduced, 'gy', [(s, i) for i, s in enumerate(sources_of(step...]
  transfers between devices with their start and end apart: 4 -> 4, of which waited for: 3 -> 2; matrix products, arithmetic and copies ran while one was open for 0% -> 0% of each run, Pallas kernels for 9% -> 12%
where the time goes in v18:
time: 40.9 us; the launch traced here: 40.6 us
  blocking collectives  25 us (61%)
  starting transfers between devices  6.23 us (15%)
  Pallas kernels  6.16 us (15%)
  waiting for transfers between devices  1.43 us (3%)
  local copies, waits for them, and re-layouts  1.08 us (3%)
  between operations  0.72 us (2%)
    all_to_all x1, blocking collectives, body(): lax.all_to_all(chunks, ('gx', 'gz'), split_axis=0, concat_axis=0, tiled=T...  16.1 us
    all_to_all x1, blocking collectives, body(): lax.all_to_all(eddy_chunks, ('gx', 'gz'), split_axis=0, concat_axis=0, ti...  8.9 us
    ppermute x3, starting transfers between devices, body(): lax.ppermute(reduced, 'gy', [(s, i) for i, s in enumerate(sources_of(step...  5.67 us
    pallas_call x1, Pallas kernels, body(): pl.pallas_call(functools.partial(germano_kernel, nz_parts, width, rows),...  4.06 us
    ppermute x3, waiting for transfers between devices, body(): lax.ppermute(reduced, 'gy', [(s, i) for i, s in enumerate(sources_of(step...  1.42 us
    unnamed x6, local copies, waits for them, and re-layouts  1.07 us
    pallas_call x1, Pallas kernels, body(): pl.pallas_call(functools.partial(finish_kernel, walls), out_shape=jax.Sha...  0.93 us
  transfers between devices with their start and end apart: 4, of which 2 were waited for; matrix products, arithmetic and copies ran while one was open for 0% of the time, Pallas kernels for 12%

profile of v18, /device:TPU:0, one launch (start us, length us, event | category | flops | bytes accessed | tf_op | source)
XLA Modules:
  0.0 40.6 jit_solution(15385939994307885611)
XLA Ops:
  0.6 0.0 copy-start
  0.6 1.1 %copy-done = f32[3,2,192,128]{3,2,1,0:T(8,128)S(1)} copy-done((f32[3,2,192,128]{3,2,1,0:T(8,128)S(1)}, f32[3,2,192,128]{3,2,1,0:T(8,128)}, u32[]{:S(2)}) %copy-start) | copy-done | bytes 589848
  1.7 0.1 pack.1
  1.8 16.1 %all_to_all.10.recv = f32[8,160,128]{2,1,0:T(8,128)S(1)} all-to-all(f32[8,160,128]{2,1,0:T(8,128)S(1)} %pack.1), channel_id=1, replica_groups=mesh['gy'=4,'gx'=4,'gz'=2] {'gx','gz'}, dimensions={0} | all-to-all | bytes 1310720 | tf_op jit(solution)/shard_map/all_to_all | solution.py:619
  17.9 0.6 %collective-permute-start = (f32[8,8,128]{2,1,0:T(8,128)S(1)}, f32[8,8,128]{2,1,0:T(8,128)S(1)}, u32[]{:S(2)}, u32[]{:S(2)}) collective-permute-start(f32[8,8,128]{2,1,0:T(8,128)S(1)} %slice.4), channel_id=1, source_target_pairs={{0,4},{1,9},{2,6},{3,7},{4,0},{5,13},{6,2},{7,3},{8,12},{9,1},{10,... | collective-permute-start | bytes 98312 | tf_op jit(solution)/shard_map/ppermute | solution.py:621
  18.5 4.1 %germano.1.given = f32[8,2,24,128]{3,2,1,0:T(8,128)S(1)} custom-call(s32[1]{0:T(128)} %bitcast.1.rank, s32[1]{0:T(128)S(6)} %rem.18.parity, f32[8,160,128]{2,1,0:T(8,128)S(1)} %all_to_all.10.recv), custom_call_target="tpu_custom_call" | custom-call | flops 14745600 | bytes 786432 | tf_op jit(solution)/shard_map/germano/pallas_call | solution.py:625
  22.5 0.0 copy-start.1
  22.5 0.0 copy-start.2
  22.6 0.0 collective-permute-done.swapped
  22.6 8.9 %all_to_all.11.back = f32[8,2,24,128]{3,2,1,0:T(8,128)S(1)} all-to-all(f32[8,2,24,128]{3,2,1,0:T(8,128)S(1)} %edge.1), channel_id=1, replica_groups=mesh['gy'=4,'gx'=4,'gz'=2] {'gx','gz'}, dimensions={0} | all-to-all | bytes 393216 | tf_op jit(solution)/shard_map/all_to_all | solution.py:653
  31.5 0.0 copy-done.1
  31.5 0.0 copy-done.2
  31.5 0.4 sweep.1
  31.9 1.6 %collective-permute-start.3 = (f32[24,128]{1,0:T(8,128)S(1)}, f32[24,128]{1,0:T(8,128)S(1)}, u32[]{:S(2)}, u32[]{:S(2)}) collective-permute-start(f32[24,128]{1,0:T(8,128)S(1)} %get-tuple-element.14.rest_0_), channel_id=1, source_target_pairs={{16,0},{0,8},{24,16},{8,24},{17,1},{1,9},{25,17},{9,25},{18,2},{2,... | collective-permute-start | bytes 36872 | tf_op jit(solution)/shard_map/ppermute | solution.py:673
  33.5 2.5 %collective-permute-start.2 = (f32[24,128]{1,0:T(8,128)S(1)}, f32[24,128]{1,0:T(8,128)S(1)}, u32[]{:S(2)}, u32[]{:S(2)}) collective-permute-start(f32[24,128]{1,0:T(8,128)S(1)} %get-tuple-element.14.rest_0_), channel_id=1, source_target_pairs={{24,0},{16,8},{8,16},{0,24},{25,1},{17,9},{9,17},{1,25},{26,2},{18... | collective-permute-start | bytes 36872 | tf_op jit(solution)/shard_map/ppermute | solution.py:673
  36.0 1.6 %collective-permute-start.1 = (f32[24,128]{1,0:T(8,128)S(1)}, f32[24,128]{1,0:T(8,128)S(1)}, u32[]{:S(2)}, u32[]{:S(2)}) collective-permute-start(f32[24,128]{1,0:T(8,128)S(1)} %get-tuple-element.14.rest_0_), channel_id=1, source_target_pairs={{8,0},{24,8},{0,16},{16,24},{9,1},{25,9},{1,17},{17,25},{10,2},{26... | collective-permute-start | bytes 36872 | tf_op jit(solution)/shard_map/ppermute | solution.py:673
  37.6 0.7 %spread.1 = (f32[3,2,192,128]{3,2,1,0:T(8,128)S(1)}, f32[2,2,192,128]{3,2,1,0:T(8,128)S(1)}, f32[2,192,128]{2,1,0:T(8,128)}) custom-call(f32[2,24,5,8,128]{4,3,2,1,0:T(8,128)S(1)} %get-tuple-element.9.factors, f32[2,3,5,8,128]{4,3,2,1,0:T(8,128)S(1)} %get-tuple-element.10.tree, f32[3,2,192,128]{3,2,1,0:T(8,128)S(1)} %copy-done.1, ...), custom_call_target="tpu_custom_call" | custom-call | flops 2949120 | bytes 2359296 | tf_op jit(solution)/shard_map/spread/pallas_call | solution.py:676
  38.3 0.0 collective-permute-done.3.rest_3_
  38.3 0.7 %collective-permute-done.2.rest_2_ = f32[24,128]{1,0:T(8,128)S(1)} collective-permute-done((f32[24,128]{1,0:T(8,128)S(1)}, f32[24,128]{1,0:T(8,128)S(1)}, u32[]{:S(2)}, u32[]{:S(2)}) %collective-permute-start.2) | collective-permute-done | bytes 12320 | tf_op jit(solution)/shard_map/ppermute | solution.py:673
  39.0 0.7 %collective-permute-done.1.rest_1_ = f32[24,128]{1,0:T(8,128)S(1)} collective-permute-done((f32[24,128]{1,0:T(8,128)S(1)}, f32[24,128]{1,0:T(8,128)S(1)}, u32[]{:S(2)}, u32[]{:S(2)}) %collective-permute-start.1) | collective-permute-done | bytes 12320 | tf_op jit(solution)/shard_map/ppermute | solution.py:673
  39.7 0.9 %finish.1 = f32[3,2,192,128]{3,2,1,0:T(8,128)} custom-call(s32[1]{0:T(128)} %bitcast.position, f32[3,2,192,128]{3,2,1,0:T(8,128)S(1)} %get-tuple-element.12.particular, f32[2,2,192,128]{3,2,1,0:T(8,128)S(1)} %get-tuple-element.13.response, f32[24,128]{1,0:T(8,128)S(1)} %get-tuple-element.14.rest_0_, f32[24,128]{1,0:T(8,128)S(1)} %collective-permute-done.1.rest_1_, ...), custom_call_target="tpu_custom_call" | custom-call | tf_op jit(solution)/shard_map/finish/pallas_call | solution.py:692
  (2 shorter events, 0.0 us)
Async XLA Ops:
  0.6 1.1 %copy-start = (f32[3,2,192,128]{3,2,1,0:T(8,128)S(1)}, f32[3,2,192,128]{3,2,1,0:T(8,128)}, u32[]{:S(2)}) copy-start(f32[3,2,192,128]{3,2,1,0:T(8,128)} %velocity.5) | copy-start | bytes 1769476
  17.9 4.7 %collective-permute-start = (f32[8,8,128]{2,1,0:T(8,128)S(1)}, f32[8,8,128]{2,1,0:T(8,128)S(1)}, u32[]{:S(2)}, u32[]{:S(2)}) collective-permute-start(f32[8,8,128]{2,1,0:T(8,128)S(1)} %slice.4), channel_id=1, source_target_pairs={{0,4},{1,9},{2,6},{3,7},{4,0},{5,13},{6,2},{7,3},{8,12},{9,1},{10,... | collective-permute-start | bytes 98312 | tf_op jit(solution)/shard_map/ppermute | solution.py:621
  22.5 9.0 %copy-start.1 = (f32[3,2,192,128]{3,2,1,0:T(8,128)S(1)}, f32[3,2,192,128]{3,2,1,0:T(8,128)}, u32[]{:S(2)}) copy-start(f32[3,2,192,128]{3,2,1,0:T(8,128)} %velocity.5) | copy-start | bytes 1769476
  22.5 9.0 %copy-start.2 = (f32[3,2,192,128]{3,2,1,0:T(8,128)S(1)}, f32[3,2,192,128]{3,2,1,0:T(8,128)}, u32[]{:S(2)}) copy-start(f32[3,2,192,128]{3,2,1,0:T(8,128)} %tendency.1) | copy-start | bytes 1769476
  31.9 6.4 %collective-permute-start.3 = (f32[24,128]{1,0:T(8,128)S(1)}, f32[24,128]{1,0:T(8,128)S(1)}, u32[]{:S(2)}, u32[]{:S(2)}) collective-permute-start(f32[24,128]{1,0:T(8,128)S(1)} %get-tuple-element.14.rest_0_), channel_id=1, source_target_pairs={{16,0},{0,8},{24,16},{8,24},{17,1},{1,9},{25,17},{9,25},{18,2},{2,... | collective-permute-start | bytes 36872 | tf_op jit(solution)/shard_map/ppermute | solution.py:673
  33.5 5.5 %collective-permute-start.2 = (f32[24,128]{1,0:T(8,128)S(1)}, f32[24,128]{1,0:T(8,128)S(1)}, u32[]{:S(2)}, u32[]{:S(2)}) collective-permute-start(f32[24,128]{1,0:T(8,128)S(1)} %get-tuple-element.14.rest_0_), channel_id=1, source_target_pairs={{24,0},{16,8},{8,16},{0,24},{25,1},{17,9},{9,17},{1,25},{26,2},{18... | collective-permute-start | bytes 36872 | tf_op jit(solution)/shard_map/ppermute | solution.py:673
  36.0 3.7 %collective-permute-start.1 = (f32[24,128]{1,0:T(8,128)S(1)}, f32[24,128]{1,0:T(8,128)S(1)}, u32[]{:S(2)}, u32[]{:S(2)}) collective-permute-start(f32[24,128]{1,0:T(8,128)S(1)} %get-tuple-element.14.rest_0_), channel_id=1, source_target_pairs={{8,0},{24,8},{0,16},{16,24},{9,1},{25,9},{1,17},{17,25},{10,2},{26... | collective-permute-start | bytes 36872 | tf_op jit(solution)/shard_map/ppermute | solution.py:673

commit v19 on v17

--- a/solution.py
+++ b/solution.py
@@ -251,7 +251,7 @@
     return jnp.maximum(plane_lm * scale / (plane_mm * scale + 1e-06), 0.0)
 
 
-def germano_kernel(nz_parts, width, rows, rank, parity, recv, out, vel, filt, ends, mag, part):
+def germano_kernel(nz_parts, width, rows, rank, parity, recv, out, vel, filt, ends, strains, means, part):
     count, _, lanes = recv.shape
     planes = 3 * width
     _, top = outer_sides(rank, parity, count)
@@ -260,8 +260,6 @@
     blocks = range(nz_parts)
     lead = 8
     inner = slice(lead, lead + rows)
-    lower = slice(lead - 1, lead - 1 + rows)
-    upper = slice(lead + 1, lead + 1 + rows)
     for k in range(count):
         x0, zb = (k // nz_parts) * width, k % nz_parts
         for c in range(3):
@@ -277,72 +275,58 @@
                     vel[c, x0 + x, zb, at : at + 1, :] = edge
                     ends[c, x0 + x, zb, side : side + 1, :] = edge
 
-    for x in range(nx):
-        left, right = (x - 1) % nx, (x + 1) % nx
-        centre = [[vel[c, x, zb, inner, :] for zb in blocks] for c in range(3)]
-        grad_x = [[vel[c, right, zb, inner, :] - vel[c, left, zb, inner, :] for zb in blocks] for c in range(3)]
-        grad_y = [[vel[c, x, zb, upper, :] - vel[c, x, zb, lower, :] for zb in blocks] for c in range(3)]
-        grad_z = []
-        for c in range(3):
-            down, up = beside(centre[c])
-            grad_z.append([u - d for u, d in zip(up, down)])
-            for zb in blocks:
-                part[c, x, zb] = (up[zb] + down[zb]) + 2.0 * centre[c][zb]
-        strain = [
-            strain_parts(*([g[c][zb] for c in range(3)] for g in (grad_x, grad_y, grad_z)))
-            for zb in blocks
-        ]
-        size = [strain_size(s) for s in strain]
-        for zb in blocks:
-            mag[x, zb] = size[zb]
-        pairs = [products([centre[c][zb] for c in range(3)]) for zb in blocks]
-        for i in range(6):
-            for base, fields in (
-                (3, [pairs[zb][i] for zb in blocks]),
-                (9, [size[zb] * strain[zb][i] for zb in blocks]),
-            ):
-                for zb, f in enumerate(smooth_z(fields)):
-                    part[base + i, x, zb] = f
+    lower = slice(lead - 1, lead - 1 + rows)
+    upper = slice(lead + 1, lead + 1 + rows)
 
     def smooth_x(read, x):
         return (read((x - 1) % nx) + read((x + 1) % nx)) + 2.0 * read(x)
 
+    def keep_strain(field, x, kept, scale):
+        left, right = (x - 1) % nx, (x + 1) % nx
+        grad_z = [slope_z([field[c, x, zb, inner, :] for zb in blocks]) for c in range(3)]
+        for zb in blocks:
+            grad_x = [field[c, right, zb, inner, :] - field[c, left, zb, inner, :] for c in range(3)]
+            grad_y = [field[c, x, zb, upper, :] - field[c, x, zb, lower, :] for c in range(3)]
+            parts = strain_parts(grad_x, grad_y, [grad_z[c][zb] for c in range(3)])
+            for i in range(6):
+                kept[i, x, zb] = parts[i]
+            kept[6, x, zb] = scale * strain_size(parts) if scale != 1.0 else strain_size(parts)
+
+    for x in range(nx):
+        keep_strain(vel, x, strains, 1.0)
+        for c in range(3):
+            for zb, f in enumerate(smooth_z([vel[c, x, zb, inner, :] for zb in blocks])):
+                part[c, x, zb] = f
     for c in range(3):
-        rims = []
-        for x in range(nx):
-            rims.append(smooth_z([ends[c, x, zb] for zb in blocks]))
+        rims = [smooth_z([ends[c, x, zb] for zb in blocks]) for x in range(nx)]
         for x in range(nx):
             for zb in blocks:
                 rim = smooth_x(lambda at: rims[at][zb], x)
                 filt[c, x, zb, lead - 1 : lead, :] = rim[0:1, :]
                 filt[c, x, zb, lead + rows : lead + rows + 1, :] = rim[1:2, :]
                 filt[c, x, zb, inner, :] = smooth_x(lambda at: part[c, at, zb], x)
+    for x in range(nx):
+        keep_strain(filt, x, means, 0.25)
+        for i, (a, b) in enumerate(((0, 0), (1, 1), (2, 2), (0, 1), (0, 2), (1, 2))):
+            fields = [vel[a, x, zb, inner, :] * vel[b, x, zb, inner, :] for zb in blocks]
+            for zb, f in enumerate(smooth_z(fields)):
+                part[3 + i, x, zb] = f
+            fields = [strains[6, x, zb] * strains[i, x, zb] for zb in blocks]
+            for zb, f in enumerate(smooth_z(fields)):
+                part[9 + i, x, zb] = f
 
     sum_lm = sum_mm = None
     for x in range(nx):
-        left, right = (x - 1) % nx, (x + 1) % nx
-        mean = [[filt[c, x, zb, inner, :] for zb in blocks] for c in range(3)]
-        grad_x = [[filt[c, right, zb, inner, :] - filt[c, left, zb, inner, :] for zb in blocks] for c in range(3)]
-        grad_y = [[filt[c, x, zb, upper, :] - filt[c, x, zb, lower, :] for zb in blocks] for c in range(3)]
-        grad_z = [slope_z(mean[c]) for c in range(3)]
         for zb in blocks:
-            strain = strain_parts(*([g[c][zb] for c in range(3)] for g in (grad_x, grad_y, grad_z)))
-            size = 0.25 * strain_size(strain)
-            v = [mean[c][zb] for c in range(3)]
+            v = [filt[c, x, zb, inner, :] for c in range(3)]
             scaled = [0.0625 * f for f in v]
-            pairs = (
-                v[0] * scaled[0],
-                v[1] * scaled[1],
-                v[2] * scaled[2],
-                v[0] * scaled[1],
-                v[0] * scaled[2],
-                v[1] * scaled[2],
-            )
-            leonard = [smooth_x(lambda at: part[3 + i, at, zb], x) - pairs[i] for i in range(6)]
-            model = [smooth_x(lambda at: part[9 + i, at, zb], x) - size * strain[i] for i in range(6)]
-            lm, mm = contracted(leonard, model)
-            sum_lm = lm if sum_lm is None else sum_lm + lm
-            sum_mm = mm if sum_mm is None else sum_mm + mm
+            size = means[6, x, zb]
+            for i, (a, b) in enumerate(((0, 0), (1, 1), (2, 2), (0, 1), (0, 2), (1, 2))):
+                leonard = smooth_x(lambda at: part[3 + i, at, zb], x) - v[a] * scaled[b]
+                model = smooth_x(lambda at: part[9 + i, at, zb], x) - size * means[i, x, zb]
+                square = model * model if i < 3 else (0.5 * model) * model
+                sum_lm = leonard * model if sum_lm is None else sum_lm + leonard * model
+                sum_mm = square if sum_mm is None else sum_mm + square
 
     coefficient = coefficient_of(
         *(jnp.sum(total, axis=1, keepdims=True) for total in (sum_lm, sum_mm)), nx * nz
@@ -350,7 +334,7 @@
     for k in range(count):
         x0, zb = (k // nz_parts) * width, k % nz_parts
         for x in range(width):
-            out[k, x] = coefficient * mag[x0 + x, zb]
+            out[k, x] = coefficient * strains[6, x0 + x, zb]
 
 
 def sweep_kernel(parity, back, velocity, tendency, eddy, reduced, factors, tree):
@@ -484,7 +468,7 @@
 
 
 def exchange_order(count):
-    return [1, *range(count - 1, 1, -1)]
+    return range(count - 1, 0, -1)
 
 
 def spread_kernel(factors, tree, velocity, eddy, particular, response, eddy_out, sent):
@@ -630,7 +614,8 @@
             pltpu.VMEM((3, nx, nz_parts, padded, lanes), f32),
             pltpu.VMEM((3, nx, nz_parts, padded, lanes), f32),
             pltpu.VMEM((3, nx, nz_parts, 8, lanes), f32),
-            pltpu.VMEM((nx, nz_parts, rows, lanes), f32),
+            pltpu.VMEM((7, nx, nz_parts, rows, lanes), f32),
+            pltpu.VMEM((7, nx, nz_parts, rows, lanes), f32),
             pltpu.VMEM((15, nx, nz_parts, rows, lanes), f32),
         ],
         compiler_params=params(),

time: 40.4 us -> 39.8 us (0.985)
    ppermute x3, waiting for transfers between devices: 1.87 us -> 1.42 us  [body(): lax.ppermute(reduced, 'gy', [(s, i) for i, s in enumerate(sources_of(step...]
where the time goes in v19:
time: 39.8 us; the launch traced here: 39.6 us
  blocking collectives  24.7 us (62%)
  starting transfers between devices  6.23 us (16%)
  Pallas kernels  4.94 us (12%)
  waiting for transfers between devices  1.89 us (5%)
  local copies, waits for them, and re-layouts  1.08 us (3%)
  between operations  0.7 us (2%)
    all_to_all x1, blocking collectives, body(): lax.all_to_all(chunks, ('gx', 'gz'), split_axis=0, concat_axis=0, tiled=T...  16.1 us
    all_to_all x1, blocking collectives, body(): lax.all_to_all(eddy_chunks, ('gx', 'gz'), split_axis=0, concat_axis=0, ti...  8.62 us
    ppermute x3, starting transfers between devices, body(): lax.ppermute(reduced, 'gy', [(s, i) for i, s in enumerate(sources_of(step...  5.67 us
    pallas_call x1, Pallas kernels, body(): pl.pallas_call(functools.partial(germano_kernel, nz_parts, width, rows),...  2.85 us
    ppermute x3, waiting for transfers between devices, body(): lax.ppermute(reduced, 'gy', [(s, i) for i, s in enumerate(sources_of(step...  1.42 us
    unnamed x6, local copies, waits for them, and re-layouts  1.07 us
    pallas_call x1, Pallas kernels, body(): pl.pallas_call(functools.partial(finish_kernel, walls), out_shape=jax.Sha...  0.93 us
  transfers between devices with their start and end apart: 4, of which 3 were waited for; matrix products, arithmetic and copies ran while one was open for 0% of the time, Pallas kernels for 9%

profile of v19, /device:TPU:0, one launch (start us, length us, event | category | flops | bytes accessed | tf_op | source)
XLA Modules:
  0.0 39.6 jit_solution(11618230422790520722)
XLA Ops:
  0.6 0.0 copy-start
  0.6 1.1 %copy-done = f32[3,2,192,128]{3,2,1,0:T(8,128)S(1)} copy-done((f32[3,2,192,128]{3,2,1,0:T(8,128)S(1)}, f32[3,2,192,128]{3,2,1,0:T(8,128)}, u32[]{:S(2)}) %copy-start) | copy-done | bytes 589848
  1.7 0.1 pack.1
  1.8 16.1 %all_to_all.10.recv = f32[8,160,128]{2,1,0:T(8,128)S(1)} all-to-all(f32[8,160,128]{2,1,0:T(8,128)S(1)} %pack.1), channel_id=1, replica_groups=mesh['gy'=4,'gx'=4,'gz'=2] {'gx','gz'}, dimensions={0} | all-to-all | bytes 1310720 | tf_op jit(solution)/shard_map/all_to_all | solution.py:602
  17.9 0.6 %collective-permute-start = (f32[8,8,128]{2,1,0:T(8,128)S(1)}, f32[8,8,128]{2,1,0:T(8,128)S(1)}, u32[]{:S(2)}, u32[]{:S(2)}) collective-permute-start(f32[8,8,128]{2,1,0:T(8,128)S(1)} %slice.4), channel_id=1, source_target_pairs={{0,4},{1,9},{2,6},{3,7},{4,0},{5,13},{6,2},{7,3},{8,12},{9,1},{10,... | collective-permute-start | bytes 98312 | tf_op jit(solution)/shard_map/ppermute | solution.py:604
  18.5 2.9 %germano.1.given = f32[8,2,24,128]{3,2,1,0:T(8,128)S(1)} custom-call(s32[1]{0:T(128)} %bitcast.1.rank, s32[1]{0:T(128)S(6)} %rem.18.parity, f32[8,160,128]{2,1,0:T(8,128)S(1)} %all_to_all.10.recv), custom_call_target="tpu_custom_call" | custom-call | flops 14745600 | bytes 786432 | tf_op jit(solution)/shard_map/germano/pallas_call | solution.py:608
  21.3 0.0 copy-start.1
  21.3 0.0 copy-start.2
  21.4 0.5 %collective-permute-done.swapped = f32[8,8,128]{2,1,0:T(8,128)S(1)} collective-permute-done((f32[8,8,128]{2,1,0:T(8,128)S(1)}, f32[8,8,128]{2,1,0:T(8,128)S(1)}, u32[]{:S(2)}, u32[]{:S(2)}) %collective-permute-start) | collective-permute-done | bytes 32800 | tf_op jit(solution)/shard_map/ppermute | solution.py:604
  21.8 8.6 %all_to_all.11.back = f32[8,2,24,128]{3,2,1,0:T(8,128)S(1)} all-to-all(f32[8,2,24,128]{3,2,1,0:T(8,128)S(1)} %edge.1), channel_id=1, replica_groups=mesh['gy'=4,'gx'=4,'gz'=2] {'gx','gz'}, dimensions={0} | all-to-all | bytes 393216 | tf_op jit(solution)/shard_map/all_to_all | solution.py:637
  30.4 0.0 copy-done.1
  30.4 0.0 copy-done.2
  30.5 0.4 %sweep.1 = (f32[2,192,128]{2,1,0:T(8,128)S(1)}, f32[24,128]{1,0:T(8,128)S(1)}, f32[2,24,5,8,128]{4,3,2,1,0:T(8,128)S(1)}, f32[2,3,5,8,128]{4,3,2,1,0:T(8,128)S(1)}) custom-call(s32[1]{0:T(128)S(6)} %rem.18.parity, f32[8,2,24,128]{3,2,1,0:T(8,128)S(1)} %all_to_all.11.back, f32[3,2,192,128]{3,2,1,0:T(8,128)S(1)} %copy-done.1, f32[3,2,192,128]{3,2,1,0:T(8,128)S(1)} %copy-done.2), custom_call_target="tpu_custom_call" | custom-call | tf_op jit(solution)/shard_map/sweep/pallas_call | solution.py:642
  30.9 1.6 %collective-permute-start.3 = (f32[24,128]{1,0:T(8,128)S(1)}, f32[24,128]{1,0:T(8,128)S(1)}, u32[]{:S(2)}, u32[]{:S(2)}) collective-permute-start(f32[24,128]{1,0:T(8,128)S(1)} %get-tuple-element.14.rest_0_), channel_id=1, source_target_pairs={{16,0},{0,8},{24,16},{8,24},{17,1},{1,9},{25,17},{9,25},{18,2},{2,... | collective-permute-start | bytes 36872 | tf_op jit(solution)/shard_map/ppermute | solution.py:657
  32.5 2.5 %collective-permute-start.2 = (f32[24,128]{1,0:T(8,128)S(1)}, f32[24,128]{1,0:T(8,128)S(1)}, u32[]{:S(2)}, u32[]{:S(2)}) collective-permute-start(f32[24,128]{1,0:T(8,128)S(1)} %get-tuple-element.14.rest_0_), channel_id=1, source_target_pairs={{24,0},{16,8},{8,16},{0,24},{25,1},{17,9},{9,17},{1,25},{26,2},{18... | collective-permute-start | bytes 36872 | tf_op jit(solution)/shard_map/ppermute | solution.py:657
  35.0 1.6 %collective-permute-start.1 = (f32[24,128]{1,0:T(8,128)S(1)}, f32[24,128]{1,0:T(8,128)S(1)}, u32[]{:S(2)}, u32[]{:S(2)}) collective-permute-start(f32[24,128]{1,0:T(8,128)S(1)} %get-tuple-element.14.rest_0_), channel_id=1, source_target_pairs={{8,0},{24,8},{0,16},{16,24},{9,1},{25,9},{1,17},{17,25},{10,2},{26... | collective-permute-start | bytes 36872 | tf_op jit(solution)/shard_map/ppermute | solution.py:657
  36.5 0.7 %spread.1 = (f32[3,2,192,128]{3,2,1,0:T(8,128)S(1)}, f32[2,2,192,128]{3,2,1,0:T(8,128)S(1)}, f32[2,192,128]{2,1,0:T(8,128)}) custom-call(f32[2,24,5,8,128]{4,3,2,1,0:T(8,128)S(1)} %get-tuple-element.9.factors, f32[2,3,5,8,128]{4,3,2,1,0:T(8,128)S(1)} %get-tuple-element.10.tree, f32[3,2,192,128]{3,2,1,0:T(8,128)S(1)} %copy-done.1, ...), custom_call_target="tpu_custom_call" | custom-call | flops 2949120 | bytes 2359296 | tf_op jit(solution)/shard_map/spread/pallas_call | solution.py:660
  37.2 0.0 collective-permute-done.3.rest_3_
  37.2 0.7 %collective-permute-done.2.rest_2_ = f32[24,128]{1,0:T(8,128)S(1)} collective-permute-done((f32[24,128]{1,0:T(8,128)S(1)}, f32[24,128]{1,0:T(8,128)S(1)}, u32[]{:S(2)}, u32[]{:S(2)}) %collective-permute-start.2) | collective-permute-done | bytes 12320 | tf_op jit(solution)/shard_map/ppermute | solution.py:657
  38.0 0.7 %collective-permute-done.1.rest_1_ = f32[24,128]{1,0:T(8,128)S(1)} collective-permute-done((f32[24,128]{1,0:T(8,128)S(1)}, f32[24,128]{1,0:T(8,128)S(1)}, u32[]{:S(2)}, u32[]{:S(2)}) %collective-permute-start.1) | collective-permute-done | bytes 12320 | tf_op jit(solution)/shard_map/ppermute | solution.py:657
  38.7 0.9 %finish.1 = f32[3,2,192,128]{3,2,1,0:T(8,128)} custom-call(s32[1]{0:T(128)} %bitcast.position, f32[3,2,192,128]{3,2,1,0:T(8,128)S(1)} %get-tuple-element.12.particular, f32[2,2,192,128]{3,2,1,0:T(8,128)S(1)} %get-tuple-element.13.response, f32[24,128]{1,0:T(8,128)S(1)} %get-tuple-element.14.rest_0_, f32[24,128]{1,0:T(8,128)S(1)} %collective-permute-done.1.rest_1_, ...), custom_call_target="tpu_custom_call" | custom-call | tf_op jit(solution)/shard_map/finish/pallas_call | solution.py:676
  (2 shorter events, 0.0 us)
Async XLA Ops:
  0.6 1.1 %copy-start = (f32[3,2,192,128]{3,2,1,0:T(8,128)S(1)}, f32[3,2,192,128]{3,2,1,0:T(8,128)}, u32[]{:S(2)}) copy-start(f32[3,2,192,128]{3,2,1,0:T(8,128)} %velocity.5) | copy-start | bytes 1769476
  17.9 3.9 %collective-permute-start = (f32[8,8,128]{2,1,0:T(8,128)S(1)}, f32[8,8,128]{2,1,0:T(8,128)S(1)}, u32[]{:S(2)}, u32[]{:S(2)}) collective-permute-start(f32[8,8,128]{2,1,0:T(8,128)S(1)} %slice.4), channel_id=1, source_target_pairs={{0,4},{1,9},{2,6},{3,7},{4,0},{5,13},{6,2},{7,3},{8,12},{9,1},{10,... | collective-permute-start | bytes 98312 | tf_op jit(solution)/shard_map/ppermute | solution.py:604
  21.3 9.1 %copy-start.1 = (f32[3,2,192,128]{3,2,1,0:T(8,128)S(1)}, f32[3,2,192,128]{3,2,1,0:T(8,128)}, u32[]{:S(2)}) copy-start(f32[3,2,192,128]{3,2,1,0:T(8,128)} %velocity.5) | copy-start | bytes 1769476
  21.3 9.1 %copy-start.2 = (f32[3,2,192,128]{3,2,1,0:T(8,128)S(1)}, f32[3,2,192,128]{3,2,1,0:T(8,128)}, u32[]{:S(2)}) copy-start(f32[3,2,192,128]{3,2,1,0:T(8,128)} %tendency.1) | copy-start | bytes 1769476
  30.9 6.4 %collective-permute-start.3 = (f32[24,128]{1,0:T(8,128)S(1)}, f32[24,128]{1,0:T(8,128)S(1)}, u32[]{:S(2)}, u32[]{:S(2)}) collective-permute-start(f32[24,128]{1,0:T(8,128)S(1)} %get-tuple-element.14.rest_0_), channel_id=1, source_target_pairs={{16,0},{0,8},{24,16},{8,24},{17,1},{1,9},{25,17},{9,25},{18,2},{2,... | collective-permute-start | bytes 36872 | tf_op jit(solution)/shard_map/ppermute | solution.py:657
  32.5 5.5 %collective-permute-start.2 = (f32[24,128]{1,0:T(8,128)S(1)}, f32[24,128]{1,0:T(8,128)S(1)}, u32[]{:S(2)}, u32[]{:S(2)}) collective-permute-start(f32[24,128]{1,0:T(8,128)S(1)} %get-tuple-element.14.rest_0_), channel_id=1, source_target_pairs={{24,0},{16,8},{8,16},{0,24},{25,1},{17,9},{9,17},{1,25},{26,2},{18... | collective-permute-start | bytes 36872 | tf_op jit(solution)/shard_map/ppermute | solution.py:657
  35.0 3.7 %collective-permute-start.1 = (f32[24,128]{1,0:T(8,128)S(1)}, f32[24,128]{1,0:T(8,128)S(1)}, u32[]{:S(2)}, u32[]{:S(2)}) collective-permute-start(f32[24,128]{1,0:T(8,128)S(1)} %get-tuple-element.14.rest_0_), channel_id=1, source_target_pairs={{8,0},{24,8},{0,16},{16,24},{9,1},{25,9},{1,17},{17,25},{10,2},{26... | collective-permute-start | bytes 36872 | tf_op jit(solution)/shard_map/ppermute | solution.py:657

commit v20 on v19

--- a/solution.py
+++ b/solution.py
@@ -52,6 +52,25 @@
 def smooth_z(blocks):
     down, up = beside(blocks)
     return [(u + d) + 2.0 * f for f, u, d in zip(blocks, up, down)]
+
+
+def band_matrix(n):
+    shape = (n, n)
+    apart = lax.broadcasted_iota(jnp.int32, shape, 0) - lax.broadcasted_iota(jnp.int32, shape, 1)
+    apart = jnp.abs(apart)
+    near = jnp.logical_or(apart == 1, apart == n - 1)
+    return jnp.where(apart == 0, 2.0, jnp.where(near, 1.0, 0.0)).astype(jnp.bfloat16)
+
+
+def times_band(f, band):
+    total = None
+    for i in range(3):
+        piece = f.astype(jnp.bfloat16)
+        product = jnp.dot(piece, band, preferred_element_type=jnp.float32)
+        total = product if total is None else total + product
+        if i < 2:
+            f = f - piece.astype(jnp.float32)
+    return total
 
 
 def products(v):
@@ -305,15 +324,29 @@
                 filt[c, x, zb, lead - 1 : lead, :] = rim[0:1, :]
                 filt[c, x, zb, lead + rows : lead + rows + 1, :] = rim[1:2, :]
                 filt[c, x, zb, inner, :] = smooth_x(lambda at: part[c, at, zb], x)
+    def filter_z(read, kept):
+        if not on_matrix_unit:
+            for x in range(nx):
+                for zb, f in enumerate(smooth_z([read(x, zb) for zb in blocks])):
+                    part[kept, x, zb] = f
+            return
+        half = nx // 2
+        for x0 in (0, half):
+            planes_here = [
+                jnp.concatenate([read(x, zb) for zb in blocks], axis=1) for x in range(x0, x0 + half)
+            ]
+            total = times_band(jnp.concatenate(planes_here, axis=0), band)
+            for x in range(half):
+                for zb in blocks:
+                    part[kept, x0 + x, zb] = total[x * rows : (x + 1) * rows, zb * lanes : (zb + 1) * lanes]
+
+    on_matrix_unit = nz <= 256 and rows * nx % 32 == 0 and rows % 8 == 0
+    band = band_matrix(nz) if on_matrix_unit else None
+    for i, (a, b) in enumerate(((0, 0), (1, 1), (2, 2), (0, 1), (0, 2), (1, 2))):
+        filter_z(lambda x, zb: vel[a, x, zb, inner, :] * vel[b, x, zb, inner, :], 3 + i)
+        filter_z(lambda x, zb: strains[6, x, zb] * strains[i, x, zb], 9 + i)
     for x in range(nx):
         keep_strain(filt, x, means, 0.25)
-        for i, (a, b) in enumerate(((0, 0), (1, 1), (2, 2), (0, 1), (0, 2), (1, 2))):
-            fields = [vel[a, x, zb, inner, :] * vel[b, x, zb, inner, :] for zb in blocks]
-            for zb, f in enumerate(smooth_z(fields)):
-                part[3 + i, x, zb] = f
-            fields = [strains[6, x, zb] * strains[i, x, zb] for zb in blocks]
-            for zb, f in enumerate(smooth_z(fields)):
-                part[9 + i, x, zb] = f
 
     sum_lm = sum_mm = None
     for x in range(nx):

time: 39.8 us -> 39.8 us (level)
  transfers between devices with their start and end apart: 4 -> 4, of which waited for: 3 -> 3; matrix products, arithmetic and copies ran while one was open for 0% -> 0% of each run, Pallas kernels for 9% -> 8%
where the time goes in v20:
time: 39.8 us; the launch traced here: 39.6 us
  blocking collectives  24.7 us (62%)
  starting transfers between devices  6.23 us (16%)
  Pallas kernels  4.62 us (12%)
  waiting for transfers between devices  2.21 us (6%)
  local copies, waits for them, and re-layouts  1.08 us (3%)
  between operations  0.7 us (2%)
    all_to_all x1, blocking collectives, body(): lax.all_to_all(chunks, ('gx', 'gz'), split_axis=0, concat_axis=0, tiled=T...  16.1 us
    all_to_all x1, blocking collectives, body(): lax.all_to_all(eddy_chunks, ('gx', 'gz'), split_axis=0, concat_axis=0, ti...  8.62 us
    ppermute x3, starting transfers between devices, body(): lax.ppermute(reduced, 'gy', [(s, i) for i, s in enumerate(sources_of(step...  5.67 us
    pallas_call x1, Pallas kernels, body(): pl.pallas_call(functools.partial(germano_kernel, nz_parts, width, rows),...  2.53 us
    ppermute x3, waiting for transfers between devices, body(): lax.ppermute(reduced, 'gy', [(s, i) for i, s in enumerate(sources_of(step...  1.42 us
    unnamed x6, local copies, waits for them, and re-layouts  1.07 us
    pallas_call x1, Pallas kernels, body(): pl.pallas_call(functools.partial(finish_kernel, walls), out_shape=jax.Sha...  0.93 us
  transfers between devices with their start and end apart: 4, of which 3 were waited for; matrix products, arithmetic and copies ran while one was open for 0% of the time, Pallas kernels for 8%

profile of v20, /device:TPU:0, one launch (start us, length us, event | category | flops | bytes accessed | tf_op | source)
XLA Modules:
  0.0 39.6 jit_solution(5460271150793943394)
XLA Ops:
  0.6 0.0 copy-start
  0.6 1.1 %copy-done = f32[3,2,192,128]{3,2,1,0:T(8,128)S(1)} copy-done((f32[3,2,192,128]{3,2,1,0:T(8,128)S(1)}, f32[3,2,192,128]{3,2,1,0:T(8,128)}, u32[]{:S(2)}) %copy-start) | copy-done | bytes 589848
  1.7 0.1 pack.1
  1.8 16.1 %all_to_all.10.recv = f32[8,160,128]{2,1,0:T(8,128)S(1)} all-to-all(f32[8,160,128]{2,1,0:T(8,128)S(1)} %pack.1), channel_id=1, replica_groups=mesh['gy'=4,'gx'=4,'gz'=2] {'gx','gz'}, dimensions={0} | all-to-all | bytes 1310720 | tf_op jit(solution)/shard_map/all_to_all | solution.py:635
  17.9 0.6 %collective-permute-start = (f32[8,8,128]{2,1,0:T(8,128)S(1)}, f32[8,8,128]{2,1,0:T(8,128)S(1)}, u32[]{:S(2)}, u32[]{:S(2)}) collective-permute-start(f32[8,8,128]{2,1,0:T(8,128)S(1)} %slice.4), channel_id=1, source_target_pairs={{0,4},{1,9},{2,6},{3,7},{4,0},{5,13},{6,2},{7,3},{8,12},{9,1},{10,... | collective-permute-start | bytes 98312 | tf_op jit(solution)/shard_map/ppermute | solution.py:637
  18.5 2.5 %germano.1.given = f32[8,2,24,128]{3,2,1,0:T(8,128)S(1)} custom-call(s32[1]{0:T(128)} %bitcast.1.rank, s32[1]{0:T(128)S(6)} %rem.18.parity, f32[8,160,128]{2,1,0:T(8,128)S(1)} %all_to_all.10.recv), custom_call_target="tpu_custom_call" | custom-call | flops 14745600 | bytes 786432 | tf_op jit(solution)/shard_map/germano/pallas_call | solution.py:641
  21.0 0.0 copy-start.1
  21.0 0.0 copy-start.2
  21.0 0.8 %collective-permute-done.swapped = f32[8,8,128]{2,1,0:T(8,128)S(1)} collective-permute-done((f32[8,8,128]{2,1,0:T(8,128)S(1)}, f32[8,8,128]{2,1,0:T(8,128)S(1)}, u32[]{:S(2)}, u32[]{:S(2)}) %collective-permute-start) | collective-permute-done | bytes 32800 | tf_op jit(solution)/shard_map/ppermute | solution.py:637
  21.8 8.6 %all_to_all.11.back = f32[8,2,24,128]{3,2,1,0:T(8,128)S(1)} all-to-all(f32[8,2,24,128]{3,2,1,0:T(8,128)S(1)} %edge.1), channel_id=1, replica_groups=mesh['gy'=4,'gx'=4,'gz'=2] {'gx','gz'}, dimensions={0} | all-to-all | bytes 393216 | tf_op jit(solution)/shard_map/all_to_all | solution.py:670
  30.4 0.0 copy-done.1
  30.4 0.0 copy-done.2
  30.5 0.4 %sweep.1 = (f32[2,192,128]{2,1,0:T(8,128)S(1)}, f32[24,128]{1,0:T(8,128)S(1)}, f32[2,24,5,8,128]{4,3,2,1,0:T(8,128)S(1)}, f32[2,3,5,8,128]{4,3,2,1,0:T(8,128)S(1)}) custom-call(s32[1]{0:T(128)S(6)} %rem.18.parity, f32[8,2,24,128]{3,2,1,0:T(8,128)S(1)} %all_to_all.11.back, f32[3,2,192,128]{3,2,1,0:T(8,128)S(1)} %copy-done.1, f32[3,2,192,128]{3,2,1,0:T(8,128)S(1)} %copy-done.2), custom_call_target="tpu_custom_call" | custom-call | tf_op jit(solution)/shard_map/sweep/pallas_call | solution.py:675
  30.9 1.6 %collective-permute-start.3 = (f32[24,128]{1,0:T(8,128)S(1)}, f32[24,128]{1,0:T(8,128)S(1)}, u32[]{:S(2)}, u32[]{:S(2)}) collective-permute-start(f32[24,128]{1,0:T(8,128)S(1)} %get-tuple-element.14.rest_0_), channel_id=1, source_target_pairs={{16,0},{0,8},{24,16},{8,24},{17,1},{1,9},{25,17},{9,25},{18,2},{2,... | collective-permute-start | bytes 36872 | tf_op jit(solution)/shard_map/ppermute | solution.py:690
  32.5 2.5 %collective-permute-start.2 = (f32[24,128]{1,0:T(8,128)S(1)}, f32[24,128]{1,0:T(8,128)S(1)}, u32[]{:S(2)}, u32[]{:S(2)}) collective-permute-start(f32[24,128]{1,0:T(8,128)S(1)} %get-tuple-element.14.rest_0_), channel_id=1, source_target_pairs={{24,0},{16,8},{8,16},{0,24},{25,1},{17,9},{9,17},{1,25},{26,2},{18... | collective-permute-start | bytes 36872 | tf_op jit(solution)/shard_map/ppermute | solution.py:690
  35.0 1.6 %collective-permute-start.1 = (f32[24,128]{1,0:T(8,128)S(1)}, f32[24,128]{1,0:T(8,128)S(1)}, u32[]{:S(2)}, u32[]{:S(2)}) collective-permute-start(f32[24,128]{1,0:T(8,128)S(1)} %get-tuple-element.14.rest_0_), channel_id=1, source_target_pairs={{8,0},{24,8},{0,16},{16,24},{9,1},{25,9},{1,17},{17,25},{10,2},{26... | collective-permute-start | bytes 36872 | tf_op jit(solution)/shard_map/ppermute | solution.py:690
  36.5 0.7 %spread.1 = (f32[3,2,192,128]{3,2,1,0:T(8,128)S(1)}, f32[2,2,192,128]{3,2,1,0:T(8,128)S(1)}, f32[2,192,128]{2,1,0:T(8,128)}) custom-call(f32[2,24,5,8,128]{4,3,2,1,0:T(8,128)S(1)} %get-tuple-element.9.factors, f32[2,3,5,8,128]{4,3,2,1,0:T(8,128)S(1)} %get-tuple-element.10.tree, f32[3,2,192,128]{3,2,1,0:T(8,128)S(1)} %copy-done.1, ...), custom_call_target="tpu_custom_call" | custom-call | flops 2949120 | bytes 2359296 | tf_op jit(solution)/shard_map/spread/pallas_call | solution.py:693
  37.2 0.0 collective-permute-done.3.rest_3_
  37.2 0.7 %collective-permute-done.2.rest_2_ = f32[24,128]{1,0:T(8,128)S(1)} collective-permute-done((f32[24,128]{1,0:T(8,128)S(1)}, f32[24,128]{1,0:T(8,128)S(1)}, u32[]{:S(2)}, u32[]{:S(2)}) %collective-permute-start.2) | collective-permute-done | bytes 12320 | tf_op jit(solution)/shard_map/ppermute | solution.py:690
  38.0 0.7 %collective-permute-done.1.rest_1_ = f32[24,128]{1,0:T(8,128)S(1)} collective-permute-done((f32[24,128]{1,0:T(8,128)S(1)}, f32[24,128]{1,0:T(8,128)S(1)}, u32[]{:S(2)}, u32[]{:S(2)}) %collective-permute-start.1) | collective-permute-done | bytes 12320 | tf_op jit(solution)/shard_map/ppermute | solution.py:690
  38.7 0.9 %finish.1 = f32[3,2,192,128]{3,2,1,0:T(8,128)} custom-call(s32[1]{0:T(128)} %bitcast.position, f32[3,2,192,128]{3,2,1,0:T(8,128)S(1)} %get-tuple-element.12.particular, f32[2,2,192,128]{3,2,1,0:T(8,128)S(1)} %get-tuple-element.13.response, f32[24,128]{1,0:T(8,128)S(1)} %get-tuple-element.14.rest_0_, f32[24,128]{1,0:T(8,128)S(1)} %collective-permute-done.1.rest_1_, ...), custom_call_target="tpu_custom_call" | custom-call | tf_op jit(solution)/shard_map/finish/pallas_call | solution.py:709
  (2 shorter events, 0.0 us)
Async XLA Ops:
  0.6 1.1 %copy-start = (f32[3,2,192,128]{3,2,1,0:T(8,128)S(1)}, f32[3,2,192,128]{3,2,1,0:T(8,128)}, u32[]{:S(2)}) copy-start(f32[3,2,192,128]{3,2,1,0:T(8,128)} %velocity.5) | copy-start | bytes 1769476
  17.9 3.9 %collective-permute-start = (f32[8,8,128]{2,1,0:T(8,128)S(1)}, f32[8,8,128]{2,1,0:T(8,128)S(1)}, u32[]{:S(2)}, u32[]{:S(2)}) collective-permute-start(f32[8,8,128]{2,1,0:T(8,128)S(1)} %slice.4), channel_id=1, source_target_pairs={{0,4},{1,9},{2,6},{3,7},{4,0},{5,13},{6,2},{7,3},{8,12},{9,1},{10,... | collective-permute-start | bytes 98312 | tf_op jit(solution)/shard_map/ppermute | solution.py:637
  21.0 9.4 %copy-start.1 = (f32[3,2,192,128]{3,2,1,0:T(8,128)S(1)}, f32[3,2,192,128]{3,2,1,0:T(8,128)}, u32[]{:S(2)}) copy-start(f32[3,2,192,128]{3,2,1,0:T(8,128)} %velocity.5) | copy-start | bytes 1769476
  21.0 9.4 %copy-start.2 = (f32[3,2,192,128]{3,2,1,0:T(8,128)S(1)}, f32[3,2,192,128]{3,2,1,0:T(8,128)}, u32[]{:S(2)}) copy-start(f32[3,2,192,128]{3,2,1,0:T(8,128)} %tendency.1) | copy-start | bytes 1769476
  30.9 6.4 %collective-permute-start.3 = (f32[24,128]{1,0:T(8,128)S(1)}, f32[24,128]{1,0:T(8,128)S(1)}, u32[]{:S(2)}, u32[]{:S(2)}) collective-permute-start(f32[24,128]{1,0:T(8,128)S(1)} %get-tuple-element.14.rest_0_), channel_id=1, source_target_pairs={{16,0},{0,8},{24,16},{8,24},{17,1},{1,9},{25,17},{9,25},{18,2},{2,... | collective-permute-start | bytes 36872 | tf_op jit(solution)/shard_map/ppermute | solution.py:690
  32.5 5.5 %collective-permute-start.2 = (f32[24,128]{1,0:T(8,128)S(1)}, f32[24,128]{1,0:T(8,128)S(1)}, u32[]{:S(2)}, u32[]{:S(2)}) collective-permute-start(f32[24,128]{1,0:T(8,128)S(1)} %get-tuple-element.14.rest_0_), channel_id=1, source_target_pairs={{24,0},{16,8},{8,16},{0,24},{25,1},{17,9},{9,17},{1,25},{26,2},{18... | collective-permute-start | bytes 36872 | tf_op jit(solution)/shard_map/ppermute | solution.py:690
  35.0 3.7 %collective-permute-start.1 = (f32[24,128]{1,0:T(8,128)S(1)}, f32[24,128]{1,0:T(8,128)S(1)}, u32[]{:S(2)}, u32[]{:S(2)}) collective-permute-start(f32[24,128]{1,0:T(8,128)S(1)} %get-tuple-element.14.rest_0_), channel_id=1, source_target_pairs={{8,0},{24,8},{0,16},{16,24},{9,1},{25,9},{1,17},{17,25},{10,2},{26... | collective-permute-start | bytes 36872 | tf_op jit(solution)/shard_map/ppermute | solution.py:690

commit v21 on v20

--- a/solution.py
+++ b/solution.py
@@ -108,14 +108,16 @@
     join((0, odd), (0, spare))
     if walls % 2 == 0:
         join((walls - 1, odd), (walls - 1, spare))
-    others = [r for r in range(count) if r not in (odd, even, spare)]
+    for wall in range(walls):
+        join((wall, 0), (wall, 1))
+    others = [r for r in range(2, count) if r not in (odd, even, spare)]
     for core in range(2):
         ranks = [r for r in others if r % 2 == core]
-        half = len(ranks) // 2
+        first = len(ranks) % 2
         for wall in range(walls):
-            for a, b in zip(ranks[:half], ranks[half : 2 * half]):
+            for a, b in zip(ranks[first::2], ranks[first + 1 :: 2]):
                 join((wall, a), (wall, b))
-        for rank in ranks[2 * half :]:
+        for rank in ranks[:first]:
             join_walls(rank, 0)
     return [
         (wall * count + rank, to[0] * count + to[1])

time: 39.8 us -> 39.5 us (level)
  blocking collectives: 24.7 us -> 25.7 us
  starting transfers between devices: 6.23 us -> 5.56 us
  waiting for transfers between devices: 2.21 us -> 1.54 us
    all_to_all x1, blocking collectives: 8.62 us -> 9.56 us  [body(): lax.all_to_all(eddy_chunks, ('gx', 'gz'), split_axis=0, concat_axis=0, ti...]
    ppermute x1, waiting for transfers between devices: 0.79 us -> 0.01 us  [body(): swapped = lax.ppermute(slot, ('gy', 'gx', 'gz'), swap_pairs(walls, count))]
    ppermute x1, starting transfers between devices: 0.56 us -> 0.01 us  [body(): swapped = lax.ppermute(slot, ('gy', 'gx', 'gz'), swap_pairs(walls, count))]
  transfers between devices with their start and end apart: 4 -> 4, of which waited for: 3 -> 2; matrix products, arithmetic and copies ran while one was open for 0% -> 0% of each run, Pallas kernels for 8% -> 8%
where the time goes in v21:
time: 39.5 us; the launch traced here: 39.2 us
  blocking collectives  25.7 us (65%)
  starting transfers between devices  5.56 us (14%)
  Pallas kernels  4.63 us (12%)
  waiting for transfers between devices  1.54 us (4%)
  local copies, waits for them, and re-layouts  1.08 us (3%)
  between operations  0.73 us (2%)
    all_to_all x1, blocking collectives, body(): lax.all_to_all(chunks, ('gx', 'gz'), split_axis=0, concat_axis=0, tiled=T...  16.1 us
    all_to_all x1, blocking collectives, body(): lax.all_to_all(eddy_chunks, ('gx', 'gz'), split_axis=0, concat_axis=0, ti...  9.56 us
    ppermute x3, starting transfers between devices, body(): lax.ppermute(reduced, 'gy', [(s, i) for i, s in enumerate(sources_of(step...  5.56 us
    pallas_call x1, Pallas kernels, body(): pl.pallas_call(functools.partial(germano_kernel, nz_parts, width, rows),...  2.53 us
    ppermute x3, waiting for transfers between devices, body(): lax.ppermute(reduced, 'gy', [(s, i) for i, s in enumerate(sources_of(step...  1.54 us
    unnamed x6, local copies, waits for them, and re-layouts  1.07 us
    pallas_call x1, Pallas kernels, body(): pl.pallas_call(functools.partial(finish_kernel, walls), out_shape=jax.Sha...  0.93 us
  transfers between devices with their start and end apart: 4, of which 2 were waited for; matrix products, arithmetic and copies ran while one was open for 0% of the time, Pallas kernels for 8%

profile of v21, /device:TPU:0, one launch (start us, length us, event | category | flops | bytes accessed | tf_op | source)
XLA Modules:
  0.0 39.2 jit_solution(4940651704029014837)
XLA Ops:
  0.6 0.0 copy-start
  0.6 1.1 %copy-done = f32[3,2,192,128]{3,2,1,0:T(8,128)S(1)} copy-done((f32[3,2,192,128]{3,2,1,0:T(8,128)S(1)}, f32[3,2,192,128]{3,2,1,0:T(8,128)}, u32[]{:S(2)}) %copy-start) | copy-done | bytes 589848
  1.7 0.1 pack.1
  1.8 16.1 %all_to_all.10.recv = f32[8,160,128]{2,1,0:T(8,128)S(1)} all-to-all(f32[8,160,128]{2,1,0:T(8,128)S(1)} %pack.1), channel_id=1, replica_groups=mesh['gy'=4,'gx'=4,'gz'=2] {'gx','gz'}, dimensions={0} | all-to-all | bytes 1310720 | tf_op jit(solution)/shard_map/all_to_all | solution.py:637
  17.9 0.0 collective-permute-start
  17.9 2.5 %germano.1.given = f32[8,2,24,128]{3,2,1,0:T(8,128)S(1)} custom-call(s32[1]{0:T(128)} %bitcast.1.rank, s32[1]{0:T(128)S(6)} %rem.18.parity, f32[8,160,128]{2,1,0:T(8,128)S(1)} %all_to_all.10.recv), custom_call_target="tpu_custom_call" | custom-call | flops 14745600 | bytes 786432 | tf_op jit(solution)/shard_map/germano/pallas_call | solution.py:643
  20.5 0.0 copy-start.1
  20.5 0.0 copy-start.2
  20.5 0.0 collective-permute-done.swapped
  20.5 9.6 %all_to_all.11.back = f32[8,2,24,128]{3,2,1,0:T(8,128)S(1)} all-to-all(f32[8,2,24,128]{3,2,1,0:T(8,128)S(1)} %edge.1), channel_id=1, replica_groups=mesh['gy'=4,'gx'=4,'gz'=2] {'gx','gz'}, dimensions={0} | all-to-all | bytes 393216 | tf_op jit(solution)/shard_map/all_to_all | solution.py:672
  30.1 0.0 copy-done.1
  30.1 0.0 copy-done.2
  30.1 0.4 %sweep.1 = (f32[2,192,128]{2,1,0:T(8,128)S(1)}, f32[24,128]{1,0:T(8,128)S(1)}, f32[2,24,5,8,128]{4,3,2,1,0:T(8,128)S(1)}, f32[2,3,5,8,128]{4,3,2,1,0:T(8,128)S(1)}) custom-call(s32[1]{0:T(128)S(6)} %rem.18.parity, f32[8,2,24,128]{3,2,1,0:T(8,128)S(1)} %all_to_all.11.back, f32[3,2,192,128]{3,2,1,0:T(8,128)S(1)} %copy-done.1, f32[3,2,192,128]{3,2,1,0:T(8,128)S(1)} %copy-done.2), custom_call_target="tpu_custom_call" | custom-call | tf_op jit(solution)/shard_map/sweep/pallas_call | solution.py:677
  30.5 1.5 %collective-permute-start.3 = (f32[24,128]{1,0:T(8,128)S(1)}, f32[24,128]{1,0:T(8,128)S(1)}, u32[]{:S(2)}, u32[]{:S(2)}) collective-permute-start(f32[24,128]{1,0:T(8,128)S(1)} %get-tuple-element.14.rest_0_), channel_id=1, source_target_pairs={{16,0},{0,8},{24,16},{8,24},{17,1},{1,9},{25,17},{9,25},{18,2},{2,... | collective-permute-start | bytes 36872 | tf_op jit(solution)/shard_map/ppermute | solution.py:692
  32.0 2.6 %collective-permute-start.2 = (f32[24,128]{1,0:T(8,128)S(1)}, f32[24,128]{1,0:T(8,128)S(1)}, u32[]{:S(2)}, u32[]{:S(2)}) collective-permute-start(f32[24,128]{1,0:T(8,128)S(1)} %get-tuple-element.14.rest_0_), channel_id=1, source_target_pairs={{24,0},{16,8},{8,16},{0,24},{25,1},{17,9},{9,17},{1,25},{26,2},{18... | collective-permute-start | bytes 36872 | tf_op jit(solution)/shard_map/ppermute | solution.py:692
  34.6 1.5 %collective-permute-start.1 = (f32[24,128]{1,0:T(8,128)S(1)}, f32[24,128]{1,0:T(8,128)S(1)}, u32[]{:S(2)}, u32[]{:S(2)}) collective-permute-start(f32[24,128]{1,0:T(8,128)S(1)} %get-tuple-element.14.rest_0_), channel_id=1, source_target_pairs={{8,0},{24,8},{0,16},{16,24},{9,1},{25,9},{1,17},{17,25},{10,2},{26... | collective-permute-start | bytes 36872 | tf_op jit(solution)/shard_map/ppermute | solution.py:692
  36.0 0.7 %spread.1 = (f32[3,2,192,128]{3,2,1,0:T(8,128)S(1)}, f32[2,2,192,128]{3,2,1,0:T(8,128)S(1)}, f32[2,192,128]{2,1,0:T(8,128)}) custom-call(f32[2,24,5,8,128]{4,3,2,1,0:T(8,128)S(1)} %get-tuple-element.9.factors, f32[2,3,5,8,128]{4,3,2,1,0:T(8,128)S(1)} %get-tuple-element.10.tree, f32[3,2,192,128]{3,2,1,0:T(8,128)S(1)} %copy-done.1, ...), custom_call_target="tpu_custom_call" | custom-call | flops 2949120 | bytes 2359296 | tf_op jit(solution)/shard_map/spread/pallas_call | solution.py:695
  36.7 0.0 collective-permute-done.3.rest_3_
  36.8 0.7 %collective-permute-done.2.rest_2_ = f32[24,128]{1,0:T(8,128)S(1)} collective-permute-done((f32[24,128]{1,0:T(8,128)S(1)}, f32[24,128]{1,0:T(8,128)S(1)}, u32[]{:S(2)}, u32[]{:S(2)}) %collective-permute-start.2) | collective-permute-done | bytes 12320 | tf_op jit(solution)/shard_map/ppermute | solution.py:692
  37.5 0.8 %collective-permute-done.1.rest_1_ = f32[24,128]{1,0:T(8,128)S(1)} collective-permute-done((f32[24,128]{1,0:T(8,128)S(1)}, f32[24,128]{1,0:T(8,128)S(1)}, u32[]{:S(2)}, u32[]{:S(2)}) %collective-permute-start.1) | collective-permute-done | bytes 12320 | tf_op jit(solution)/shard_map/ppermute | solution.py:692
  38.3 0.9 %finish.1 = f32[3,2,192,128]{3,2,1,0:T(8,128)} custom-call(s32[1]{0:T(128)} %bitcast.position, f32[3,2,192,128]{3,2,1,0:T(8,128)S(1)} %get-tuple-element.12.particular, f32[2,2,192,128]{3,2,1,0:T(8,128)S(1)} %get-tuple-element.13.response, f32[24,128]{1,0:T(8,128)S(1)} %get-tuple-element.14.rest_0_, f32[24,128]{1,0:T(8,128)S(1)} %collective-permute-done.1.rest_1_, ...), custom_call_target="tpu_custom_call" | custom-call | tf_op jit(solution)/shard_map/finish/pallas_call | solution.py:711
  (2 shorter events, 0.0 us)
Async XLA Ops:
  0.6 1.1 %copy-start = (f32[3,2,192,128]{3,2,1,0:T(8,128)S(1)}, f32[3,2,192,128]{3,2,1,0:T(8,128)}, u32[]{:S(2)}) copy-start(f32[3,2,192,128]{3,2,1,0:T(8,128)} %velocity.5) | copy-start | bytes 1769476
  17.9 2.6 %collective-permute-start = (f32[8,8,128]{2,1,0:T(8,128)S(1)}, f32[8,8,128]{2,1,0:T(8,128)S(1)}, u32[]{:S(2)}, u32[]{:S(2)}) collective-permute-start(f32[8,8,128]{2,1,0:T(8,128)S(1)} %slice.4), channel_id=1, source_target_pairs={{0,1},{1,0},{2,10},{3,7},{4,6},{5,13},{6,4},{7,3},{8,9},{9,8},{10,... | collective-permute-start | bytes 98312 | tf_op jit(solution)/shard_map/ppermute | solution.py:639
  20.5 9.6 %copy-start.1 = (f32[3,2,192,128]{3,2,1,0:T(8,128)S(1)}, f32[3,2,192,128]{3,2,1,0:T(8,128)}, u32[]{:S(2)}) copy-start(f32[3,2,192,128]{3,2,1,0:T(8,128)} %velocity.5) | copy-start | bytes 1769476
  20.5 9.6 %copy-start.2 = (f32[3,2,192,128]{3,2,1,0:T(8,128)S(1)}, f32[3,2,192,128]{3,2,1,0:T(8,128)}, u32[]{:S(2)}) copy-start(f32[3,2,192,128]{3,2,1,0:T(8,128)} %tendency.1) | copy-start | bytes 1769476
  30.5 6.3 %collective-permute-start.3 = (f32[24,128]{1,0:T(8,128)S(1)}, f32[24,128]{1,0:T(8,128)S(1)}, u32[]{:S(2)}, u32[]{:S(2)}) collective-permute-start(f32[24,128]{1,0:T(8,128)S(1)} %get-tuple-element.14.rest_0_), channel_id=1, source_target_pairs={{16,0},{0,8},{24,16},{8,24},{17,1},{1,9},{25,17},{9,25},{18,2},{2,... | collective-permute-start | bytes 36872 | tf_op jit(solution)/shard_map/ppermute | solution.py:692
  32.0 5.5 %collective-permute-start.2 = (f32[24,128]{1,0:T(8,128)S(1)}, f32[24,128]{1,0:T(8,128)S(1)}, u32[]{:S(2)}, u32[]{:S(2)}) collective-permute-start(f32[24,128]{1,0:T(8,128)S(1)} %get-tuple-element.14.rest_0_), channel_id=1, source_target_pairs={{24,0},{16,8},{8,16},{0,24},{25,1},{17,9},{9,17},{1,25},{26,2},{18... | collective-permute-start | bytes 36872 | tf_op jit(solution)/shard_map/ppermute | solution.py:692
  34.6 3.7 %collective-permute-start.1 = (f32[24,128]{1,0:T(8,128)S(1)}, f32[24,128]{1,0:T(8,128)S(1)}, u32[]{:S(2)}, u32[]{:S(2)}) collective-permute-start(f32[24,128]{1,0:T(8,128)S(1)} %get-tuple-element.14.rest_0_), channel_id=1, source_target_pairs={{8,0},{24,8},{0,16},{16,24},{9,1},{25,9},{1,17},{17,25},{10,2},{26... | collective-permute-start | bytes 36872 | tf_op jit(solution)/shard_map/ppermute | solution.py:692

commit v22 on v20

--- a/solution.py
+++ b/solution.py
@@ -78,7 +78,7 @@
 
 
 def outer_ranks(count):
-    return (count - 1, count - 3)
+    return (count - 3, count - 1)
 
 
 def places(parity, count):
@@ -92,31 +92,21 @@
 
 def swap_pairs(walls, count):
     odd, even = outer_ranks(count)
-    spare = count - 5
     partners = {}
 
     def join(a, b):
         partners[a], partners[b] = b, a
 
-    def join_walls(rank, first):
-        for wall in range(first, walls - 1, 2):
-            join((wall, rank), (wall + 1, rank))
-
-    join_walls(even, 0)
-    join_walls(odd, 1)
-    join_walls(spare, 1)
-    join((0, odd), (0, spare))
-    if walls % 2 == 0:
-        join((walls - 1, odd), (walls - 1, spare))
-    others = [r for r in range(count) if r not in (odd, even, spare)]
-    for core in range(2):
-        ranks = [r for r in others if r % 2 == core]
-        half = len(ranks) // 2
+    for core in range(0, count, 2):
+        here = (core, core + 1)
+        if odd in here or even in here:
+            first = 1 if odd in here else 0
+            for wall in range(first, walls - 1, 2):
+                for rank in here:
+                    join((wall, rank), (wall + 1, rank))
         for wall in range(walls):
-            for a, b in zip(ranks[:half], ranks[half : 2 * half]):
-                join((wall, a), (wall, b))
-        for rank in ranks[2 * half :]:
-            join_walls(rank, 0)
+            if (wall, core) not in partners:
+                join((wall, core), (wall, core + 1))
     return [
         (wall * count + rank, to[0] * count + to[1])
         for wall in range(walls)

time: 39.8 us -> 39.5 us (level)
  blocking collectives: 24.7 us -> 25.7 us
  starting transfers between devices: 6.23 us -> 5.27 us
    all_to_all x1, blocking collectives: 8.62 us -> 9.56 us  [body(): lax.all_to_all(eddy_chunks, ('gx', 'gz'), split_axis=0, concat_axis=0, ti...]
    ppermute x1, waiting for transfers between devices: 0.79 us -> 0.01 us  [body(): swapped = lax.ppermute(slot, ('gy', 'gx', 'gz'), swap_pairs(walls, count))]
    ppermute x1, starting transfers between devices: 0.56 us -> 0.01 us  [body(): swapped = lax.ppermute(slot, ('gy', 'gx', 'gz'), swap_pairs(walls, count))]
    ppermute x3, starting transfers between devices: 5.67 us -> 5.27 us  [body(): lax.ppermute(reduced, 'gy', [(s, i) for i, s in enumerate(sources_of(step...]
  transfers between devices with their start and end apart: 4 -> 4, of which waited for: 3 -> 2; matrix products, arithmetic and copies ran while one was open for 0% -> 0% of each run, Pallas kernels for 8% -> 8%
where the time goes in v22:
time: 39.5 us; the launch traced here: 39.2 us
  blocking collectives  25.7 us (65%)
  starting transfers between devices  5.27 us (13%)
  Pallas kernels  4.63 us (12%)
  waiting for transfers between devices  1.82 us (5%)
  local copies, waits for them, and re-layouts  1.08 us (3%)
  between operations  0.73 us (2%)
    all_to_all x1, blocking collectives, body(): lax.all_to_all(chunks, ('gx', 'gz'), split_axis=0, concat_axis=0, tiled=T...  16.1 us
    all_to_all x1, blocking collectives, body(): lax.all_to_all(eddy_chunks, ('gx', 'gz'), split_axis=0, concat_axis=0, ti...  9.56 us
    ppermute x3, starting transfers between devices, body(): lax.ppermute(reduced, 'gy', [(s, i) for i, s in enumerate(sources_of(step...  5.27 us
    pallas_call x1, Pallas kernels, body(): pl.pallas_call(functools.partial(germano_kernel, nz_parts, width, rows),...  2.53 us
    ppermute x3, waiting for transfers between devices, body(): lax.ppermute(reduced, 'gy', [(s, i) for i, s in enumerate(sources_of(step...  1.82 us
    unnamed x6, local copies, waits for them, and re-layouts  1.07 us
    pallas_call x1, Pallas kernels, body(): pl.pallas_call(functools.partial(finish_kernel, walls), out_shape=jax.Sha...  0.93 us
  transfers between devices with their start and end apart: 4, of which 2 were waited for; matrix products, arithmetic and copies ran while one was open for 0% of the time, Pallas kernels for 8%

profile of v22, /device:TPU:0, one launch (start us, length us, event | category | flops | bytes accessed | tf_op | source)
XLA Modules:
  0.0 39.2 jit_solution(6776473901364373438)
XLA Ops:
  0.6 0.0 copy-start
  0.6 1.1 %copy-done = f32[3,2,192,128]{3,2,1,0:T(8,128)S(1)} copy-done((f32[3,2,192,128]{3,2,1,0:T(8,128)S(1)}, f32[3,2,192,128]{3,2,1,0:T(8,128)}, u32[]{:S(2)}) %copy-start) | copy-done | bytes 589848
  1.7 0.1 pack.1
  1.8 16.1 %all_to_all.10.recv = f32[8,160,128]{2,1,0:T(8,128)S(1)} all-to-all(f32[8,160,128]{2,1,0:T(8,128)S(1)} %pack.1), channel_id=1, replica_groups=mesh['gy'=4,'gx'=4,'gz'=2] {'gx','gz'}, dimensions={0} | all-to-all | bytes 1310720 | tf_op jit(solution)/shard_map/all_to_all | solution.py:625
  17.9 0.0 collective-permute-start
  17.9 2.5 %germano.1.given = f32[8,2,24,128]{3,2,1,0:T(8,128)S(1)} custom-call(s32[1]{0:T(128)} %bitcast.1.rank, s32[1]{0:T(128)S(6)} %rem.18.parity, f32[8,160,128]{2,1,0:T(8,128)S(1)} %all_to_all.10.recv), custom_call_target="tpu_custom_call" | custom-call | flops 14745600 | bytes 786432 | tf_op jit(solution)/shard_map/germano/pallas_call | solution.py:631
  20.5 0.0 copy-start.1
  20.5 0.0 copy-start.2
  20.5 0.0 collective-permute-done.swapped
  20.5 9.6 %all_to_all.11.back = f32[8,2,24,128]{3,2,1,0:T(8,128)S(1)} all-to-all(f32[8,2,24,128]{3,2,1,0:T(8,128)S(1)} %edge.1), channel_id=1, replica_groups=mesh['gy'=4,'gx'=4,'gz'=2] {'gx','gz'}, dimensions={0} | all-to-all | bytes 393216 | tf_op jit(solution)/shard_map/all_to_all | solution.py:660
  30.1 0.0 copy-done.1
  30.1 0.0 copy-done.2
  30.1 0.4 %sweep.1 = (f32[2,192,128]{2,1,0:T(8,128)S(1)}, f32[24,128]{1,0:T(8,128)S(1)}, f32[2,24,5,8,128]{4,3,2,1,0:T(8,128)S(1)}, f32[2,3,5,8,128]{4,3,2,1,0:T(8,128)S(1)}) custom-call(s32[1]{0:T(128)S(6)} %rem.18.parity, f32[8,2,24,128]{3,2,1,0:T(8,128)S(1)} %all_to_all.11.back, f32[3,2,192,128]{3,2,1,0:T(8,128)S(1)} %copy-done.1, f32[3,2,192,128]{3,2,1,0:T(8,128)S(1)} %copy-done.2), custom_call_target="tpu_custom_call" | custom-call | tf_op jit(solution)/shard_map/sweep/pallas_call | solution.py:665
  30.5 1.6 %collective-permute-start.3 = (f32[24,128]{1,0:T(8,128)S(1)}, f32[24,128]{1,0:T(8,128)S(1)}, u32[]{:S(2)}, u32[]{:S(2)}) collective-permute-start(f32[24,128]{1,0:T(8,128)S(1)} %get-tuple-element.14.rest_0_), channel_id=1, source_target_pairs={{16,0},{0,8},{24,16},{8,24},{17,1},{1,9},{25,17},{9,25},{18,2},{2,... | collective-permute-start | bytes 36872 | tf_op jit(solution)/shard_map/ppermute | solution.py:680
  32.1 2.5 %collective-permute-start.2 = (f32[24,128]{1,0:T(8,128)S(1)}, f32[24,128]{1,0:T(8,128)S(1)}, u32[]{:S(2)}, u32[]{:S(2)}) collective-permute-start(f32[24,128]{1,0:T(8,128)S(1)} %get-tuple-element.14.rest_0_), channel_id=1, source_target_pairs={{24,0},{16,8},{8,16},{0,24},{25,1},{17,9},{9,17},{1,25},{26,2},{18... | collective-permute-start | bytes 36872 | tf_op jit(solution)/shard_map/ppermute | solution.py:680
  34.6 1.2 %collective-permute-start.1 = (f32[24,128]{1,0:T(8,128)S(1)}, f32[24,128]{1,0:T(8,128)S(1)}, u32[]{:S(2)}, u32[]{:S(2)}) collective-permute-start(f32[24,128]{1,0:T(8,128)S(1)} %get-tuple-element.14.rest_0_), channel_id=1, source_target_pairs={{8,0},{24,8},{0,16},{16,24},{9,1},{25,9},{1,17},{17,25},{10,2},{26... | collective-permute-start | bytes 36872 | tf_op jit(solution)/shard_map/ppermute | solution.py:680
  35.8 0.7 %spread.1 = (f32[3,2,192,128]{3,2,1,0:T(8,128)S(1)}, f32[2,2,192,128]{3,2,1,0:T(8,128)S(1)}, f32[2,192,128]{2,1,0:T(8,128)}) custom-call(f32[2,24,5,8,128]{4,3,2,1,0:T(8,128)S(1)} %get-tuple-element.9.factors, f32[2,3,5,8,128]{4,3,2,1,0:T(8,128)S(1)} %get-tuple-element.10.tree, f32[3,2,192,128]{3,2,1,0:T(8,128)S(1)} %copy-done.1, ...), custom_call_target="tpu_custom_call" | custom-call | flops 2949120 | bytes 2359296 | tf_op jit(solution)/shard_map/spread/pallas_call | solution.py:683
  36.5 0.0 collective-permute-done.3.rest_3_
  36.5 1.1 %collective-permute-done.2.rest_2_ = f32[24,128]{1,0:T(8,128)S(1)} collective-permute-done((f32[24,128]{1,0:T(8,128)S(1)}, f32[24,128]{1,0:T(8,128)S(1)}, u32[]{:S(2)}, u32[]{:S(2)}) %collective-permute-start.2) | collective-permute-done | bytes 12320 | tf_op jit(solution)/shard_map/ppermute | solution.py:680
  37.6 0.7 %collective-permute-done.1.rest_1_ = f32[24,128]{1,0:T(8,128)S(1)} collective-permute-done((f32[24,128]{1,0:T(8,128)S(1)}, f32[24,128]{1,0:T(8,128)S(1)}, u32[]{:S(2)}, u32[]{:S(2)}) %collective-permute-start.1) | collective-permute-done | bytes 12320 | tf_op jit(solution)/shard_map/ppermute | solution.py:680
  38.3 0.9 %finish.1 = f32[3,2,192,128]{3,2,1,0:T(8,128)} custom-call(s32[1]{0:T(128)} %bitcast.position, f32[3,2,192,128]{3,2,1,0:T(8,128)S(1)} %get-tuple-element.12.particular, f32[2,2,192,128]{3,2,1,0:T(8,128)S(1)} %get-tuple-element.13.response, f32[24,128]{1,0:T(8,128)S(1)} %get-tuple-element.14.rest_0_, f32[24,128]{1,0:T(8,128)S(1)} %collective-permute-done.1.rest_1_, ...), custom_call_target="tpu_custom_call" | custom-call | tf_op jit(solution)/shard_map/finish/pallas_call | solution.py:699
  (2 shorter events, 0.0 us)
Async XLA Ops:
  0.6 1.1 %copy-start = (f32[3,2,192,128]{3,2,1,0:T(8,128)S(1)}, f32[3,2,192,128]{3,2,1,0:T(8,128)}, u32[]{:S(2)}) copy-start(f32[3,2,192,128]{3,2,1,0:T(8,128)} %velocity.5) | copy-start | bytes 1769476
  17.9 2.6 %collective-permute-start = (f32[8,8,128]{2,1,0:T(8,128)S(1)}, f32[8,8,128]{2,1,0:T(8,128)S(1)}, u32[]{:S(2)}, u32[]{:S(2)}) collective-permute-start(f32[8,8,128]{2,1,0:T(8,128)S(1)} %slice.4), channel_id=1, source_target_pairs={{0,1},{1,0},{2,3},{3,2},{4,5},{5,4},{6,14},{7,15},{8,9},{9,8},{10,... | collective-permute-start | bytes 98312 | tf_op jit(solution)/shard_map/ppermute | solution.py:627
  20.5 9.6 %copy-start.1 = (f32[3,2,192,128]{3,2,1,0:T(8,128)S(1)}, f32[3,2,192,128]{3,2,1,0:T(8,128)}, u32[]{:S(2)}) copy-start(f32[3,2,192,128]{3,2,1,0:T(8,128)} %velocity.5) | copy-start | bytes 1769476
  20.5 9.6 %copy-start.2 = (f32[3,2,192,128]{3,2,1,0:T(8,128)S(1)}, f32[3,2,192,128]{3,2,1,0:T(8,128)}, u32[]{:S(2)}) copy-start(f32[3,2,192,128]{3,2,1,0:T(8,128)} %tendency.1) | copy-start | bytes 1769476
  30.5 6.0 %collective-permute-start.3 = (f32[24,128]{1,0:T(8,128)S(1)}, f32[24,128]{1,0:T(8,128)S(1)}, u32[]{:S(2)}, u32[]{:S(2)}) collective-permute-start(f32[24,128]{1,0:T(8,128)S(1)} %get-tuple-element.14.rest_0_), channel_id=1, source_target_pairs={{16,0},{0,8},{24,16},{8,24},{17,1},{1,9},{25,17},{9,25},{18,2},{2,... | collective-permute-start | bytes 36872 | tf_op jit(solution)/shard_map/ppermute | solution.py:680
  32.1 5.5 %collective-permute-start.2 = (f32[24,128]{1,0:T(8,128)S(1)}, f32[24,128]{1,0:T(8,128)S(1)}, u32[]{:S(2)}, u32[]{:S(2)}) collective-permute-start(f32[24,128]{1,0:T(8,128)S(1)} %get-tuple-element.14.rest_0_), channel_id=1, source_target_pairs={{24,0},{16,8},{8,16},{0,24},{25,1},{17,9},{9,17},{1,25},{26,2},{18... | collective-permute-start | bytes 36872 | tf_op jit(solution)/shard_map/ppermute | solution.py:680
  34.6 3.7 %collective-permute-start.1 = (f32[24,128]{1,0:T(8,128)S(1)}, f32[24,128]{1,0:T(8,128)S(1)}, u32[]{:S(2)}, u32[]{:S(2)}) collective-permute-start(f32[24,128]{1,0:T(8,128)S(1)} %get-tuple-element.14.rest_0_), channel_id=1, source_target_pairs={{8,0},{24,8},{0,16},{16,24},{9,1},{25,9},{1,17},{17,25},{10,2},{26... | collective-permute-start | bytes 36872 | tf_op jit(solution)/shard_map/ppermute | solution.py:680

commit v23 on v22

--- a/solution.py
+++ b/solution.py
@@ -239,7 +239,7 @@
             for k in range(count):
                 x0, zb = (k // nz_parts) * width, k % nz_parts
                 for x in range(width):
-                    out[k, x, at : at + 1, :] = eddy[x0 + x : x0 + x + 1, zb * lanes : (zb + 1) * lanes]
+                    out[count - 1 - k, x, at : at + 1, :] = eddy[x0 + x : x0 + x + 1, zb * lanes : (zb + 1) * lanes]
 
         pl.when(bottom)(lambda: put(0))
         pl.when(top)(lambda: put(rows - 1))
@@ -357,7 +357,7 @@
     for k in range(count):
         x0, zb = (k // nz_parts) * width, k % nz_parts
         for x in range(width):
-            out[k, x] = coefficient * strains[6, x0 + x, zb]
+            out[count - 1 - k, x] = coefficient * strains[6, x0 + x, zb]
 
 
 def sweep_kernel(parity, back, velocity, tendency, eddy, reduced, factors, tree):
@@ -366,7 +366,7 @@
 
     def fill(rank, place):
         for x in range(width):
-            eddy[x, place * rows : (place + 1) * rows, :] = back[rank, x]
+            eddy[x, place * rows : (place + 1) * rows, :] = back[count - 1 - rank, x]
 
     by_parity(parity, count, fill)
 
@@ -657,7 +657,14 @@
         compiler_params=params(),
         name="edge",
     )(rank, position, recv, swapped, provisional)
-    back = lax.all_to_all(eddy_chunks, ("gx", "gz"), split_axis=0, concat_axis=0, tiled=True)
+    back = lax.all_to_all(
+        eddy_chunks,
+        ("gx", "gz"),
+        split_axis=0,
+        concat_axis=0,
+        tiled=True,
+        axis_index_groups=[list(range(count - 1, -1, -1))],
+    )
 
     length = cells // SEGMENTS
     levels = SEGMENTS.bit_length() - 1

time: 39.5 us -> 37.6 us (0.952)
  blocking collectives: 25.7 us -> 23.7 us
    all_to_all x1, blocking collectives: 9.56 us -> 7.59 us  [body(): lax.all_to_all(eddy_chunks, ('gx', 'gz'), split_axis=0, concat_axis=0, ti...]
  transfers between devices with their start and end apart: 4 -> 4, of which waited for: 2 -> 2; matrix products, arithmetic and copies ran while one was open for 0% -> 0% of each run, Pallas kernels for 8% -> 9%
where the time goes in v23:
time: 37.6 us; the launch traced here: 37.3 us
  blocking collectives  23.7 us (63%)
  starting transfers between devices  5.6 us (15%)
  Pallas kernels  4.63 us (12%)
  waiting for transfers between devices  1.59 us (4%)
  local copies, waits for them, and re-layouts  1.08 us (3%)
  between operations  0.73 us (2%)
    all_to_all x1, blocking collectives, body(): lax.all_to_all(chunks, ('gx', 'gz'), split_axis=0, concat_axis=0, tiled=T...  16.1 us
    all_to_all x1, blocking collectives, body(): lax.all_to_all(eddy_chunks, ('gx', 'gz'), split_axis=0, concat_axis=0, ti...  7.59 us
    ppermute x3, starting transfers between devices, body(): lax.ppermute(reduced, 'gy', [(s, i) for i, s in enumerate(sources_of(step...  5.6 us
    pallas_call x1, Pallas kernels, body(): pl.pallas_call(functools.partial(germano_kernel, nz_parts, width, rows),...  2.53 us
    ppermute x3, waiting for transfers between devices, body(): lax.ppermute(reduced, 'gy', [(s, i) for i, s in enumerate(sources_of(step...  1.58 us
    unnamed x6, local copies, waits for them, and re-layouts  1.07 us
    pallas_call x1, Pallas kernels, body(): pl.pallas_call(functools.partial(finish_kernel, walls), out_shape=jax.Sha...  0.93 us
  transfers between devices with their start and end apart: 4, of which 2 were waited for; matrix products, arithmetic and copies ran while one was open for 0% of the time, Pallas kernels for 9%

profile of v23, /device:TPU:0, one launch (start us, length us, event | category | flops | bytes accessed | tf_op | source)
XLA Modules:
  0.0 37.3 jit_solution(17365792574332823443)
XLA Ops:
  0.6 0.0 copy-start
  0.6 1.1 %copy-done = f32[3,2,192,128]{3,2,1,0:T(8,128)S(1)} copy-done((f32[3,2,192,128]{3,2,1,0:T(8,128)S(1)}, f32[3,2,192,128]{3,2,1,0:T(8,128)}, u32[]{:S(2)}) %copy-start) | copy-done | bytes 589848
  1.7 0.1 pack.1
  1.8 16.1 %all_to_all.10.recv = f32[8,160,128]{2,1,0:T(8,128)S(1)} all-to-all(f32[8,160,128]{2,1,0:T(8,128)S(1)} %pack.1), channel_id=1, replica_groups=mesh['gy'=4,'gx'=4,'gz'=2] {'gx','gz'}, dimensions={0} | all-to-all | bytes 1310720 | tf_op jit(solution)/shard_map/all_to_all | solution.py:625
  17.9 0.0 collective-permute-start
  17.9 2.5 %germano.1.given = f32[8,2,24,128]{3,2,1,0:T(8,128)S(1)} custom-call(s32[1]{0:T(128)} %bitcast.1.rank, s32[1]{0:T(128)S(6)} %rem.18.parity, f32[8,160,128]{2,1,0:T(8,128)S(1)} %all_to_all.10.recv), custom_call_target="tpu_custom_call" | custom-call | flops 14745600 | bytes 786432 | tf_op jit(solution)/shard_map/germano/pallas_call | solution.py:631
  20.5 0.0 copy-start.1
  20.5 0.0 copy-start.2
  20.5 0.0 collective-permute-done.swapped
  20.5 7.6 %all_to_all.11.back = f32[8,2,24,128]{3,2,1,0:T(8,128)S(1)} all-to-all(f32[8,2,24,128]{3,2,1,0:T(8,128)S(1)} %edge.1), channel_id=1, replica_groups={{7,6,5,4,3,2,1,0},{15,14,13,12,11,10,9,8},{23,22,21,20,19,18,17,16},{31..., dimensions={0} | all-to-all | bytes 393216 | tf_op jit(solution)/shard_map/all_to_all | solution.py:660
  28.1 0.0 copy-done.1
  28.1 0.0 copy-done.2
  28.1 0.4 %sweep.1 = (f32[2,192,128]{2,1,0:T(8,128)S(1)}, f32[24,128]{1,0:T(8,128)S(1)}, f32[2,24,5,8,128]{4,3,2,1,0:T(8,128)S(1)}, f32[2,3,5,8,128]{4,3,2,1,0:T(8,128)S(1)}) custom-call(s32[1]{0:T(128)S(6)} %rem.18.parity, f32[8,2,24,128]{3,2,1,0:T(8,128)S(1)} %all_to_all.11.back, f32[3,2,192,128]{3,2,1,0:T(8,128)S(1)} %copy-done.1, f32[3,2,192,128]{3,2,1,0:T(8,128)S(1)} %copy-done.2), custom_call_target="tpu_custom_call" | custom-call | tf_op jit(solution)/shard_map/sweep/pallas_call | solution.py:672
  28.5 2.1 %collective-permute-start.3 = (f32[24,128]{1,0:T(8,128)S(1)}, f32[24,128]{1,0:T(8,128)S(1)}, u32[]{:S(2)}, u32[]{:S(2)}) collective-permute-start(f32[24,128]{1,0:T(8,128)S(1)} %get-tuple-element.14.rest_0_), channel_id=1, source_target_pairs={{16,0},{0,8},{24,16},{8,24},{17,1},{1,9},{25,17},{9,25},{18,2},{2,... | collective-permute-start | bytes 36872 | tf_op jit(solution)/shard_map/ppermute | solution.py:687
  30.6 2.1 %collective-permute-start.2 = (f32[24,128]{1,0:T(8,128)S(1)}, f32[24,128]{1,0:T(8,128)S(1)}, u32[]{:S(2)}, u32[]{:S(2)}) collective-permute-start(f32[24,128]{1,0:T(8,128)S(1)} %get-tuple-element.14.rest_0_), channel_id=1, source_target_pairs={{24,0},{16,8},{8,16},{0,24},{25,1},{17,9},{9,17},{1,25},{26,2},{18... | collective-permute-start | bytes 36872 | tf_op jit(solution)/shard_map/ppermute | solution.py:687
  32.7 1.4 %collective-permute-start.1 = (f32[24,128]{1,0:T(8,128)S(1)}, f32[24,128]{1,0:T(8,128)S(1)}, u32[]{:S(2)}, u32[]{:S(2)}) collective-permute-start(f32[24,128]{1,0:T(8,128)S(1)} %get-tuple-element.14.rest_0_), channel_id=1, source_target_pairs={{8,0},{24,8},{0,16},{16,24},{9,1},{25,9},{1,17},{17,25},{10,2},{26... | collective-permute-start | bytes 36872 | tf_op jit(solution)/shard_map/ppermute | solution.py:687
  34.1 0.7 %spread.1 = (f32[3,2,192,128]{3,2,1,0:T(8,128)S(1)}, f32[2,2,192,128]{3,2,1,0:T(8,128)S(1)}, f32[2,192,128]{2,1,0:T(8,128)}) custom-call(f32[2,24,5,8,128]{4,3,2,1,0:T(8,128)S(1)} %get-tuple-element.9.factors, f32[2,3,5,8,128]{4,3,2,1,0:T(8,128)S(1)} %get-tuple-element.10.tree, f32[3,2,192,128]{3,2,1,0:T(8,128)S(1)} %copy-done.1, ...), custom_call_target="tpu_custom_call" | custom-call | flops 2949120 | bytes 2359296 | tf_op jit(solution)/shard_map/spread/pallas_call | solution.py:690
  34.8 0.0 collective-permute-done.3.rest_3_
  34.8 1.3 %collective-permute-done.2.rest_2_ = f32[24,128]{1,0:T(8,128)S(1)} collective-permute-done((f32[24,128]{1,0:T(8,128)S(1)}, f32[24,128]{1,0:T(8,128)S(1)}, u32[]{:S(2)}, u32[]{:S(2)}) %collective-permute-start.2) | collective-permute-done | bytes 12320 | tf_op jit(solution)/shard_map/ppermute | solution.py:687
  36.1 0.3 collective-permute-done.1.rest_1_
  36.4 0.9 %finish.1 = f32[3,2,192,128]{3,2,1,0:T(8,128)} custom-call(s32[1]{0:T(128)} %bitcast.position, f32[3,2,192,128]{3,2,1,0:T(8,128)S(1)} %get-tuple-element.12.particular, f32[2,2,192,128]{3,2,1,0:T(8,128)S(1)} %get-tuple-element.13.response, f32[24,128]{1,0:T(8,128)S(1)} %get-tuple-element.14.rest_0_, f32[24,128]{1,0:T(8,128)S(1)} %collective-permute-done.1.rest_1_, ...), custom_call_target="tpu_custom_call" | custom-call | tf_op jit(solution)/shard_map/finish/pallas_call | solution.py:706
  (2 shorter events, 0.0 us)
Async XLA Ops:
  0.6 1.1 %copy-start = (f32[3,2,192,128]{3,2,1,0:T(8,128)S(1)}, f32[3,2,192,128]{3,2,1,0:T(8,128)}, u32[]{:S(2)}) copy-start(f32[3,2,192,128]{3,2,1,0:T(8,128)} %velocity.5) | copy-start | bytes 1769476
  17.9 2.6 %collective-permute-start = (f32[8,8,128]{2,1,0:T(8,128)S(1)}, f32[8,8,128]{2,1,0:T(8,128)S(1)}, u32[]{:S(2)}, u32[]{:S(2)}) collective-permute-start(f32[8,8,128]{2,1,0:T(8,128)S(1)} %slice.4), channel_id=1, source_target_pairs={{0,1},{1,0},{2,3},{3,2},{4,5},{5,4},{6,14},{7,15},{8,9},{9,8},{10,... | collective-permute-start | bytes 98312 | tf_op jit(solution)/shard_map/ppermute | solution.py:627
  20.5 7.7 %copy-start.1 = (f32[3,2,192,128]{3,2,1,0:T(8,128)S(1)}, f32[3,2,192,128]{3,2,1,0:T(8,128)}, u32[]{:S(2)}) copy-start(f32[3,2,192,128]{3,2,1,0:T(8,128)} %velocity.5) | copy-start | bytes 1769476
  20.5 7.6 %copy-start.2 = (f32[3,2,192,128]{3,2,1,0:T(8,128)S(1)}, f32[3,2,192,128]{3,2,1,0:T(8,128)}, u32[]{:S(2)}) copy-start(f32[3,2,192,128]{3,2,1,0:T(8,128)} %tendency.1) | copy-start | bytes 1769476
  28.5 6.3 %collective-permute-start.3 = (f32[24,128]{1,0:T(8,128)S(1)}, f32[24,128]{1,0:T(8,128)S(1)}, u32[]{:S(2)}, u32[]{:S(2)}) collective-permute-start(f32[24,128]{1,0:T(8,128)S(1)} %get-tuple-element.14.rest_0_), channel_id=1, source_target_pairs={{16,0},{0,8},{24,16},{8,24},{17,1},{1,9},{25,17},{9,25},{18,2},{2,... | collective-permute-start | bytes 36872 | tf_op jit(solution)/shard_map/ppermute | solution.py:687
  30.6 5.5 %collective-permute-start.2 = (f32[24,128]{1,0:T(8,128)S(1)}, f32[24,128]{1,0:T(8,128)S(1)}, u32[]{:S(2)}, u32[]{:S(2)}) collective-permute-start(f32[24,128]{1,0:T(8,128)S(1)} %get-tuple-element.14.rest_0_), channel_id=1, source_target_pairs={{24,0},{16,8},{8,16},{0,24},{25,1},{17,9},{9,17},{1,25},{26,2},{18... | collective-permute-start | bytes 36872 | tf_op jit(solution)/shard_map/ppermute | solution.py:687
  32.7 3.7 %collective-permute-start.1 = (f32[24,128]{1,0:T(8,128)S(1)}, f32[24,128]{1,0:T(8,128)S(1)}, u32[]{:S(2)}, u32[]{:S(2)}) collective-permute-start(f32[24,128]{1,0:T(8,128)S(1)} %get-tuple-element.14.rest_0_), channel_id=1, source_target_pairs={{8,0},{24,8},{0,16},{16,24},{9,1},{25,9},{1,17},{17,25},{10,2},{26... | collective-permute-start | bytes 36872 | tf_op jit(solution)/shard_map/ppermute | solution.py:687

commit v24 on v22

--- a/solution.py
+++ b/solution.py
@@ -115,6 +115,20 @@
     ]
 
 
+def out_order(count):
+    odd, even = outer_ranks(count)
+    late = (1, 0, even, odd, even - 1)
+    return [r for r in range(count) if r not in late] + list(late)
+
+
+def back_order(count):
+    return [*range(count - 1, 0, -2), *range(count - 2, -1, -2)]
+
+
+def slots_of(order):
+    return [order.index(r) for r in range(len(order))]
+
+
 def by_parity(parity, count, fill):
     outer = outer_ranks(count)
     for rank, place in enumerate(places(0, count)):
@@ -138,7 +152,10 @@
     planes = 3 * width
     slots = planes * rows
 
+    slot_of = slots_of(out_order(count))
+
     def fill(rank, place):
+        rank = slot_of[rank]
         first = place * rows
         beside = [first - 1, first + rows]
         if place == 0:
@@ -177,11 +194,13 @@
     nx = (count // nz_parts) * width
     nz = nz_parts * lanes
     bottom, top = outer_sides(rank, [lax.rem(position[0], 2)], count)
+    came, to = slots_of(out_order(count)), slots_of(back_order(count))
     at_wall = jnp.logical_or(
         jnp.logical_and(bottom, position[0] == 0), jnp.logical_and(top, position[0] == walls - 1)
     )
 
     def rows_of(k, i):
+        k = came[k]
         first = i * rows
         own = [recv[k, first + j : first + j + 1, :] for j in (0, 1, rows - 2, rows - 1)]
         far = jnp.where(at_wall, 0.0, swapped[k, i : i + 1, :])
@@ -239,7 +258,7 @@
             for k in range(count):
                 x0, zb = (k // nz_parts) * width, k % nz_parts
                 for x in range(width):
-                    out[k, x, at : at + 1, :] = eddy[x0 + x : x0 + x + 1, zb * lanes : (zb + 1) * lanes]
+                    out[to[k], x, at : at + 1, :] = eddy[x0 + x : x0 + x + 1, zb * lanes : (zb + 1) * lanes]
 
         pl.when(bottom)(lambda: put(0))
         pl.when(top)(lambda: put(rows - 1))
@@ -264,6 +283,7 @@
     count, _, lanes = recv.shape
     planes = 3 * width
     _, top = outer_sides(rank, parity, count)
+    came, to = slots_of(out_order(count)), slots_of(back_order(count))
     nx = (count // nz_parts) * width
     nz = nz_parts * lanes
     blocks = range(nz_parts)
@@ -274,11 +294,11 @@
         for c in range(3):
             for x in range(width):
                 i = c * width + x
-                vel[c, x0 + x, zb, inner, :] = recv[k, i * rows : (i + 1) * rows, :]
+                vel[c, x0 + x, zb, inner, :] = recv[came[k], i * rows : (i + 1) * rows, :]
                 slots = planes * rows + i
-                near = recv[k, slots : slots + 1, :]
+                near = recv[came[k], slots : slots + 1, :]
                 slots += aligned(planes)
-                other = recv[k, slots : slots + 1, :]
+                other = recv[came[k], slots : slots + 1, :]
                 below = jnp.where(top, other, near)
                 for side, (edge, at) in enumerate(((below, lead - 1), (other, lead + rows))):
                     vel[c, x0 + x, zb, at : at + 1, :] = edge
@@ -357,16 +377,17 @@
     for k in range(count):
         x0, zb = (k // nz_parts) * width, k % nz_parts
         for x in range(width):
-            out[k, x] = coefficient * strains[6, x0 + x, zb]
+            out[to[k], x] = coefficient * strains[6, x0 + x, zb]
 
 
 def sweep_kernel(parity, back, velocity, tendency, eddy, reduced, factors, tree):
     count, width, rows, _ = back.shape
     length = count * rows // SEGMENTS
+    slots = slots_of(back_order(count))
 
     def fill(rank, place):
         for x in range(width):
-            eddy[x, place * rows : (place + 1) * rows, :] = back[rank, x]
+            eddy[x, place * rows : (place + 1) * rows, :] = back[slots[rank], x]
 
     by_parity(parity, count, fill)
 
@@ -600,6 +621,12 @@
     return pltpu.CompilerParams(vmem_limit_bytes=VMEM_BYTES)
 
 
+def swap_chunks(chunks, order):
+    return lax.all_to_all(
+        chunks, ("gx", "gz"), split_axis=0, concat_axis=0, tiled=True, axis_index_groups=[order]
+    )
+
+
 def body(velocity, tendency):
     _, width, cells, lanes = velocity.shape
     nz_parts = lax.axis_size("gz")
@@ -622,7 +649,7 @@
         compiler_params=params(),
         name="pack",
     )(parity, velocity)
-    recv = lax.all_to_all(chunks, ("gx", "gz"), split_axis=0, concat_axis=0, tiled=True)
+    recv = swap_chunks(chunks, out_order(count))
     slot = lax.slice_in_dim(recv, planes * rows, planes * rows + aligned(planes), axis=1)
     swapped = lax.ppermute(slot, ("gy", "gx", "gz"), swap_pairs(walls, count))
     rank = lax.axis_index(("gx", "gz")).astype(jnp.int32).reshape(1)
@@ -657,7 +684,7 @@
         compiler_params=params(),
         name="edge",
     )(rank, position, recv, swapped, provisional)
-    back = lax.all_to_all(eddy_chunks, ("gx", "gz"), split_axis=0, concat_axis=0, tiled=True)
+    back = swap_chunks(eddy_chunks, back_order(count))
 
     length = cells // SEGMENTS
     levels = SEGMENTS.bit_length() - 1

time: 39.5 us -> 37.6 us (0.952)
  blocking collectives: 25.7 us -> 23.7 us
  waiting for transfers between devices: 1.82 us -> 2.23 us
    all_to_all x2, blocking collectives: 25.7 us -> 23.7 us  [swap_chunks(): lax.all_to_all(chunks, ('gx', 'gz'), split_axis=0, concat_axis=0, tiled=T...]
    ppermute x3, waiting for transfers between devices: 1.82 us -> 2.23 us  [body(): lax.ppermute(reduced, 'gy', [(s, i) for i, s in enumerate(sources_of(step...]
    ppermute x3, starting transfers between devices: 5.27 us -> 4.87 us  [body(): lax.ppermute(reduced, 'gy', [(s, i) for i, s in enumerate(sources_of(step...]
  transfers between devices with their start and end apart: 4 -> 4, of which waited for: 2 -> 2; matrix products, arithmetic and copies ran while one was open for 0% -> 0% of each run, Pallas kernels for 8% -> 9%
where the time goes in v24:
time: 37.6 us; the launch traced here: 37.3 us
  blocking collectives  23.7 us (63%)
  starting transfers between devices  4.98 us (13%)
  Pallas kernels  4.63 us (12%)
  waiting for transfers between devices  2.23 us (6%)
  local copies, waits for them, and re-layouts  1.08 us (3%)
  between operations  0.72 us (2%)
    all_to_all x2, blocking collectives, swap_chunks(): lax.all_to_all(chunks, ('gx', 'gz'), split_axis=0, concat_axis=0, tiled=T...  23.7 us
    ppermute x3, starting transfers between devices, body(): lax.ppermute(reduced, 'gy', [(s, i) for i, s in enumerate(sources_of(step...  4.87 us
    pallas_call x1, Pallas kernels, body(): pl.pallas_call(functools.partial(germano_kernel, nz_parts, width, rows),...  2.53 us
    ppermute x3, waiting for transfers between devices, body(): lax.ppermute(reduced, 'gy', [(s, i) for i, s in enumerate(sources_of(step...  2.23 us
    unnamed x6, local copies, waits for them, and re-layouts  1.07 us
    pallas_call x1, Pallas kernels, body(): pl.pallas_call(functools.partial(finish_kernel, walls), out_shape=jax.Sha...  0.93 us
  transfers between devices with their start and end apart: 4, of which 2 were waited for; matrix products, arithmetic and copies ran while one was open for 0% of the time, Pallas kernels for 9%

profile of v24, /device:TPU:0, one launch (start us, length us, event | category | flops | bytes accessed | tf_op | source)
XLA Modules:
  0.0 37.3 jit_solution(9530807960349757354)
XLA Ops:
  0.6 0.0 copy-start
  0.6 1.1 %copy-done = f32[3,2,192,128]{3,2,1,0:T(8,128)S(1)} copy-done((f32[3,2,192,128]{3,2,1,0:T(8,128)S(1)}, f32[3,2,192,128]{3,2,1,0:T(8,128)}, u32[]{:S(2)}) %copy-start) | copy-done | bytes 589848
  1.7 0.1 pack.1
  1.8 15.1 %all_to_all.10.recv = f32[8,160,128]{2,1,0:T(8,128)S(1)} all-to-all(f32[8,160,128]{2,1,0:T(8,128)S(1)} %pack.1), channel_id=1, replica_groups={{2,3,4,1,0,7,5,6},{10,11,12,9,8,15,13,14},{18,19,20,17,16,23,21,22},{26..., dimensions={0} | all-to-all | bytes 1310720 | tf_op jit(solution)/shard_map/all_to_all | solution.py:625
  16.8 0.1 collective-permute-start
  17.0 2.5 %germano.1.given = f32[8,2,24,128]{3,2,1,0:T(8,128)S(1)} custom-call(s32[1]{0:T(128)} %bitcast.1.rank, s32[1]{0:T(128)S(6)} %rem.18.parity, f32[8,160,128]{2,1,0:T(8,128)S(1)} %all_to_all.10.recv), custom_call_target="tpu_custom_call" | custom-call | flops 14745600 | bytes 786432 | tf_op jit(solution)/shard_map/germano/pallas_call | solution.py:658
  19.5 0.0 copy-start.1
  19.5 0.0 copy-start.2
  19.5 0.0 collective-permute-done.swapped
  19.6 8.7 %all_to_all.11.back = f32[8,2,24,128]{3,2,1,0:T(8,128)S(1)} all-to-all(f32[8,2,24,128]{3,2,1,0:T(8,128)S(1)} %edge.1), channel_id=1, replica_groups={{7,5,3,1,6,4,2,0},{15,13,11,9,14,12,10,8},{23,21,19,17,22,20,18,16},{31..., dimensions={0} | all-to-all | bytes 393216 | tf_op jit(solution)/shard_map/all_to_all | solution.py:625
  28.2 0.0 copy-done.1
  28.2 0.0 copy-done.2
  28.2 0.4 %sweep.1 = (f32[2,192,128]{2,1,0:T(8,128)S(1)}, f32[24,128]{1,0:T(8,128)S(1)}, f32[2,24,5,8,128]{4,3,2,1,0:T(8,128)S(1)}, f32[2,3,5,8,128]{4,3,2,1,0:T(8,128)S(1)}) custom-call(s32[1]{0:T(128)S(6)} %rem.18.parity, f32[8,2,24,128]{3,2,1,0:T(8,128)S(1)} %all_to_all.11.back, f32[3,2,192,128]{3,2,1,0:T(8,128)S(1)} %copy-done.1, f32[3,2,192,128]{3,2,1,0:T(8,128)S(1)} %copy-done.2), custom_call_target="tpu_custom_call" | custom-call | tf_op jit(solution)/shard_map/sweep/pallas_call | solution.py:692
  28.6 1.2 %collective-permute-start.3 = (f32[24,128]{1,0:T(8,128)S(1)}, f32[24,128]{1,0:T(8,128)S(1)}, u32[]{:S(2)}, u32[]{:S(2)}) collective-permute-start(f32[24,128]{1,0:T(8,128)S(1)} %get-tuple-element.14.rest_0_), channel_id=1, source_target_pairs={{16,0},{0,8},{24,16},{8,24},{17,1},{1,9},{25,17},{9,25},{18,2},{2,... | collective-permute-start | bytes 36872 | tf_op jit(solution)/shard_map/ppermute | solution.py:707
  29.8 2.9 %collective-permute-start.2 = (f32[24,128]{1,0:T(8,128)S(1)}, f32[24,128]{1,0:T(8,128)S(1)}, u32[]{:S(2)}, u32[]{:S(2)}) collective-permute-start(f32[24,128]{1,0:T(8,128)S(1)} %get-tuple-element.14.rest_0_), channel_id=1, source_target_pairs={{24,0},{16,8},{8,16},{0,24},{25,1},{17,9},{9,17},{1,25},{26,2},{18... | collective-permute-start | bytes 36872 | tf_op jit(solution)/shard_map/ppermute | solution.py:707
  32.7 0.8 %collective-permute-start.1 = (f32[24,128]{1,0:T(8,128)S(1)}, f32[24,128]{1,0:T(8,128)S(1)}, u32[]{:S(2)}, u32[]{:S(2)}) collective-permute-start(f32[24,128]{1,0:T(8,128)S(1)} %get-tuple-element.14.rest_0_), channel_id=1, source_target_pairs={{8,0},{24,8},{0,16},{16,24},{9,1},{25,9},{1,17},{17,25},{10,2},{26... | collective-permute-start | bytes 36872 | tf_op jit(solution)/shard_map/ppermute | solution.py:707
  33.5 0.7 %spread.1 = (f32[3,2,192,128]{3,2,1,0:T(8,128)S(1)}, f32[2,2,192,128]{3,2,1,0:T(8,128)S(1)}, f32[2,192,128]{2,1,0:T(8,128)}) custom-call(f32[2,24,5,8,128]{4,3,2,1,0:T(8,128)S(1)} %get-tuple-element.9.factors, f32[2,3,5,8,128]{4,3,2,1,0:T(8,128)S(1)} %get-tuple-element.10.tree, f32[3,2,192,128]{3,2,1,0:T(8,128)S(1)} %copy-done.1, ...), custom_call_target="tpu_custom_call" | custom-call | flops 2949120 | bytes 2359296 | tf_op jit(solution)/shard_map/spread/pallas_call | solution.py:710
  34.2 0.0 collective-permute-done.3.rest_3_
  34.2 1.1 %collective-permute-done.2.rest_2_ = f32[24,128]{1,0:T(8,128)S(1)} collective-permute-done((f32[24,128]{1,0:T(8,128)S(1)}, f32[24,128]{1,0:T(8,128)S(1)}, u32[]{:S(2)}, u32[]{:S(2)}) %collective-permute-start.2) | collective-permute-done | bytes 12320 | tf_op jit(solution)/shard_map/ppermute | solution.py:707
  35.3 1.1 %collective-permute-done.1.rest_1_ = f32[24,128]{1,0:T(8,128)S(1)} collective-permute-done((f32[24,128]{1,0:T(8,128)S(1)}, f32[24,128]{1,0:T(8,128)S(1)}, u32[]{:S(2)}, u32[]{:S(2)}) %collective-permute-start.1) | collective-permute-done | bytes 12320 | tf_op jit(solution)/shard_map/ppermute | solution.py:707
  36.4 0.9 %finish.1 = f32[3,2,192,128]{3,2,1,0:T(8,128)} custom-call(s32[1]{0:T(128)} %bitcast.position, f32[3,2,192,128]{3,2,1,0:T(8,128)S(1)} %get-tuple-element.12.particular, f32[2,2,192,128]{3,2,1,0:T(8,128)S(1)} %get-tuple-element.13.response, f32[24,128]{1,0:T(8,128)S(1)} %get-tuple-element.14.rest_0_, f32[24,128]{1,0:T(8,128)S(1)} %collective-permute-done.1.rest_1_, ...), custom_call_target="tpu_custom_call" | custom-call | tf_op jit(solution)/shard_map/finish/pallas_call | solution.py:726
  (2 shorter events, 0.0 us)
Async XLA Ops:
  0.6 1.1 %copy-start = (f32[3,2,192,128]{3,2,1,0:T(8,128)S(1)}, f32[3,2,192,128]{3,2,1,0:T(8,128)}, u32[]{:S(2)}) copy-start(f32[3,2,192,128]{3,2,1,0:T(8,128)} %velocity.5) | copy-start | bytes 1769476
  16.8 2.7 %collective-permute-start = (f32[8,8,128]{2,1,0:T(8,128)S(1)}, f32[8,8,128]{2,1,0:T(8,128)S(1)}, u32[]{:S(2)}, u32[]{:S(2)}) collective-permute-start(f32[8,8,128]{2,1,0:T(8,128)S(1)} %slice.4), channel_id=1, source_target_pairs={{0,1},{1,0},{2,3},{3,2},{4,5},{5,4},{6,14},{7,15},{8,9},{9,8},{10,... | collective-permute-start | bytes 98312 | tf_op jit(solution)/shard_map/ppermute | solution.py:654
  19.5 8.7 %copy-start.1 = (f32[3,2,192,128]{3,2,1,0:T(8,128)S(1)}, f32[3,2,192,128]{3,2,1,0:T(8,128)}, u32[]{:S(2)}) copy-start(f32[3,2,192,128]{3,2,1,0:T(8,128)} %velocity.5) | copy-start | bytes 1769476
  19.5 8.7 %copy-start.2 = (f32[3,2,192,128]{3,2,1,0:T(8,128)S(1)}, f32[3,2,192,128]{3,2,1,0:T(8,128)}, u32[]{:S(2)}) copy-start(f32[3,2,192,128]{3,2,1,0:T(8,128)} %tendency.1) | copy-start | bytes 1769476
  28.6 5.6 %collective-permute-start.3 = (f32[24,128]{1,0:T(8,128)S(1)}, f32[24,128]{1,0:T(8,128)S(1)}, u32[]{:S(2)}, u32[]{:S(2)}) collective-permute-start(f32[24,128]{1,0:T(8,128)S(1)} %get-tuple-element.14.rest_0_), channel_id=1, source_target_pairs={{16,0},{0,8},{24,16},{8,24},{17,1},{1,9},{25,17},{9,25},{18,2},{2,... | collective-permute-start | bytes 36872 | tf_op jit(solution)/shard_map/ppermute | solution.py:707
  29.8 5.5 %collective-permute-start.2 = (f32[24,128]{1,0:T(8,128)S(1)}, f32[24,128]{1,0:T(8,128)S(1)}, u32[]{:S(2)}, u32[]{:S(2)}) collective-permute-start(f32[24,128]{1,0:T(8,128)S(1)} %get-tuple-element.14.rest_0_), channel_id=1, source_target_pairs={{24,0},{16,8},{8,16},{0,24},{25,1},{17,9},{9,17},{1,25},{26,2},{18... | collective-permute-start | bytes 36872 | tf_op jit(solution)/shard_map/ppermute | solution.py:707
  32.7 3.7 %collective-permute-start.1 = (f32[24,128]{1,0:T(8,128)S(1)}, f32[24,128]{1,0:T(8,128)S(1)}, u32[]{:S(2)}, u32[]{:S(2)}) collective-permute-start(f32[24,128]{1,0:T(8,128)S(1)} %get-tuple-element.14.rest_0_), channel_id=1, source_target_pairs={{8,0},{24,8},{0,16},{16,24},{9,1},{25,9},{1,17},{17,25},{10,2},{26... | collective-permute-start | bytes 36872 | tf_op jit(solution)/shard_map/ppermute | solution.py:707

commit v25 on v24

--- a/solution.py
+++ b/solution.py
@@ -115,14 +115,21 @@
     ]
 
 
+def ring_of(count):
+    return [0, *range(1, count, 2), *range(count - 2 + count % 2, 0, -2)]
+
+
+def by_core(chips):
+    return [2 * chip + 1 for chip in chips] + [2 * chip for chip in chips]
+
+
 def out_order(count):
-    odd, even = outer_ranks(count)
-    late = (1, 0, even, odd, even - 1)
-    return [r for r in range(count) if r not in late] + list(late)
+    return by_core(ring_of(count // 2))
 
 
 def back_order(count):
-    return [*range(count - 1, 0, -2), *range(count - 2, -1, -2)]
+    first, *others = ring_of(count // 2)
+    return by_core([*others, first])
 
 
 def slots_of(order):
@@ -507,7 +514,7 @@
 
 
 def sources_of(step, count):
-    ring = [0, *range(1, count, 2), *range(count - 2 + count % 2, 0, -2)]
+    ring = ring_of(count)
     return [ring[(ring.index(i) - step) % count] for i in range(count)]
 
 

time: 37.6 us -> 38.4 us (1.021)
  starting transfers between devices: 4.98 us -> 5.76 us
    ppermute x3, starting transfers between devices: 4.87 us -> 5.64 us  [body(): lax.ppermute(reduced, 'gy', [(s, i) for i, s in enumerate(sources_of(step...]
  transfers between devices with their start and end apart: 4 -> 4, of which waited for: 2 -> 2; matrix products, arithmetic and copies ran while one was open for 0% -> 0% of each run, Pallas kernels for 9% -> 8%
where the time goes in v25:
time: 38.4 us; the launch traced here: 38.2 us
  blocking collectives  23.8 us (62%)
  starting transfers between devices  5.76 us (15%)
  Pallas kernels  4.63 us (12%)
  waiting for transfers between devices  2.23 us (6%)
  local copies, waits for them, and re-layouts  1.08 us (3%)
  between operations  0.72 us (2%)
    all_to_all x2, blocking collectives, swap_chunks(): lax.all_to_all(chunks, ('gx', 'gz'), split_axis=0, concat_axis=0, tiled=T...  23.8 us
    ppermute x3, starting transfers between devices, body(): lax.ppermute(reduced, 'gy', [(s, i) for i, s in enumerate(sources_of(step...  5.64 us
    pallas_call x1, Pallas kernels, body(): pl.pallas_call(functools.partial(germano_kernel, nz_parts, width, rows),...  2.53 us
    ppermute x3, waiting for transfers between devices, body(): lax.ppermute(reduced, 'gy', [(s, i) for i, s in enumerate(sources_of(step...  2.23 us
    unnamed x6, local copies, waits for them, and re-layouts  1.07 us
    pallas_call x1, Pallas kernels, body(): pl.pallas_call(functools.partial(finish_kernel, walls), out_shape=jax.Sha...  0.93 us
  transfers between devices with their start and end apart: 4, of which 2 were waited for; matrix products, arithmetic and copies ran while one was open for 0% of the time, Pallas kernels for 8%

profile of v25, /device:TPU:0, one launch (start us, length us, event | category | flops | bytes accessed | tf_op | source)
XLA Modules:
  0.0 38.2 jit_solution(15319714258410539444)
XLA Ops:
  0.6 0.0 copy-start
  0.6 1.1 %copy-done = f32[3,2,192,128]{3,2,1,0:T(8,128)S(1)} copy-done((f32[3,2,192,128]{3,2,1,0:T(8,128)S(1)}, f32[3,2,192,128]{3,2,1,0:T(8,128)}, u32[]{:S(2)}) %copy-start) | copy-done | bytes 589848
  1.7 0.1 pack.1
  1.8 15.3 %all_to_all.10.recv = f32[8,160,128]{2,1,0:T(8,128)S(1)} all-to-all(f32[8,160,128]{2,1,0:T(8,128)S(1)} %pack.1), channel_id=1, replica_groups={{1,3,7,5,0,2,6,4},{9,11,15,13,8,10,14,12},{17,19,23,21,16,18,22,20},{25..., dimensions={0} | all-to-all | bytes 1310720 | tf_op jit(solution)/shard_map/all_to_all | solution.py:632
  17.1 0.1 collective-permute-start
  17.2 2.5 %germano.1.given = f32[8,2,24,128]{3,2,1,0:T(8,128)S(1)} custom-call(s32[1]{0:T(128)} %bitcast.1.rank, s32[1]{0:T(128)S(6)} %rem.18.parity, f32[8,160,128]{2,1,0:T(8,128)S(1)} %all_to_all.10.recv), custom_call_target="tpu_custom_call" | custom-call | flops 14745600 | bytes 786432 | tf_op jit(solution)/shard_map/germano/pallas_call | solution.py:665
  19.7 0.0 copy-start.1
  19.7 0.0 copy-start.2
  19.7 0.0 collective-permute-done.swapped
  19.8 8.5 %all_to_all.11.back = f32[8,2,24,128]{3,2,1,0:T(8,128)S(1)} all-to-all(f32[8,2,24,128]{3,2,1,0:T(8,128)S(1)} %edge.1), channel_id=1, replica_groups={{3,7,5,1,2,6,4,0},{11,15,13,9,10,14,12,8},{19,23,21,17,18,22,20,16},{27..., dimensions={0} | all-to-all | bytes 393216 | tf_op jit(solution)/shard_map/all_to_all | solution.py:632
  28.3 0.0 copy-done.1
  28.3 0.0 copy-done.2
  28.3 0.4 %sweep.1 = (f32[2,192,128]{2,1,0:T(8,128)S(1)}, f32[24,128]{1,0:T(8,128)S(1)}, f32[2,24,5,8,128]{4,3,2,1,0:T(8,128)S(1)}, f32[2,3,5,8,128]{4,3,2,1,0:T(8,128)S(1)}) custom-call(s32[1]{0:T(128)S(6)} %rem.18.parity, f32[8,2,24,128]{3,2,1,0:T(8,128)S(1)} %all_to_all.11.back, f32[3,2,192,128]{3,2,1,0:T(8,128)S(1)} %copy-done.1, f32[3,2,192,128]{3,2,1,0:T(8,128)S(1)} %copy-done.2), custom_call_target="tpu_custom_call" | custom-call | tf_op jit(solution)/shard_map/sweep/pallas_call | solution.py:699
  28.7 2.8 %collective-permute-start.3 = (f32[24,128]{1,0:T(8,128)S(1)}, f32[24,128]{1,0:T(8,128)S(1)}, u32[]{:S(2)}, u32[]{:S(2)}) collective-permute-start(f32[24,128]{1,0:T(8,128)S(1)} %get-tuple-element.14.rest_0_), channel_id=1, source_target_pairs={{16,0},{0,8},{24,16},{8,24},{17,1},{1,9},{25,17},{9,25},{18,2},{2,... | collective-permute-start | bytes 36872 | tf_op jit(solution)/shard_map/ppermute | solution.py:714
  31.5 2.1 %collective-permute-start.2 = (f32[24,128]{1,0:T(8,128)S(1)}, f32[24,128]{1,0:T(8,128)S(1)}, u32[]{:S(2)}, u32[]{:S(2)}) collective-permute-start(f32[24,128]{1,0:T(8,128)S(1)} %get-tuple-element.14.rest_0_), channel_id=1, source_target_pairs={{24,0},{16,8},{8,16},{0,24},{25,1},{17,9},{9,17},{1,25},{26,2},{18... | collective-permute-start | bytes 36872 | tf_op jit(solution)/shard_map/ppermute | solution.py:714
  33.6 0.8 %collective-permute-start.1 = (f32[24,128]{1,0:T(8,128)S(1)}, f32[24,128]{1,0:T(8,128)S(1)}, u32[]{:S(2)}, u32[]{:S(2)}) collective-permute-start(f32[24,128]{1,0:T(8,128)S(1)} %get-tuple-element.14.rest_0_), channel_id=1, source_target_pairs={{8,0},{24,8},{0,16},{16,24},{9,1},{25,9},{1,17},{17,25},{10,2},{26... | collective-permute-start | bytes 36872 | tf_op jit(solution)/shard_map/ppermute | solution.py:714
  34.3 0.7 %spread.1 = (f32[3,2,192,128]{3,2,1,0:T(8,128)S(1)}, f32[2,2,192,128]{3,2,1,0:T(8,128)S(1)}, f32[2,192,128]{2,1,0:T(8,128)}) custom-call(f32[2,24,5,8,128]{4,3,2,1,0:T(8,128)S(1)} %get-tuple-element.9.factors, f32[2,3,5,8,128]{4,3,2,1,0:T(8,128)S(1)} %get-tuple-element.10.tree, f32[3,2,192,128]{3,2,1,0:T(8,128)S(1)} %copy-done.1, ...), custom_call_target="tpu_custom_call" | custom-call | flops 2949120 | bytes 2359296 | tf_op jit(solution)/shard_map/spread/pallas_call | solution.py:717
  35.0 0.0 collective-permute-done.3.rest_3_
  35.0 1.9 %collective-permute-done.2.rest_2_ = f32[24,128]{1,0:T(8,128)S(1)} collective-permute-done((f32[24,128]{1,0:T(8,128)S(1)}, f32[24,128]{1,0:T(8,128)S(1)}, u32[]{:S(2)}, u32[]{:S(2)}) %collective-permute-start.2) | collective-permute-done | bytes 12320 | tf_op jit(solution)/shard_map/ppermute | solution.py:714
  37.0 0.3 collective-permute-done.1.rest_1_
  37.3 0.9 %finish.1 = f32[3,2,192,128]{3,2,1,0:T(8,128)} custom-call(s32[1]{0:T(128)} %bitcast.position, f32[3,2,192,128]{3,2,1,0:T(8,128)S(1)} %get-tuple-element.12.particular, f32[2,2,192,128]{3,2,1,0:T(8,128)S(1)} %get-tuple-element.13.response, f32[24,128]{1,0:T(8,128)S(1)} %get-tuple-element.14.rest_0_, f32[24,128]{1,0:T(8,128)S(1)} %collective-permute-done.1.rest_1_, ...), custom_call_target="tpu_custom_call" | custom-call | tf_op jit(solution)/shard_map/finish/pallas_call | solution.py:733
  (2 shorter events, 0.0 us)
Async XLA Ops:
  0.6 1.1 %copy-start = (f32[3,2,192,128]{3,2,1,0:T(8,128)S(1)}, f32[3,2,192,128]{3,2,1,0:T(8,128)}, u32[]{:S(2)}) copy-start(f32[3,2,192,128]{3,2,1,0:T(8,128)} %velocity.5) | copy-start | bytes 1769476
  17.1 2.7 %collective-permute-start = (f32[8,8,128]{2,1,0:T(8,128)S(1)}, f32[8,8,128]{2,1,0:T(8,128)S(1)}, u32[]{:S(2)}, u32[]{:S(2)}) collective-permute-start(f32[8,8,128]{2,1,0:T(8,128)S(1)} %slice.4), channel_id=1, source_target_pairs={{0,1},{1,0},{2,3},{3,2},{4,5},{5,4},{6,14},{7,15},{8,9},{9,8},{10,... | collective-permute-start | bytes 98312 | tf_op jit(solution)/shard_map/ppermute | solution.py:661
  19.7 8.6 %copy-start.1 = (f32[3,2,192,128]{3,2,1,0:T(8,128)S(1)}, f32[3,2,192,128]{3,2,1,0:T(8,128)}, u32[]{:S(2)}) copy-start(f32[3,2,192,128]{3,2,1,0:T(8,128)} %velocity.5) | copy-start | bytes 1769476
  19.7 8.5 %copy-start.2 = (f32[3,2,192,128]{3,2,1,0:T(8,128)S(1)}, f32[3,2,192,128]{3,2,1,0:T(8,128)}, u32[]{:S(2)}) copy-start(f32[3,2,192,128]{3,2,1,0:T(8,128)} %tendency.1) | copy-start | bytes 1769476
  28.7 6.3 %collective-permute-start.3 = (f32[24,128]{1,0:T(8,128)S(1)}, f32[24,128]{1,0:T(8,128)S(1)}, u32[]{:S(2)}, u32[]{:S(2)}) collective-permute-start(f32[24,128]{1,0:T(8,128)S(1)} %get-tuple-element.14.rest_0_), channel_id=1, source_target_pairs={{16,0},{0,8},{24,16},{8,24},{17,1},{1,9},{25,17},{9,25},{18,2},{2,... | collective-permute-start | bytes 36872 | tf_op jit(solution)/shard_map/ppermute | solution.py:714
  31.5 5.5 %collective-permute-start.2 = (f32[24,128]{1,0:T(8,128)S(1)}, f32[24,128]{1,0:T(8,128)S(1)}, u32[]{:S(2)}, u32[]{:S(2)}) collective-permute-start(f32[24,128]{1,0:T(8,128)S(1)} %get-tuple-element.14.rest_0_), channel_id=1, source_target_pairs={{24,0},{16,8},{8,16},{0,24},{25,1},{17,9},{9,17},{1,25},{26,2},{18... | collective-permute-start | bytes 36872 | tf_op jit(solution)/shard_map/ppermute | solution.py:714
  33.6 3.7 %collective-permute-start.1 = (f32[24,128]{1,0:T(8,128)S(1)}, f32[24,128]{1,0:T(8,128)S(1)}, u32[]{:S(2)}, u32[]{:S(2)}) collective-permute-start(f32[24,128]{1,0:T(8,128)S(1)} %get-tuple-element.14.rest_0_), channel_id=1, source_target_pairs={{8,0},{24,8},{0,16},{16,24},{9,1},{25,9},{1,17},{17,25},{10,2},{26... | collective-permute-start | bytes 36872 | tf_op jit(solution)/shard_map/ppermute | solution.py:714

commit v26 on v25

--- a/solution.py
+++ b/solution.py
@@ -128,8 +128,7 @@
 
 
 def back_order(count):
-    first, *others = ring_of(count // 2)
-    return by_core([*others, first])
+    return by_core(range(count // 2 - 1, -1, -1))
 
 
 def slots_of(order):

time: 38.4 us -> 37.5 us (0.977)
  starting transfers between devices: 5.76 us -> 5.26 us
    ppermute x3, starting transfers between devices: 5.64 us -> 5.14 us  [body(): lax.ppermute(reduced, 'gy', [(s, i) for i, s in enumerate(sources_of(step...]
  transfers between devices with their start and end apart: 4 -> 4, of which waited for: 2 -> 2; matrix products, arithmetic and copies ran while one was open for 0% -> 0% of each run, Pallas kernels for 8% -> 9%
where the time goes in v26:
time: 37.5 us; the launch traced here: 37.3 us
  blocking collectives  23.5 us (63%)
  starting transfers between devices  5.26 us (14%)
  Pallas kernels  4.63 us (12%)
  waiting for transfers between devices  2.08 us (6%)
  local copies, waits for them, and re-layouts  1.08 us (3%)
  between operations  0.72 us (2%)
    all_to_all x2, blocking collectives, swap_chunks(): lax.all_to_all(chunks, ('gx', 'gz'), split_axis=0, concat_axis=0, tiled=T...  23.5 us
    ppermute x3, starting transfers between devices, body(): lax.ppermute(reduced, 'gy', [(s, i) for i, s in enumerate(sources_of(step...  5.14 us
    pallas_call x1, Pallas kernels, body(): pl.pallas_call(functools.partial(germano_kernel, nz_parts, width, rows),...  2.53 us
    ppermute x3, waiting for transfers between devices, body(): lax.ppermute(reduced, 'gy', [(s, i) for i, s in enumerate(sources_of(step...  2.08 us
    unnamed x6, local copies, waits for them, and re-layouts  1.07 us
    pallas_call x1, Pallas kernels, body(): pl.pallas_call(functools.partial(finish_kernel, walls), out_shape=jax.Sha...  0.93 us
  transfers between devices with their start and end apart: 4, of which 2 were waited for; matrix products, arithmetic and copies ran while one was open for 0% of the time, Pallas kernels for 9%

profile of v26, /device:TPU:0, one launch (start us, length us, event | category | flops | bytes accessed | tf_op | source)
XLA Modules:
  0.0 37.3 jit_solution(17079377515087793914)
XLA Ops:
  0.6 0.0 copy-start
  0.6 1.1 %copy-done = f32[3,2,192,128]{3,2,1,0:T(8,128)S(1)} copy-done((f32[3,2,192,128]{3,2,1,0:T(8,128)S(1)}, f32[3,2,192,128]{3,2,1,0:T(8,128)}, u32[]{:S(2)}) %copy-start) | copy-done | bytes 589848
  1.7 0.1 pack.1
  1.8 15.3 %all_to_all.10.recv = f32[8,160,128]{2,1,0:T(8,128)S(1)} all-to-all(f32[8,160,128]{2,1,0:T(8,128)S(1)} %pack.1), channel_id=1, replica_groups={{1,3,7,5,0,2,6,4},{9,11,15,13,8,10,14,12},{17,19,23,21,16,18,22,20},{25..., dimensions={0} | all-to-all | bytes 1310720 | tf_op jit(solution)/shard_map/all_to_all | solution.py:631
  17.1 0.1 collective-permute-start
  17.2 2.5 %germano.1.given = f32[8,2,24,128]{3,2,1,0:T(8,128)S(1)} custom-call(s32[1]{0:T(128)} %bitcast.1.rank, s32[1]{0:T(128)S(6)} %rem.18.parity, f32[8,160,128]{2,1,0:T(8,128)S(1)} %all_to_all.10.recv), custom_call_target="tpu_custom_call" | custom-call | flops 14745600 | bytes 786432 | tf_op jit(solution)/shard_map/germano/pallas_call | solution.py:664
  19.7 0.0 copy-start.1
  19.7 0.0 copy-start.2
  19.7 0.0 collective-permute-done.swapped
  19.8 8.2 %all_to_all.11.back = f32[8,2,24,128]{3,2,1,0:T(8,128)S(1)} all-to-all(f32[8,2,24,128]{3,2,1,0:T(8,128)S(1)} %edge.1), channel_id=1, replica_groups={{7,5,3,1,6,4,2,0},{15,13,11,9,14,12,10,8},{23,21,19,17,22,20,18,16},{31..., dimensions={0} | all-to-all | bytes 393216 | tf_op jit(solution)/shard_map/all_to_all | solution.py:631
  28.0 0.0 copy-done.1
  28.0 0.0 copy-done.2
  28.0 0.4 %sweep.1 = (f32[2,192,128]{2,1,0:T(8,128)S(1)}, f32[24,128]{1,0:T(8,128)S(1)}, f32[2,24,5,8,128]{4,3,2,1,0:T(8,128)S(1)}, f32[2,3,5,8,128]{4,3,2,1,0:T(8,128)S(1)}) custom-call(s32[1]{0:T(128)S(6)} %rem.18.parity, f32[8,2,24,128]{3,2,1,0:T(8,128)S(1)} %all_to_all.11.back, f32[3,2,192,128]{3,2,1,0:T(8,128)S(1)} %copy-done.1, f32[3,2,192,128]{3,2,1,0:T(8,128)S(1)} %copy-done.2), custom_call_target="tpu_custom_call" | custom-call | tf_op jit(solution)/shard_map/sweep/pallas_call | solution.py:698
  28.4 2.2 %collective-permute-start.3 = (f32[24,128]{1,0:T(8,128)S(1)}, f32[24,128]{1,0:T(8,128)S(1)}, u32[]{:S(2)}, u32[]{:S(2)}) collective-permute-start(f32[24,128]{1,0:T(8,128)S(1)} %get-tuple-element.14.rest_0_), channel_id=1, source_target_pairs={{16,0},{0,8},{24,16},{8,24},{17,1},{1,9},{25,17},{9,25},{18,2},{2,... | collective-permute-start | bytes 36872 | tf_op jit(solution)/shard_map/ppermute | solution.py:713
  30.6 2.1 %collective-permute-start.2 = (f32[24,128]{1,0:T(8,128)S(1)}, f32[24,128]{1,0:T(8,128)S(1)}, u32[]{:S(2)}, u32[]{:S(2)}) collective-permute-start(f32[24,128]{1,0:T(8,128)S(1)} %get-tuple-element.14.rest_0_), channel_id=1, source_target_pairs={{24,0},{16,8},{8,16},{0,24},{25,1},{17,9},{9,17},{1,25},{26,2},{18... | collective-permute-start | bytes 36872 | tf_op jit(solution)/shard_map/ppermute | solution.py:713
  32.7 0.9 %collective-permute-start.1 = (f32[24,128]{1,0:T(8,128)S(1)}, f32[24,128]{1,0:T(8,128)S(1)}, u32[]{:S(2)}, u32[]{:S(2)}) collective-permute-start(f32[24,128]{1,0:T(8,128)S(1)} %get-tuple-element.14.rest_0_), channel_id=1, source_target_pairs={{8,0},{24,8},{0,16},{16,24},{9,1},{25,9},{1,17},{17,25},{10,2},{26... | collective-permute-start | bytes 36872 | tf_op jit(solution)/shard_map/ppermute | solution.py:713
  33.6 0.7 %spread.1 = (f32[3,2,192,128]{3,2,1,0:T(8,128)S(1)}, f32[2,2,192,128]{3,2,1,0:T(8,128)S(1)}, f32[2,192,128]{2,1,0:T(8,128)}) custom-call(f32[2,24,5,8,128]{4,3,2,1,0:T(8,128)S(1)} %get-tuple-element.9.factors, f32[2,3,5,8,128]{4,3,2,1,0:T(8,128)S(1)} %get-tuple-element.10.tree, f32[3,2,192,128]{3,2,1,0:T(8,128)S(1)} %copy-done.1, ...), custom_call_target="tpu_custom_call" | custom-call | flops 2949120 | bytes 2359296 | tf_op jit(solution)/shard_map/spread/pallas_call | solution.py:716
  34.3 0.0 collective-permute-done.3.rest_3_
  34.3 1.8 %collective-permute-done.2.rest_2_ = f32[24,128]{1,0:T(8,128)S(1)} collective-permute-done((f32[24,128]{1,0:T(8,128)S(1)}, f32[24,128]{1,0:T(8,128)S(1)}, u32[]{:S(2)}, u32[]{:S(2)}) %collective-permute-start.2) | collective-permute-done | bytes 12320 | tf_op jit(solution)/shard_map/ppermute | solution.py:713
  36.1 0.3 collective-permute-done.1.rest_1_
  36.4 0.9 %finish.1 = f32[3,2,192,128]{3,2,1,0:T(8,128)} custom-call(s32[1]{0:T(128)} %bitcast.position, f32[3,2,192,128]{3,2,1,0:T(8,128)S(1)} %get-tuple-element.12.particular, f32[2,2,192,128]{3,2,1,0:T(8,128)S(1)} %get-tuple-element.13.response, f32[24,128]{1,0:T(8,128)S(1)} %get-tuple-element.14.rest_0_, f32[24,128]{1,0:T(8,128)S(1)} %collective-permute-done.1.rest_1_, ...), custom_call_target="tpu_custom_call" | custom-call | tf_op jit(solution)/shard_map/finish/pallas_call | solution.py:732
  (2 shorter events, 0.0 us)
Async XLA Ops:
  0.6 1.1 %copy-start = (f32[3,2,192,128]{3,2,1,0:T(8,128)S(1)}, f32[3,2,192,128]{3,2,1,0:T(8,128)}, u32[]{:S(2)}) copy-start(f32[3,2,192,128]{3,2,1,0:T(8,128)} %velocity.5) | copy-start | bytes 1769476
  17.1 2.7 %collective-permute-start = (f32[8,8,128]{2,1,0:T(8,128)S(1)}, f32[8,8,128]{2,1,0:T(8,128)S(1)}, u32[]{:S(2)}, u32[]{:S(2)}) collective-permute-start(f32[8,8,128]{2,1,0:T(8,128)S(1)} %slice.4), channel_id=1, source_target_pairs={{0,1},{1,0},{2,3},{3,2},{4,5},{5,4},{6,14},{7,15},{8,9},{9,8},{10,... | collective-permute-start | bytes 98312 | tf_op jit(solution)/shard_map/ppermute | solution.py:660
  19.7 8.3 %copy-start.1 = (f32[3,2,192,128]{3,2,1,0:T(8,128)S(1)}, f32[3,2,192,128]{3,2,1,0:T(8,128)}, u32[]{:S(2)}) copy-start(f32[3,2,192,128]{3,2,1,0:T(8,128)} %velocity.5) | copy-start | bytes 1769476
  19.7 8.3 %copy-start.2 = (f32[3,2,192,128]{3,2,1,0:T(8,128)S(1)}, f32[3,2,192,128]{3,2,1,0:T(8,128)}, u32[]{:S(2)}) copy-start(f32[3,2,192,128]{3,2,1,0:T(8,128)} %tendency.1) | copy-start | bytes 1769476
  28.4 5.8 %collective-permute-start.3 = (f32[24,128]{1,0:T(8,128)S(1)}, f32[24,128]{1,0:T(8,128)S(1)}, u32[]{:S(2)}, u32[]{:S(2)}) collective-permute-start(f32[24,128]{1,0:T(8,128)S(1)} %get-tuple-element.14.rest_0_), channel_id=1, source_target_pairs={{16,0},{0,8},{24,16},{8,24},{17,1},{1,9},{25,17},{9,25},{18,2},{2,... | collective-permute-start | bytes 36872 | tf_op jit(solution)/shard_map/ppermute | solution.py:713
  30.6 5.5 %collective-permute-start.2 = (f32[24,128]{1,0:T(8,128)S(1)}, f32[24,128]{1,0:T(8,128)S(1)}, u32[]{:S(2)}, u32[]{:S(2)}) collective-permute-start(f32[24,128]{1,0:T(8,128)S(1)} %get-tuple-element.14.rest_0_), channel_id=1, source_target_pairs={{24,0},{16,8},{8,16},{0,24},{25,1},{17,9},{9,17},{1,25},{26,2},{18... | collective-permute-start | bytes 36872 | tf_op jit(solution)/shard_map/ppermute | solution.py:713
  32.7 3.7 %collective-permute-start.1 = (f32[24,128]{1,0:T(8,128)S(1)}, f32[24,128]{1,0:T(8,128)S(1)}, u32[]{:S(2)}, u32[]{:S(2)}) collective-permute-start(f32[24,128]{1,0:T(8,128)S(1)} %get-tuple-element.14.rest_0_), channel_id=1, source_target_pairs={{8,0},{24,8},{0,16},{16,24},{9,1},{25,9},{1,17},{17,25},{10,2},{26... | collective-permute-start | bytes 36872 | tf_op jit(solution)/shard_map/ppermute | solution.py:713

commit v27 on v26

--- a/solution.py
+++ b/solution.py
@@ -513,8 +513,7 @@
 
 
 def sources_of(step, count):
-    ring = ring_of(count)
-    return [ring[(ring.index(i) - step) % count] for i in range(count)]
+    return [(i - step) % count for i in range(count)]
 
 
 def exchange_order(count):

time: 37.5 us -> 37 us (0.987)
  waiting for transfers between devices: 2.08 us -> 0.99 us
  starting transfers between devices: 5.26 us -> 5.81 us
    ppermute x3, waiting for transfers between devices: 2.08 us -> 0.98 us  [body(): lax.ppermute(reduced, 'gy', [(s, i) for i, s in enumerate(sources_of(step...]
    ppermute x3, starting transfers between devices: 5.14 us -> 5.69 us  [body(): lax.ppermute(reduced, 'gy', [(s, i) for i, s in enumerate(sources_of(step...]
where the time goes in v27:
time: 37 us; the launch traced here: 36.7 us
  blocking collectives  23.5 us (64%)
  starting transfers between devices  5.81 us (16%)
  Pallas kernels  4.63 us (13%)
  local copies, waits for them, and re-layouts  1.08 us (3%)
  waiting for transfers between devices  0.99 us (3%)
  between operations  0.72 us (2%)
    all_to_all x2, blocking collectives, swap_chunks(): lax.all_to_all(chunks, ('gx', 'gz'), split_axis=0, concat_axis=0, tiled=T...  23.5 us
    ppermute x3, starting transfers between devices, body(): lax.ppermute(reduced, 'gy', [(s, i) for i, s in enumerate(sources_of(step...  5.69 us
    pallas_call x1, Pallas kernels, body(): pl.pallas_call(functools.partial(germano_kernel, nz_parts, width, rows),...  2.53 us
    unnamed x6, local copies, waits for them, and re-layouts  1.07 us
    ppermute x3, waiting for transfers between devices, body(): lax.ppermute(reduced, 'gy', [(s, i) for i, s in enumerate(sources_of(step...  0.98 us
    pallas_call x1, Pallas kernels, body(): pl.pallas_call(functools.partial(finish_kernel, walls), out_shape=jax.Sha...  0.93 us
  transfers between devices with their start and end apart: 4, of which 2 were waited for; matrix products, arithmetic and copies ran while one was open for 0% of the time, Pallas kernels for 9%

profile of v27, /device:TPU:0, one launch (start us, length us, event | category | flops | bytes accessed | tf_op | source)
XLA Modules:
  0.0 36.7 jit_solution(3332254046755487183)
XLA Ops:
  0.6 0.0 copy-start
  0.6 1.1 %copy-done = f32[3,2,192,128]{3,2,1,0:T(8,128)S(1)} copy-done((f32[3,2,192,128]{3,2,1,0:T(8,128)S(1)}, f32[3,2,192,128]{3,2,1,0:T(8,128)}, u32[]{:S(2)}) %copy-start) | copy-done | bytes 589848
  1.7 0.1 pack.1
  1.8 15.3 %all_to_all.10.recv = f32[8,160,128]{2,1,0:T(8,128)S(1)} all-to-all(f32[8,160,128]{2,1,0:T(8,128)S(1)} %pack.1), channel_id=1, replica_groups={{1,3,7,5,0,2,6,4},{9,11,15,13,8,10,14,12},{17,19,23,21,16,18,22,20},{25..., dimensions={0} | all-to-all | bytes 1310720 | tf_op jit(solution)/shard_map/all_to_all | solution.py:630
  17.1 0.1 collective-permute-start
  17.2 2.5 %germano.1.given = f32[8,2,24,128]{3,2,1,0:T(8,128)S(1)} custom-call(s32[1]{0:T(128)} %bitcast.1.rank, s32[1]{0:T(128)S(6)} %rem.18.parity, f32[8,160,128]{2,1,0:T(8,128)S(1)} %all_to_all.10.recv), custom_call_target="tpu_custom_call" | custom-call | flops 14745600 | bytes 786432 | tf_op jit(solution)/shard_map/germano/pallas_call | solution.py:663
  19.7 0.0 copy-start.1
  19.7 0.0 copy-start.2
  19.7 0.0 collective-permute-done.swapped
  19.8 8.2 %all_to_all.11.back = f32[8,2,24,128]{3,2,1,0:T(8,128)S(1)} all-to-all(f32[8,2,24,128]{3,2,1,0:T(8,128)S(1)} %edge.1), channel_id=1, replica_groups={{7,5,3,1,6,4,2,0},{15,13,11,9,14,12,10,8},{23,21,19,17,22,20,18,16},{31..., dimensions={0} | all-to-all | bytes 393216 | tf_op jit(solution)/shard_map/all_to_all | solution.py:630
  28.0 0.0 copy-done.1
  28.0 0.0 copy-done.2
  28.0 0.4 %sweep.1 = (f32[2,192,128]{2,1,0:T(8,128)S(1)}, f32[24,128]{1,0:T(8,128)S(1)}, f32[2,24,5,8,128]{4,3,2,1,0:T(8,128)S(1)}, f32[2,3,5,8,128]{4,3,2,1,0:T(8,128)S(1)}) custom-call(s32[1]{0:T(128)S(6)} %rem.18.parity, f32[8,2,24,128]{3,2,1,0:T(8,128)S(1)} %all_to_all.11.back, f32[3,2,192,128]{3,2,1,0:T(8,128)S(1)} %copy-done.1, f32[3,2,192,128]{3,2,1,0:T(8,128)S(1)} %copy-done.2), custom_call_target="tpu_custom_call" | custom-call | tf_op jit(solution)/shard_map/sweep/pallas_call | solution.py:697
  28.4 2.2 %collective-permute-start.3 = (f32[24,128]{1,0:T(8,128)S(1)}, f32[24,128]{1,0:T(8,128)S(1)}, u32[]{:S(2)}, u32[]{:S(2)}) collective-permute-start(f32[24,128]{1,0:T(8,128)S(1)} %get-tuple-element.14.rest_0_), channel_id=1, source_target_pairs={{24,0},{0,8},{8,16},{16,24},{25,1},{1,9},{9,17},{17,25},{26,2},{2,... | collective-permute-start | bytes 36872 | tf_op jit(solution)/shard_map/ppermute | solution.py:712
  30.6 1.5 %collective-permute-start.2 = (f32[24,128]{1,0:T(8,128)S(1)}, f32[24,128]{1,0:T(8,128)S(1)}, u32[]{:S(2)}, u32[]{:S(2)}) collective-permute-start(f32[24,128]{1,0:T(8,128)S(1)} %get-tuple-element.14.rest_0_), channel_id=1, source_target_pairs={{16,0},{24,8},{0,16},{8,24},{17,1},{25,9},{1,17},{9,25},{18,2},{26... | collective-permute-start | bytes 36872 | tf_op jit(solution)/shard_map/ppermute | solution.py:712
  32.1 2.0 %collective-permute-start.1 = (f32[24,128]{1,0:T(8,128)S(1)}, f32[24,128]{1,0:T(8,128)S(1)}, u32[]{:S(2)}, u32[]{:S(2)}) collective-permute-start(f32[24,128]{1,0:T(8,128)S(1)} %get-tuple-element.14.rest_0_), channel_id=1, source_target_pairs={{8,0},{16,8},{24,16},{0,24},{9,1},{17,9},{25,17},{1,25},{10,2},{18... | collective-permute-start | bytes 36872 | tf_op jit(solution)/shard_map/ppermute | solution.py:712
  34.1 0.7 %spread.1 = (f32[3,2,192,128]{3,2,1,0:T(8,128)S(1)}, f32[2,2,192,128]{3,2,1,0:T(8,128)S(1)}, f32[2,192,128]{2,1,0:T(8,128)}) custom-call(f32[2,24,5,8,128]{4,3,2,1,0:T(8,128)S(1)} %get-tuple-element.9.factors, f32[2,3,5,8,128]{4,3,2,1,0:T(8,128)S(1)} %get-tuple-element.10.tree, f32[3,2,192,128]{3,2,1,0:T(8,128)S(1)} %copy-done.1, ...), custom_call_target="tpu_custom_call" | custom-call | flops 2949120 | bytes 2359296 | tf_op jit(solution)/shard_map/spread/pallas_call | solution.py:715
  34.8 0.0 collective-permute-done.3.rest_3_
  34.8 0.3 collective-permute-done.2.rest_2_
  35.2 0.6 %collective-permute-done.1.rest_1_ = f32[24,128]{1,0:T(8,128)S(1)} collective-permute-done((f32[24,128]{1,0:T(8,128)S(1)}, f32[24,128]{1,0:T(8,128)S(1)}, u32[]{:S(2)}, u32[]{:S(2)}) %collective-permute-start.1) | collective-permute-done | bytes 12320 | tf_op jit(solution)/shard_map/ppermute | solution.py:712
  35.8 0.9 %finish.1 = f32[3,2,192,128]{3,2,1,0:T(8,128)} custom-call(s32[1]{0:T(128)} %bitcast.position, f32[3,2,192,128]{3,2,1,0:T(8,128)S(1)} %get-tuple-element.12.particular, f32[2,2,192,128]{3,2,1,0:T(8,128)S(1)} %get-tuple-element.13.response, f32[24,128]{1,0:T(8,128)S(1)} %get-tuple-element.14.rest_0_, f32[24,128]{1,0:T(8,128)S(1)} %collective-permute-done.1.rest_1_, ...), custom_call_target="tpu_custom_call" | custom-call | tf_op jit(solution)/shard_map/finish/pallas_call | solution.py:731
  (2 shorter events, 0.0 us)
Async XLA Ops:
  0.6 1.1 %copy-start = (f32[3,2,192,128]{3,2,1,0:T(8,128)S(1)}, f32[3,2,192,128]{3,2,1,0:T(8,128)}, u32[]{:S(2)}) copy-start(f32[3,2,192,128]{3,2,1,0:T(8,128)} %velocity.5) | copy-start | bytes 1769476
  17.1 2.7 %collective-permute-start = (f32[8,8,128]{2,1,0:T(8,128)S(1)}, f32[8,8,128]{2,1,0:T(8,128)S(1)}, u32[]{:S(2)}, u32[]{:S(2)}) collective-permute-start(f32[8,8,128]{2,1,0:T(8,128)S(1)} %slice.4), channel_id=1, source_target_pairs={{0,1},{1,0},{2,3},{3,2},{4,5},{5,4},{6,14},{7,15},{8,9},{9,8},{10,... | collective-permute-start | bytes 98312 | tf_op jit(solution)/shard_map/ppermute | solution.py:659
  19.7 8.3 %copy-start.1 = (f32[3,2,192,128]{3,2,1,0:T(8,128)S(1)}, f32[3,2,192,128]{3,2,1,0:T(8,128)}, u32[]{:S(2)}) copy-start(f32[3,2,192,128]{3,2,1,0:T(8,128)} %velocity.5) | copy-start | bytes 1769476
  19.7 8.3 %copy-start.2 = (f32[3,2,192,128]{3,2,1,0:T(8,128)S(1)}, f32[3,2,192,128]{3,2,1,0:T(8,128)}, u32[]{:S(2)}) copy-start(f32[3,2,192,128]{3,2,1,0:T(8,128)} %tendency.1) | copy-start | bytes 1769476
  28.4 6.4 %collective-permute-start.3 = (f32[24,128]{1,0:T(8,128)S(1)}, f32[24,128]{1,0:T(8,128)S(1)}, u32[]{:S(2)}, u32[]{:S(2)}) collective-permute-start(f32[24,128]{1,0:T(8,128)S(1)} %get-tuple-element.14.rest_0_), channel_id=1, source_target_pairs={{24,0},{0,8},{8,16},{16,24},{25,1},{1,9},{9,17},{17,25},{26,2},{2,... | collective-permute-start | bytes 36872 | tf_op jit(solution)/shard_map/ppermute | solution.py:712
  30.6 4.6 %collective-permute-start.2 = (f32[24,128]{1,0:T(8,128)S(1)}, f32[24,128]{1,0:T(8,128)S(1)}, u32[]{:S(2)}, u32[]{:S(2)}) collective-permute-start(f32[24,128]{1,0:T(8,128)S(1)} %get-tuple-element.14.rest_0_), channel_id=1, source_target_pairs={{16,0},{24,8},{0,16},{8,24},{17,1},{25,9},{1,17},{9,25},{18,2},{26... | collective-permute-start | bytes 36872 | tf_op jit(solution)/shard_map/ppermute | solution.py:712
  32.1 3.7 %collective-permute-start.1 = (f32[24,128]{1,0:T(8,128)S(1)}, f32[24,128]{1,0:T(8,128)S(1)}, u32[]{:S(2)}, u32[]{:S(2)}) collective-permute-start(f32[24,128]{1,0:T(8,128)S(1)} %get-tuple-element.14.rest_0_), channel_id=1, source_target_pairs={{8,0},{16,8},{24,16},{0,24},{9,1},{17,9},{25,17},{1,25},{10,2},{18... | collective-permute-start | bytes 36872 | tf_op jit(solution)/shard_map/ppermute | solution.py:712

commit v28 on v27

--- a/solution.py
+++ b/solution.py
@@ -313,8 +313,11 @@
     lower = slice(lead - 1, lead - 1 + rows)
     upper = slice(lead + 1, lead + 1 + rows)
 
-    def smooth_x(read, x):
-        return (read((x - 1) % nx) + read((x + 1) % nx)) + 2.0 * read(x)
+    def paired(read, x):
+        return read(x) + read((x + 1) % nx)
+
+    def smooth_x(sums, x):
+        return sums((x - 1) % nx) + sums(x)
 
     def keep_strain(field, x, kept, scale):
         left, right = (x - 1) % nx, (x + 1) % nx
@@ -330,10 +333,11 @@
     for x in range(nx):
         keep_strain(vel, x, strains, 1.0)
         for c in range(3):
-            for zb, f in enumerate(smooth_z([vel[c, x, zb, inner, :] for zb in blocks])):
+            fields = [paired(lambda at: vel[c, at, zb, inner, :], x) for zb in blocks]
+            for zb, f in enumerate(smooth_z(fields)):
                 part[c, x, zb] = f
     for c in range(3):
-        rims = [smooth_z([ends[c, x, zb] for zb in blocks]) for x in range(nx)]
+        rims = [smooth_z([paired(lambda at: ends[c, at, zb], x) for zb in blocks]) for x in range(nx)]
         for x in range(nx):
             for zb in blocks:
                 rim = smooth_x(lambda at: rims[at][zb], x)
@@ -343,13 +347,16 @@
     def filter_z(read, kept):
         if not on_matrix_unit:
             for x in range(nx):
-                for zb, f in enumerate(smooth_z([read(x, zb) for zb in blocks])):
+                fields = [paired(lambda at: read(at, zb), x) for zb in blocks]
+                for zb, f in enumerate(smooth_z(fields)):
                     part[kept, x, zb] = f
             return
         half = nx // 2
         for x0 in (0, half):
+            fields = [[read((x0 + x) % nx, zb) for zb in blocks] for x in range(half + 1)]
             planes_here = [
-                jnp.concatenate([read(x, zb) for zb in blocks], axis=1) for x in range(x0, x0 + half)
+                jnp.concatenate([f + g for f, g in zip(fields[x], fields[x + 1])], axis=1)
+                for x in range(half)
             ]
             total = times_band(jnp.concatenate(planes_here, axis=0), band)
             for x in range(half):

time: 37 us -> 36.9 us (level)
  no operation moved by 1% of the time
where the time goes in v28:
time: 36.9 us; the launch traced here: 36.7 us
  blocking collectives  23.5 us (64%)
  starting transfers between devices  5.89 us (16%)
  Pallas kernels  4.55 us (12%)
  local copies, waits for them, and re-layouts  1.08 us (3%)
  waiting for transfers between devices  0.9 us (2%)
  between operations  0.72 us (2%)
    all_to_all x2, blocking collectives, swap_chunks(): lax.all_to_all(chunks, ('gx', 'gz'), split_axis=0, concat_axis=0, tiled=T...  23.5 us
    ppermute x3, starting transfers between devices, body(): lax.ppermute(reduced, 'gy', [(s, i) for i, s in enumerate(sources_of(step...  5.78 us
    pallas_call x1, Pallas kernels, body(): pl.pallas_call(functools.partial(germano_kernel, nz_parts, width, rows),...  2.45 us
    unnamed x6, local copies, waits for them, and re-layouts  1.07 us
    pallas_call x1, Pallas kernels, body(): pl.pallas_call(functools.partial(finish_kernel, walls), out_shape=jax.Sha...  0.93 us
    ppermute x3, waiting for transfers between devices, body(): lax.ppermute(reduced, 'gy', [(s, i) for i, s in enumerate(sources_of(step...  0.9 us
  transfers between devices with their start and end apart: 4, of which 2 were waited for; matrix products, arithmetic and copies ran while one was open for 0% of the time, Pallas kernels for 9%

profile of v28, /device:TPU:0, one launch (start us, length us, event | category | flops | bytes accessed | tf_op | source)
XLA Modules:
  0.0 36.7 jit_solution(16265272605122260381)
XLA Ops:
  0.6 0.0 copy-start
  0.6 1.1 %copy-done = f32[3,2,192,128]{3,2,1,0:T(8,128)S(1)} copy-done((f32[3,2,192,128]{3,2,1,0:T(8,128)S(1)}, f32[3,2,192,128]{3,2,1,0:T(8,128)}, u32[]{:S(2)}) %copy-start) | copy-done | bytes 589848
  1.7 0.1 pack.1
  1.8 15.3 %all_to_all.10.recv = f32[8,160,128]{2,1,0:T(8,128)S(1)} all-to-all(f32[8,160,128]{2,1,0:T(8,128)S(1)} %pack.1), channel_id=1, replica_groups={{1,3,7,5,0,2,6,4},{9,11,15,13,8,10,14,12},{17,19,23,21,16,18,22,20},{25..., dimensions={0} | all-to-all | bytes 1310720 | tf_op jit(solution)/shard_map/all_to_all | solution.py:637
  17.1 0.1 collective-permute-start
  17.2 2.4 %germano.1.given = f32[8,2,24,128]{3,2,1,0:T(8,128)S(1)} custom-call(s32[1]{0:T(128)} %bitcast.1.rank, s32[1]{0:T(128)S(6)} %rem.18.parity, f32[8,160,128]{2,1,0:T(8,128)S(1)} %all_to_all.10.recv), custom_call_target="tpu_custom_call" | custom-call | flops 14745600 | bytes 786432 | tf_op jit(solution)/shard_map/germano/pallas_call | solution.py:670
  19.6 0.0 copy-start.1
  19.6 0.0 copy-start.2
  19.7 0.0 collective-permute-done.swapped
  19.7 8.2 %all_to_all.11.back = f32[8,2,24,128]{3,2,1,0:T(8,128)S(1)} all-to-all(f32[8,2,24,128]{3,2,1,0:T(8,128)S(1)} %edge.1), channel_id=1, replica_groups={{7,5,3,1,6,4,2,0},{15,13,11,9,14,12,10,8},{23,21,19,17,22,20,18,16},{31..., dimensions={0} | all-to-all | bytes 393216 | tf_op jit(solution)/shard_map/all_to_all | solution.py:637
  27.9 0.0 copy-done.1
  27.9 0.0 copy-done.2
  27.9 0.4 %sweep.1 = (f32[2,192,128]{2,1,0:T(8,128)S(1)}, f32[24,128]{1,0:T(8,128)S(1)}, f32[2,24,5,8,128]{4,3,2,1,0:T(8,128)S(1)}, f32[2,3,5,8,128]{4,3,2,1,0:T(8,128)S(1)}) custom-call(s32[1]{0:T(128)S(6)} %rem.18.parity, f32[8,2,24,128]{3,2,1,0:T(8,128)S(1)} %all_to_all.11.back, f32[3,2,192,128]{3,2,1,0:T(8,128)S(1)} %copy-done.1, f32[3,2,192,128]{3,2,1,0:T(8,128)S(1)} %copy-done.2), custom_call_target="tpu_custom_call" | custom-call | tf_op jit(solution)/shard_map/sweep/pallas_call | solution.py:704
  28.4 2.2 %collective-permute-start.3 = (f32[24,128]{1,0:T(8,128)S(1)}, f32[24,128]{1,0:T(8,128)S(1)}, u32[]{:S(2)}, u32[]{:S(2)}) collective-permute-start(f32[24,128]{1,0:T(8,128)S(1)} %get-tuple-element.14.rest_0_), channel_id=1, source_target_pairs={{24,0},{0,8},{8,16},{16,24},{25,1},{1,9},{9,17},{17,25},{26,2},{2,... | collective-permute-start | bytes 36872 | tf_op jit(solution)/shard_map/ppermute | solution.py:719
  30.5 1.5 %collective-permute-start.2 = (f32[24,128]{1,0:T(8,128)S(1)}, f32[24,128]{1,0:T(8,128)S(1)}, u32[]{:S(2)}, u32[]{:S(2)}) collective-permute-start(f32[24,128]{1,0:T(8,128)S(1)} %get-tuple-element.14.rest_0_), channel_id=1, source_target_pairs={{16,0},{24,8},{0,16},{8,24},{17,1},{25,9},{1,17},{9,25},{18,2},{26... | collective-permute-start | bytes 36872 | tf_op jit(solution)/shard_map/ppermute | solution.py:719
  32.0 2.1 %collective-permute-start.1 = (f32[24,128]{1,0:T(8,128)S(1)}, f32[24,128]{1,0:T(8,128)S(1)}, u32[]{:S(2)}, u32[]{:S(2)}) collective-permute-start(f32[24,128]{1,0:T(8,128)S(1)} %get-tuple-element.14.rest_0_), channel_id=1, source_target_pairs={{8,0},{16,8},{24,16},{0,24},{9,1},{17,9},{25,17},{1,25},{10,2},{18... | collective-permute-start | bytes 36872 | tf_op jit(solution)/shard_map/ppermute | solution.py:719
  34.1 0.7 %spread.1 = (f32[3,2,192,128]{3,2,1,0:T(8,128)S(1)}, f32[2,2,192,128]{3,2,1,0:T(8,128)S(1)}, f32[2,192,128]{2,1,0:T(8,128)}) custom-call(f32[2,24,5,8,128]{4,3,2,1,0:T(8,128)S(1)} %get-tuple-element.9.factors, f32[2,3,5,8,128]{4,3,2,1,0:T(8,128)S(1)} %get-tuple-element.10.tree, f32[3,2,192,128]{3,2,1,0:T(8,128)S(1)} %copy-done.1, ...), custom_call_target="tpu_custom_call" | custom-call | flops 2949120 | bytes 2359296 | tf_op jit(solution)/shard_map/spread/pallas_call | solution.py:722
  34.8 0.0 collective-permute-done.3.rest_3_
  34.8 0.3 collective-permute-done.2.rest_2_
  35.1 0.6 %collective-permute-done.1.rest_1_ = f32[24,128]{1,0:T(8,128)S(1)} collective-permute-done((f32[24,128]{1,0:T(8,128)S(1)}, f32[24,128]{1,0:T(8,128)S(1)}, u32[]{:S(2)}, u32[]{:S(2)}) %collective-permute-start.1) | collective-permute-done | bytes 12320 | tf_op jit(solution)/shard_map/ppermute | solution.py:719
  35.7 0.9 %finish.1 = f32[3,2,192,128]{3,2,1,0:T(8,128)} custom-call(s32[1]{0:T(128)} %bitcast.position, f32[3,2,192,128]{3,2,1,0:T(8,128)S(1)} %get-tuple-element.12.particular, f32[2,2,192,128]{3,2,1,0:T(8,128)S(1)} %get-tuple-element.13.response, f32[24,128]{1,0:T(8,128)S(1)} %get-tuple-element.14.rest_0_, f32[24,128]{1,0:T(8,128)S(1)} %collective-permute-done.1.rest_1_, ...), custom_call_target="tpu_custom_call" | custom-call | tf_op jit(solution)/shard_map/finish/pallas_call | solution.py:738
  (2 shorter events, 0.0 us)
Async XLA Ops:
  0.6 1.1 %copy-start = (f32[3,2,192,128]{3,2,1,0:T(8,128)S(1)}, f32[3,2,192,128]{3,2,1,0:T(8,128)}, u32[]{:S(2)}) copy-start(f32[3,2,192,128]{3,2,1,0:T(8,128)} %velocity.5) | copy-start | bytes 1769476
  17.1 2.6 %collective-permute-start = (f32[8,8,128]{2,1,0:T(8,128)S(1)}, f32[8,8,128]{2,1,0:T(8,128)S(1)}, u32[]{:S(2)}, u32[]{:S(2)}) collective-permute-start(f32[8,8,128]{2,1,0:T(8,128)S(1)} %slice.4), channel_id=1, source_target_pairs={{0,1},{1,0},{2,3},{3,2},{4,5},{5,4},{6,14},{7,15},{8,9},{9,8},{10,... | collective-permute-start | bytes 98312 | tf_op jit(solution)/shard_map/ppermute | solution.py:666
  19.6 8.3 %copy-start.1 = (f32[3,2,192,128]{3,2,1,0:T(8,128)S(1)}, f32[3,2,192,128]{3,2,1,0:T(8,128)}, u32[]{:S(2)}) copy-start(f32[3,2,192,128]{3,2,1,0:T(8,128)} %velocity.5) | copy-start | bytes 1769476
  19.6 8.3 %copy-start.2 = (f32[3,2,192,128]{3,2,1,0:T(8,128)S(1)}, f32[3,2,192,128]{3,2,1,0:T(8,128)}, u32[]{:S(2)}) copy-start(f32[3,2,192,128]{3,2,1,0:T(8,128)} %tendency.1) | copy-start | bytes 1769476
  28.4 6.5 %collective-permute-start.3 = (f32[24,128]{1,0:T(8,128)S(1)}, f32[24,128]{1,0:T(8,128)S(1)}, u32[]{:S(2)}, u32[]{:S(2)}) collective-permute-start(f32[24,128]{1,0:T(8,128)S(1)} %get-tuple-element.14.rest_0_), channel_id=1, source_target_pairs={{24,0},{0,8},{8,16},{16,24},{25,1},{1,9},{9,17},{17,25},{26,2},{2,... | collective-permute-start | bytes 36872 | tf_op jit(solution)/shard_map/ppermute | solution.py:719
  30.5 4.6 %collective-permute-start.2 = (f32[24,128]{1,0:T(8,128)S(1)}, f32[24,128]{1,0:T(8,128)S(1)}, u32[]{:S(2)}, u32[]{:S(2)}) collective-permute-start(f32[24,128]{1,0:T(8,128)S(1)} %get-tuple-element.14.rest_0_), channel_id=1, source_target_pairs={{16,0},{24,8},{0,16},{8,24},{17,1},{25,9},{1,17},{9,25},{18,2},{26... | collective-permute-start | bytes 36872 | tf_op jit(solution)/shard_map/ppermute | solution.py:719
  32.0 3.7 %collective-permute-start.1 = (f32[24,128]{1,0:T(8,128)S(1)}, f32[24,128]{1,0:T(8,128)S(1)}, u32[]{:S(2)}, u32[]{:S(2)}) collective-permute-start(f32[24,128]{1,0:T(8,128)S(1)} %get-tuple-element.14.rest_0_), channel_id=1, source_target_pairs={{8,0},{16,8},{24,16},{0,24},{9,1},{17,9},{25,17},{1,25},{10,2},{18... | collective-permute-start | bytes 36872 | tf_op jit(solution)/shard_map/ppermute | solution.py:719

commit v29 on v28

--- a/solution.py
+++ b/solution.py
@@ -201,15 +201,15 @@
     nz = nz_parts * lanes
     bottom, top = outer_sides(rank, [lax.rem(position[0], 2)], count)
     came, to = slots_of(out_order(count)), slots_of(back_order(count))
-    at_wall = jnp.logical_or(
-        jnp.logical_and(bottom, position[0] == 0), jnp.logical_and(top, position[0] == walls - 1)
+    at_seam = jnp.logical_or(
+        jnp.logical_and(bottom, position[0] > 0), jnp.logical_and(top, position[0] < walls - 1)
     )
 
     def rows_of(k, i):
         k = came[k]
         first = i * rows
         own = [recv[k, first + j : first + j + 1, :] for j in (0, 1, rows - 2, rows - 1)]
-        far = jnp.where(at_wall, 0.0, swapped[k, i : i + 1, :])
+        far = swapped[k, i : i + 1, :]
         return (
             jnp.where(bottom, far, own[2]),
             jnp.where(bottom, own[0], own[3]),
@@ -236,7 +236,7 @@
             [roll_z(f, -1) - roll_z(f, 1) for f in centre],
         )
 
-    @pl.when(jnp.logical_or(bottom, top))
+    @pl.when(at_seam)
     def _():
         for k in range(count):
             x0, zb = (k // nz_parts) * width, k % nz_parts
@@ -285,10 +285,12 @@
     return jnp.maximum(plane_lm * scale / (plane_mm * scale + 1e-06), 0.0)
 
 
-def germano_kernel(nz_parts, width, rows, rank, parity, recv, out, vel, filt, ends, strains, means, part):
+def germano_kernel(nz_parts, width, rows, walls, rank, position, recv, out, vel, filt, ends, strains, means, part):
     count, _, lanes = recv.shape
     planes = 3 * width
-    _, top = outer_sides(rank, parity, count)
+    bottom, top = outer_sides(rank, [lax.rem(position[0], 2)], count)
+    floor = jnp.logical_and(bottom, position[0] == 0)
+    ceiling = jnp.logical_and(top, position[0] == walls - 1)
     came, to = slots_of(out_order(count)), slots_of(back_order(count))
     nx = (count // nz_parts) * width
     nz = nz_parts * lanes
@@ -305,8 +307,9 @@
                 near = recv[came[k], slots : slots + 1, :]
                 slots += aligned(planes)
                 other = recv[came[k], slots : slots + 1, :]
-                below = jnp.where(top, other, near)
-                for side, (edge, at) in enumerate(((below, lead - 1), (other, lead + rows))):
+                below = jnp.where(floor, 0.0, jnp.where(top, other, near))
+                above = jnp.where(ceiling, 0.0, other)
+                for side, (edge, at) in enumerate(((below, lead - 1), (above, lead + rows))):
                     vel[c, x0 + x, zb, at : at + 1, :] = edge
                     ends[c, x0 + x, zb, side : side + 1, :] = edge
 
@@ -668,7 +671,7 @@
     chunk_shape = jax.ShapeDtypeStruct((count, width, rows, lanes), f32)
     cells_here = nx * nz_parts * rows * lanes
     provisional = pl.pallas_call(
-        functools.partial(germano_kernel, nz_parts, width, rows),
+        functools.partial(germano_kernel, nz_parts, width, rows, walls),
         out_shape=chunk_shape,
         in_specs=in_smem(2) + in_vmem(1),
         out_specs=pl.BlockSpec(memory_space=pltpu.VMEM),
@@ -685,7 +688,7 @@
             flops=300 * cells_here, bytes_accessed=16 * cells_here, transcendentals=2 * cells_here
         ),
         name="germano",
-    )(rank, parity, recv)
+    )(rank, position, recv)
     eddy_chunks = pl.pallas_call(
         functools.partial(edge_kernel, nz_parts, width, rows, walls),
         out_shape=chunk_shape,

time: 36.9 us -> 36.9 us (level)
  no operation moved by 1% of the time
where the time goes in v29:
time: 36.9 us; the launch traced here: 36.7 us
  blocking collectives  23.5 us (64%)
  starting transfers between devices  5.88 us (16%)
  Pallas kernels  4.56 us (12%)
  local copies, waits for them, and re-layouts  1.08 us (3%)
  waiting for transfers between devices  0.92 us (2%)
  between operations  0.72 us (2%)
    all_to_all x2, blocking collectives, swap_chunks(): lax.all_to_all(chunks, ('gx', 'gz'), split_axis=0, concat_axis=0, tiled=T...  23.5 us
    ppermute x3, starting transfers between devices, body(): lax.ppermute(reduced, 'gy', [(s, i) for i, s in enumerate(sources_of(step...  5.77 us
    pallas_call x1, Pallas kernels, body(): pl.pallas_call(functools.partial(germano_kernel, nz_parts, width, rows, w...  2.46 us
    unnamed x6, local copies, waits for them, and re-layouts  1.07 us
    pallas_call x1, Pallas kernels, body(): pl.pallas_call(functools.partial(finish_kernel, walls), out_shape=jax.Sha...  0.93 us
    ppermute x3, waiting for transfers between devices, body(): lax.ppermute(reduced, 'gy', [(s, i) for i, s in enumerate(sources_of(step...  0.92 us
  transfers between devices with their start and end apart: 4, of which 2 were waited for; matrix products, arithmetic and copies ran while one was open for 0% of the time, Pallas kernels for 9%

profile of v29, /device:TPU:0, one launch (start us, length us, event | category | flops | bytes accessed | tf_op | source)
XLA Modules:
  0.0 36.7 jit_solution(16673065898494854716)
XLA Ops:
  0.6 0.0 copy-start
  0.6 1.1 %copy-done = f32[3,2,192,128]{3,2,1,0:T(8,128)S(1)} copy-done((f32[3,2,192,128]{3,2,1,0:T(8,128)S(1)}, f32[3,2,192,128]{3,2,1,0:T(8,128)}, u32[]{:S(2)}) %copy-start) | copy-done | bytes 589848
  1.7 0.1 pack.1
  1.8 15.3 %all_to_all.10.recv = f32[8,160,128]{2,1,0:T(8,128)S(1)} all-to-all(f32[8,160,128]{2,1,0:T(8,128)S(1)} %pack.1), channel_id=1, replica_groups={{1,3,7,5,0,2,6,4},{9,11,15,13,8,10,14,12},{17,19,23,21,16,18,22,20},{25..., dimensions={0} | all-to-all | bytes 1310720 | tf_op jit(solution)/shard_map/all_to_all | solution.py:640
  17.1 0.1 collective-permute-start
  17.2 2.5 %germano.1.given = f32[8,2,24,128]{3,2,1,0:T(8,128)S(1)} custom-call(s32[1]{0:T(128)} %bitcast.1.rank, s32[1]{0:T(128)} %bitcast.position, f32[8,160,128]{2,1,0:T(8,128)S(1)} %all_to_all.10.recv), custom_call_target="tpu_custom_call" | custom-call | flops 14745600 | bytes 786432 | tf_op jit(solution)/shard_map/germano/pallas_call | solution.py:673
  19.6 0.0 copy-start.1
  19.7 0.0 copy-start.2
  19.7 0.0 collective-permute-done.swapped
  19.7 8.2 %all_to_all.11.back = f32[8,2,24,128]{3,2,1,0:T(8,128)S(1)} all-to-all(f32[8,2,24,128]{3,2,1,0:T(8,128)S(1)} %edge.1), channel_id=1, replica_groups={{7,5,3,1,6,4,2,0},{15,13,11,9,14,12,10,8},{23,21,19,17,22,20,18,16},{31..., dimensions={0} | all-to-all | bytes 393216 | tf_op jit(solution)/shard_map/all_to_all | solution.py:640
  27.9 0.0 copy-done.1
  28.0 0.0 copy-done.2
  28.0 0.4 %sweep.1 = (f32[2,192,128]{2,1,0:T(8,128)S(1)}, f32[24,128]{1,0:T(8,128)S(1)}, f32[2,24,5,8,128]{4,3,2,1,0:T(8,128)S(1)}, f32[2,3,5,8,128]{4,3,2,1,0:T(8,128)S(1)}) custom-call(s32[1]{0:T(128)S(6)} %rem.18.parity, f32[8,2,24,128]{3,2,1,0:T(8,128)S(1)} %all_to_all.11.back, f32[3,2,192,128]{3,2,1,0:T(8,128)S(1)} %copy-done.1, f32[3,2,192,128]{3,2,1,0:T(8,128)S(1)} %copy-done.2), custom_call_target="tpu_custom_call" | custom-call | tf_op jit(solution)/shard_map/sweep/pallas_call | solution.py:707
  28.4 2.2 %collective-permute-start.3 = (f32[24,128]{1,0:T(8,128)S(1)}, f32[24,128]{1,0:T(8,128)S(1)}, u32[]{:S(2)}, u32[]{:S(2)}) collective-permute-start(f32[24,128]{1,0:T(8,128)S(1)} %get-tuple-element.14.rest_0_), channel_id=1, source_target_pairs={{24,0},{0,8},{8,16},{16,24},{25,1},{1,9},{9,17},{17,25},{26,2},{2,... | collective-permute-start | bytes 36872 | tf_op jit(solution)/shard_map/ppermute | solution.py:722
  30.5 1.5 %collective-permute-start.2 = (f32[24,128]{1,0:T(8,128)S(1)}, f32[24,128]{1,0:T(8,128)S(1)}, u32[]{:S(2)}, u32[]{:S(2)}) collective-permute-start(f32[24,128]{1,0:T(8,128)S(1)} %get-tuple-element.14.rest_0_), channel_id=1, source_target_pairs={{16,0},{24,8},{0,16},{8,24},{17,1},{25,9},{1,17},{9,25},{18,2},{26... | collective-permute-start | bytes 36872 | tf_op jit(solution)/shard_map/ppermute | solution.py:722
  32.0 2.1 %collective-permute-start.1 = (f32[24,128]{1,0:T(8,128)S(1)}, f32[24,128]{1,0:T(8,128)S(1)}, u32[]{:S(2)}, u32[]{:S(2)}) collective-permute-start(f32[24,128]{1,0:T(8,128)S(1)} %get-tuple-element.14.rest_0_), channel_id=1, source_target_pairs={{8,0},{16,8},{24,16},{0,24},{9,1},{17,9},{25,17},{1,25},{10,2},{18... | collective-permute-start | bytes 36872 | tf_op jit(solution)/shard_map/ppermute | solution.py:722
  34.1 0.7 %spread.1 = (f32[3,2,192,128]{3,2,1,0:T(8,128)S(1)}, f32[2,2,192,128]{3,2,1,0:T(8,128)S(1)}, f32[2,192,128]{2,1,0:T(8,128)}) custom-call(f32[2,24,5,8,128]{4,3,2,1,0:T(8,128)S(1)} %get-tuple-element.9.factors, f32[2,3,5,8,128]{4,3,2,1,0:T(8,128)S(1)} %get-tuple-element.10.tree, f32[3,2,192,128]{3,2,1,0:T(8,128)S(1)} %copy-done.1, ...), custom_call_target="tpu_custom_call" | custom-call | flops 2949120 | bytes 2359296 | tf_op jit(solution)/shard_map/spread/pallas_call | solution.py:725
  34.8 0.0 collective-permute-done.3.rest_3_
  34.8 0.3 collective-permute-done.2.rest_2_
  35.1 0.6 %collective-permute-done.1.rest_1_ = f32[24,128]{1,0:T(8,128)S(1)} collective-permute-done((f32[24,128]{1,0:T(8,128)S(1)}, f32[24,128]{1,0:T(8,128)S(1)}, u32[]{:S(2)}, u32[]{:S(2)}) %collective-permute-start.1) | collective-permute-done | bytes 12320 | tf_op jit(solution)/shard_map/ppermute | solution.py:722
  35.7 0.9 %finish.1 = f32[3,2,192,128]{3,2,1,0:T(8,128)} custom-call(s32[1]{0:T(128)} %bitcast.position, f32[3,2,192,128]{3,2,1,0:T(8,128)S(1)} %get-tuple-element.12.particular, f32[2,2,192,128]{3,2,1,0:T(8,128)S(1)} %get-tuple-element.13.response, f32[24,128]{1,0:T(8,128)S(1)} %get-tuple-element.14.rest_0_, f32[24,128]{1,0:T(8,128)S(1)} %collective-permute-done.1.rest_1_, ...), custom_call_target="tpu_custom_call" | custom-call | tf_op jit(solution)/shard_map/finish/pallas_call | solution.py:741
  (2 shorter events, 0.0 us)
Async XLA Ops:
  0.6 1.1 %copy-start = (f32[3,2,192,128]{3,2,1,0:T(8,128)S(1)}, f32[3,2,192,128]{3,2,1,0:T(8,128)}, u32[]{:S(2)}) copy-start(f32[3,2,192,128]{3,2,1,0:T(8,128)} %velocity.5) | copy-start | bytes 1769476
  17.1 2.6 %collective-permute-start = (f32[8,8,128]{2,1,0:T(8,128)S(1)}, f32[8,8,128]{2,1,0:T(8,128)S(1)}, u32[]{:S(2)}, u32[]{:S(2)}) collective-permute-start(f32[8,8,128]{2,1,0:T(8,128)S(1)} %slice.4), channel_id=1, source_target_pairs={{0,1},{1,0},{2,3},{3,2},{4,5},{5,4},{6,14},{7,15},{8,9},{9,8},{10,... | collective-permute-start | bytes 98312 | tf_op jit(solution)/shard_map/ppermute | solution.py:669
  19.6 8.3 %copy-start.1 = (f32[3,2,192,128]{3,2,1,0:T(8,128)S(1)}, f32[3,2,192,128]{3,2,1,0:T(8,128)}, u32[]{:S(2)}) copy-start(f32[3,2,192,128]{3,2,1,0:T(8,128)} %velocity.5) | copy-start | bytes 1769476
  19.7 8.3 %copy-start.2 = (f32[3,2,192,128]{3,2,1,0:T(8,128)S(1)}, f32[3,2,192,128]{3,2,1,0:T(8,128)}, u32[]{:S(2)}) copy-start(f32[3,2,192,128]{3,2,1,0:T(8,128)} %tendency.1) | copy-start | bytes 1769476
  28.4 6.5 %collective-permute-start.3 = (f32[24,128]{1,0:T(8,128)S(1)}, f32[24,128]{1,0:T(8,128)S(1)}, u32[]{:S(2)}, u32[]{:S(2)}) collective-permute-start(f32[24,128]{1,0:T(8,128)S(1)} %get-tuple-element.14.rest_0_), channel_id=1, source_target_pairs={{24,0},{0,8},{8,16},{16,24},{25,1},{1,9},{9,17},{17,25},{26,2},{2,... | collective-permute-start | bytes 36872 | tf_op jit(solution)/shard_map/ppermute | solution.py:722
  30.5 4.6 %collective-permute-start.2 = (f32[24,128]{1,0:T(8,128)S(1)}, f32[24,128]{1,0:T(8,128)S(1)}, u32[]{:S(2)}, u32[]{:S(2)}) collective-permute-start(f32[24,128]{1,0:T(8,128)S(1)} %get-tuple-element.14.rest_0_), channel_id=1, source_target_pairs={{16,0},{24,8},{0,16},{8,24},{17,1},{25,9},{1,17},{9,25},{18,2},{26... | collective-permute-start | bytes 36872 | tf_op jit(solution)/shard_map/ppermute | solution.py:722
  32.0 3.7 %collective-permute-start.1 = (f32[24,128]{1,0:T(8,128)S(1)}, f32[24,128]{1,0:T(8,128)S(1)}, u32[]{:S(2)}, u32[]{:S(2)}) collective-permute-start(f32[24,128]{1,0:T(8,128)S(1)} %get-tuple-element.14.rest_0_), channel_id=1, source_target_pairs={{8,0},{16,8},{24,16},{0,24},{9,1},{17,9},{25,17},{1,25},{10,2},{18... | collective-permute-start | bytes 36872 | tf_op jit(solution)/shard_map/ppermute | solution.py:722

commit v30 on v29

--- a/solution.py
+++ b/solution.py
@@ -333,20 +333,6 @@
                 kept[i, x, zb] = parts[i]
             kept[6, x, zb] = scale * strain_size(parts) if scale != 1.0 else strain_size(parts)
 
-    for x in range(nx):
-        keep_strain(vel, x, strains, 1.0)
-        for c in range(3):
-            fields = [paired(lambda at: vel[c, at, zb, inner, :], x) for zb in blocks]
-            for zb, f in enumerate(smooth_z(fields)):
-                part[c, x, zb] = f
-    for c in range(3):
-        rims = [smooth_z([paired(lambda at: ends[c, at, zb], x) for zb in blocks]) for x in range(nx)]
-        for x in range(nx):
-            for zb in blocks:
-                rim = smooth_x(lambda at: rims[at][zb], x)
-                filt[c, x, zb, lead - 1 : lead, :] = rim[0:1, :]
-                filt[c, x, zb, lead + rows : lead + rows + 1, :] = rim[1:2, :]
-                filt[c, x, zb, inner, :] = smooth_x(lambda at: part[c, at, zb], x)
     def filter_z(read, kept):
         if not on_matrix_unit:
             for x in range(nx):
@@ -368,6 +354,19 @@
 
     on_matrix_unit = nz <= 256 and rows * nx % 32 == 0 and rows % 8 == 0
     band = band_matrix(nz) if on_matrix_unit else None
+
+    for c in range(3):
+        filter_z(lambda x, zb: vel[c, x, zb, inner, :], c)
+    for x in range(nx):
+        keep_strain(vel, x, strains, 1.0)
+    for c in range(3):
+        rims = [smooth_z([paired(lambda at: ends[c, at, zb], x) for zb in blocks]) for x in range(nx)]
+        for x in range(nx):
+            for zb in blocks:
+                rim = smooth_x(lambda at: rims[at][zb], x)
+                filt[c, x, zb, lead - 1 : lead, :] = rim[0:1, :]
+                filt[c, x, zb, lead + rows : lead + rows + 1, :] = rim[1:2, :]
+                filt[c, x, zb, inner, :] = smooth_x(lambda at: part[c, at, zb], x)
     for i, (a, b) in enumerate(((0, 0), (1, 1), (2, 2), (0, 1), (0, 2), (1, 2))):
         filter_z(lambda x, zb: vel[a, x, zb, inner, :] * vel[b, x, zb, inner, :], 3 + i)
         filter_z(lambda x, zb: strains[6, x, zb] * strains[i, x, zb], 9 + i)

time: 36.9 us -> 37.3 us (1.011)
  no operation moved by 1% of the time
where the time goes in v30:
time: 37.3 us; the launch traced here: 37 us
  blocking collectives  23.5 us (63%)
  starting transfers between devices  5.68 us (15%)
  Pallas kernels  4.91 us (13%)
  waiting for transfers between devices  1.12 us (3%)
  local copies, waits for them, and re-layouts  1.08 us (3%)
  between operations  0.72 us (2%)
    all_to_all x2, blocking collectives, swap_chunks(): lax.all_to_all(chunks, ('gx', 'gz'), split_axis=0, concat_axis=0, tiled=T...  23.5 us
    ppermute x3, starting transfers between devices, body(): lax.ppermute(reduced, 'gy', [(s, i) for i, s in enumerate(sources_of(step...  5.57 us
    pallas_call x1, Pallas kernels, body(): pl.pallas_call(functools.partial(germano_kernel, nz_parts, width, rows, w...  2.81 us
    ppermute x3, waiting for transfers between devices, body(): lax.ppermute(reduced, 'gy', [(s, i) for i, s in enumerate(sources_of(step...  1.11 us
    unnamed x6, local copies, waits for them, and re-layouts  1.07 us
    pallas_call x1, Pallas kernels, body(): pl.pallas_call(functools.partial(finish_kernel, walls), out_shape=jax.Sha...  0.93 us
  transfers between devices with their start and end apart: 4, of which 2 were waited for; matrix products, arithmetic and copies ran while one was open for 0% of the time, Pallas kernels for 9%

profile of v30, /device:TPU:0, one launch (start us, length us, event | category | flops | bytes accessed | tf_op | source)
XLA Modules:
  0.0 37.0 jit_solution(7222324525586640404)
XLA Ops:
  0.6 0.0 copy-start
  0.6 1.1 %copy-done = f32[3,2,192,128]{3,2,1,0:T(8,128)S(1)} copy-done((f32[3,2,192,128]{3,2,1,0:T(8,128)S(1)}, f32[3,2,192,128]{3,2,1,0:T(8,128)}, u32[]{:S(2)}) %copy-start) | copy-done | bytes 589848
  1.7 0.1 pack.1
  1.8 15.3 %all_to_all.10.recv = f32[8,160,128]{2,1,0:T(8,128)S(1)} all-to-all(f32[8,160,128]{2,1,0:T(8,128)S(1)} %pack.1), channel_id=1, replica_groups={{1,3,7,5,0,2,6,4},{9,11,15,13,8,10,14,12},{17,19,23,21,16,18,22,20},{25..., dimensions={0} | all-to-all | bytes 1310720 | tf_op jit(solution)/shard_map/all_to_all | solution.py:639
  17.1 0.1 collective-permute-start
  17.2 2.8 %germano.1.given = f32[8,2,24,128]{3,2,1,0:T(8,128)S(1)} custom-call(s32[1]{0:T(128)} %bitcast.1.rank, s32[1]{0:T(128)} %bitcast.position, f32[8,160,128]{2,1,0:T(8,128)S(1)} %all_to_all.10.recv), custom_call_target="tpu_custom_call" | custom-call | flops 14745600 | bytes 786432 | tf_op jit(solution)/shard_map/germano/pallas_call | solution.py:672
  20.0 0.0 copy-start.1
  20.0 0.0 copy-start.2
  20.0 0.0 collective-permute-done.swapped
  20.1 8.2 %all_to_all.11.back = f32[8,2,24,128]{3,2,1,0:T(8,128)S(1)} all-to-all(f32[8,2,24,128]{3,2,1,0:T(8,128)S(1)} %edge.1), channel_id=1, replica_groups={{7,5,3,1,6,4,2,0},{15,13,11,9,14,12,10,8},{23,21,19,17,22,20,18,16},{31..., dimensions={0} | all-to-all | bytes 393216 | tf_op jit(solution)/shard_map/all_to_all | solution.py:639
  28.3 0.0 copy-done.1
  28.3 0.0 copy-done.2
  28.3 0.4 %sweep.1 = (f32[2,192,128]{2,1,0:T(8,128)S(1)}, f32[24,128]{1,0:T(8,128)S(1)}, f32[2,24,5,8,128]{4,3,2,1,0:T(8,128)S(1)}, f32[2,3,5,8,128]{4,3,2,1,0:T(8,128)S(1)}) custom-call(s32[1]{0:T(128)S(6)} %rem.18.parity, f32[8,2,24,128]{3,2,1,0:T(8,128)S(1)} %all_to_all.11.back, f32[3,2,192,128]{3,2,1,0:T(8,128)S(1)} %copy-done.1, f32[3,2,192,128]{3,2,1,0:T(8,128)S(1)} %copy-done.2), custom_call_target="tpu_custom_call" | custom-call | tf_op jit(solution)/shard_map/sweep/pallas_call | solution.py:706
  28.7 2.2 %collective-permute-start.3 = (f32[24,128]{1,0:T(8,128)S(1)}, f32[24,128]{1,0:T(8,128)S(1)}, u32[]{:S(2)}, u32[]{:S(2)}) collective-permute-start(f32[24,128]{1,0:T(8,128)S(1)} %get-tuple-element.14.rest_0_), channel_id=1, source_target_pairs={{24,0},{0,8},{8,16},{16,24},{25,1},{1,9},{9,17},{17,25},{26,2},{2,... | collective-permute-start | bytes 36872 | tf_op jit(solution)/shard_map/ppermute | solution.py:721
  30.9 1.5 %collective-permute-start.2 = (f32[24,128]{1,0:T(8,128)S(1)}, f32[24,128]{1,0:T(8,128)S(1)}, u32[]{:S(2)}, u32[]{:S(2)}) collective-permute-start(f32[24,128]{1,0:T(8,128)S(1)} %get-tuple-element.14.rest_0_), channel_id=1, source_target_pairs={{16,0},{24,8},{0,16},{8,24},{17,1},{25,9},{1,17},{9,25},{18,2},{26... | collective-permute-start | bytes 36872 | tf_op jit(solution)/shard_map/ppermute | solution.py:721
  32.4 1.9 %collective-permute-start.1 = (f32[24,128]{1,0:T(8,128)S(1)}, f32[24,128]{1,0:T(8,128)S(1)}, u32[]{:S(2)}, u32[]{:S(2)}) collective-permute-start(f32[24,128]{1,0:T(8,128)S(1)} %get-tuple-element.14.rest_0_), channel_id=1, source_target_pairs={{8,0},{16,8},{24,16},{0,24},{9,1},{17,9},{25,17},{1,25},{10,2},{18... | collective-permute-start | bytes 36872 | tf_op jit(solution)/shard_map/ppermute | solution.py:721
  34.3 0.7 %spread.1 = (f32[3,2,192,128]{3,2,1,0:T(8,128)S(1)}, f32[2,2,192,128]{3,2,1,0:T(8,128)S(1)}, f32[2,192,128]{2,1,0:T(8,128)}) custom-call(f32[2,24,5,8,128]{4,3,2,1,0:T(8,128)S(1)} %get-tuple-element.9.factors, f32[2,3,5,8,128]{4,3,2,1,0:T(8,128)S(1)} %get-tuple-element.10.tree, f32[3,2,192,128]{3,2,1,0:T(8,128)S(1)} %copy-done.1, ...), custom_call_target="tpu_custom_call" | custom-call | flops 2949120 | bytes 2359296 | tf_op jit(solution)/shard_map/spread/pallas_call | solution.py:724
  35.0 0.0 collective-permute-done.3.rest_3_
  35.0 0.5 %collective-permute-done.2.rest_2_ = f32[24,128]{1,0:T(8,128)S(1)} collective-permute-done((f32[24,128]{1,0:T(8,128)S(1)}, f32[24,128]{1,0:T(8,128)S(1)}, u32[]{:S(2)}, u32[]{:S(2)}) %collective-permute-start.2) | collective-permute-done | bytes 12320 | tf_op jit(solution)/shard_map/ppermute | solution.py:721
  35.5 0.6 %collective-permute-done.1.rest_1_ = f32[24,128]{1,0:T(8,128)S(1)} collective-permute-done((f32[24,128]{1,0:T(8,128)S(1)}, f32[24,128]{1,0:T(8,128)S(1)}, u32[]{:S(2)}, u32[]{:S(2)}) %collective-permute-start.1) | collective-permute-done | bytes 12320 | tf_op jit(solution)/shard_map/ppermute | solution.py:721
  36.1 0.9 %finish.1 = f32[3,2,192,128]{3,2,1,0:T(8,128)} custom-call(s32[1]{0:T(128)} %bitcast.position, f32[3,2,192,128]{3,2,1,0:T(8,128)S(1)} %get-tuple-element.12.particular, f32[2,2,192,128]{3,2,1,0:T(8,128)S(1)} %get-tuple-element.13.response, f32[24,128]{1,0:T(8,128)S(1)} %get-tuple-element.14.rest_0_, f32[24,128]{1,0:T(8,128)S(1)} %collective-permute-done.1.rest_1_, ...), custom_call_target="tpu_custom_call" | custom-call | tf_op jit(solution)/shard_map/finish/pallas_call | solution.py:740
  (2 shorter events, 0.0 us)
Async XLA Ops:
  0.6 1.1 %copy-start = (f32[3,2,192,128]{3,2,1,0:T(8,128)S(1)}, f32[3,2,192,128]{3,2,1,0:T(8,128)}, u32[]{:S(2)}) copy-start(f32[3,2,192,128]{3,2,1,0:T(8,128)} %velocity.5) | copy-start | bytes 1769476
  17.1 3.0 %collective-permute-start = (f32[8,8,128]{2,1,0:T(8,128)S(1)}, f32[8,8,128]{2,1,0:T(8,128)S(1)}, u32[]{:S(2)}, u32[]{:S(2)}) collective-permute-start(f32[8,8,128]{2,1,0:T(8,128)S(1)} %slice.4), channel_id=1, source_target_pairs={{0,1},{1,0},{2,3},{3,2},{4,5},{5,4},{6,14},{7,15},{8,9},{9,8},{10,... | collective-permute-start | bytes 98312 | tf_op jit(solution)/shard_map/ppermute | solution.py:668
  20.0 8.3 %copy-start.1 = (f32[3,2,192,128]{3,2,1,0:T(8,128)S(1)}, f32[3,2,192,128]{3,2,1,0:T(8,128)}, u32[]{:S(2)}) copy-start(f32[3,2,192,128]{3,2,1,0:T(8,128)} %velocity.5) | copy-start | bytes 1769476
  20.0 8.3 %copy-start.2 = (f32[3,2,192,128]{3,2,1,0:T(8,128)S(1)}, f32[3,2,192,128]{3,2,1,0:T(8,128)}, u32[]{:S(2)}) copy-start(f32[3,2,192,128]{3,2,1,0:T(8,128)} %tendency.1) | copy-start | bytes 1769476
  28.7 6.3 %collective-permute-start.3 = (f32[24,128]{1,0:T(8,128)S(1)}, f32[24,128]{1,0:T(8,128)S(1)}, u32[]{:S(2)}, u32[]{:S(2)}) collective-permute-start(f32[24,128]{1,0:T(8,128)S(1)} %get-tuple-element.14.rest_0_), channel_id=1, source_target_pairs={{24,0},{0,8},{8,16},{16,24},{25,1},{1,9},{9,17},{17,25},{26,2},{2,... | collective-permute-start | bytes 36872 | tf_op jit(solution)/shard_map/ppermute | solution.py:721
  30.9 4.6 %collective-permute-start.2 = (f32[24,128]{1,0:T(8,128)S(1)}, f32[24,128]{1,0:T(8,128)S(1)}, u32[]{:S(2)}, u32[]{:S(2)}) collective-permute-start(f32[24,128]{1,0:T(8,128)S(1)} %get-tuple-element.14.rest_0_), channel_id=1, source_target_pairs={{16,0},{24,8},{0,16},{8,24},{17,1},{25,9},{1,17},{9,25},{18,2},{26... | collective-permute-start | bytes 36872 | tf_op jit(solution)/shard_map/ppermute | solution.py:721
  32.4 3.7 %collective-permute-start.1 = (f32[24,128]{1,0:T(8,128)S(1)}, f32[24,128]{1,0:T(8,128)S(1)}, u32[]{:S(2)}, u32[]{:S(2)}) collective-permute-start(f32[24,128]{1,0:T(8,128)S(1)} %get-tuple-element.14.rest_0_), channel_id=1, source_target_pairs={{8,0},{16,8},{24,16},{0,24},{9,1},{17,9},{25,17},{1,25},{10,2},{18... | collective-permute-start | bytes 36872 | tf_op jit(solution)/shard_map/ppermute | solution.py:721

commit v31 on v29

--- a/solution.py
+++ b/solution.py
@@ -347,8 +347,8 @@
                 filt[c, x, zb, lead - 1 : lead, :] = rim[0:1, :]
                 filt[c, x, zb, lead + rows : lead + rows + 1, :] = rim[1:2, :]
                 filt[c, x, zb, inner, :] = smooth_x(lambda at: part[c, at, zb], x)
-    def filter_z(read, kept):
-        if not on_matrix_unit:
+    def filter_z(read, kept, rotate=False):
+        if rotate or not on_matrix_unit:
             for x in range(nx):
                 fields = [paired(lambda at: read(at, zb), x) for zb in blocks]
                 for zb, f in enumerate(smooth_z(fields)):
@@ -369,7 +369,7 @@
     on_matrix_unit = nz <= 256 and rows * nx % 32 == 0 and rows % 8 == 0
     band = band_matrix(nz) if on_matrix_unit else None
     for i, (a, b) in enumerate(((0, 0), (1, 1), (2, 2), (0, 1), (0, 2), (1, 2))):
-        filter_z(lambda x, zb: vel[a, x, zb, inner, :] * vel[b, x, zb, inner, :], 3 + i)
+        filter_z(lambda x, zb: vel[a, x, zb, inner, :] * vel[b, x, zb, inner, :], 3 + i, i % 2 == 1)
         filter_z(lambda x, zb: strains[6, x, zb] * strains[i, x, zb], 9 + i)
     for x in range(nx):
         keep_strain(filt, x, means, 0.25)

time: 36.9 us -> 36.8 us (level)
  transfers between devices with their start and end apart: 4 -> 4, of which waited for: 2 -> 2; matrix products, arithmetic and copies ran while one was open for 0% -> 0% of each run, Pallas kernels for 9% -> 8%
where the time goes in v31:
time: 36.8 us; the launch traced here: 36.5 us
  blocking collectives  23.5 us (64%)
  starting transfers between devices  6.04 us (16%)
  Pallas kernels  4.41 us (12%)
  local copies, waits for them, and re-layouts  1.08 us (3%)
  waiting for transfers between devices  0.76 us (2%)
  between operations  0.72 us (2%)
    all_to_all x2, blocking collectives, swap_chunks(): lax.all_to_all(chunks, ('gx', 'gz'), split_axis=0, concat_axis=0, tiled=T...  23.5 us
    ppermute x3, starting transfers between devices, body(): lax.ppermute(reduced, 'gy', [(s, i) for i, s in enumerate(sources_of(step...  5.92 us
    pallas_call x1, Pallas kernels, body(): pl.pallas_call(functools.partial(germano_kernel, nz_parts, width, rows, w...  2.31 us
    unnamed x6, local copies, waits for them, and re-layouts  1.07 us
    pallas_call x1, Pallas kernels, body(): pl.pallas_call(functools.partial(finish_kernel, walls), out_shape=jax.Sha...  0.93 us
    ppermute x3, waiting for transfers between devices, body(): lax.ppermute(reduced, 'gy', [(s, i) for i, s in enumerate(sources_of(step...  0.76 us
  transfers between devices with their start and end apart: 4, of which 2 were waited for; matrix products, arithmetic and copies ran while one was open for 0% of the time, Pallas kernels for 8%

profile of v31, /device:TPU:0, one launch (start us, length us, event | category | flops | bytes accessed | tf_op | source)
XLA Modules:
  0.0 36.5 jit_solution(11294538402378362290)
XLA Ops:
  0.6 0.0 copy-start
  0.6 1.1 %copy-done = f32[3,2,192,128]{3,2,1,0:T(8,128)S(1)} copy-done((f32[3,2,192,128]{3,2,1,0:T(8,128)S(1)}, f32[3,2,192,128]{3,2,1,0:T(8,128)}, u32[]{:S(2)}) %copy-start) | copy-done | bytes 589848
  1.7 0.1 pack.1
  1.8 15.3 %all_to_all.10.recv = f32[8,160,128]{2,1,0:T(8,128)S(1)} all-to-all(f32[8,160,128]{2,1,0:T(8,128)S(1)} %pack.1), channel_id=1, replica_groups={{1,3,7,5,0,2,6,4},{9,11,15,13,8,10,14,12},{17,19,23,21,16,18,22,20},{25..., dimensions={0} | all-to-all | bytes 1310720 | tf_op jit(solution)/shard_map/all_to_all | solution.py:640
  17.1 0.1 collective-permute-start
  17.2 2.3 %germano.1.given = f32[8,2,24,128]{3,2,1,0:T(8,128)S(1)} custom-call(s32[1]{0:T(128)} %bitcast.1.rank, s32[1]{0:T(128)} %bitcast.position, f32[8,160,128]{2,1,0:T(8,128)S(1)} %all_to_all.10.recv), custom_call_target="tpu_custom_call" | custom-call | flops 14745600 | bytes 786432 | tf_op jit(solution)/shard_map/germano/pallas_call | solution.py:673
  19.5 0.0 copy-start.1
  19.5 0.0 copy-start.2
  19.5 0.0 collective-permute-done.swapped
  19.6 8.2 %all_to_all.11.back = f32[8,2,24,128]{3,2,1,0:T(8,128)S(1)} all-to-all(f32[8,2,24,128]{3,2,1,0:T(8,128)S(1)} %edge.1), channel_id=1, replica_groups={{7,5,3,1,6,4,2,0},{15,13,11,9,14,12,10,8},{23,21,19,17,22,20,18,16},{31..., dimensions={0} | all-to-all | bytes 393216 | tf_op jit(solution)/shard_map/all_to_all | solution.py:640
  27.8 0.0 copy-done.1
  27.8 0.0 copy-done.2
  27.8 0.4 %sweep.1 = (f32[2,192,128]{2,1,0:T(8,128)S(1)}, f32[24,128]{1,0:T(8,128)S(1)}, f32[2,24,5,8,128]{4,3,2,1,0:T(8,128)S(1)}, f32[2,3,5,8,128]{4,3,2,1,0:T(8,128)S(1)}) custom-call(s32[1]{0:T(128)S(6)} %rem.18.parity, f32[8,2,24,128]{3,2,1,0:T(8,128)S(1)} %all_to_all.11.back, f32[3,2,192,128]{3,2,1,0:T(8,128)S(1)} %copy-done.1, f32[3,2,192,128]{3,2,1,0:T(8,128)S(1)} %copy-done.2), custom_call_target="tpu_custom_call" | custom-call | tf_op jit(solution)/shard_map/sweep/pallas_call | solution.py:707
  28.2 2.2 %collective-permute-start.3 = (f32[24,128]{1,0:T(8,128)S(1)}, f32[24,128]{1,0:T(8,128)S(1)}, u32[]{:S(2)}, u32[]{:S(2)}) collective-permute-start(f32[24,128]{1,0:T(8,128)S(1)} %get-tuple-element.14.rest_0_), channel_id=1, source_target_pairs={{24,0},{0,8},{8,16},{16,24},{25,1},{1,9},{9,17},{17,25},{26,2},{2,... | collective-permute-start | bytes 36872 | tf_op jit(solution)/shard_map/ppermute | solution.py:722
  30.4 1.5 %collective-permute-start.2 = (f32[24,128]{1,0:T(8,128)S(1)}, f32[24,128]{1,0:T(8,128)S(1)}, u32[]{:S(2)}, u32[]{:S(2)}) collective-permute-start(f32[24,128]{1,0:T(8,128)S(1)} %get-tuple-element.14.rest_0_), channel_id=1, source_target_pairs={{16,0},{24,8},{0,16},{8,24},{17,1},{25,9},{1,17},{9,25},{18,2},{26... | collective-permute-start | bytes 36872 | tf_op jit(solution)/shard_map/ppermute | solution.py:722
  31.9 2.2 %collective-permute-start.1 = (f32[24,128]{1,0:T(8,128)S(1)}, f32[24,128]{1,0:T(8,128)S(1)}, u32[]{:S(2)}, u32[]{:S(2)}) collective-permute-start(f32[24,128]{1,0:T(8,128)S(1)} %get-tuple-element.14.rest_0_), channel_id=1, source_target_pairs={{8,0},{16,8},{24,16},{0,24},{9,1},{17,9},{25,17},{1,25},{10,2},{18... | collective-permute-start | bytes 36872 | tf_op jit(solution)/shard_map/ppermute | solution.py:722
  34.1 0.7 %spread.1 = (f32[3,2,192,128]{3,2,1,0:T(8,128)S(1)}, f32[2,2,192,128]{3,2,1,0:T(8,128)S(1)}, f32[2,192,128]{2,1,0:T(8,128)}) custom-call(f32[2,24,5,8,128]{4,3,2,1,0:T(8,128)S(1)} %get-tuple-element.9.factors, f32[2,3,5,8,128]{4,3,2,1,0:T(8,128)S(1)} %get-tuple-element.10.tree, f32[3,2,192,128]{3,2,1,0:T(8,128)S(1)} %copy-done.1, ...), custom_call_target="tpu_custom_call" | custom-call | flops 2949120 | bytes 2359296 | tf_op jit(solution)/shard_map/spread/pallas_call | solution.py:725
  34.8 0.0 collective-permute-done.3.rest_3_
  34.8 0.1 collective-permute-done.2.rest_2_
  35.0 0.6 %collective-permute-done.1.rest_1_ = f32[24,128]{1,0:T(8,128)S(1)} collective-permute-done((f32[24,128]{1,0:T(8,128)S(1)}, f32[24,128]{1,0:T(8,128)S(1)}, u32[]{:S(2)}, u32[]{:S(2)}) %collective-permute-start.1) | collective-permute-done | bytes 12320 | tf_op jit(solution)/shard_map/ppermute | solution.py:722
  35.6 0.9 %finish.1 = f32[3,2,192,128]{3,2,1,0:T(8,128)} custom-call(s32[1]{0:T(128)} %bitcast.position, f32[3,2,192,128]{3,2,1,0:T(8,128)S(1)} %get-tuple-element.12.particular, f32[2,2,192,128]{3,2,1,0:T(8,128)S(1)} %get-tuple-element.13.response, f32[24,128]{1,0:T(8,128)S(1)} %get-tuple-element.14.rest_0_, f32[24,128]{1,0:T(8,128)S(1)} %collective-permute-done.1.rest_1_, ...), custom_call_target="tpu_custom_call" | custom-call | tf_op jit(solution)/shard_map/finish/pallas_call | solution.py:741
  (2 shorter events, 0.0 us)
Async XLA Ops:
  0.6 1.1 %copy-start = (f32[3,2,192,128]{3,2,1,0:T(8,128)S(1)}, f32[3,2,192,128]{3,2,1,0:T(8,128)}, u32[]{:S(2)}) copy-start(f32[3,2,192,128]{3,2,1,0:T(8,128)} %velocity.5) | copy-start | bytes 1769476
  17.1 2.5 %collective-permute-start = (f32[8,8,128]{2,1,0:T(8,128)S(1)}, f32[8,8,128]{2,1,0:T(8,128)S(1)}, u32[]{:S(2)}, u32[]{:S(2)}) collective-permute-start(f32[8,8,128]{2,1,0:T(8,128)S(1)} %slice.4), channel_id=1, source_target_pairs={{0,1},{1,0},{2,3},{3,2},{4,5},{5,4},{6,14},{7,15},{8,9},{9,8},{10,... | collective-permute-start | bytes 98312 | tf_op jit(solution)/shard_map/ppermute | solution.py:669
  19.5 8.3 %copy-start.1 = (f32[3,2,192,128]{3,2,1,0:T(8,128)S(1)}, f32[3,2,192,128]{3,2,1,0:T(8,128)}, u32[]{:S(2)}) copy-start(f32[3,2,192,128]{3,2,1,0:T(8,128)} %velocity.5) | copy-start | bytes 1769476
  19.5 8.3 %copy-start.2 = (f32[3,2,192,128]{3,2,1,0:T(8,128)S(1)}, f32[3,2,192,128]{3,2,1,0:T(8,128)}, u32[]{:S(2)}) copy-start(f32[3,2,192,128]{3,2,1,0:T(8,128)} %tendency.1) | copy-start | bytes 1769476
  28.2 6.6 %collective-permute-start.3 = (f32[24,128]{1,0:T(8,128)S(1)}, f32[24,128]{1,0:T(8,128)S(1)}, u32[]{:S(2)}, u32[]{:S(2)}) collective-permute-start(f32[24,128]{1,0:T(8,128)S(1)} %get-tuple-element.14.rest_0_), channel_id=1, source_target_pairs={{24,0},{0,8},{8,16},{16,24},{25,1},{1,9},{9,17},{17,25},{26,2},{2,... | collective-permute-start | bytes 36872 | tf_op jit(solution)/shard_map/ppermute | solution.py:722
  30.4 4.6 %collective-permute-start.2 = (f32[24,128]{1,0:T(8,128)S(1)}, f32[24,128]{1,0:T(8,128)S(1)}, u32[]{:S(2)}, u32[]{:S(2)}) collective-permute-start(f32[24,128]{1,0:T(8,128)S(1)} %get-tuple-element.14.rest_0_), channel_id=1, source_target_pairs={{16,0},{24,8},{0,16},{8,24},{17,1},{25,9},{1,17},{9,25},{18,2},{26... | collective-permute-start | bytes 36872 | tf_op jit(solution)/shard_map/ppermute | solution.py:722
  31.9 3.7 %collective-permute-start.1 = (f32[24,128]{1,0:T(8,128)S(1)}, f32[24,128]{1,0:T(8,128)S(1)}, u32[]{:S(2)}, u32[]{:S(2)}) collective-permute-start(f32[24,128]{1,0:T(8,128)S(1)} %get-tuple-element.14.rest_0_), channel_id=1, source_target_pairs={{8,0},{16,8},{24,16},{0,24},{9,1},{17,9},{25,17},{1,25},{10,2},{18... | collective-permute-start | bytes 36872 | tf_op jit(solution)/shard_map/ppermute | solution.py:722
